TPU v7x, 32 devices: a whole 2x2x4 slice. The times are simulated.
32 devices in a mesh: grp: 2 (over y), seq: 16 (over z, x, core).
Axes of the slice: x: 2, y: 2, z: 4, core: 2. Of those that a mesh axis runs over, the one named last changes fastest.
Arguments:
- streams: bfloat16 [3, 4096, 4096], P(None, ('grp', 'seq')), parts along dimension 1, may hold values from -12 to 12
- long_filter: bfloat16 [4096, 2048], P('seq'), may hold values from -1 to 1
- gain: bfloat16 [4096], replicated, may hold values from 0.099609375 to 1.8984375
- unembed: bfloat16 [4096, 512], P('seq'), may hold values from -8 to 8
- offsets: int32 [32], P('grp'), parts along dimension 0, may hold values from 0 to 127
- ref_ids: int32 [32], P(('grp', 'seq')), parts along dimension 0, may hold values from 0 to 511
- alt_ids: int32 [32], P(('grp', 'seq')), parts along dimension 0, may hold values from 0 to 511
Outputs:
- mixed: bfloat16 [4096, 4096], P(('grp', 'seq')), parts along dimension 0
- scores: float32 [2, 32], P(None, ('grp', 'seq')), parts along dimension 1
There are 2 independent parts, one for each index of `grp`. A program takes and returns all parts, laid end to end along the dimension named above; an argument that names none is the same for every part. Nothing has to cross between parts.
All inputs are finite; a program needn't handle non-finite values.
Results may differ from a plain program's by a relative error of at most 0.0057.
Values may be sent and summed in bfloat16 or wider, within the bound.
No kernel may reach another device: no remote copies, remote signals or barrier semaphores. Data moves between devices by JAX's collectives and lax.ppermute only.
A program may use at most 128 MiB of HBM per device.

v0:
```python
import functools
import math

import jax
import jax.numpy as jnp
import numpy as np
from jax import lax
from jax.experimental import pallas as pl
from jax.experimental.pallas import tpu as pltpu
from jax.sharding import PartitionSpec as P

norm_eps = 1e-06
f32 = jnp.float32
bf16 = jnp.bfloat16
row_tile = 16
lane_tile = 128
max_chunks = 2
MIB = 1 << 20


def round_up(value, step):
    return -(-value // step) * step


def split_bf16(values):
    high = values.astype(bf16)
    low = (values - high.astype(f32)).astype(bf16)
    return high, low


def block_tables(block):
    turns = (4 * np.arange(block)[:, None] + 1) * np.arange(block)[None, :] % (4 * block)
    theta = turns * (math.pi / (2 * block))
    table = np.concatenate([np.cos(theta), np.sin(theta)], axis=0)
    parts = []
    for matrix in (table, table.T / block):
        high = matrix.astype(bf16)
        low = (matrix - high.astype(np.float64)).astype(bf16)
        parts.append(np.concatenate([high, low], axis=0))
    return parts


def block_devices(n_devices, tok_rows):
    target = math.isqrt(32 * n_devices * tok_rows)
    count = 1
    while n_devices % (2 * count) == 0 and 2 * count * tok_rows <= target:
        count *= 2
    return count


def whole_spec():
    return pl.BlockSpec(memory_space=pltpu.VMEM)


def product_kernel(chunks, width, vars_dev, rows_ref, streams_ref, *out_refs):
    tok_rows = streams_ref.shape[1]
    n_owners = out_refs[0].shape[0]
    extra = out_refs[0].shape[1] - tok_rows
    place = lax.broadcasted_iota(jnp.int32, (extra, tok_rows), 0)
    column = lax.broadcasted_iota(jnp.int32, (extra, tok_rows), 1)
    for owner in range(n_owners):
        gates = jnp.zeros((extra, width), f32)
        for chunk in range(chunks):
            lanes = pl.ds((owner * chunks + chunk) * width, width)
            left = streams_ref[1, :, lanes].astype(f32)
            right = streams_ref[2, :, lanes].astype(f32)
            out_refs[chunk][owner, :tok_rows, :] = (left * right).astype(bf16)
            picker = jnp.zeros((extra, tok_rows), jnp.bool_)
            for var in range(vars_dev):
                picker |= (place == chunk * vars_dev + var) & (column == rows_ref[var])
            gates += jnp.dot(
                picker.astype(f32).astype(bf16),
                streams_ref[0, :, lanes],
                preferred_element_type=f32,
            )
        out_refs[0][owner, tok_rows:, :] = gates.astype(bf16)


def make_products(streams, local_rows, n_devices, chunks, extra):
    _, tok_rows, model_width = streams.shape
    vars_dev = local_rows.shape[0]
    group_width = model_width // n_devices
    width = group_width // chunks
    owners = max(1, n_devices // 4)
    while owners * group_width % lane_tile:
        owners *= 2
    steps = n_devices // owners
    rows_out = [tok_rows + extra] + [tok_rows] * (chunks - 1)
    return pl.pallas_call(
        functools.partial(product_kernel, chunks, width, vars_dev),
        grid=(steps,),
        in_specs=[
            pl.BlockSpec(memory_space=pltpu.SMEM),
            pl.BlockSpec((3, tok_rows, owners * group_width), lambda i: (0, 0, i)),
        ],
        out_specs=[pl.BlockSpec((owners, rows, width), lambda i: (i, 0, 0)) for rows in rows_out],
        out_shape=[jax.ShapeDtypeStruct((n_devices, rows, width), bf16) for rows in rows_out],
        compiler_params=pltpu.CompilerParams(vmem_limit_bytes=24 * MIB),
        name="products",
    )(local_rows, streams)


def spectrum_kernel(block, filter_ref, forward_ref, out_ref):
    n_blocks = out_ref.shape[0]
    for index in range(n_blocks):
        taps = filter_ref[:, index * block : (index + 1) * block]
        both = lax.dot_general(
            forward_ref[...], taps, (((1,), (1,)), ((), ())), preferred_element_type=f32
        )
        out_ref[index] = both[: 2 * block] + both[2 * block :]


def filter_spectrum(taps, forward, block):
    width, length = taps.shape
    n_blocks = length // block
    return pl.pallas_call(
        functools.partial(spectrum_kernel, block),
        in_specs=[whole_spec(), whole_spec()],
        out_specs=whole_spec(),
        out_shape=jax.ShapeDtypeStruct((n_blocks, 2 * block, width), f32),
        compiler_params=pltpu.CompilerParams(vmem_limit_bytes=40 * MIB),
        cost_estimate=pl.CostEstimate(
            flops=8 * block * length * width, bytes_accessed=4 * MIB, transcendentals=0
        ),
        name="filter_spectrum",
    )(taps, forward)


def convolve(chunk_ref, spectrum_ref, forward_ref, inverse_ref, out_ref, points, tok_rows):
    n_blocks, double, width = points.shape
    block = double // 2
    per_block = block // tok_rows
    group = max(1, min(n_blocks, 256 // width)) if width % lane_tile == 0 else 1

    def forward_step(step, carry):
        pieces = []
        for member in range(group):
            start = (step * group + member) * per_block
            rows = chunk_ref[pl.ds(start, per_block), :tok_rows, :]
            pieces.append(rows.reshape(block, width))
        signal = pieces[0] if group == 1 else jnp.concatenate(pieces, axis=1)
        both = jnp.dot(forward_ref[...], signal, preferred_element_type=f32)
        total = both[:double] + both[double:]
        for member in range(group):
            points[step * group + member] = total[:, member * width : (member + 1) * width]
        return carry

    lax.fori_loop(0, n_blocks // group, forward_step, 0)

    def multiply_step(step, carry):
        start = pl.multiple_of(step * row_tile, row_tile)
        upper = pl.ds(start, row_tile)
        lower = pl.ds(pl.multiple_of(block + start, row_tile), row_tile)

        def block_sum(total):
            sum_re = jnp.zeros((row_tile, width), f32)
            sum_im = jnp.zeros((row_tile, width), f32)
            for delay in range(total + 1):
                a_re = points[total - delay, upper, :]
                a_im = points[total - delay, lower, :]
                b_re = spectrum_ref[delay, upper, :]
                b_im = spectrum_ref[delay, lower, :]
                sum_re += a_re * b_re - a_im * b_im
                sum_im += a_re * b_im + a_im * b_re
            return sum_re, sum_im

        after_re, after_im = block_sum(n_blocks - 1)
        for total in range(n_blocks - 1, 0, -1):
            sum_re, sum_im = block_sum(total - 1)
            points[total, upper, :] = after_re + sum_im
            points[total, lower, :] = after_im - sum_re
            after_re, after_im = sum_re, sum_im
        points[0, upper, :] = after_re
        points[0, lower, :] = after_im
        return carry

    lax.fori_loop(0, block // row_tile, multiply_step, 0)

    def inverse_step(step, carry):
        first = step * group
        pieces = [points[first + member] for member in range(group)]
        highs, lows = split_bf16(pieces[0] if group == 1 else jnp.concatenate(pieces, axis=1))
        both = jnp.dot(inverse_ref[...], highs, preferred_element_type=f32)
        rest = jnp.dot(inverse_ref[:block, :], lows, preferred_element_type=f32)
        result = (both[:block] + both[block:] + rest).astype(bf16)
        for member in range(group):
            piece = result[:, member * width : (member + 1) * width]
            out_ref[pl.ds((first + member) * per_block, per_block), :tok_rows, :] = piece.reshape(
                per_block, tok_rows, width
            )
        return carry

    lax.fori_loop(0, n_blocks // group, inverse_step, 0)


def score_rows(index, vars_dev, tok_rows, positions, gate_block, out_ref, gain_row, unembed):
    n_devices, extra, width = gate_block.shape
    gates = gate_block.astype(f32)
    place = lax.broadcasted_iota(jnp.int32, (n_devices, extra, width), 1)
    picked = [
        jnp.sum(jnp.where(place == index * vars_dev + var, gates, 0.0), axis=1)
        for var in range(vars_dev)
    ]
    gate_rows = picked[0] if vars_dev == 1 else jnp.concatenate(picked, axis=0)
    length = n_devices * tok_rows
    column = lax.broadcasted_iota(jnp.int32, (positions.shape[0], length), 1)
    picker = (column == positions).astype(f32).astype(bf16)
    filtered = jnp.dot(
        picker, out_ref[:, :tok_rows, :].reshape(length, width), preferred_element_type=f32
    )
    rows = (gate_rows * filtered).astype(bf16).astype(f32)
    weighted = (rows * gain_row).astype(bf16)
    return jnp.dot(weighted, unembed, preferred_element_type=f32), rows * rows


def chunk_kernel(index, chunks, vars_dev, tok_rows, *refs):
    refs = list(refs)
    chunk_ref, spectrum_ref, forward_ref, inverse_ref = refs[:4]
    positions_ref, gain_ref, unembed_ref = refs[4:7]
    refs = refs[7:]
    first, last = index == 0, index == chunks - 1
    gates_ref = None if first else refs.pop(0)
    raw_before, square_before = (None, None) if first else (refs.pop(0), refs.pop(0))
    out_ref = refs.pop(0)
    raw_out, square_out = (None, None) if last else (refs.pop(0), refs.pop(0))
    gates_out = refs.pop(0) if first and not last else None
    points = refs[0]
    convolve(chunk_ref, spectrum_ref, forward_ref, inverse_ref, out_ref, points, tok_rows)
    gate_block = chunk_ref[:, tok_rows:, :] if first else gates_ref[...]
    raw, squares = score_rows(
        index, vars_dev, tok_rows, positions_ref[...], gate_block, out_ref, gain_ref[...], unembed_ref[...]
    )
    if not first:
        raw = raw + raw_before[...]
        squares = squares + square_before[...]
    if gates_out is not None:
        gates_out[...] = gate_block
    if not last:
        raw_out[...] = raw
        square_out[...] = squares
        return
    packed = refs[1]
    n_devices, _, width = out_ref.shape
    extra = out_ref.shape[1] - tok_rows
    per_row = raw.shape[1] // width
    packed[...] = jnp.zeros_like(packed)
    for var in range(vars_dev):
        mine = slice(var * n_devices, (var + 1) * n_devices)
        pieces = [raw[mine, r * width : (r + 1) * width] for r in range(per_row)] + [squares[mine]]
        for row, piece in enumerate(pieces):
            rounded = piece.astype(bf16).astype(f32)
            base = var * 2 * (per_row + 1) + row
            packed[pl.ds(base, n_devices, stride=extra), :] = rounded
            packed[pl.ds(base + per_row + 1, n_devices, stride=extra), :] = piece - rounded
    out_ref[:, tok_rows:, :] = packed[...].reshape(n_devices, extra, width).astype(bf16)


def filter_chunk(index, chunks, vars_dev, tok_rows, extra, operands, carried):
    moved, spectrum = operands[:2]
    n_devices, _, width = moved.shape
    n_blocks, double, _ = spectrum.shape
    vocab = operands[6].shape[1]
    n_vars = operands[4].shape[0]
    first, last = index == 0, index == chunks - 1
    rows_out = tok_rows + (extra if last else 0)
    out_shape = [jax.ShapeDtypeStruct((n_devices, rows_out, width), bf16)]
    scratch = [pltpu.VMEM((n_blocks, double, width), f32)]
    if last:
        scratch.append(pltpu.VMEM((n_devices * extra, width), f32))
    else:
        out_shape.append(jax.ShapeDtypeStruct((n_vars, vocab), f32))
        out_shape.append(jax.ShapeDtypeStruct((n_vars, width), f32))
    if first and not last:
        out_shape.append(jax.ShapeDtypeStruct((n_devices, moved.shape[1] - tok_rows, width), bf16))
    flops = 2 * width * n_blocks * (double * double * 5 // 2 + 4 * n_blocks * double)
    return pl.pallas_call(
        functools.partial(chunk_kernel, index, chunks, vars_dev, tok_rows),
        in_specs=[whole_spec()] * (len(operands) + len(carried)),
        out_specs=[whole_spec()] * len(out_shape),
        out_shape=out_shape,
        scratch_shapes=scratch,
        compiler_params=pltpu.CompilerParams(vmem_limit_bytes=(20 if n_blocks <= 8 else 58) * MIB),
        cost_estimate=pl.CostEstimate(flops=flops, bytes_accessed=8 * MIB, transcendentals=0),
        name="filter_chunk",
    )(*operands, *carried)


def finish_kernel(chunks, vars_dev, vocab, ref_ref, alt_ref, streams_ref, *refs):
    back_refs, mixed_ref, scores_ref, sums = refs[:chunks], refs[chunks], refs[chunks + 1], refs[chunks + 2]
    tok_rows = streams_ref.shape[1]
    owners, _, width = back_refs[0].shape
    step = pl.program_id(0)
    for owner in range(owners):
        for chunk in range(chunks):
            lanes = pl.ds((owner * chunks + chunk) * width, width)
            gate = streams_ref[0, :, lanes].astype(f32)
            filtered = back_refs[chunk][owner, :tok_rows, :].astype(f32)
            mixed_ref[:, lanes] = (gate * filtered).astype(bf16)
    part = jnp.sum(back_refs[-1][:, tok_rows:, :].astype(f32), axis=0)

    @pl.when(step == 0)
    def _():
        sums[...] = part

    @pl.when(step > 0)
    def _():
        sums[...] += part

    @pl.when(step == pl.num_programs(0) - 1)
    def _():
        per_row = vocab // width
        model_width = pl.num_programs(0) * owners * chunks * width
        ids = lax.broadcasted_iota(jnp.int32, (per_row, width), 0) * width
        ids += lax.broadcasted_iota(jnp.int32, (per_row, width), 1)
        row = lax.broadcasted_iota(jnp.int32, (2, vars_dev), 0)
        column = lax.broadcasted_iota(jnp.int32, (2, vars_dev), 1)
        scores = jnp.zeros((2, vars_dev), f32)
        for var in range(vars_dev):
            base = var * 2 * (per_row + 1)
            both = sums[base : base + per_row + 1, :]
            both = both + sums[base + per_row + 1 : base + 2 * (per_row + 1), :]
            square = jnp.sum(both[per_row:, :], axis=1, keepdims=True)
            logits = both[:per_row, :] * lax.rsqrt(square / model_width + norm_eps)

            def whole_sum(values):
                return jnp.sum(jnp.sum(values, axis=1, keepdims=True), axis=0, keepdims=True)

            largest = jnp.max(jnp.max(logits, axis=1, keepdims=True), axis=0, keepdims=True)
            log_total = largest + jnp.log(whole_sum(jnp.exp(logits - largest)))
            ref_logit = whole_sum(jnp.where(ids == ref_ref[var], logits, 0.0))
            alt_logit = whole_sum(jnp.where(ids == alt_ref[var], logits, 0.0))
            pair = jnp.where(row == 0, ref_logit - log_total, alt_logit - ref_logit)
            scores = jnp.where(column == var, pair, scores)
        scores_ref[...] = scores


def finish(streams, backs, ref_ids, alt_ids, vocab):
    _, tok_rows, model_width = streams.shape
    chunks = len(backs)
    n_devices, _, width = backs[0].shape
    vars_dev = ref_ids.shape[0]
    owners = max(1, n_devices // 4)
    while owners * chunks * width % lane_tile:
        owners *= 2
    extra = backs[-1].shape[1] - tok_rows
    return pl.pallas_call(
        functools.partial(finish_kernel, chunks, vars_dev, vocab),
        grid=(n_devices // owners,),
        in_specs=[
            pl.BlockSpec(memory_space=pltpu.SMEM),
            pl.BlockSpec(memory_space=pltpu.SMEM),
            pl.BlockSpec((1, tok_rows, owners * chunks * width), lambda i: (0, 0, i)),
        ]
        + [pl.BlockSpec((owners, back.shape[1], width), lambda i: (i, 0, 0)) for back in backs],
        out_specs=[
            pl.BlockSpec((tok_rows, owners * chunks * width), lambda i: (0, i)),
            pl.BlockSpec((2, vars_dev), lambda i: (0, 0)),
        ],
        out_shape=[
            jax.ShapeDtypeStruct((tok_rows, model_width), bf16),
            jax.ShapeDtypeStruct((2, vars_dev), f32),
        ],
        scratch_shapes=[pltpu.VMEM((extra, width), f32)],
        compiler_params=pltpu.CompilerParams(vmem_limit_bytes=24 * MIB),
        name="finish",
    )(ref_ids, alt_ids, streams, *backs)


def shards(streams, long_filter, gain, unembed, offsets, ref_ids, alt_ids):
    n_devices = lax.axis_size("seq")
    my_index = lax.axis_index("seq")
    _, tok_rows, model_width = streams.shape
    group_width = model_width // n_devices
    vars_dev = ref_ids.shape[0]
    vocab = unembed.shape[1]
    chunks = max(1, min(max_chunks, group_width // lane_tile))
    width = group_width // chunks
    block = tok_rows * block_devices(n_devices, tok_rows)
    forward, inverse = (jnp.asarray(table) for table in block_tables(block))

    slot = tok_rows // vars_dev
    starts = jnp.arange(vars_dev, dtype=jnp.int32) * slot
    local_rows = starts + lax.dynamic_slice_in_dim(offsets, my_index * vars_dev, vars_dev)
    by_device = offsets.reshape(n_devices, vars_dev)
    positions = by_device + starts[None, :]
    positions += jnp.arange(n_devices, dtype=jnp.int32)[:, None] * tok_rows
    positions = positions.T.reshape(n_devices * vars_dev, 1)
    my_gain = lax.dynamic_slice_in_dim(gain, my_index * group_width, group_width).astype(f32)

    gate_extra = round_up(chunks * vars_dev, row_tile)
    score_extra = round_up(vars_dev * 2 * (vocab // width + 1), row_tile)
    products = make_products(streams, local_rows, n_devices, chunks, gate_extra)
    moved = [lax.all_to_all(part, "seq", split_axis=0, concat_axis=0, tiled=True) for part in products]
    carried = ()
    backs = []
    for chunk in range(chunks):
        mine = slice(chunk * width, (chunk + 1) * width)
        spectrum = filter_spectrum(long_filter[mine], forward, block)
        operands = (
            moved[chunk], spectrum, forward, inverse, positions,
            my_gain[None, mine], unembed[mine],
        )
        if chunk > 0:
            carried = (gates,) + tuple(carried)
        results = filter_chunk(chunk, chunks, vars_dev, tok_rows, score_extra, operands, carried)
        carried = results[1:3]
        if chunk == 0 and chunks > 1:
            gates = results[3]
        backs.append(lax.all_to_all(results[0], "seq", split_axis=0, concat_axis=0, tiled=True))
    mixed, scores = finish(streams, backs, ref_ids, alt_ids, vocab)
    return (mixed, scores)


def solution(mesh):
    placed = (
        P(None, ("grp", "seq"), None),
        P("seq", None),
        P(),
        P("seq", None),
        P("grp"),
        P(("grp", "seq")),
        P(("grp", "seq")),
    )
    return jax.shard_map(
        shards,
        mesh=mesh,
        in_specs=placed,
        out_specs=(P(("grp", "seq"), None), P(None, ("grp", "seq"))),
        check_vma=False,
    )
```

profile of v0, /device:TPU:13, one launch (start us, length us, event | category | flops | bytes accessed | tf_op | source)
XLA Modules:
  0.0 91.1 jit_solution(624098322741242133)
XLA Ops:
  0.6 1.2 %dynamic_slice.6.rows_ref = s32[1]{0:T(128)} dynamic-slice(s32[16]{0:T(128)} %param.13, s32[]{:T(128)S(6)} %select_n.6), dynamic_slice_sizes={1} | dynamic-slice | bytes 12 | tf_op jit(solution)/shard_map/dynamic_slice | solution.py:383
  1.9 0.0 copy-start
  1.9 1.9 %copy-done = bf16[3,128,4096]{2,1,0:T(8,128)(2,1)S(1)} copy-done((bf16[3,128,4096]{2,1,0:T(8,128)(2,1)S(1)}, bf16[3,128,4096]{2,1,0:T(8,128)(2,1)}, u32[]{:S(2)}) %copy-start) | copy-done | bytes 3145752
  3.8 2.6 %products.1 = (bf16[16,144,128]{2,1,0:T(8,128)(2,1)S(1)}, bf16[16,128,128]{2,1,0:T(8,128)(2,1)}) custom-call(s32[1]{0:T(128)} %dynamic_slice.6.rows_ref, bf16[3,128,4096]{2,1,0:T(8,128)(2,1)S(1)} %copy-done), custom_call_target="tpu_custom_call" | custom-call | tf_op jit(solution)/shard_map/products/pallas_call | solution.py:89
  6.4 0.0 copy-start.10
  6.4 0.0 copy-start.2
  6.4 22.5 %all_to_all.20.refs_0_ = bf16[16,144,128]{2,1,0:T(8,128)(2,1)S(1)} all-to-all(bf16[16,144,128]{2,1,0:T(8,128)(2,1)S(1)} %get-tuple-element.8), channel_id=1, replica_groups=mesh['grp'=2,'seq'=16] {'seq'}, dimensions={0} | all-to-all | bytes 1179648 | tf_op jit(solution)/shard_map/all_to_all | solution.py:393
  28.9 4.8 %all-to-all-start.2 = ((bf16[16,128,128]{2,1,0:T(8,128)(2,1)}), bf16[16,128,128]{2,1,0:T(8,128)(2,1)S(1)}, u32[]{:S(2)}, u32[]{:S(2)}) async-start(bf16[16,128,128]{2,1,0:T(8,128)(2,1)} %get-tuple-element.10), calls=%async_computation.2 | async-start | bytes 1048576 | tf_op jit(solution)/shard_map/all_to_all | solution.py:393
  33.7 1.3 %fusion = (bf16[128,2048]{1,0:T(8,128)(2,1)S(1)}, bf16[128,2048]{1,0:T(8,128)(2,1)S(1)}) fusion(bf16[256,2048]{1,0:T(8,128)(2,1)} %param.10), kind=kLoop, calls=%fused_computation.4 | loop fusion | bytes 2097152 | tf_op jit(solution)/shard_map/slice | solution.py:398
  34.9 0.0 copy-start.9
  34.9 0.0 copy-done.10
  35.0 0.1 copy.11.refs_4_
  35.0 0.0 copy-done.2
  35.0 1.2 %filter_spectrum.2.refs_1_ = f32[8,512,128]{2,1,0:T(8,128)S(1)} custom-call(bf16[128,2048]{1,0:T(8,128)(2,1)S(1)} %get-tuple-element.17.filter_ref, bf16[1024,256]{1,0:T(8,128)(2,1)S(1)} %copy-done.2), custom_call_target="tpu_custom_call" | custom-call | flops 536870912 | bytes 4194304 | tf_op jit(solution)/shard_map/filter_spectrum/pallas_call | solution.py:116
  36.3 0.8 dynamic-slice_convert_fusion
  37.1 0.0 copy-done.9
  37.1 0.0 copy-start.7
  37.1 1.0 %copy-done.7 = bf16[512,512]{1,0:T(8,128)(2,1)S(1)} copy-done((bf16[512,512]{1,0:T(8,128)(2,1)S(1)}, bf16[512,512]{1,0:T(8,128)(2,1)}, u32[]{:S(2)}) %copy-start.7) | copy-done | bytes 524312
  38.1 5.1 %filter_chunk.2 = (bf16[16,128,128]{2,1,0:T(8,128)(2,1)}, f32[16,512]{1,0:T(8,128)S(1)}, f32[16,128]{1,0:T(8,128)S(1)}, bf16[16,16,128]{2,1,0:T(8,128)(2,1)S(1)}) custom-call(bf16[16,144,128]{2,1,0:T(8,128)(2,1)S(1)} %all_to_all.20.refs_0_, f32[8,512,128]{2,1,0:T(8,128)S(1)} %filter_spectrum.2.refs_1_, bf16[1024,256]{1,0:T(8,128)(2,1)S(1)} %copy-done.2, ...), custom_call_target="tpu_custom_call" | custom-call | flops 1375731712 | bytes 8388608 | tf_op jit(solution)/shard_map/filter_chunk/pallas_call | solution.py:276
  43.2 4.6 %all-to-all-done.2.refs_0_ = bf16[16,128,128]{2,1,0:T(8,128)(2,1)S(1)} async-done(((bf16[16,128,128]{2,1,0:T(8,128)(2,1)}), bf16[16,128,128]{2,1,0:T(8,128)(2,1)S(1)}, u32[]{:S(2)}, u32[]{:S(2)}) %all-to-all-start.2) | async-done | bytes 524320 | tf_op jit(solution)/shard_map/all_to_all | solution.py:393
  47.8 0.0 copy-start.5
  47.8 4.4 %all-to-all-start.1 = ((bf16[16,128,128]{2,1,0:T(8,128)(2,1)}), bf16[16,128,128]{2,1,0:T(8,128)(2,1)}, u32[]{:S(2)}, u32[]{:S(2)}) async-start(bf16[16,128,128]{2,1,0:T(8,128)(2,1)} %get-tuple-element.9), calls=%async_computation.1 | async-start | bytes 1048576 | tf_op jit(solution)/shard_map/all_to_all | solution.py:409
  52.3 0.0 copy-start.3
  52.3 0.0 copy-start.8
  52.3 1.2 %filter_spectrum.3.refs_1_ = f32[8,512,128]{2,1,0:T(8,128)S(1)} custom-call(bf16[128,2048]{1,0:T(8,128)(2,1)S(1)} %get-tuple-element.16.filter_ref, bf16[1024,256]{1,0:T(8,128)(2,1)S(1)} %copy-done.2), custom_call_target="tpu_custom_call" | custom-call | flops 536870912 | bytes 4194304 | tf_op jit(solution)/shard_map/filter_spectrum/pallas_call | solution.py:116
  53.5 0.0 copy-done.5
  53.5 0.0 copy-done.3
  53.6 0.0 copy-done.8
  53.6 0.0 copy-start.6
  53.6 1.0 %copy-done.6 = bf16[16,128,128]{2,1,0:T(8,128)(2,1)S(1)} copy-done((bf16[16,128,128]{2,1,0:T(8,128)(2,1)S(1)}, bf16[16,128,128]{2,1,0:T(8,128)(2,1)}, u32[]{:S(2)}) %copy-start.6) | copy-done | bytes 524312
  54.6 0.0 copy-start.1
  54.6 4.5 %filter_chunk.3 = bf16[16,144,128]{2,1,0:T(8,128)(2,1)S(1)} custom-call(bf16[16,128,128]{2,1,0:T(8,128)(2,1)S(1)} %copy-done.6, f32[8,512,128]{2,1,0:T(8,128)S(1)} %filter_spectrum.3.refs_1_, bf16[1024,256]{1,0:T(8,128)(2,1)S(1)} %copy-done.3, bf16[512,512]{1,0:T(8,128)(2,1)S(1)} %copy-done.8, s32[16,1]{1,0:T(8,128)S(1)} %copy.11.refs_4_, ...), custom_call_target="tpu_custom_call" | custom-call | flops 1375731712 | bytes 8388608 | tf_op jit(solution)/shard_map/filter_chunk/pallas_call | solution.py:276
  59.1 0.0 copy-start.4
  59.1 0.8 copy-done.4
  60.0 6.6 %all-to-all-done.1.refs_0_ = bf16[16,128,128]{2,1,0:T(8,128)(2,1)} async-done(((bf16[16,128,128]{2,1,0:T(8,128)(2,1)}), bf16[16,128,128]{2,1,0:T(8,128)(2,1)}, u32[]{:S(2)}, u32[]{:S(2)}) %all-to-all-start.1) | async-done | bytes 524320 | tf_op jit(solution)/shard_map/all_to_all | solution.py:409
  66.5 4.4 %all-to-all-start.3 = ((bf16[16,144,128]{2,1,0:T(8,128)(2,1)}), bf16[16,144,128]{2,1,0:T(8,128)(2,1)}, u32[]{:S(2)}, u32[]{:S(2)}) async-start(bf16[16,144,128]{2,1,0:T(8,128)(2,1)} %copy-done.4), calls=%async_computation.3 | async-start | bytes 1179648 | tf_op jit(solution)/shard_map/all_to_all | solution.py:409
  72.3 14.4 %all-to-all-done.3.refs_1_ = bf16[16,144,128]{2,1,0:T(8,128)(2,1)} async-done(((bf16[16,144,128]{2,1,0:T(8,128)(2,1)}), bf16[16,144,128]{2,1,0:T(8,128)(2,1)}, u32[]{:S(2)}, u32[]{:S(2)}) %all-to-all-start.3) | async-done | bytes 589856 | tf_op jit(solution)/shard_map/all_to_all | solution.py:409
  86.7 0.0 copy-done.1
  86.7 3.8 %finish.1 = (bf16[128,4096]{1,0:T(8,128)(2,1)}, f32[2,1]{1,0:T(2,128)S(1)}) custom-call(s32[1]{0:T(128)S(6)} %copy.14.ref_ref, s32[1]{0:T(128)S(6)} %copy.15.alt_ref, bf16[3,128,4096]{2,1,0:T(8,128)(2,1)S(1)} %copy-done.1, bf16[16,128,128]{2,1,0:T(8,128)(2,1)} %all-to-all-done.1.refs_0_, bf16[16,144,128]{2,1,0:T(8,128)(2,1)} %all-to-all-done.3.refs_1_), custom_call_target="tpu_custom_call" | custom-call | tf_op jit(solution)/shard_map/finish/pallas_call | solution.py:346
  90.5 0.6 copy.13
  (3 shorter events, 0.0 us)
Async XLA Ops:
  1.9 1.9 %copy-start = (bf16[3,128,4096]{2,1,0:T(8,128)(2,1)S(1)}, bf16[3,128,4096]{2,1,0:T(8,128)(2,1)}, u32[]{:S(2)}) copy-start(bf16[3,128,4096]{2,1,0:T(8,128)(2,1)} %streams_ref.3) | copy-start | bytes 9437188
  6.4 28.5 %copy-start.10 = (s32[16]{0:T(128)S(1)}, s32[16]{0:T(128)}, u32[]{:S(2)}) copy-start(s32[16]{0:T(128)} %param.13) | copy-start | bytes 196
  6.4 28.7 %copy-start.2 = (bf16[1024,256]{1,0:T(8,128)(2,1)S(1)}, bf16[1024,256]{1,0:T(8,128)(2,1)}, u32[]{:S(2)}) copy-start(bf16[1024,256]{1,0:T(8,128)(2,1)} %constant.18.clone.forward_ref.refs_2_) | copy-start | bytes 1572868
  28.9 19.0 %all-to-all-start.2 = ((bf16[16,128,128]{2,1,0:T(8,128)(2,1)}), bf16[16,128,128]{2,1,0:T(8,128)(2,1)S(1)}, u32[]{:S(2)}, u32[]{:S(2)}) async-start(bf16[16,128,128]{2,1,0:T(8,128)(2,1)} %get-tuple-element.10), calls=%async_computation.2 | async-start | bytes 1048576 | tf_op jit(solution)/shard_map/all_to_all | solution.py:393
  34.9 2.1 %copy-start.9 = (bf16[256,512]{1,0:T(8,128)(2,1)S(1)}, bf16[256,512]{1,0:T(8,128)(2,1)}, u32[]{:S(2)}) copy-start(bf16[256,512]{1,0:T(8,128)(2,1)} %param.12) | copy-start | bytes 786436
  37.1 1.0 %copy-start.7 = (bf16[512,512]{1,0:T(8,128)(2,1)S(1)}, bf16[512,512]{1,0:T(8,128)(2,1)}, u32[]{:S(2)}) copy-start(bf16[512,512]{1,0:T(8,128)(2,1)} %constant.19.clone.refs_3_) | copy-start | bytes 1572868
  47.8 5.7 %copy-start.5 = (bf16[16,128,128]{2,1,0:T(8,128)(2,1)}, bf16[16,128,128]{2,1,0:T(8,128)(2,1)S(1)}, u32[]{:S(2)}) copy-start(bf16[16,128,128]{2,1,0:T(8,128)(2,1)S(1)} %all-to-all-done.2.refs_0_) | copy-start | bytes 1572868
  47.8 18.7 %all-to-all-start.1 = ((bf16[16,128,128]{2,1,0:T(8,128)(2,1)}), bf16[16,128,128]{2,1,0:T(8,128)(2,1)}, u32[]{:S(2)}, u32[]{:S(2)}) async-start(bf16[16,128,128]{2,1,0:T(8,128)(2,1)} %get-tuple-element.9), calls=%async_computation.1 | async-start | bytes 1048576 | tf_op jit(solution)/shard_map/all_to_all | solution.py:409
  52.3 1.3 %copy-start.3 = (bf16[1024,256]{1,0:T(8,128)(2,1)S(1)}, bf16[1024,256]{1,0:T(8,128)(2,1)}, u32[]{:S(2)}) copy-start(bf16[1024,256]{1,0:T(8,128)(2,1)} %constant.18.clone.forward_ref.refs_2_) | copy-start | bytes 1572868
  52.3 1.3 %copy-start.8 = (bf16[512,512]{1,0:T(8,128)(2,1)S(1)}, bf16[512,512]{1,0:T(8,128)(2,1)}, u32[]{:S(2)}) copy-start(bf16[512,512]{1,0:T(8,128)(2,1)} %constant.19.clone.refs_3_) | copy-start | bytes 1572868
  53.6 1.0 %copy-start.6 = (bf16[16,128,128]{2,1,0:T(8,128)(2,1)S(1)}, bf16[16,128,128]{2,1,0:T(8,128)(2,1)}, u32[]{:S(2)}) copy-start(bf16[16,128,128]{2,1,0:T(8,128)(2,1)} %copy-done.5) | copy-start | bytes 1572868
  54.6 32.1 %copy-start.1 = (bf16[3,128,4096]{2,1,0:T(8,128)(2,1)S(1)}, bf16[3,128,4096]{2,1,0:T(8,128)(2,1)}, u32[]{:S(2)}) copy-start(bf16[3,128,4096]{2,1,0:T(8,128)(2,1)} %streams_ref.3) | copy-start | bytes 9437188
  59.1 0.8 copy-start.4
  66.5 20.1 %all-to-all-start.3 = ((bf16[16,144,128]{2,1,0:T(8,128)(2,1)}), bf16[16,144,128]{2,1,0:T(8,128)(2,1)}, u32[]{:S(2)}, u32[]{:S(2)}) async-start(bf16[16,144,128]{2,1,0:T(8,128)(2,1)} %copy-done.4), calls=%async_computation.3 | async-start | bytes 1179648 | tf_op jit(solution)/shard_map/all_to_all | solution.py:409
where the time goes:
time: 92.7 us; the launch traced here: 91.1 us
  waiting for transfers between devices  25.6 us (28%)
  blocking collectives  22.5 us (24%)
  Pallas kernels  18.6 us (20%)
  starting transfers between devices  13.7 us (15%)
  local copies, waits for them, and re-layouts  8.02 us (9%)
  between operations  2.06 us (2%)
    all_to_all x1, blocking collectives, shards(): lax.all_to_all(part, 'seq', split_axis=0, concat_axis=0, tiled=True)  22.5 us
    all_to_all x2, waiting for transfers between devices, shards(): lax.all_to_all(results[0], 'seq', split_axis=0, concat_axis=0, tiled=True)  21 us
    pallas_call x2, Pallas kernels, filter_chunk(): pl.pallas_call(functools.partial(chunk_kernel, index, chunks, vars_dev, t...  9.6 us
    all_to_all x2, starting transfers between devices, shards(): lax.all_to_all(results[0], 'seq', split_axis=0, concat_axis=0, tiled=True)  8.88 us
    unnamed x22, local copies, waits for them, and re-layouts  4.8 us
    all_to_all x1, starting transfers between devices, shards(): lax.all_to_all(part, 'seq', split_axis=0, concat_axis=0, tiled=True)  4.79 us
    all_to_all x1, waiting for transfers between devices, shards(): lax.all_to_all(part, 'seq', split_axis=0, concat_axis=0, tiled=True)  4.61 us
    pallas_call x1, Pallas kernels, finish(): pl.pallas_call(functools.partial(finish_kernel, chunks, vars_dev, vocab),...  3.85 us
  transfers between devices with their start and end apart: 3, of which 3 were waited for; matrix products, arithmetic and copies ran while one was open for 2% of the time, Pallas kernels for 13%

commit v1 on v0

--- a/solution.py
+++ b/solution.py
@@ -14,7 +14,6 @@
 bf16 = jnp.bfloat16
 row_tile = 16
 lane_tile = 128
-max_chunks = 2
 MIB = 1 << 20
 
 
@@ -126,6 +125,40 @@
     )(taps, forward)
 
 
+def multiply_points(points, spectrum_ref):
+    n_blocks, double, width = points.shape
+    block = double // 2
+
+    def multiply_step(step, carry):
+        start = pl.multiple_of(step * row_tile, row_tile)
+        upper = pl.ds(start, row_tile)
+        lower = pl.ds(pl.multiple_of(block + start, row_tile), row_tile)
+
+        def block_sum(total):
+            sum_re = jnp.zeros((row_tile, width), f32)
+            sum_im = jnp.zeros((row_tile, width), f32)
+            for delay in range(total + 1):
+                a_re = points[total - delay, upper, :]
+                a_im = points[total - delay, lower, :]
+                b_re = spectrum_ref[delay, upper, :]
+                b_im = spectrum_ref[delay, lower, :]
+                sum_re += a_re * b_re - a_im * b_im
+                sum_im += a_re * b_im + a_im * b_re
+            return sum_re, sum_im
+
+        after_re, after_im = block_sum(n_blocks - 1)
+        for total in range(n_blocks - 1, 0, -1):
+            sum_re, sum_im = block_sum(total - 1)
+            points[total, upper, :] = after_re + sum_im
+            points[total, lower, :] = after_im - sum_re
+            after_re, after_im = sum_re, sum_im
+        points[0, upper, :] = after_re
+        points[0, lower, :] = after_im
+        return carry
+
+    lax.fori_loop(0, block // row_tile, multiply_step, 0)
+
+
 def convolve(chunk_ref, spectrum_ref, forward_ref, inverse_ref, out_ref, points, tok_rows):
     n_blocks, double, width = points.shape
     block = double // 2
@@ -147,34 +180,7 @@
 
     lax.fori_loop(0, n_blocks // group, forward_step, 0)
 
-    def multiply_step(step, carry):
-        start = pl.multiple_of(step * row_tile, row_tile)
-        upper = pl.ds(start, row_tile)
-        lower = pl.ds(pl.multiple_of(block + start, row_tile), row_tile)
-
-        def block_sum(total):
-            sum_re = jnp.zeros((row_tile, width), f32)
-            sum_im = jnp.zeros((row_tile, width), f32)
-            for delay in range(total + 1):
-                a_re = points[total - delay, upper, :]
-                a_im = points[total - delay, lower, :]
-                b_re = spectrum_ref[delay, upper, :]
-                b_im = spectrum_ref[delay, lower, :]
-                sum_re += a_re * b_re - a_im * b_im
-                sum_im += a_re * b_im + a_im * b_re
-            return sum_re, sum_im
-
-        after_re, after_im = block_sum(n_blocks - 1)
-        for total in range(n_blocks - 1, 0, -1):
-            sum_re, sum_im = block_sum(total - 1)
-            points[total, upper, :] = after_re + sum_im
-            points[total, lower, :] = after_im - sum_re
-            after_re, after_im = sum_re, sum_im
-        points[0, upper, :] = after_re
-        points[0, lower, :] = after_im
-        return carry
-
-    lax.fori_loop(0, block // row_tile, multiply_step, 0)
+    multiply_points(points, spectrum_ref)
 
     def inverse_step(step, carry):
         first = step * group
@@ -211,6 +217,21 @@
     rows = (gate_rows * filtered).astype(bf16).astype(f32)
     weighted = (rows * gain_row).astype(bf16)
     return jnp.dot(weighted, unembed, preferred_element_type=f32), rows * rows
+
+
+def pack_scores(raw, squares, vars_dev, packed, n_devices):
+    total, width = packed.shape
+    extra = total // n_devices
+    per_row = raw.shape[1] // width
+    packed[...] = jnp.zeros_like(packed)
+    for var in range(vars_dev):
+        mine = slice(var * n_devices, (var + 1) * n_devices)
+        pieces = [raw[mine, r * width : (r + 1) * width] for r in range(per_row)] + [squares[mine]]
+        for row, piece in enumerate(pieces):
+            rounded = piece.astype(bf16).astype(f32)
+            base = var * 2 * (per_row + 1) + row
+            packed[pl.ds(base, n_devices, stride=extra), :] = rounded
+            packed[pl.ds(base + per_row + 1, n_devices, stride=extra), :] = piece - rounded
 
 
 def chunk_kernel(index, chunks, vars_dev, tok_rows, *refs):
@@ -242,16 +263,7 @@
     packed = refs[1]
     n_devices, _, width = out_ref.shape
     extra = out_ref.shape[1] - tok_rows
-    per_row = raw.shape[1] // width
-    packed[...] = jnp.zeros_like(packed)
-    for var in range(vars_dev):
-        mine = slice(var * n_devices, (var + 1) * n_devices)
-        pieces = [raw[mine, r * width : (r + 1) * width] for r in range(per_row)] + [squares[mine]]
-        for row, piece in enumerate(pieces):
-            rounded = piece.astype(bf16).astype(f32)
-            base = var * 2 * (per_row + 1) + row
-            packed[pl.ds(base, n_devices, stride=extra), :] = rounded
-            packed[pl.ds(base + per_row + 1, n_devices, stride=extra), :] = piece - rounded
+    pack_scores(raw, squares, vars_dev, packed, n_devices)
     out_ref[:, tok_rows:, :] = packed[...].reshape(n_devices, extra, width).astype(bf16)
 
 
@@ -285,6 +297,33 @@
     )(*operands, *carried)
 
 
+def final_scores(sums, vars_dev, vocab, model_width, ref_ref, alt_ref):
+    width = sums.shape[1]
+    per_row = vocab // width
+    ids = lax.broadcasted_iota(jnp.int32, (per_row, width), 0) * width
+    ids += lax.broadcasted_iota(jnp.int32, (per_row, width), 1)
+    row = lax.broadcasted_iota(jnp.int32, (2, vars_dev), 0)
+    column = lax.broadcasted_iota(jnp.int32, (2, vars_dev), 1)
+    scores = jnp.zeros((2, vars_dev), f32)
+
+    def whole_sum(values):
+        return jnp.sum(jnp.sum(values, axis=1, keepdims=True), axis=0, keepdims=True)
+
+    for var in range(vars_dev):
+        base = var * 2 * (per_row + 1)
+        both = sums[base : base + per_row + 1, :]
+        both = both + sums[base + per_row + 1 : base + 2 * (per_row + 1), :]
+        square = jnp.sum(both[per_row:, :], axis=1, keepdims=True)
+        logits = both[:per_row, :] * lax.rsqrt(square / model_width + norm_eps)
+        largest = jnp.max(jnp.max(logits, axis=1, keepdims=True), axis=0, keepdims=True)
+        log_total = largest + jnp.log(whole_sum(jnp.exp(logits - largest)))
+        ref_logit = whole_sum(jnp.where(ids == ref_ref[var], logits, 0.0))
+        alt_logit = whole_sum(jnp.where(ids == alt_ref[var], logits, 0.0))
+        pair = jnp.where(row == 0, ref_logit - log_total, alt_logit - ref_logit)
+        scores = jnp.where(column == var, pair, scores)
+    return scores
+
+
 def finish_kernel(chunks, vars_dev, vocab, ref_ref, alt_ref, streams_ref, *refs):
     back_refs, mixed_ref, scores_ref, sums = refs[:chunks], refs[chunks], refs[chunks + 1], refs[chunks + 2]
     tok_rows = streams_ref.shape[1]
@@ -308,30 +347,8 @@
 
     @pl.when(step == pl.num_programs(0) - 1)
     def _():
-        per_row = vocab // width
         model_width = pl.num_programs(0) * owners * chunks * width
-        ids = lax.broadcasted_iota(jnp.int32, (per_row, width), 0) * width
-        ids += lax.broadcasted_iota(jnp.int32, (per_row, width), 1)
-        row = lax.broadcasted_iota(jnp.int32, (2, vars_dev), 0)
-        column = lax.broadcasted_iota(jnp.int32, (2, vars_dev), 1)
-        scores = jnp.zeros((2, vars_dev), f32)
-        for var in range(vars_dev):
-            base = var * 2 * (per_row + 1)
-            both = sums[base : base + per_row + 1, :]
-            both = both + sums[base + per_row + 1 : base + 2 * (per_row + 1), :]
-            square = jnp.sum(both[per_row:, :], axis=1, keepdims=True)
-            logits = both[:per_row, :] * lax.rsqrt(square / model_width + norm_eps)
-
-            def whole_sum(values):
-                return jnp.sum(jnp.sum(values, axis=1, keepdims=True), axis=0, keepdims=True)
-
-            largest = jnp.max(jnp.max(logits, axis=1, keepdims=True), axis=0, keepdims=True)
-            log_total = largest + jnp.log(whole_sum(jnp.exp(logits - largest)))
-            ref_logit = whole_sum(jnp.where(ids == ref_ref[var], logits, 0.0))
-            alt_logit = whole_sum(jnp.where(ids == alt_ref[var], logits, 0.0))
-            pair = jnp.where(row == 0, ref_logit - log_total, alt_logit - ref_logit)
-            scores = jnp.where(column == var, pair, scores)
-        scores_ref[...] = scores
+        scores_ref[...] = final_scores(sums[...], vars_dev, vocab, model_width, ref_ref, alt_ref)
 
 
 def finish(streams, backs, ref_ids, alt_ids, vocab):
@@ -365,6 +382,254 @@
         name="finish",
     )(ref_ids, alt_ids, streams, *backs)
 
+def stacked(buffer, device, half, tok_rows):
+    return buffer[device, half * tok_rows : (half + 1) * tok_rows, :]
+
+
+def send_products_kernel(halves, vars_dev, me_ref, rows_ref, streams_ref, *refs):
+    n_devices = len(refs) - 4
+    out_refs = refs[:n_devices]
+    pairs, gates, pair_sems, gate_sems = refs[n_devices:]
+    tok_rows = streams_ref.shape[1]
+    width = halves * lane_tile
+    me = me_ref[0]
+
+    def pair_copy(step):
+        start = pl.multiple_of((me ^ step) * width, lane_tile)
+        return pltpu.make_async_copy(
+            streams_ref.at[pl.ds(1, 2), :, pl.ds(start, width)], pairs.at[step], pair_sems.at[step]
+        )
+
+    def gate_copy(var):
+        start = pl.multiple_of(rows_ref[var] // row_tile * row_tile, row_tile)
+        return pltpu.make_async_copy(
+            streams_ref.at[0, pl.ds(start, row_tile), :], gates.at[var], gate_sems.at[var]
+        )
+
+    for var in range(vars_dev):
+        gate_copy(var).start()
+    for step in range(n_devices):
+        pair_copy(step).start()
+    for var in range(vars_dev):
+        gate_copy(var).wait()
+    extra = out_refs[0].shape[0] - halves * tok_rows
+    row = lax.broadcasted_iota(jnp.int32, (row_tile, lane_tile), 0)
+    place = lax.broadcasted_iota(jnp.int32, (extra, lane_tile), 0)
+    for step in range(n_devices):
+        pair_copy(step).wait()
+        tail = jnp.zeros((extra, lane_tile), f32)
+        for half in range(halves):
+            lanes = slice(half * lane_tile, (half + 1) * lane_tile)
+            left = pairs[step, 0, :, lanes].astype(f32)
+            right = pairs[step, 1, :, lanes].astype(f32)
+            rows = slice(half * tok_rows, (half + 1) * tok_rows)
+            out_refs[step][rows, :] = (left * right).astype(bf16)
+            start = pl.multiple_of((me ^ step) * width + half * lane_tile, lane_tile)
+            for var in range(vars_dev):
+                tile = gates[var, :, pl.ds(start, lane_tile)].astype(f32)
+                mine = jnp.where(row == rows_ref[var] % row_tile, tile, 0.0)
+                mine = jnp.sum(mine, axis=0, keepdims=True)
+                tail = jnp.where(place == half * vars_dev + var, mine, tail)
+        out_refs[step][halves * tok_rows :, :] = tail.astype(bf16)
+
+
+def send_products(me, local_rows, streams, n_devices, extra):
+    _, tok_rows, model_width = streams.shape
+    vars_dev = local_rows.shape[0]
+    halves = model_width // n_devices // lane_tile
+    rows_out = halves * tok_rows + extra
+    return pl.pallas_call(
+        functools.partial(send_products_kernel, halves, vars_dev),
+        in_specs=[
+            pl.BlockSpec(memory_space=pltpu.SMEM),
+            pl.BlockSpec(memory_space=pltpu.SMEM),
+            pl.BlockSpec(memory_space=pltpu.HBM),
+        ],
+        out_specs=[whole_spec()] * n_devices,
+        out_shape=[jax.ShapeDtypeStruct((rows_out, lane_tile), bf16)] * n_devices,
+        scratch_shapes=[
+            pltpu.VMEM((n_devices, 2, tok_rows, halves * lane_tile), bf16),
+            pltpu.VMEM((vars_dev, row_tile, model_width), bf16),
+            pltpu.SemaphoreType.DMA((n_devices,)),
+            pltpu.SemaphoreType.DMA((vars_dev,)),
+        ],
+        compiler_params=pltpu.CompilerParams(vmem_limit_bytes=60 * MIB),
+        cost_estimate=pl.CostEstimate(
+            flops=tok_rows * model_width, bytes_accessed=6 * tok_rows * model_width, transcendentals=0
+        ),
+        name="send_products",
+    )(me, local_rows, streams)
+
+
+def direct_filter_kernel(vars_dev, halves, tok_rows, me_ref, *refs):
+    spectrum_ref, forward_ref, inverse_ref, positions_ref, gain_ref, unembed_ref = refs[:6]
+    points, arrived, leaving, packed = refs[-4:]
+    n_devices = arrived.shape[0]
+    in_refs, out_refs = refs[6 : 6 + n_devices], refs[6 + n_devices : 6 + 2 * n_devices]
+    me = me_ref[0]
+    for step in range(n_devices):
+        arrived[me ^ step] = in_refs[step][...]
+
+    n_blocks, double, width = points.shape
+    block = double // 2
+    per_block = block // tok_rows
+
+    def forward_step(step, carry):
+        pieces = []
+        for half in range(halves):
+            parts = [stacked(arrived, step * per_block + m, half, tok_rows) for m in range(per_block)]
+            pieces.append(jnp.concatenate(parts, axis=0))
+        signal = jnp.concatenate(pieces, axis=1)
+        both = jnp.dot(forward_ref[...], signal, preferred_element_type=f32)
+        points[step] = both[:double] + both[double:]
+        return carry
+
+    lax.fori_loop(0, n_blocks, forward_step, 0)
+    multiply_points(points, spectrum_ref)
+
+    def inverse_step(step, carry):
+        highs, lows = split_bf16(points[step])
+        both = jnp.dot(inverse_ref[...], highs, preferred_element_type=f32)
+        rest = jnp.dot(inverse_ref[:block, :], lows, preferred_element_type=f32)
+        result = (both[:block] + both[block:] + rest).astype(bf16)
+        for member in range(per_block):
+            for half in range(halves):
+                leaving[step * per_block + member, half * tok_rows : (half + 1) * tok_rows, :] = result[
+                    member * tok_rows : (member + 1) * tok_rows,
+                    half * lane_tile : (half + 1) * lane_tile,
+                ]
+        return carry
+
+    lax.fori_loop(0, n_blocks, inverse_step, 0)
+
+    length = n_devices * tok_rows
+    column = lax.broadcasted_iota(jnp.int32, (positions_ref.shape[0], length), 1)
+    picker = (column == positions_ref[...]).astype(f32).astype(bf16)
+    tails = arrived[:, halves * tok_rows :, :].astype(f32)
+    place = lax.broadcasted_iota(jnp.int32, tails.shape, 1)
+    raw = None
+    squares = None
+    for half in range(halves):
+        lanes = slice(half * lane_tile, (half + 1) * lane_tile)
+        picked = [
+            jnp.sum(jnp.where(place == half * vars_dev + var, tails, 0.0), axis=1)
+            for var in range(vars_dev)
+        ]
+        gate_rows = picked[0] if vars_dev == 1 else jnp.concatenate(picked, axis=0)
+        filtered = leaving[:, half * tok_rows : (half + 1) * tok_rows, :].reshape(length, lane_tile)
+        filtered = jnp.dot(picker, filtered, preferred_element_type=f32)
+        rows = (gate_rows * filtered).astype(bf16).astype(f32)
+        weighted = (rows * gain_ref[:, lanes]).astype(bf16)
+        part = jnp.dot(weighted, unembed_ref[lanes, :], preferred_element_type=f32)
+        raw = part if raw is None else raw + part
+        squares = rows * rows if squares is None else squares + rows * rows
+    pack_scores(raw, squares, vars_dev, packed, n_devices)
+    extra = packed.shape[0] // n_devices
+    leaving[:, halves * tok_rows :, :] = packed[...].reshape(n_devices, extra, lane_tile).astype(bf16)
+    for step in range(n_devices):
+        out_refs[step][...] = leaving[me ^ step]
+
+
+def direct_filter(me, operands, arrivals, vars_dev, tok_rows, extra):
+    n_devices = len(arrivals)
+    n_blocks, double, width = operands[0].shape
+    halves = width // lane_tile
+    rows_out = halves * tok_rows + extra
+    flops = 2 * width * n_blocks * (double * double * 5 // 2 + 4 * n_blocks * double)
+    return pl.pallas_call(
+        functools.partial(direct_filter_kernel, vars_dev, halves, tok_rows),
+        in_specs=[pl.BlockSpec(memory_space=pltpu.SMEM)]
+        + [whole_spec()] * (len(operands) + n_devices),
+        out_specs=[whole_spec()] * n_devices,
+        out_shape=[jax.ShapeDtypeStruct((rows_out, lane_tile), bf16)] * n_devices,
+        scratch_shapes=[
+            pltpu.VMEM((n_blocks, double, width), f32),
+            pltpu.VMEM((n_devices, arrivals[0].shape[0], lane_tile), bf16),
+            pltpu.VMEM((n_devices, rows_out, lane_tile), bf16),
+            pltpu.VMEM((n_devices * extra, lane_tile), f32),
+        ],
+        compiler_params=pltpu.CompilerParams(vmem_limit_bytes=32 * MIB),
+        cost_estimate=pl.CostEstimate(flops=flops, bytes_accessed=8 * MIB, transcendentals=0),
+        name="direct_filter",
+    )(me, *operands, *arrivals)
+
+
+def direct_finish_kernel(halves, vars_dev, vocab, me_ref, ref_ref, alt_ref, streams_ref, *refs):
+    gates, results, gate_sems, out_sems = refs[-4:]
+    n_devices = gates.shape[0]
+    back_refs, mixed_ref, scores_ref = refs[:n_devices], refs[n_devices], refs[n_devices + 1]
+    tok_rows = streams_ref.shape[1]
+    width = halves * lane_tile
+    me = me_ref[0]
+
+    def lanes_of(step):
+        return pl.ds(pl.multiple_of((me ^ step) * width, lane_tile), width)
+
+    def gate_copy(step):
+        return pltpu.make_async_copy(
+            streams_ref.at[0, :, lanes_of(step)], gates.at[step], gate_sems.at[step]
+        )
+
+    def out_copy(step):
+        return pltpu.make_async_copy(
+            results.at[step], mixed_ref.at[:, lanes_of(step)], out_sems.at[step]
+        )
+
+    for step in range(n_devices):
+        gate_copy(step).start()
+    sums = None
+    for step in range(n_devices):
+        gate_copy(step).wait()
+        for half in range(halves):
+            lanes = slice(half * lane_tile, (half + 1) * lane_tile)
+            filtered = back_refs[step][half * tok_rows : (half + 1) * tok_rows, :].astype(f32)
+            results[step, :, lanes] = (gates[step, :, lanes].astype(f32) * filtered).astype(bf16)
+        out_copy(step).start()
+        tail = back_refs[step][halves * tok_rows :, :].astype(f32)
+        sums = tail if sums is None else sums + tail
+    model_width = n_devices * width
+    scores_ref[...] = final_scores(sums, vars_dev, vocab, model_width, ref_ref, alt_ref)
+    for step in range(n_devices):
+        out_copy(step).wait()
+
+
+def direct_finish(me, ref_ids, alt_ids, streams, backs, vocab):
+    _, tok_rows, model_width = streams.shape
+    n_devices = len(backs)
+    vars_dev = ref_ids.shape[0]
+    width = model_width // n_devices
+    return pl.pallas_call(
+        functools.partial(direct_finish_kernel, width // lane_tile, vars_dev, vocab),
+        in_specs=[pl.BlockSpec(memory_space=pltpu.SMEM)] * 3
+        + [pl.BlockSpec(memory_space=pltpu.HBM)]
+        + [whole_spec()] * n_devices,
+        out_specs=[pl.BlockSpec(memory_space=pltpu.HBM), whole_spec()],
+        out_shape=[
+            jax.ShapeDtypeStruct((tok_rows, model_width), bf16),
+            jax.ShapeDtypeStruct((2, vars_dev), f32),
+        ],
+        scratch_shapes=[
+            pltpu.VMEM((n_devices, tok_rows, width), bf16),
+            pltpu.VMEM((n_devices, tok_rows, width), bf16),
+            pltpu.SemaphoreType.DMA((n_devices,)),
+            pltpu.SemaphoreType.DMA((n_devices,)),
+        ],
+        compiler_params=pltpu.CompilerParams(vmem_limit_bytes=12 * MIB),
+        cost_estimate=pl.CostEstimate(
+            flops=tok_rows * model_width, bytes_accessed=6 * tok_rows * model_width, transcendentals=0
+        ),
+        name="direct_finish",
+    )(me, ref_ids, alt_ids, streams, *backs)
+
+
+def exchange(parts):
+    n_devices = len(parts)
+    moved = [parts[0]] + [None] * (n_devices - 1)
+    for step in range(n_devices - 1, 0, -1):
+        pairs = [(device, device ^ step) for device in range(n_devices)]
+        moved[step] = lax.ppermute(parts[step], "seq", pairs)
+    return moved
+
 
 def shards(streams, long_filter, gain, unembed, offsets, ref_ids, alt_ids):
     n_devices = lax.axis_size("seq")
@@ -373,7 +638,7 @@
     group_width = model_width // n_devices
     vars_dev = ref_ids.shape[0]
     vocab = unembed.shape[1]
-    chunks = max(1, min(max_chunks, group_width // lane_tile))
+    chunks = max(1, group_width // lane_tile)
     width = group_width // chunks
     block = tok_rows * block_devices(n_devices, tok_rows)
     forward, inverse = (jnp.asarray(table) for table in block_tables(block))
@@ -386,6 +651,17 @@
     positions += jnp.arange(n_devices, dtype=jnp.int32)[:, None] * tok_rows
     positions = positions.T.reshape(n_devices * vars_dev, 1)
     my_gain = lax.dynamic_slice_in_dim(gain, my_index * group_width, group_width).astype(f32)
+
+    if chunks * lane_tile == group_width and n_devices & (n_devices - 1) == 0:
+        me = jnp.reshape(my_index, (1,)).astype(jnp.int32)
+        gate_extra = round_up(chunks * vars_dev, row_tile)
+        score_extra = round_up(vars_dev * 2 * (vocab // lane_tile + 1), row_tile)
+        arrivals = exchange(send_products(me, local_rows, streams, n_devices, gate_extra))
+        spectrum = filter_spectrum(long_filter, forward, block)
+        operands = (spectrum, forward, inverse, positions, my_gain[None, :], unembed)
+        leaving = direct_filter(me, operands, arrivals, vars_dev, tok_rows, score_extra)
+        mixed, scores = direct_finish(me, ref_ids, alt_ids, streams, exchange(leaving), vocab)
+        return (mixed, scores)
 
     gate_extra = round_up(chunks * vars_dev, row_tile)
     score_extra = round_up(vars_dev * 2 * (vocab // width + 1), row_tile)

time: 92.7 us -> 87.7 us (0.946); the launches traced: 91.1 us -> 87.4 us
  starting transfers between devices: 13.7 us -> 40.8 us
  blocking collectives: 22.5 us -> 0 us
  local copies, waits for them, and re-layouts: 8.02 us -> 4.26 us
  waiting for transfers between devices: 25.6 us -> 22.7 us
  Pallas kernels: 18.6 us -> 16.2 us
    ppermute x0 -> x30, starting transfers between devices: none -> 40.8 us  [exchange(): moved[step] = lax.ppermute(parts[step], 'seq', pairs)]
    all_to_all x3 -> x0, waiting for transfers between devices: 25.6 us -> none  [the longest x2 21 us: shards(): lax.all_to_all(results[0], 'seq', split_axis=0, concat_axis=0, tiled=True)]
    ppermute x0 -> x30, waiting for transfers between devices: none -> 22.7 us  [exchange(): moved[step] = lax.ppermute(parts[step], 'seq', pairs)]
    all_to_all x1 -> x0, blocking collectives: 22.5 us -> none  [shards(): lax.all_to_all(part, 'seq', split_axis=0, concat_axis=0, tiled=True)]
    all_to_all x3 -> x0, starting transfers between devices: 13.7 us -> none  [the longest x2 8.88 us: shards(): lax.all_to_all(results[0], 'seq', split_axis=0, concat_axis=0, tiled=True)]
    unnamed x22 -> x14, local copies, waits for them, and re-layouts: 4.8 us -> 2.29 us
    slice x2 -> x0, local copies, waits for them, and re-layouts: 1.29 us -> none  [the longest x1 1.27 us: shards(): spectrum = filter_spectrum(long_filter[mine], forward, block)]
    pallas_call x2 -> x1, Pallas kernels: 2.48 us -> 1.28 us  [filter_spectrum(): pl.pallas_call(functools.partial(spectrum_kernel, block), in_specs=[whole...]
  transfers between devices with their start and end apart: 3 -> 30, of which waited for: 3 -> 12; matrix products, arithmetic and copies ran while one was open for 2% -> 2% of each run, Pallas kernels for 13% -> 1%
where the time goes in v1:
time: 87.7 us; the launch traced here: 87.4 us
  starting transfers between devices  40.8 us (47%)
  waiting for transfers between devices  22.7 us (26%)
  Pallas kernels  16.2 us (18%)
  local copies, waits for them, and re-layouts  4.26 us (5%)
  between operations  2.04 us (2%)
  other arithmetic  1.41 us (2%)
    ppermute x30, starting transfers between devices, exchange(): moved[step] = lax.ppermute(parts[step], 'seq', pairs)  40.8 us
    ppermute x30, waiting for transfers between devices, exchange(): moved[step] = lax.ppermute(parts[step], 'seq', pairs)  22.7 us
    pallas_call x1, Pallas kernels, direct_filter(): pl.pallas_call(functools.partial(direct_filter_kernel, vars_dev, halves,...  9.26 us
    pallas_call x1, Pallas kernels, send_products(): pl.pallas_call(functools.partial(send_products_kernel, halves, vars_dev),...  3.92 us
    unnamed x14, local copies, waits for them, and re-layouts  2.29 us
  transfers between devices with their start and end apart: 30, of which 12 were waited for; matrix products, arithmetic and copies ran while one was open for 2% of the time, Pallas kernels for 1%

profile of v1, /device:TPU:13, one launch (start us, length us, event | category | flops | bytes accessed | tf_op | source)
XLA Modules:
  0.0 87.4 jit_solution(4518047493531886494)
XLA Ops:
  0.6 1.3 %dynamic_slice.7.rows_ref = s32[1]{0:T(128)} dynamic-slice(s32[16]{0:T(128)} %param.13, s32[]{:T(128)S(6)} %select_n.7), dynamic_slice_sizes={1} | dynamic-slice | bytes 12 | tf_op jit(solution)/shard_map/dynamic_slice | solution.py:648
  1.9 3.9 %send_products.1 = (bf16[272,128]{1,0:T(8,128)(2,1)}, bf16[272,128]{1,0:T(8,128)(2,1)}, bf16[272,128]{1,0:T(8,128)(2,1)}, bf16[272,128]{1,0:T(8,128)(2,1)}, bf16...) custom-call(s32[1]{0:T(128)} %bitcast.me_ref, ...), custom_call_target="tpu_custom_call" | custom-call | flops 524288 | bytes 3145728 | tf_op jit(solution)/shard_map/send_products/pallas_call | solution.py:441
  5.9 0.7 collective-permute-start
  6.6 1.2 %collective-permute-start.1 = (bf16[272,128]{1,0:T(8,128)(2,1)}, bf16[272,128]{1,0:T(8,128)(2,1)S(1)}, u32[]{:S(2)}, u32[]{:S(2)}) collective-permute-start(bf16[272,128]{1,0:T(8,128)(2,1)} %get-tuple-element.36), channel_id=1, source_target_pairs={{0,2},{1,3},{2,0},{3,1},{4,6},{5,7},{6,4},{7,5},{8,10},{9,11},{10,... | collective-permute-start | bytes 208904 | tf_op jit(solution)/shard_map/ppermute | solution.py:630
  7.8 2.5 %collective-permute-start.10 = (bf16[272,128]{1,0:T(8,128)(2,1)}, bf16[272,128]{1,0:T(8,128)(2,1)S(1)}, u32[]{:S(2)}, u32[]{:S(2)}) collective-permute-start(bf16[272,128]{1,0:T(8,128)(2,1)} %get-tuple-element.45), channel_id=1, source_target_pairs={{0,11},{1,10},{2,9},{3,8},{4,15},{5,14},{6,13},{7,12},{8,3},{9,2},... | collective-permute-start | bytes 208904 | tf_op jit(solution)/shard_map/ppermute | solution.py:630
  10.3 0.0 collective-permute-start.11
  10.3 1.8 %collective-permute-start.12 = (bf16[272,128]{1,0:T(8,128)(2,1)}, bf16[272,128]{1,0:T(8,128)(2,1)S(1)}, u32[]{:S(2)}, u32[]{:S(2)}) collective-permute-start(bf16[272,128]{1,0:T(8,128)(2,1)} %get-tuple-element.47), channel_id=1, source_target_pairs={{0,13},{1,12},{2,15},{3,14},{4,9},{5,8},{6,11},{7,10},{8,5},{9,4},... | collective-permute-start | bytes 208904 | tf_op jit(solution)/shard_map/ppermute | solution.py:630
  12.2 0.7 add_bitcast_fusion
  12.8 0.1 copy.11.refs_3_
  12.9 0.0 collective-permute-done.refs_7_
  12.9 0.7 collective-permute-start.13
  13.6 1.9 %collective-permute-start.14 = (bf16[272,128]{1,0:T(8,128)(2,1)}, bf16[272,128]{1,0:T(8,128)(2,1)S(1)}, u32[]{:S(2)}, u32[]{:S(2)}) collective-permute-start(bf16[272,128]{1,0:T(8,128)(2,1)} %get-tuple-element.49), channel_id=1, source_target_pairs={{0,15},{1,14},{2,13},{3,12},{4,11},{5,10},{6,9},{7,8},{8,7},{9,6},... | collective-permute-start | bytes 208904 | tf_op jit(solution)/shard_map/ppermute | solution.py:630
  15.5 1.4 %collective-permute-done.10.refs_17_ = bf16[272,128]{1,0:T(8,128)(2,1)S(1)} collective-permute-done((bf16[272,128]{1,0:T(8,128)(2,1)}, bf16[272,128]{1,0:T(8,128)(2,1)S(1)}, u32[]{:S(2)}, u32[]{:S(2)}) %collective-permute-start.10) | collective-permute-done | bytes 69664 | tf_op jit(solution)/shard_map/ppermute | solution.py:630
  16.8 3.2 %collective-permute-start.2 = (bf16[272,128]{1,0:T(8,128)(2,1)}, bf16[272,128]{1,0:T(8,128)(2,1)S(1)}, u32[]{:S(2)}, u32[]{:S(2)}) collective-permute-start(bf16[272,128]{1,0:T(8,128)(2,1)} %get-tuple-element.37), channel_id=1, source_target_pairs={{0,3},{1,2},{2,1},{3,0},{4,7},{5,6},{6,5},{7,4},{8,11},{9,10},{10,... | collective-permute-start | bytes 208904 | tf_op jit(solution)/shard_map/ppermute | solution.py:630
  20.0 0.0 collective-permute-done.11.refs_18_
  20.0 0.5 collective-permute-start.3
  20.5 2.4 %collective-permute-done.12.refs_19_ = bf16[272,128]{1,0:T(8,128)(2,1)S(1)} collective-permute-done((bf16[272,128]{1,0:T(8,128)(2,1)}, bf16[272,128]{1,0:T(8,128)(2,1)S(1)}, u32[]{:S(2)}, u32[]{:S(2)}) %collective-permute-start.12) | collective-permute-done | bytes 69664 | tf_op jit(solution)/shard_map/ppermute | solution.py:630
  23.0 0.0 collective-permute-start.4
  23.0 0.8 dynamic-slice_convert_fusion
  23.7 1.2 %collective-permute-done.13.refs_20_ = bf16[272,128]{1,0:T(8,128)(2,1)S(1)} collective-permute-done((bf16[272,128]{1,0:T(8,128)(2,1)}, bf16[272,128]{1,0:T(8,128)(2,1)S(1)}, u32[]{:S(2)}, u32[]{:S(2)}) %collective-permute-start.13) | collective-permute-done | bytes 69664 | tf_op jit(solution)/shard_map/ppermute | solution.py:630
  24.9 1.5 %collective-permute-start.5 = (bf16[272,128]{1,0:T(8,128)(2,1)}, bf16[272,128]{1,0:T(8,128)(2,1)S(1)}, u32[]{:S(2)}, u32[]{:S(2)}) collective-permute-start(bf16[272,128]{1,0:T(8,128)(2,1)} %get-tuple-element.40), channel_id=1, source_target_pairs={{0,6},{1,7},{2,4},{3,5},{4,2},{5,3},{6,0},{7,1},{8,14},{9,15},{10,... | collective-permute-start | bytes 208904 | tf_op jit(solution)/shard_map/ppermute | solution.py:630
  26.4 0.0 collective-permute-done.14.refs_21_
  26.5 1.9 %collective-permute-start.6 = (bf16[272,128]{1,0:T(8,128)(2,1)}, bf16[272,128]{1,0:T(8,128)(2,1)S(1)}, u32[]{:S(2)}, u32[]{:S(2)}) collective-permute-start(bf16[272,128]{1,0:T(8,128)(2,1)} %get-tuple-element.41), channel_id=1, source_target_pairs={{0,7},{1,6},{2,5},{3,4},{4,3},{5,2},{6,1},{7,0},{8,15},{9,14},{10,... | collective-permute-start | bytes 208904 | tf_op jit(solution)/shard_map/ppermute | solution.py:630
  28.4 2.1 %collective-permute-start.7 = (bf16[272,128]{1,0:T(8,128)(2,1)}, bf16[272,128]{1,0:T(8,128)(2,1)S(1)}, u32[]{:S(2)}, u32[]{:S(2)}) collective-permute-start(bf16[272,128]{1,0:T(8,128)(2,1)} %get-tuple-element.42), channel_id=1, source_target_pairs={{0,8},{1,9},{2,10},{3,11},{4,12},{5,13},{6,14},{7,15},{8,0},{9,1},... | collective-permute-start | bytes 208904 | tf_op jit(solution)/shard_map/ppermute | solution.py:630
  30.4 0.0 collective-permute-done.3.refs_10_
  30.4 0.0 collective-permute-start.8
  30.5 0.0 collective-permute-done.4.refs_11_
  30.5 3.5 %collective-permute-start.9 = (bf16[272,128]{1,0:T(8,128)(2,1)}, bf16[272,128]{1,0:T(8,128)(2,1)S(1)}, u32[]{:S(2)}, u32[]{:S(2)}) collective-permute-start(bf16[272,128]{1,0:T(8,128)(2,1)} %get-tuple-element.44), channel_id=1, source_target_pairs={{0,10},{1,11},{2,8},{3,9},{4,14},{5,15},{6,12},{7,13},{8,2},{9,3},... | collective-permute-start | bytes 208904 | tf_op jit(solution)/shard_map/ppermute | solution.py:630
  34.0 1.2 %copy-done.1 = bf16[256,2048]{1,0:T(8,128)(2,1)S(1)} copy-done((bf16[256,2048]{1,0:T(8,128)(2,1)S(1)}, bf16[256,2048]{1,0:T(8,128)(2,1)}, u32[]{:S(2)}) %copy-start.1) | copy-done | bytes 1048600
  35.2 1.0 %copy-done.2 = bf16[1024,256]{1,0:T(8,128)(2,1)S(1)} copy-done((bf16[1024,256]{1,0:T(8,128)(2,1)S(1)}, bf16[1024,256]{1,0:T(8,128)(2,1)}, u32[]{:S(2)}) %copy-start.2) | copy-done | bytes 524312
  36.3 1.3 %filter_spectrum.1.refs_0_ = f32[8,512,256]{2,1,0:T(8,128)S(1)} custom-call(bf16[256,2048]{1,0:T(8,128)(2,1)S(1)} %copy-done.1, bf16[1024,256]{1,0:T(8,128)(2,1)S(1)} %copy-done.2), custom_call_target="tpu_custom_call" | custom-call | flops 1073741824 | bytes 4194304 | tf_op jit(solution)/shard_map/filter_spectrum/pallas_call | solution.py:115
  37.5 0.0 collective-permute-done.6.refs_13_
  37.6 0.7 collective-permute-done.8.refs_15_
  38.2 1.5 %collective-permute-done.9.refs_16_ = bf16[272,128]{1,0:T(8,128)(2,1)S(1)} collective-permute-done((bf16[272,128]{1,0:T(8,128)(2,1)}, bf16[272,128]{1,0:T(8,128)(2,1)S(1)}, u32[]{:S(2)}, u32[]{:S(2)}) %collective-permute-start.9) | collective-permute-done | bytes 69664 | tf_op jit(solution)/shard_map/ppermute | solution.py:630
  39.7 0.0 copy-start
  39.8 9.3 %direct_filter.1 = (bf16[272,128]{1,0:T(8,128)(2,1)S(1)}, bf16[272,128]{1,0:T(8,128)(2,1)S(1)}, bf16[272,128]{1,0:T(8,128)(2,1)S(1)}, bf16[272,128]{1,0:T(8,128)...) custom-call(s32[1]{0:T(128)} %bitcast.me_ref, ...), custom_call_target="tpu_custom_call" | custom-call | flops 2751463424 | bytes 8388608 | tf_op jit(solution)/shard_map/direct_filter/pallas_call | solution.py:539
  49.0 0.9 %collective-permute-start.15 = (bf16[272,128]{1,0:T(8,128)(2,1)S(1)}, bf16[272,128]{1,0:T(8,128)(2,1)S(1)}, u32[]{:S(2)}, u32[]{:S(2)}) collective-permute-start(bf16[272,128]{1,0:T(8,128)(2,1)S(1)} %get-tuple-element.51), channel_id=1, source_target_pairs={{0,1},{1,0},{2,3},{3,2},{4,5},{5,4},{6,7},{7,6},{8,9},{9,8},{10,11... | collective-permute-start | bytes 208904 | tf_op jit(solution)/shard_map/ppermute | solution.py:630
  50.0 1.2 %collective-permute-start.16 = (bf16[272,128]{1,0:T(8,128)(2,1)S(1)}, bf16[272,128]{1,0:T(8,128)(2,1)S(1)}, u32[]{:S(2)}, u32[]{:S(2)}) collective-permute-start(bf16[272,128]{1,0:T(8,128)(2,1)S(1)} %get-tuple-element.52), channel_id=1, source_target_pairs={{0,2},{1,3},{2,0},{3,1},{4,6},{5,7},{6,4},{7,5},{8,10},{9,11},{10,... | collective-permute-start | bytes 208904 | tf_op jit(solution)/shard_map/ppermute | solution.py:630
  51.2 0.5 collective-permute-start.17
  51.7 2.5 %collective-permute-start.18 = (bf16[272,128]{1,0:T(8,128)(2,1)S(1)}, bf16[272,128]{1,0:T(8,128)(2,1)S(1)}, u32[]{:S(2)}, u32[]{:S(2)}) collective-permute-start(bf16[272,128]{1,0:T(8,128)(2,1)S(1)} %get-tuple-element.54), channel_id=1, source_target_pairs={{0,4},{1,5},{2,6},{3,7},{4,0},{5,1},{6,2},{7,3},{8,12},{9,13},{10,... | collective-permute-start | bytes 208904 | tf_op jit(solution)/shard_map/ppermute | solution.py:630
  54.2 0.1 collective-permute-start.19
  54.3 1.9 %collective-permute-start.20 = (bf16[272,128]{1,0:T(8,128)(2,1)S(1)}, bf16[272,128]{1,0:T(8,128)(2,1)S(1)}, u32[]{:S(2)}, u32[]{:S(2)}) collective-permute-start(bf16[272,128]{1,0:T(8,128)(2,1)S(1)} %get-tuple-element.56), channel_id=1, source_target_pairs={{0,6},{1,7},{2,4},{3,5},{4,2},{5,3},{6,0},{7,1},{8,14},{9,15},{10,... | collective-permute-start | bytes 208904 | tf_op jit(solution)/shard_map/ppermute | solution.py:630
  56.2 1.3 %collective-permute-start.21 = (bf16[272,128]{1,0:T(8,128)(2,1)S(1)}, bf16[272,128]{1,0:T(8,128)(2,1)S(1)}, u32[]{:S(2)}, u32[]{:S(2)}) collective-permute-start(bf16[272,128]{1,0:T(8,128)(2,1)S(1)} %get-tuple-element.57), channel_id=1, source_target_pairs={{0,7},{1,6},{2,5},{3,4},{4,3},{5,2},{6,1},{7,0},{8,15},{9,14},{10,... | collective-permute-start | bytes 208904 | tf_op jit(solution)/shard_map/ppermute | solution.py:630
  57.5 0.0 collective-permute-done.17.refs_3_
  57.5 2.5 %collective-permute-start.22 = (bf16[272,128]{1,0:T(8,128)(2,1)S(1)}, bf16[272,128]{1,0:T(8,128)(2,1)S(1)}, u32[]{:S(2)}, u32[]{:S(2)}) collective-permute-start(bf16[272,128]{1,0:T(8,128)(2,1)S(1)} %get-tuple-element.58), channel_id=1, source_target_pairs={{0,8},{1,9},{2,10},{3,11},{4,12},{5,13},{6,14},{7,15},{8,0},{9,1},... | collective-permute-start | bytes 208904 | tf_op jit(solution)/shard_map/ppermute | solution.py:630
  60.0 0.7 collective-permute-start.23
  60.7 2.1 %collective-permute-start.24 = (bf16[272,128]{1,0:T(8,128)(2,1)S(1)}, bf16[272,128]{1,0:T(8,128)(2,1)S(1)}, u32[]{:S(2)}, u32[]{:S(2)}) collective-permute-start(bf16[272,128]{1,0:T(8,128)(2,1)S(1)} %get-tuple-element.60), channel_id=1, source_target_pairs={{0,10},{1,11},{2,8},{3,9},{4,14},{5,15},{6,12},{7,13},{8,2},{9,3},... | collective-permute-start | bytes 208904 | tf_op jit(solution)/shard_map/ppermute | solution.py:630
  62.7 0.0 collective-permute-done.20.refs_6_
  62.7 1.8 %collective-permute-start.25 = (bf16[272,128]{1,0:T(8,128)(2,1)S(1)}, bf16[272,128]{1,0:T(8,128)(2,1)S(1)}, u32[]{:S(2)}, u32[]{:S(2)}) collective-permute-start(bf16[272,128]{1,0:T(8,128)(2,1)S(1)} %get-tuple-element.61), channel_id=1, source_target_pairs={{0,11},{1,10},{2,9},{3,8},{4,15},{5,14},{6,13},{7,12},{8,3},{9,2},... | collective-permute-start | bytes 208904 | tf_op jit(solution)/shard_map/ppermute | solution.py:630
  64.5 0.0 collective-permute-done.21.refs_7_
  64.5 0.5 collective-permute-start.26
  65.1 2.4 %collective-permute-done.22.refs_8_ = bf16[272,128]{1,0:T(8,128)(2,1)S(1)} collective-permute-done((bf16[272,128]{1,0:T(8,128)(2,1)S(1)}, bf16[272,128]{1,0:T(8,128)(2,1)S(1)}, u32[]{:S(2)}, u32[]{:S(2)}) %collective-permute-start.22) | collective-permute-done | bytes 69664 | tf_op jit(solution)/shard_map/ppermute | solution.py:630
  67.5 0.0 collective-permute-start.27
  67.5 3.1 %collective-permute-done.23.refs_9_ = bf16[272,128]{1,0:T(8,128)(2,1)S(1)} collective-permute-done((bf16[272,128]{1,0:T(8,128)(2,1)S(1)}, bf16[272,128]{1,0:T(8,128)(2,1)S(1)}, u32[]{:S(2)}, u32[]{:S(2)}) %collective-permute-start.23) | collective-permute-done | bytes 69664 | tf_op jit(solution)/shard_map/ppermute | solution.py:630
  70.6 1.2 %collective-permute-start.28 = (bf16[272,128]{1,0:T(8,128)(2,1)S(1)}, bf16[272,128]{1,0:T(8,128)(2,1)S(1)}, u32[]{:S(2)}, u32[]{:S(2)}) collective-permute-start(bf16[272,128]{1,0:T(8,128)(2,1)S(1)} %get-tuple-element.64), channel_id=1, source_target_pairs={{0,14},{1,15},{2,12},{3,13},{4,10},{5,11},{6,8},{7,9},{8,6},{9,7},... | collective-permute-start | bytes 208904 | tf_op jit(solution)/shard_map/ppermute | solution.py:630
  71.8 0.3 collective-permute-done.24.refs_10_
  72.1 2.1 %collective-permute-start.29 = (bf16[272,128]{1,0:T(8,128)(2,1)S(1)}, bf16[272,128]{1,0:T(8,128)(2,1)S(1)}, u32[]{:S(2)}, u32[]{:S(2)}) collective-permute-start(bf16[272,128]{1,0:T(8,128)(2,1)S(1)} %get-tuple-element.65), channel_id=1, source_target_pairs={{0,15},{1,14},{2,13},{3,12},{4,11},{5,10},{6,9},{7,8},{8,7},{9,6},... | collective-permute-start | bytes 208904 | tf_op jit(solution)/shard_map/ppermute | solution.py:630
  75.5 0.0 collective-permute-done.25.refs_11_
  75.5 2.6 %collective-permute-done.26.refs_12_ = bf16[272,128]{1,0:T(8,128)(2,1)S(1)} collective-permute-done((bf16[272,128]{1,0:T(8,128)(2,1)S(1)}, bf16[272,128]{1,0:T(8,128)(2,1)S(1)}, u32[]{:S(2)}, u32[]{:S(2)}) %collective-permute-start.26) | collective-permute-done | bytes 69664 | tf_op jit(solution)/shard_map/ppermute | solution.py:630
  78.1 3.9 %collective-permute-done.27.refs_13_ = bf16[272,128]{1,0:T(8,128)(2,1)S(1)} collective-permute-done((bf16[272,128]{1,0:T(8,128)(2,1)S(1)}, bf16[272,128]{1,0:T(8,128)(2,1)S(1)}, u32[]{:S(2)}, u32[]{:S(2)}) %collective-permute-start.27) | collective-permute-done | bytes 69664 | tf_op jit(solution)/shard_map/ppermute | solution.py:630
  82.0 1.5 %collective-permute-done.28.refs_14_ = bf16[272,128]{1,0:T(8,128)(2,1)S(1)} collective-permute-done((bf16[272,128]{1,0:T(8,128)(2,1)S(1)}, bf16[272,128]{1,0:T(8,128)(2,1)S(1)}, u32[]{:S(2)}, u32[]{:S(2)}) %collective-permute-start.28) | collective-permute-done | bytes 69664 | tf_op jit(solution)/shard_map/ppermute | solution.py:630
  83.6 1.5 %collective-permute-done.29.refs_15_ = bf16[272,128]{1,0:T(8,128)(2,1)S(1)} collective-permute-done((bf16[272,128]{1,0:T(8,128)(2,1)S(1)}, bf16[272,128]{1,0:T(8,128)(2,1)S(1)}, u32[]{:S(2)}, u32[]{:S(2)}) %collective-permute-start.29) | collective-permute-done | bytes 69664 | tf_op jit(solution)/shard_map/ppermute | solution.py:630
  85.1 1.7 %direct_finish.1 = (bf16[128,4096]{1,0:T(8,128)(2,1)}, f32[2,1]{1,0:T(2,128)S(1)}) custom-call(s32[1]{0:T(128)} %bitcast.me_ref, s32[1]{0:T(128)S(6)} %copy.13.ref_ref, s32[1]{0:T(128)S(6)} %copy.14.alt_ref, bf16[3,128,4096]{2,1,0:T(8,128)(2,1)S(1)} %copy-done, bf16[272,128]{1,0:T(8,128)(2,1)S(1)} %get-tuple-element.50.refs_0_, ...), custom_call_target="tpu_custom_call" | custom-call | flops 524288 | bytes 3145728 | tf_op jit(solution)/shard_map/direct_finish/pallas_call | solution.py:601
  86.8 0.6 copy.12
  (19 shorter events, 0.0 us)
Async XLA Ops:
  1.9 37.8 %copy-start.3 = (bf16[1024,256]{1,0:T(8,128)(2,1)S(1)}, bf16[1024,256]{1,0:T(8,128)(2,1)}, u32[]{:S(2)}) copy-start(bf16[1024,256]{1,0:T(8,128)(2,1)} %constant.18.clone.forward_ref.refs_1_) | copy-start | bytes 1572868
  1.9 37.8 %copy-start.4 = (bf16[256,512]{1,0:T(8,128)(2,1)S(1)}, bf16[256,512]{1,0:T(8,128)(2,1)}, u32[]{:S(2)}) copy-start(bf16[256,512]{1,0:T(8,128)(2,1)} %refs_5_.1) | copy-start | bytes 786436
  1.9 37.8 %copy-start.6 = (bf16[512,512]{1,0:T(8,128)(2,1)S(1)}, bf16[512,512]{1,0:T(8,128)(2,1)}, u32[]{:S(2)}) copy-start(bf16[512,512]{1,0:T(8,128)(2,1)} %constant.19.clone.refs_2_) | copy-start | bytes 1572868
  5.9 7.0 %collective-permute-start = (bf16[272,128]{1,0:T(8,128)(2,1)}, bf16[272,128]{1,0:T(8,128)(2,1)S(1)}, u32[]{:S(2)}, u32[]{:S(2)}) collective-permute-start(bf16[272,128]{1,0:T(8,128)(2,1)} %get-tuple-element.35), channel_id=1, source_target_pairs={{0,1},{1,0},{2,3},{3,2},{4,5},{5,4},{6,7},{7,6},{8,9},{9,8},{10,11... | collective-permute-start | bytes 208904 | tf_op jit(solution)/shard_map/ppermute | solution.py:630
  6.6 7.0 %collective-permute-start.1 = (bf16[272,128]{1,0:T(8,128)(2,1)}, bf16[272,128]{1,0:T(8,128)(2,1)S(1)}, u32[]{:S(2)}, u32[]{:S(2)}) collective-permute-start(bf16[272,128]{1,0:T(8,128)(2,1)} %get-tuple-element.36), channel_id=1, source_target_pairs={{0,2},{1,3},{2,0},{3,1},{4,6},{5,7},{6,4},{7,5},{8,10},{9,11},{10,... | collective-permute-start | bytes 208904 | tf_op jit(solution)/shard_map/ppermute | solution.py:630
  7.8 9.0 %collective-permute-start.10 = (bf16[272,128]{1,0:T(8,128)(2,1)}, bf16[272,128]{1,0:T(8,128)(2,1)S(1)}, u32[]{:S(2)}, u32[]{:S(2)}) collective-permute-start(bf16[272,128]{1,0:T(8,128)(2,1)} %get-tuple-element.45), channel_id=1, source_target_pairs={{0,11},{1,10},{2,9},{3,8},{4,15},{5,14},{6,13},{7,12},{8,3},{9,2},... | collective-permute-start | bytes 208904 | tf_op jit(solution)/shard_map/ppermute | solution.py:630
  10.3 9.7 %collective-permute-start.11 = (bf16[272,128]{1,0:T(8,128)(2,1)}, bf16[272,128]{1,0:T(8,128)(2,1)S(1)}, u32[]{:S(2)}, u32[]{:S(2)}) collective-permute-start(bf16[272,128]{1,0:T(8,128)(2,1)} %get-tuple-element.46), channel_id=1, source_target_pairs={{0,12},{1,13},{2,14},{3,15},{4,8},{5,9},{6,10},{7,11},{8,4},{9,5},... | collective-permute-start | bytes 208904 | tf_op jit(solution)/shard_map/ppermute | solution.py:630
  10.3 12.6 %collective-permute-start.12 = (bf16[272,128]{1,0:T(8,128)(2,1)}, bf16[272,128]{1,0:T(8,128)(2,1)S(1)}, u32[]{:S(2)}, u32[]{:S(2)}) collective-permute-start(bf16[272,128]{1,0:T(8,128)(2,1)} %get-tuple-element.47), channel_id=1, source_target_pairs={{0,13},{1,12},{2,15},{3,14},{4,9},{5,8},{6,11},{7,10},{8,5},{9,4},... | collective-permute-start | bytes 208904 | tf_op jit(solution)/shard_map/ppermute | solution.py:630
  12.9 12.0 %collective-permute-start.13 = (bf16[272,128]{1,0:T(8,128)(2,1)}, bf16[272,128]{1,0:T(8,128)(2,1)S(1)}, u32[]{:S(2)}, u32[]{:S(2)}) collective-permute-start(bf16[272,128]{1,0:T(8,128)(2,1)} %get-tuple-element.48), channel_id=1, source_target_pairs={{0,14},{1,15},{2,12},{3,13},{4,10},{5,11},{6,8},{7,9},{8,6},{9,7},... | collective-permute-start | bytes 208904 | tf_op jit(solution)/shard_map/ppermute | solution.py:630
  13.6 12.9 %collective-permute-start.14 = (bf16[272,128]{1,0:T(8,128)(2,1)}, bf16[272,128]{1,0:T(8,128)(2,1)S(1)}, u32[]{:S(2)}, u32[]{:S(2)}) collective-permute-start(bf16[272,128]{1,0:T(8,128)(2,1)} %get-tuple-element.49), channel_id=1, source_target_pairs={{0,15},{1,14},{2,13},{3,12},{4,11},{5,10},{6,9},{7,8},{8,7},{9,6},... | collective-permute-start | bytes 208904 | tf_op jit(solution)/shard_map/ppermute | solution.py:630
  16.8 11.5 %collective-permute-start.2 = (bf16[272,128]{1,0:T(8,128)(2,1)}, bf16[272,128]{1,0:T(8,128)(2,1)S(1)}, u32[]{:S(2)}, u32[]{:S(2)}) collective-permute-start(bf16[272,128]{1,0:T(8,128)(2,1)} %get-tuple-element.37), channel_id=1, source_target_pairs={{0,3},{1,2},{2,1},{3,0},{4,7},{5,6},{6,5},{7,4},{8,11},{9,10},{10,... | collective-permute-start | bytes 208904 | tf_op jit(solution)/shard_map/ppermute | solution.py:630
  20.0 10.4 %collective-permute-start.3 = (bf16[272,128]{1,0:T(8,128)(2,1)}, bf16[272,128]{1,0:T(8,128)(2,1)S(1)}, u32[]{:S(2)}, u32[]{:S(2)}) collective-permute-start(bf16[272,128]{1,0:T(8,128)(2,1)} %get-tuple-element.38), channel_id=1, source_target_pairs={{0,4},{1,5},{2,6},{3,7},{4,0},{5,1},{6,2},{7,3},{8,12},{9,13},{10,... | collective-permute-start | bytes 208904 | tf_op jit(solution)/shard_map/ppermute | solution.py:630
  23.0 7.5 %collective-permute-start.4 = (bf16[272,128]{1,0:T(8,128)(2,1)}, bf16[272,128]{1,0:T(8,128)(2,1)S(1)}, u32[]{:S(2)}, u32[]{:S(2)}) collective-permute-start(bf16[272,128]{1,0:T(8,128)(2,1)} %get-tuple-element.39), channel_id=1, source_target_pairs={{0,5},{1,4},{2,7},{3,6},{4,1},{5,0},{6,3},{7,2},{8,13},{9,12},{10,... | collective-permute-start | bytes 208904 | tf_op jit(solution)/shard_map/ppermute | solution.py:630
  24.9 12.6 %collective-permute-start.5 = (bf16[272,128]{1,0:T(8,128)(2,1)}, bf16[272,128]{1,0:T(8,128)(2,1)S(1)}, u32[]{:S(2)}, u32[]{:S(2)}) collective-permute-start(bf16[272,128]{1,0:T(8,128)(2,1)} %get-tuple-element.40), channel_id=1, source_target_pairs={{0,6},{1,7},{2,4},{3,5},{4,2},{5,3},{6,0},{7,1},{8,14},{9,15},{10,... | collective-permute-start | bytes 208904 | tf_op jit(solution)/shard_map/ppermute | solution.py:630
  26.5 11.1 %collective-permute-start.6 = (bf16[272,128]{1,0:T(8,128)(2,1)}, bf16[272,128]{1,0:T(8,128)(2,1)S(1)}, u32[]{:S(2)}, u32[]{:S(2)}) collective-permute-start(bf16[272,128]{1,0:T(8,128)(2,1)} %get-tuple-element.41), channel_id=1, source_target_pairs={{0,7},{1,6},{2,5},{3,4},{4,3},{5,2},{6,1},{7,0},{8,15},{9,14},{10,... | collective-permute-start | bytes 208904 | tf_op jit(solution)/shard_map/ppermute | solution.py:630
  28.4 9.2 %collective-permute-start.7 = (bf16[272,128]{1,0:T(8,128)(2,1)}, bf16[272,128]{1,0:T(8,128)(2,1)S(1)}, u32[]{:S(2)}, u32[]{:S(2)}) collective-permute-start(bf16[272,128]{1,0:T(8,128)(2,1)} %get-tuple-element.42), channel_id=1, source_target_pairs={{0,8},{1,9},{2,10},{3,11},{4,12},{5,13},{6,14},{7,15},{8,0},{9,1},... | collective-permute-start | bytes 208904 | tf_op jit(solution)/shard_map/ppermute | solution.py:630
  30.4 7.8 %collective-permute-start.8 = (bf16[272,128]{1,0:T(8,128)(2,1)}, bf16[272,128]{1,0:T(8,128)(2,1)S(1)}, u32[]{:S(2)}, u32[]{:S(2)}) collective-permute-start(bf16[272,128]{1,0:T(8,128)(2,1)} %get-tuple-element.43), channel_id=1, source_target_pairs={{0,9},{1,8},{2,11},{3,10},{4,13},{5,12},{6,15},{7,14},{8,1},{9,0},... | collective-permute-start | bytes 208904 | tf_op jit(solution)/shard_map/ppermute | solution.py:630
  30.5 9.3 %collective-permute-start.9 = (bf16[272,128]{1,0:T(8,128)(2,1)}, bf16[272,128]{1,0:T(8,128)(2,1)S(1)}, u32[]{:S(2)}, u32[]{:S(2)}) collective-permute-start(bf16[272,128]{1,0:T(8,128)(2,1)} %get-tuple-element.44), channel_id=1, source_target_pairs={{0,10},{1,11},{2,8},{3,9},{4,14},{5,15},{6,12},{7,13},{8,2},{9,3},... | collective-permute-start | bytes 208904 | tf_op jit(solution)/shard_map/ppermute | solution.py:630
  34.0 1.2 %copy-start.1 = (bf16[256,2048]{1,0:T(8,128)(2,1)S(1)}, bf16[256,2048]{1,0:T(8,128)(2,1)}, u32[]{:S(2)}) copy-start(bf16[256,2048]{1,0:T(8,128)(2,1)} %filter_ref.1) | copy-start | bytes 3145732
  35.2 1.0 %copy-start.2 = (bf16[1024,256]{1,0:T(8,128)(2,1)S(1)}, bf16[1024,256]{1,0:T(8,128)(2,1)}, u32[]{:S(2)}) copy-start(bf16[1024,256]{1,0:T(8,128)(2,1)} %constant.18.clone.forward_ref.refs_1_) | copy-start | bytes 1572868
  36.2 3.5 %copy-start.5 = (bf16[272,128]{1,0:T(8,128)(2,1)S(1)}, bf16[272,128]{1,0:T(8,128)(2,1)}, u32[]{:S(2)}) copy-start(bf16[272,128]{1,0:T(8,128)(2,1)} %get-tuple-element.34.refs_6_) | copy-start | bytes 208900
  39.7 45.3 %copy-start = (bf16[3,128,4096]{2,1,0:T(8,128)(2,1)S(1)}, bf16[3,128,4096]{2,1,0:T(8,128)(2,1)}, u32[]{:S(2)}) copy-start(bf16[3,128,4096]{2,1,0:T(8,128)(2,1)} %streams_ref.3) | copy-start | bytes 9437188
  49.0 5.3 %collective-permute-start.15 = (bf16[272,128]{1,0:T(8,128)(2,1)S(1)}, bf16[272,128]{1,0:T(8,128)(2,1)S(1)}, u32[]{:S(2)}, u32[]{:S(2)}) collective-permute-start(bf16[272,128]{1,0:T(8,128)(2,1)S(1)} %get-tuple-element.51), channel_id=1, source_target_pairs={{0,1},{1,0},{2,3},{3,2},{4,5},{5,4},{6,7},{7,6},{8,9},{9,8},{10,11... | collective-permute-start | bytes 208904 | tf_op jit(solution)/shard_map/ppermute | solution.py:630
  50.0 6.3 %collective-permute-start.16 = (bf16[272,128]{1,0:T(8,128)(2,1)S(1)}, bf16[272,128]{1,0:T(8,128)(2,1)S(1)}, u32[]{:S(2)}, u32[]{:S(2)}) collective-permute-start(bf16[272,128]{1,0:T(8,128)(2,1)S(1)} %get-tuple-element.52), channel_id=1, source_target_pairs={{0,2},{1,3},{2,0},{3,1},{4,6},{5,7},{6,4},{7,5},{8,10},{9,11},{10,... | collective-permute-start | bytes 208904 | tf_op jit(solution)/shard_map/ppermute | solution.py:630
  51.2 6.3 %collective-permute-start.17 = (bf16[272,128]{1,0:T(8,128)(2,1)S(1)}, bf16[272,128]{1,0:T(8,128)(2,1)S(1)}, u32[]{:S(2)}, u32[]{:S(2)}) collective-permute-start(bf16[272,128]{1,0:T(8,128)(2,1)S(1)} %get-tuple-element.53), channel_id=1, source_target_pairs={{0,3},{1,2},{2,1},{3,0},{4,7},{5,6},{6,5},{7,4},{8,11},{9,10},{10,... | collective-permute-start | bytes 208904 | tf_op jit(solution)/shard_map/ppermute | solution.py:630
  51.7 8.3 %collective-permute-start.18 = (bf16[272,128]{1,0:T(8,128)(2,1)S(1)}, bf16[272,128]{1,0:T(8,128)(2,1)S(1)}, u32[]{:S(2)}, u32[]{:S(2)}) collective-permute-start(bf16[272,128]{1,0:T(8,128)(2,1)S(1)} %get-tuple-element.54), channel_id=1, source_target_pairs={{0,4},{1,5},{2,6},{3,7},{4,0},{5,1},{6,2},{7,3},{8,12},{9,13},{10,... | collective-permute-start | bytes 208904 | tf_op jit(solution)/shard_map/ppermute | solution.py:630
  54.2 6.5 %collective-permute-start.19 = (bf16[272,128]{1,0:T(8,128)(2,1)S(1)}, bf16[272,128]{1,0:T(8,128)(2,1)S(1)}, u32[]{:S(2)}, u32[]{:S(2)}) collective-permute-start(bf16[272,128]{1,0:T(8,128)(2,1)S(1)} %get-tuple-element.55), channel_id=1, source_target_pairs={{0,5},{1,4},{2,7},{3,6},{4,1},{5,0},{6,3},{7,2},{8,13},{9,12},{10,... | collective-permute-start | bytes 208904 | tf_op jit(solution)/shard_map/ppermute | solution.py:630
  54.3 8.4 %collective-permute-start.20 = (bf16[272,128]{1,0:T(8,128)(2,1)S(1)}, bf16[272,128]{1,0:T(8,128)(2,1)S(1)}, u32[]{:S(2)}, u32[]{:S(2)}) collective-permute-start(bf16[272,128]{1,0:T(8,128)(2,1)S(1)} %get-tuple-element.56), channel_id=1, source_target_pairs={{0,6},{1,7},{2,4},{3,5},{4,2},{5,3},{6,0},{7,1},{8,14},{9,15},{10,... | collective-permute-start | bytes 208904 | tf_op jit(solution)/shard_map/ppermute | solution.py:630
  56.2 8.3 %collective-permute-start.21 = (bf16[272,128]{1,0:T(8,128)(2,1)S(1)}, bf16[272,128]{1,0:T(8,128)(2,1)S(1)}, u32[]{:S(2)}, u32[]{:S(2)}) collective-permute-start(bf16[272,128]{1,0:T(8,128)(2,1)S(1)} %get-tuple-element.57), channel_id=1, source_target_pairs={{0,7},{1,6},{2,5},{3,4},{4,3},{5,2},{6,1},{7,0},{8,15},{9,14},{10,... | collective-permute-start | bytes 208904 | tf_op jit(solution)/shard_map/ppermute | solution.py:630
  57.5 10.0 %collective-permute-start.22 = (bf16[272,128]{1,0:T(8,128)(2,1)S(1)}, bf16[272,128]{1,0:T(8,128)(2,1)S(1)}, u32[]{:S(2)}, u32[]{:S(2)}) collective-permute-start(bf16[272,128]{1,0:T(8,128)(2,1)S(1)} %get-tuple-element.58), channel_id=1, source_target_pairs={{0,8},{1,9},{2,10},{3,11},{4,12},{5,13},{6,14},{7,15},{8,0},{9,1},... | collective-permute-start | bytes 208904 | tf_op jit(solution)/shard_map/ppermute | solution.py:630
  60.0 10.6 %collective-permute-start.23 = (bf16[272,128]{1,0:T(8,128)(2,1)S(1)}, bf16[272,128]{1,0:T(8,128)(2,1)S(1)}, u32[]{:S(2)}, u32[]{:S(2)}) collective-permute-start(bf16[272,128]{1,0:T(8,128)(2,1)S(1)} %get-tuple-element.59), channel_id=1, source_target_pairs={{0,9},{1,8},{2,11},{3,10},{4,13},{5,12},{6,15},{7,14},{8,1},{9,0},... | collective-permute-start | bytes 208904 | tf_op jit(solution)/shard_map/ppermute | solution.py:630
  60.7 11.5 %collective-permute-start.24 = (bf16[272,128]{1,0:T(8,128)(2,1)S(1)}, bf16[272,128]{1,0:T(8,128)(2,1)S(1)}, u32[]{:S(2)}, u32[]{:S(2)}) collective-permute-start(bf16[272,128]{1,0:T(8,128)(2,1)S(1)} %get-tuple-element.60), channel_id=1, source_target_pairs={{0,10},{1,11},{2,8},{3,9},{4,14},{5,15},{6,12},{7,13},{8,2},{9,3},... | collective-permute-start | bytes 208904 | tf_op jit(solution)/shard_map/ppermute | solution.py:630
  62.7 12.8 %collective-permute-start.25 = (bf16[272,128]{1,0:T(8,128)(2,1)S(1)}, bf16[272,128]{1,0:T(8,128)(2,1)S(1)}, u32[]{:S(2)}, u32[]{:S(2)}) collective-permute-start(bf16[272,128]{1,0:T(8,128)(2,1)S(1)} %get-tuple-element.61), channel_id=1, source_target_pairs={{0,11},{1,10},{2,9},{3,8},{4,15},{5,14},{6,13},{7,12},{8,3},{9,2},... | collective-permute-start | bytes 208904 | tf_op jit(solution)/shard_map/ppermute | solution.py:630
  64.5 13.5 %collective-permute-start.26 = (bf16[272,128]{1,0:T(8,128)(2,1)S(1)}, bf16[272,128]{1,0:T(8,128)(2,1)S(1)}, u32[]{:S(2)}, u32[]{:S(2)}) collective-permute-start(bf16[272,128]{1,0:T(8,128)(2,1)S(1)} %get-tuple-element.62), channel_id=1, source_target_pairs={{0,12},{1,13},{2,14},{3,15},{4,8},{5,9},{6,10},{7,11},{8,4},{9,5},... | collective-permute-start | bytes 208904 | tf_op jit(solution)/shard_map/ppermute | solution.py:630
  67.5 14.5 %collective-permute-start.27 = (bf16[272,128]{1,0:T(8,128)(2,1)S(1)}, bf16[272,128]{1,0:T(8,128)(2,1)S(1)}, u32[]{:S(2)}, u32[]{:S(2)}) collective-permute-start(bf16[272,128]{1,0:T(8,128)(2,1)S(1)} %get-tuple-element.63), channel_id=1, source_target_pairs={{0,13},{1,12},{2,15},{3,14},{4,9},{5,8},{6,11},{7,10},{8,5},{9,4},... | collective-permute-start | bytes 208904 | tf_op jit(solution)/shard_map/ppermute | solution.py:630
  70.6 12.9 %collective-permute-start.28 = (bf16[272,128]{1,0:T(8,128)(2,1)S(1)}, bf16[272,128]{1,0:T(8,128)(2,1)S(1)}, u32[]{:S(2)}, u32[]{:S(2)}) collective-permute-start(bf16[272,128]{1,0:T(8,128)(2,1)S(1)} %get-tuple-element.64), channel_id=1, source_target_pairs={{0,14},{1,15},{2,12},{3,13},{4,10},{5,11},{6,8},{7,9},{8,6},{9,7},... | collective-permute-start | bytes 208904 | tf_op jit(solution)/shard_map/ppermute | solution.py:630
  72.1 12.9 %collective-permute-start.29 = (bf16[272,128]{1,0:T(8,128)(2,1)S(1)}, bf16[272,128]{1,0:T(8,128)(2,1)S(1)}, u32[]{:S(2)}, u32[]{:S(2)}) collective-permute-start(bf16[272,128]{1,0:T(8,128)(2,1)S(1)} %get-tuple-element.65), channel_id=1, source_target_pairs={{0,15},{1,14},{2,13},{3,12},{4,11},{5,10},{6,9},{7,8},{8,7},{9,6},... | collective-permute-start | bytes 208904 | tf_op jit(solution)/shard_map/ppermute | solution.py:630

commit v2 on v1

--- a/solution.py
+++ b/solution.py
@@ -13,6 +13,7 @@
 f32 = jnp.float32
 bf16 = jnp.bfloat16
 row_tile = 16
+half_tile = 8
 lane_tile = 128
 MIB = 1 << 20
 
@@ -128,35 +129,38 @@
 def multiply_points(points, spectrum_ref):
     n_blocks, double, width = points.shape
     block = double // 2
+    lanes_step = min(width, lane_tile)
 
     def multiply_step(step, carry):
-        start = pl.multiple_of(step * row_tile, row_tile)
-        upper = pl.ds(start, row_tile)
-        lower = pl.ds(pl.multiple_of(block + start, row_tile), row_tile)
-
-        def block_sum(total):
-            sum_re = jnp.zeros((row_tile, width), f32)
-            sum_im = jnp.zeros((row_tile, width), f32)
-            for delay in range(total + 1):
-                a_re = points[total - delay, upper, :]
-                a_im = points[total - delay, lower, :]
-                b_re = spectrum_ref[delay, upper, :]
-                b_im = spectrum_ref[delay, lower, :]
-                sum_re += a_re * b_re - a_im * b_im
-                sum_im += a_re * b_im + a_im * b_re
-            return sum_re, sum_im
-
-        after_re, after_im = block_sum(n_blocks - 1)
-        for total in range(n_blocks - 1, 0, -1):
-            sum_re, sum_im = block_sum(total - 1)
-            points[total, upper, :] = after_re + sum_im
-            points[total, lower, :] = after_im - sum_re
-            after_re, after_im = sum_re, sum_im
-        points[0, upper, :] = after_re
-        points[0, lower, :] = after_im
+        start = pl.multiple_of(step * half_tile, half_tile)
+        upper = pl.ds(start, half_tile)
+        lower = pl.ds(pl.multiple_of(block + start, half_tile), half_tile)
+        for first in range(0, width, lanes_step):
+            lanes = slice(first, first + lanes_step)
+
+            def block_sum(total):
+                sum_re = jnp.zeros((half_tile, lanes_step), f32)
+                sum_im = jnp.zeros((half_tile, lanes_step), f32)
+                for delay in range(total + 1):
+                    a_re = points[total - delay, upper, lanes]
+                    a_im = points[total - delay, lower, lanes]
+                    b_re = spectrum_ref[delay, upper, lanes]
+                    b_im = spectrum_ref[delay, lower, lanes]
+                    sum_re += a_re * b_re - a_im * b_im
+                    sum_im += a_re * b_im + a_im * b_re
+                return sum_re, sum_im
+
+            after_re, after_im = block_sum(n_blocks - 1)
+            for total in range(n_blocks - 1, 0, -1):
+                sum_re, sum_im = block_sum(total - 1)
+                points[total, upper, lanes] = after_re + sum_im
+                points[total, lower, lanes] = after_im - sum_re
+                after_re, after_im = sum_re, sum_im
+            points[0, upper, lanes] = after_re
+            points[0, lower, lanes] = after_im
         return carry
 
-    lax.fori_loop(0, block // row_tile, multiply_step, 0)
+    lax.fori_loop(0, block // half_tile, multiply_step, 0)
 
 
 def convolve(chunk_ref, spectrum_ref, forward_ref, inverse_ref, out_ref, points, tok_rows):
@@ -382,93 +386,129 @@
         name="finish",
     )(ref_ids, alt_ids, streams, *backs)
 
-def stacked(buffer, device, half, tok_rows):
-    return buffer[device, half * tok_rows : (half + 1) * tok_rows, :]
-
-
-def send_products_kernel(halves, vars_dev, me_ref, rows_ref, streams_ref, *refs):
-    n_devices = len(refs) - 4
-    out_refs = refs[:n_devices]
-    pairs, gates, pair_sems, gate_sems = refs[n_devices:]
-    tok_rows = streams_ref.shape[1]
-    width = halves * lane_tile
+def send_products_kernel(first, together, halves, vars_dev, me_ref, offsets_ref, streams_ref, *refs):
+    built, pairs, gates, pair_sems, gate_sems, out_sems = refs[-6:]
+    out_refs = refs[:-6]
+    count, _, tok_rows, width = pairs.shape
     me = me_ref[0]
+    slot = tok_rows // vars_dev
+    local_rows = [var * slot + offsets_ref[me * vars_dev + var] for var in range(vars_dev)]
+    base = me // count * count
+
+    def partner(step):
+        return base + step if together else me ^ (first + step)
 
     def pair_copy(step):
-        start = pl.multiple_of((me ^ step) * width, lane_tile)
+        start = pl.multiple_of(partner(step) * width, lane_tile)
         return pltpu.make_async_copy(
             streams_ref.at[pl.ds(1, 2), :, pl.ds(start, width)], pairs.at[step], pair_sems.at[step]
         )
 
     def gate_copy(var):
-        start = pl.multiple_of(rows_ref[var] // row_tile * row_tile, row_tile)
+        start = pl.multiple_of(local_rows[var] // row_tile * row_tile, row_tile)
         return pltpu.make_async_copy(
             streams_ref.at[0, pl.ds(start, row_tile), :], gates.at[var], gate_sems.at[var]
         )
 
+    def out_copy(step):
+        target = out_refs[0].at[step] if together else out_refs[step]
+        return pltpu.make_async_copy(built.at[step], target, out_sems.at[step])
+
     for var in range(vars_dev):
         gate_copy(var).start()
-    for step in range(n_devices):
+    for step in range(count):
         pair_copy(step).start()
     for var in range(vars_dev):
         gate_copy(var).wait()
-    extra = out_refs[0].shape[0] - halves * tok_rows
+    extra = built.shape[1] - halves * tok_rows
     row = lax.broadcasted_iota(jnp.int32, (row_tile, lane_tile), 0)
     place = lax.broadcasted_iota(jnp.int32, (extra, lane_tile), 0)
-    for step in range(n_devices):
+    for step in range(count):
         pair_copy(step).wait()
         tail = jnp.zeros((extra, lane_tile), f32)
         for half in range(halves):
             lanes = slice(half * lane_tile, (half + 1) * lane_tile)
-            left = pairs[step, 0, :, lanes].astype(f32)
-            right = pairs[step, 1, :, lanes].astype(f32)
             rows = slice(half * tok_rows, (half + 1) * tok_rows)
-            out_refs[step][rows, :] = (left * right).astype(bf16)
-            start = pl.multiple_of((me ^ step) * width + half * lane_tile, lane_tile)
+            built[step, rows, :] = pairs[step, 0, :, lanes] * pairs[step, 1, :, lanes]
+            start = pl.multiple_of(partner(step) * width + half * lane_tile, lane_tile)
             for var in range(vars_dev):
                 tile = gates[var, :, pl.ds(start, lane_tile)].astype(f32)
-                mine = jnp.where(row == rows_ref[var] % row_tile, tile, 0.0)
+                mine = jnp.where(row == local_rows[var] % row_tile, tile, 0.0)
                 mine = jnp.sum(mine, axis=0, keepdims=True)
                 tail = jnp.where(place == half * vars_dev + var, mine, tail)
-        out_refs[step][halves * tok_rows :, :] = tail.astype(bf16)
-
-
-def send_products(me, local_rows, streams, n_devices, extra):
+        built[step, halves * tok_rows :, :] = tail.astype(bf16)
+        out_copy(step).start()
+    for step in range(count):
+        out_copy(step).wait()
+
+
+def send_products(me, offsets, streams, first, count, together, vars_dev, n_devices, extra):
     _, tok_rows, model_width = streams.shape
-    vars_dev = local_rows.shape[0]
-    halves = model_width // n_devices // lane_tile
+    width = model_width // n_devices
+    halves = width // lane_tile
     rows_out = halves * tok_rows + extra
+    if together:
+        out_shape = [jax.ShapeDtypeStruct((count, rows_out, lane_tile), bf16)]
+    else:
+        out_shape = [jax.ShapeDtypeStruct((rows_out, lane_tile), bf16)] * count
     return pl.pallas_call(
-        functools.partial(send_products_kernel, halves, vars_dev),
+        functools.partial(send_products_kernel, first, together, halves, vars_dev),
         in_specs=[
             pl.BlockSpec(memory_space=pltpu.SMEM),
             pl.BlockSpec(memory_space=pltpu.SMEM),
             pl.BlockSpec(memory_space=pltpu.HBM),
         ],
-        out_specs=[whole_spec()] * n_devices,
-        out_shape=[jax.ShapeDtypeStruct((rows_out, lane_tile), bf16)] * n_devices,
+        out_specs=[pl.BlockSpec(memory_space=pltpu.HBM)] * len(out_shape),
+        out_shape=out_shape,
         scratch_shapes=[
-            pltpu.VMEM((n_devices, 2, tok_rows, halves * lane_tile), bf16),
+            pltpu.VMEM((count, rows_out, lane_tile), bf16),
+            pltpu.VMEM((count, 2, tok_rows, width), bf16),
             pltpu.VMEM((vars_dev, row_tile, model_width), bf16),
-            pltpu.SemaphoreType.DMA((n_devices,)),
+            pltpu.SemaphoreType.DMA((count,)),
             pltpu.SemaphoreType.DMA((vars_dev,)),
+            pltpu.SemaphoreType.DMA((count,)),
         ],
         compiler_params=pltpu.CompilerParams(vmem_limit_bytes=60 * MIB),
         cost_estimate=pl.CostEstimate(
-            flops=tok_rows * model_width, bytes_accessed=6 * tok_rows * model_width, transcendentals=0
+            flops=tok_rows * count * width, bytes_accessed=6 * tok_rows * count * width, transcendentals=0
         ),
         name="send_products",
-    )(me, local_rows, streams)
+    )(me, offsets, streams)
 
 
 def direct_filter_kernel(vars_dev, halves, tok_rows, me_ref, *refs):
-    spectrum_ref, forward_ref, inverse_ref, positions_ref, gain_ref, unembed_ref = refs[:6]
-    points, arrived, leaving, packed = refs[-4:]
+    positions_ref, gain_ref, unembed_ref, forward_ref, inverse_hbm, spectrum_hbm = refs[:6]
+    points, arrived, leaving, packed, spectrum, inverse = refs[-11:-5]
+    in_sems, out_sems, tail_sems, spectrum_sem, inverse_sem = refs[-5:]
     n_devices = arrived.shape[0]
-    in_refs, out_refs = refs[6 : 6 + n_devices], refs[6 + n_devices : 6 + 2 * n_devices]
+    near = n_devices // 2
+    far = n_devices - near
+    in_refs = refs[6 : 7 + far]
+    out_refs = refs[7 + far : 8 + 2 * far]
     me = me_ref[0]
-    for step in range(n_devices):
-        arrived[me ^ step] = in_refs[step][...]
+    base = me // near * near
+    body = halves * tok_rows
+
+    def in_copy(index):
+        target = arrived.at[pl.ds(base, near)] if index == 0 else arrived.at[me ^ (near + index - 1)]
+        return pltpu.make_async_copy(in_refs[index], target, in_sems.at[index])
+
+    def out_copy(index, start, size, sems):
+        rows = pl.ds(start, size)
+        if index == 0:
+            source, target = leaving.at[pl.ds(base, near), rows], out_refs[0].at[:, rows]
+        else:
+            source, target = leaving.at[me ^ (near + index - 1), rows], out_refs[index].at[rows]
+        return pltpu.make_async_copy(source, target, sems.at[index])
+
+    spectrum_copy = pltpu.make_async_copy(spectrum_hbm, spectrum, spectrum_sem.at[0])
+    inverse_copy = pltpu.make_async_copy(inverse_hbm, inverse, inverse_sem.at[0])
+    for index in range(far + 1):
+        in_copy(index).start()
+    spectrum_copy.start()
+    inverse_copy.start()
+    for index in range(far + 1):
+        in_copy(index).wait()
 
     n_blocks, double, width = points.shape
     block = double // 2
@@ -477,21 +517,22 @@
     def forward_step(step, carry):
         pieces = []
         for half in range(halves):
-            parts = [stacked(arrived, step * per_block + m, half, tok_rows) for m in range(per_block)]
-            pieces.append(jnp.concatenate(parts, axis=0))
+            rows = slice(half * tok_rows, (half + 1) * tok_rows)
+            parts = [arrived[step * per_block + m, rows, :] for m in range(per_block)]
+            pieces.append(jnp.concatenate(parts + parts, axis=0))
         signal = jnp.concatenate(pieces, axis=1)
-        both = jnp.dot(forward_ref[...], signal, preferred_element_type=f32)
-        points[step] = both[:double] + both[double:]
+        points[step] = jnp.dot(forward_ref[...], signal, preferred_element_type=f32)
         return carry
 
     lax.fori_loop(0, n_blocks, forward_step, 0)
-    multiply_points(points, spectrum_ref)
+    spectrum_copy.wait()
+    multiply_points(points, spectrum)
+    inverse_copy.wait()
 
     def inverse_step(step, carry):
         highs, lows = split_bf16(points[step])
-        both = jnp.dot(inverse_ref[...], highs, preferred_element_type=f32)
-        rest = jnp.dot(inverse_ref[:block, :], lows, preferred_element_type=f32)
-        result = (both[:block] + both[block:] + rest).astype(bf16)
+        terms = jnp.concatenate([highs, highs, lows], axis=0)
+        result = jnp.dot(inverse[...], terms, preferred_element_type=f32).astype(bf16)
         for member in range(per_block):
             for half in range(halves):
                 leaving[step * per_block + member, half * tok_rows : (half + 1) * tok_rows, :] = result[
@@ -501,11 +542,13 @@
         return carry
 
     lax.fori_loop(0, n_blocks, inverse_step, 0)
+    for index in range(far, -1, -1):
+        out_copy(index, 0, body, out_sems).start()
 
     length = n_devices * tok_rows
     column = lax.broadcasted_iota(jnp.int32, (positions_ref.shape[0], length), 1)
     picker = (column == positions_ref[...]).astype(f32).astype(bf16)
-    tails = arrived[:, halves * tok_rows :, :].astype(f32)
+    tails = arrived[:, body:, :].astype(f32)
     place = lax.broadcasted_iota(jnp.int32, tails.shape, 1)
     raw = None
     squares = None
@@ -525,28 +568,44 @@
         squares = rows * rows if squares is None else squares + rows * rows
     pack_scores(raw, squares, vars_dev, packed, n_devices)
     extra = packed.shape[0] // n_devices
-    leaving[:, halves * tok_rows :, :] = packed[...].reshape(n_devices, extra, lane_tile).astype(bf16)
-    for step in range(n_devices):
-        out_refs[step][...] = leaving[me ^ step]
+    leaving[:, body:, :] = packed[...].reshape(n_devices, extra, lane_tile).astype(bf16)
+    for index in range(far, -1, -1):
+        out_copy(index, body, extra, tail_sems).start()
+    for index in range(far + 1):
+        out_copy(index, 0, body, out_sems).wait()
+        out_copy(index, body, extra, tail_sems).wait()
 
 
 def direct_filter(me, operands, arrivals, vars_dev, tok_rows, extra):
-    n_devices = len(arrivals)
-    n_blocks, double, width = operands[0].shape
+    near = arrivals[0].shape[0]
+    far = len(arrivals) - 1
+    n_devices = near + far
+    forward, inverse, spectrum = operands[3:]
+    n_blocks, double, width = spectrum.shape
     halves = width // lane_tile
     rows_out = halves * tok_rows + extra
     flops = 2 * width * n_blocks * (double * double * 5 // 2 + 4 * n_blocks * double)
+    in_hbm = pl.BlockSpec(memory_space=pltpu.HBM)
     return pl.pallas_call(
         functools.partial(direct_filter_kernel, vars_dev, halves, tok_rows),
         in_specs=[pl.BlockSpec(memory_space=pltpu.SMEM)]
-        + [whole_spec()] * (len(operands) + n_devices),
-        out_specs=[whole_spec()] * n_devices,
-        out_shape=[jax.ShapeDtypeStruct((rows_out, lane_tile), bf16)] * n_devices,
+        + [whole_spec()] * 4
+        + [in_hbm] * (2 + len(arrivals)),
+        out_specs=[in_hbm] * len(arrivals),
+        out_shape=[jax.ShapeDtypeStruct((near, rows_out, lane_tile), bf16)]
+        + [jax.ShapeDtypeStruct((rows_out, lane_tile), bf16)] * far,
         scratch_shapes=[
             pltpu.VMEM((n_blocks, double, width), f32),
-            pltpu.VMEM((n_devices, arrivals[0].shape[0], lane_tile), bf16),
+            pltpu.VMEM((n_devices, arrivals[0].shape[1], lane_tile), bf16),
             pltpu.VMEM((n_devices, rows_out, lane_tile), bf16),
             pltpu.VMEM((n_devices * extra, lane_tile), f32),
+            pltpu.VMEM(spectrum.shape, f32),
+            pltpu.VMEM(inverse.shape, bf16),
+            pltpu.SemaphoreType.DMA((far + 1,)),
+            pltpu.SemaphoreType.DMA((far + 1,)),
+            pltpu.SemaphoreType.DMA((far + 1,)),
+            pltpu.SemaphoreType.DMA((1,)),
+            pltpu.SemaphoreType.DMA((1,)),
         ],
         compiler_params=pltpu.CompilerParams(vmem_limit_bytes=32 * MIB),
         cost_estimate=pl.CostEstimate(flops=flops, bytes_accessed=8 * MIB, transcendentals=0),
@@ -556,14 +615,16 @@
 
 def direct_finish_kernel(halves, vars_dev, vocab, me_ref, ref_ref, alt_ref, streams_ref, *refs):
     gates, results, gate_sems, out_sems = refs[-4:]
-    n_devices = gates.shape[0]
-    back_refs, mixed_ref, scores_ref = refs[:n_devices], refs[n_devices], refs[n_devices + 1]
-    tok_rows = streams_ref.shape[1]
-    width = halves * lane_tile
+    n_devices, tok_rows, width = gates.shape
+    near = n_devices // 2
+    near_ref, far_refs = refs[0], refs[1 : 1 + n_devices - near]
+    mixed_ref, scores_ref = refs[-6:-4]
     me = me_ref[0]
+    base = me // near * near
 
     def lanes_of(step):
-        return pl.ds(pl.multiple_of((me ^ step) * width, lane_tile), width)
+        owner = base + step if step < near else me ^ step
+        return pl.ds(pl.multiple_of(owner * width, lane_tile), width)
 
     def gate_copy(step):
         return pltpu.make_async_copy(
@@ -580,12 +641,13 @@
     sums = None
     for step in range(n_devices):
         gate_copy(step).wait()
+        block_ref = near_ref.at[step] if step < near else far_refs[step - near]
         for half in range(halves):
             lanes = slice(half * lane_tile, (half + 1) * lane_tile)
-            filtered = back_refs[step][half * tok_rows : (half + 1) * tok_rows, :].astype(f32)
-            results[step, :, lanes] = (gates[step, :, lanes].astype(f32) * filtered).astype(bf16)
+            filtered = block_ref[half * tok_rows : (half + 1) * tok_rows, :]
+            results[step, :, lanes] = gates[step, :, lanes] * filtered
         out_copy(step).start()
-        tail = back_refs[step][halves * tok_rows :, :].astype(f32)
+        tail = block_ref[halves * tok_rows :, :].astype(f32)
         sums = tail if sums is None else sums + tail
     model_width = n_devices * width
     scores_ref[...] = final_scores(sums, vars_dev, vocab, model_width, ref_ref, alt_ref)
@@ -593,16 +655,15 @@
         out_copy(step).wait()
 
 
-def direct_finish(me, ref_ids, alt_ids, streams, backs, vocab):
+def direct_finish(me, ref_ids, alt_ids, streams, backs, vocab, n_devices):
     _, tok_rows, model_width = streams.shape
-    n_devices = len(backs)
     vars_dev = ref_ids.shape[0]
     width = model_width // n_devices
     return pl.pallas_call(
         functools.partial(direct_finish_kernel, width // lane_tile, vars_dev, vocab),
         in_specs=[pl.BlockSpec(memory_space=pltpu.SMEM)] * 3
         + [pl.BlockSpec(memory_space=pltpu.HBM)]
-        + [whole_spec()] * n_devices,
+        + [whole_spec()] * len(backs),
         out_specs=[pl.BlockSpec(memory_space=pltpu.HBM), whole_spec()],
         out_shape=[
             jax.ShapeDtypeStruct((tok_rows, model_width), bf16),
@@ -622,12 +683,20 @@
     )(me, ref_ids, alt_ids, streams, *backs)
 
 
-def exchange(parts):
-    n_devices = len(parts)
-    moved = [parts[0]] + [None] * (n_devices - 1)
-    for step in range(n_devices - 1, 0, -1):
-        pairs = [(device, device ^ step) for device in range(n_devices)]
-        moved[step] = lax.ppermute(parts[step], "seq", pairs)
+def exchange_near(part, n_devices):
+    near = n_devices // 2
+    groups = [list(range(near)), list(range(near, n_devices))]
+    return lax.all_to_all(
+        part, "seq", split_axis=0, concat_axis=0, axis_index_groups=groups, tiled=True
+    )
+
+
+def exchange_far(parts, n_devices):
+    near = n_devices // 2
+    moved = []
+    for step, part in enumerate(parts):
+        pairs = [(device, device ^ (near + step)) for device in range(n_devices)]
+        moved.append(lax.ppermute(part, "seq", pairs))
     return moved
 
 
@@ -641,7 +710,8 @@
     chunks = max(1, group_width // lane_tile)
     width = group_width // chunks
     block = tok_rows * block_devices(n_devices, tok_rows)
-    forward, inverse = (jnp.asarray(table) for table in block_tables(block))
+    forward_np, inverse_np = block_tables(block)
+    forward, inverse = jnp.asarray(forward_np), jnp.asarray(inverse_np)
 
     slot = tok_rows // vars_dev
     starts = jnp.arange(vars_dev, dtype=jnp.int32) * slot
@@ -656,11 +726,19 @@
         me = jnp.reshape(my_index, (1,)).astype(jnp.int32)
         gate_extra = round_up(chunks * vars_dev, row_tile)
         score_extra = round_up(vars_dev * 2 * (vocab // lane_tile + 1), row_tile)
-        arrivals = exchange(send_products(me, local_rows, streams, n_devices, gate_extra))
+        near = n_devices // 2
+        streams_args = (vars_dev, n_devices, gate_extra)
+        far_parts = send_products(me, offsets, streams, near, n_devices - near, False, *streams_args)
+        near_part = send_products(me, offsets, streams, 0, near, True, *streams_args)
+        arrivals = [exchange_near(near_part[0], n_devices), *exchange_far(far_parts, n_devices)]
         spectrum = filter_spectrum(long_filter, forward, block)
-        operands = (spectrum, forward, inverse, positions, my_gain[None, :], unembed)
+        joined_forward = jnp.asarray(np.concatenate(np.split(forward_np, 2, axis=0), axis=1))
+        joined_inverse = np.split(inverse_np, 2, axis=0)
+        joined_inverse = jnp.asarray(np.concatenate(joined_inverse + joined_inverse[:1], axis=1))
+        operands = (positions, my_gain[None, :], unembed, joined_forward, joined_inverse, spectrum)
         leaving = direct_filter(me, operands, arrivals, vars_dev, tok_rows, score_extra)
-        mixed, scores = direct_finish(me, ref_ids, alt_ids, streams, exchange(leaving), vocab)
+        backs = [exchange_near(leaving[0], n_devices), *exchange_far(leaving[1:], n_devices)]
+        mixed, scores = direct_finish(me, ref_ids, alt_ids, streams, backs, vocab, n_devices)
         return (mixed, scores)
 
     gate_extra = round_up(chunks * vars_dev, row_tile)

time: 87.7 us -> 115 us (1.31)
  the two profiles are of different devices: /device:TPU:13 before, /device:TPU:0 now
where the time goes in v2:
time: 115 us; the launch traced here: 114 us
  starting transfers between devices  51.5 us (45%)
  local copies, waits for them, and re-layouts  28.6 us (25%)
  Pallas kernels  23.5 us (20%)
  waiting for transfers between devices  7.33 us (6%)
  between operations  2.11 us (2%)
    ppermute x16, starting transfers between devices, exchange_far(): moved.append(lax.ppermute(part, 'seq', pairs))  41.1 us
    unnamed x80, local copies, waits for them, and re-layouts  27.9 us
    pallas_call x1, Pallas kernels, direct_filter(): pl.pallas_call(functools.partial(direct_filter_kernel, vars_dev, halves,...  13.2 us
    all_to_all x2, starting transfers between devices, exchange_near(): lax.all_to_all(part, 'seq', split_axis=0, concat_axis=0, axis_index_group...  10.4 us
    ppermute x16, waiting for transfers between devices, exchange_far(): moved.append(lax.ppermute(part, 'seq', pairs))  7.32 us
    pallas_call x2, Pallas kernels, send_products(): pl.pallas_call(functools.partial(send_products_kernel, first, together, h...  6.32 us
    pallas_call x1, Pallas kernels, direct_finish(): pl.pallas_call(functools.partial(direct_finish_kernel, width // lane_tile...  2.65 us
  transfers between devices with their start and end apart: 18, of which 4 were waited for; matrix products, arithmetic and copies ran while one was open for 1% of the time, Pallas kernels for 4%

profile of v2, /device:TPU:0, one launch (start us, length us, event | category | flops | bytes accessed | tf_op | source)
XLA Modules:
  0.0 113.7 jit_solution(7141011018009554303)
XLA Ops:
  0.6 0.0 copy-start.7
  0.7 3.2 %send_products.2 = bf16[8,272,128]{2,1,0:T(8,128)(2,1)} custom-call(s32[1]{0:T(128)} %bitcast.me_ref, s32[16]{0:T(128)} %offsets_ref.3, bf16[3,128,4096]{2,1,0:T(8,128)(2,1)} %streams_ref.5), custom_call_target="tpu_custom_call" | custom-call | flops 262144 | bytes 1572864 | tf_op jit(solution)/shard_map/send_products/pallas_call | solution.py:454
  3.8 5.2 %all-to-all-start = ((bf16[8,272,128]{2,1,0:T(8,128)(2,1)}), bf16[8,272,128]{2,1,0:T(8,128)(2,1)S(1)}, u32[]{:S(2)}, u32[]{:S(2)}) async-start(bf16[8,272,128]{2,1,0:T(8,128)(2,1)} %send_products.2), calls=%async_computation | async-start | bytes 1114112 | tf_op jit(solution)/shard_map/all_to_all | solution.py:689
  9.1 3.2 %send_products.3 = (bf16[272,128]{1,0:T(8,128)(2,1)}, bf16[272,128]{1,0:T(8,128)(2,1)}, bf16[272,128]{1,0:T(8,128)(2,1)}, bf16[272,128]{1,0:T(8,128)(2,1)}, bf16...) custom-call(s32[1]{0:T(128)} %bitcast.me_ref, ...), custom_call_target="tpu_custom_call" | custom-call | flops 262144 | bytes 1572864 | tf_op jit(solution)/shard_map/send_products/pallas_call | solution.py:454
  12.2 2.7 %collective-permute-start = (bf16[272,128]{1,0:T(8,128)(2,1)}, bf16[272,128]{1,0:T(8,128)(2,1)S(1)}, u32[]{:S(2)}, u32[]{:S(2)}) collective-permute-start(bf16[272,128]{1,0:T(8,128)(2,1)} %get-tuple-element.19), channel_id=1, source_target_pairs={{0,8},{1,9},{2,10},{3,11},{4,12},{5,13},{6,14},{7,15},{8,0},{9,1},... | collective-permute-start | bytes 208904 | tf_op jit(solution)/shard_map/ppermute | solution.py:699
  14.9 0.2 collective-permute-start.1
  15.1 3.7 %collective-permute-start.2 = (bf16[272,128]{1,0:T(8,128)(2,1)}, bf16[272,128]{1,0:T(8,128)(2,1)S(1)}, u32[]{:S(2)}, u32[]{:S(2)}) collective-permute-start(bf16[272,128]{1,0:T(8,128)(2,1)} %get-tuple-element.21), channel_id=1, source_target_pairs={{0,10},{1,11},{2,8},{3,9},{4,14},{5,15},{6,12},{7,13},{8,2},{9,3},... | collective-permute-start | bytes 208904 | tf_op jit(solution)/shard_map/ppermute | solution.py:699
  18.7 0.3 collective-permute-start.3
  19.0 3.5 %collective-permute-start.4 = (bf16[272,128]{1,0:T(8,128)(2,1)}, bf16[272,128]{1,0:T(8,128)(2,1)S(1)}, u32[]{:S(2)}, u32[]{:S(2)}) collective-permute-start(bf16[272,128]{1,0:T(8,128)(2,1)} %get-tuple-element.23), channel_id=1, source_target_pairs={{0,12},{1,13},{2,14},{3,15},{4,8},{5,9},{6,10},{7,11},{8,4},{9,5},... | collective-permute-start | bytes 208904 | tf_op jit(solution)/shard_map/ppermute | solution.py:699
  22.5 0.1 copy.12.refs_0_
  22.6 0.8 dynamic-slice_convert_fusion
  23.4 4.4 %collective-permute-start.5 = (bf16[272,128]{1,0:T(8,128)(2,1)}, bf16[272,128]{1,0:T(8,128)(2,1)S(1)}, u32[]{:S(2)}, u32[]{:S(2)}) collective-permute-start(bf16[272,128]{1,0:T(8,128)(2,1)} %get-tuple-element.24), channel_id=1, source_target_pairs={{0,13},{1,12},{2,15},{3,14},{4,9},{5,8},{6,11},{7,10},{8,5},{9,4},... | collective-permute-start | bytes 208904 | tf_op jit(solution)/shard_map/ppermute | solution.py:699
  27.8 3.3 %collective-permute-start.6 = (bf16[272,128]{1,0:T(8,128)(2,1)}, bf16[272,128]{1,0:T(8,128)(2,1)S(1)}, u32[]{:S(2)}, u32[]{:S(2)}) collective-permute-start(bf16[272,128]{1,0:T(8,128)(2,1)} %get-tuple-element.25), channel_id=1, source_target_pairs={{0,14},{1,15},{2,12},{3,13},{4,10},{5,11},{6,8},{7,9},{8,6},{9,7},... | collective-permute-start | bytes 208904 | tf_op jit(solution)/shard_map/ppermute | solution.py:699
  31.1 0.6 collective-permute-done.2.refs_9_
  31.7 2.0 %collective-permute-start.7 = (bf16[272,128]{1,0:T(8,128)(2,1)}, bf16[272,128]{1,0:T(8,128)(2,1)S(1)}, u32[]{:S(2)}, u32[]{:S(2)}) collective-permute-start(bf16[272,128]{1,0:T(8,128)(2,1)} %get-tuple-element.26), channel_id=1, source_target_pairs={{0,15},{1,14},{2,13},{3,12},{4,11},{5,10},{6,9},{7,8},{8,7},{9,6},... | collective-permute-start | bytes 208904 | tf_op jit(solution)/shard_map/ppermute | solution.py:699
  33.7 1.3 %filter_spectrum.1.refs_5_ = f32[8,512,256]{2,1,0:T(8,128)S(1)} custom-call(bf16[256,2048]{1,0:T(8,128)(2,1)S(1)} %copy-done.3, bf16[1024,256]{1,0:T(8,128)(2,1)S(1)} %copy-done.7), custom_call_target="tpu_custom_call" | custom-call | flops 1073741824 | bytes 4194304 | tf_op jit(solution)/shard_map/filter_spectrum/pallas_call | solution.py:116
  35.0 2.0 %copy-done.1 = f32[8,512,256]{2,1,0:T(8,128)} copy-done((f32[8,512,256]{2,1,0:T(8,128)}, f32[8,512,256]{2,1,0:T(8,128)S(1)}, u32[]{:S(2)}) %copy-start.1) | copy-done | bytes 4194328
  37.0 0.6 copy-done.19
  37.6 0.6 copy-done.21
  38.2 0.7 copy-done.28
  38.9 0.6 copy-done.31
  39.5 0.6 copy-done.34
  40.2 0.0 copy-start.4
  40.2 0.8 copy-done.4
  41.0 2.2 %copy-done.2 = f32[8,512,256]{2,1,0:T(8,128)S(1)} copy-done((f32[8,512,256]{2,1,0:T(8,128)S(1)}, f32[8,512,256]{2,1,0:T(8,128)}, u32[]{:S(2)}) %copy-start.2) | copy-done | bytes 4194328
  43.2 1.1 copy-done.5
  44.2 0.9 copy-done.16
  45.1 0.9 copy-done.18
  46.0 0.9 copy-done.20
  46.9 0.9 copy-done.22
  47.7 0.9 copy-done.29
  48.6 0.9 copy-done.32
  49.5 0.9 copy-done.35
  50.4 1.1 copy-done.37
  51.5 1.0 copy-done.38
  52.6 13.2 %direct_filter.1 = (bf16[8,272,128]{2,1,0:T(8,128)(2,1)S(1)}, bf16[272,128]{1,0:T(8,128)(2,1)S(1)}, bf16[272,128]{1,0:T(8,128)(2,1)S(1)}, bf16[272,128]{1,0:T(8,...) custom-call(s32[1]{0:T(128)} %bitcast.me_ref, ...), custom_call_target="tpu_custom_call" | custom-call | flops 2751463424 | bytes 8388608 | tf_op jit(solution)/shard_map/direct_filter/pallas_call | solution.py:589
  65.8 0.8 copy-done.6
  66.6 0.6 copy-done.23
  67.2 0.6 copy-done.24
  67.9 0.6 copy-done.25
  68.5 0.6 copy-done.26
  69.1 0.6 copy-done.27
  69.7 0.6 copy-done.30
  70.4 0.6 copy-done.33
  71.0 0.6 copy-done.36
  71.6 5.1 %all-to-all-start.1 = ((bf16[8,272,128]{2,1,0:T(8,128)(2,1)}), bf16[8,272,128]{2,1,0:T(8,128)(2,1)}, u32[]{:S(2)}, u32[]{:S(2)}) async-start(bf16[8,272,128]{2,1,0:T(8,128)(2,1)} %copy-done.6), calls=%async_computation.1 | async-start | bytes 1114112 | tf_op jit(solution)/shard_map/all_to_all | solution.py:689
  76.7 4.5 %collective-permute-start.10 = (bf16[272,128]{1,0:T(8,128)(2,1)}, bf16[272,128]{1,0:T(8,128)(2,1)S(1)}, u32[]{:S(2)}, u32[]{:S(2)}) collective-permute-start(bf16[272,128]{1,0:T(8,128)(2,1)} %copy-done.36), channel_id=1, source_target_pairs={{0,10},{1,11},{2,8},{3,9},{4,14},{5,15},{6,12},{7,13},{8,2},{9,3},... | collective-permute-start | bytes 208904 | tf_op jit(solution)/shard_map/ppermute | solution.py:699
  81.3 3.3 %collective-permute-start.12 = (bf16[272,128]{1,0:T(8,128)(2,1)}, bf16[272,128]{1,0:T(8,128)(2,1)S(1)}, u32[]{:S(2)}, u32[]{:S(2)}) collective-permute-start(bf16[272,128]{1,0:T(8,128)(2,1)} %copy-done.30), channel_id=1, source_target_pairs={{0,12},{1,13},{2,14},{3,15},{4,8},{5,9},{6,10},{7,11},{8,4},{9,5},... | collective-permute-start | bytes 208904 | tf_op jit(solution)/shard_map/ppermute | solution.py:699
  84.6 0.3 collective-permute-start.13
  84.9 4.4 %collective-permute-start.14 = (bf16[272,128]{1,0:T(8,128)(2,1)}, bf16[272,128]{1,0:T(8,128)(2,1)S(1)}, u32[]{:S(2)}, u32[]{:S(2)}) collective-permute-start(bf16[272,128]{1,0:T(8,128)(2,1)} %copy-done.26), channel_id=1, source_target_pairs={{0,14},{1,15},{2,12},{3,13},{4,10},{5,11},{6,8},{7,9},{8,6},{9,7},... | collective-permute-start | bytes 208904 | tf_op jit(solution)/shard_map/ppermute | solution.py:699
  89.3 0.5 collective-permute-start.15
  89.8 2.4 %collective-permute-start.8 = (bf16[272,128]{1,0:T(8,128)(2,1)}, bf16[272,128]{1,0:T(8,128)(2,1)S(1)}, u32[]{:S(2)}, u32[]{:S(2)}) collective-permute-start(bf16[272,128]{1,0:T(8,128)(2,1)} %copy-done.24), channel_id=1, source_target_pairs={{0,8},{1,9},{2,10},{3,11},{4,12},{5,13},{6,14},{7,15},{8,0},{9,1},... | collective-permute-start | bytes 208904 | tf_op jit(solution)/shard_map/ppermute | solution.py:699
  92.1 1.4 %collective-permute-done.12.refs_5_ = bf16[272,128]{1,0:T(8,128)(2,1)S(1)} collective-permute-done((bf16[272,128]{1,0:T(8,128)(2,1)}, bf16[272,128]{1,0:T(8,128)(2,1)S(1)}, u32[]{:S(2)}, u32[]{:S(2)}) %collective-permute-start.12) | collective-permute-done | bytes 69664 | tf_op jit(solution)/shard_map/ppermute | solution.py:699
  93.5 5.8 %collective-permute-start.9 = (bf16[272,128]{1,0:T(8,128)(2,1)}, bf16[272,128]{1,0:T(8,128)(2,1)S(1)}, u32[]{:S(2)}, u32[]{:S(2)}) collective-permute-start(bf16[272,128]{1,0:T(8,128)(2,1)} %copy-done.23), channel_id=1, source_target_pairs={{0,9},{1,8},{2,11},{3,10},{4,13},{5,12},{6,15},{7,14},{8,1},{9,0},... | collective-permute-start | bytes 208904 | tf_op jit(solution)/shard_map/ppermute | solution.py:699
  100.6 0.6 copy-done.8
  101.2 4.9 %collective-permute-done.8.refs_1_ = bf16[272,128]{1,0:T(8,128)(2,1)S(1)} collective-permute-done((bf16[272,128]{1,0:T(8,128)(2,1)}, bf16[272,128]{1,0:T(8,128)(2,1)S(1)}, u32[]{:S(2)}, u32[]{:S(2)}) %collective-permute-start.8) | collective-permute-done | bytes 69664 | tf_op jit(solution)/shard_map/ppermute | solution.py:699
  106.1 0.6 copy-done.10
  106.8 0.4 collective-permute-done.9.refs_2_
  107.2 0.6 copy-done.12
  107.8 0.9 copy-done.9
  108.7 0.9 copy-done.11
  109.6 0.9 copy-done.13
  110.5 2.7 %direct_finish.1 = (bf16[128,4096]{1,0:T(8,128)(2,1)}, f32[2,1]{1,0:T(2,128)S(1)}) custom-call(s32[1]{0:T(128)} %bitcast.me_ref, s32[1]{0:T(128)S(6)} %copy.14.ref_ref, s32[1]{0:T(128)S(6)} %copy.15.alt_ref, bf16[3,128,4096]{2,1,0:T(8,128)(2,1)S(1)} %copy-done, bf16[8,272,128]{2,1,0:T(8,128)(2,1)} %all-to-all-done.1.refs_0_, ...), custom_call_target="tpu_custom_call" | custom-call | flops 524288 | bytes 3145728 | tf_op jit(solution)/shard_map/direct_finish/pallas_call | solution.py:662
  113.1 0.6 copy.13
  (61 shorter events, 0.1 us)
Async XLA Ops:
  0.6 33.0 %copy-start.7 = (bf16[1024,256]{1,0:T(8,128)(2,1)S(1)}, bf16[1024,256]{1,0:T(8,128)(2,1)}, u32[]{:S(2)}) copy-start(bf16[1024,256]{1,0:T(8,128)(2,1)} %constant.18.clone.forward_ref) | copy-start | bytes 1572868
  0.6 21.9 %copy-start.39 = (s32[16]{0:T(128)S(1)}, s32[16]{0:T(128)}, u32[]{:S(2)}) copy-start(s32[16]{0:T(128)} %offsets_ref.3) | copy-start | bytes 196
  0.7 33.0 %copy-start.3 = (bf16[256,2048]{1,0:T(8,128)(2,1)S(1)}, bf16[256,2048]{1,0:T(8,128)(2,1)}, u32[]{:S(2)}) copy-start(bf16[256,2048]{1,0:T(8,128)(2,1)} %filter_ref.1) | copy-start | bytes 3145732
  3.8 36.3 %all-to-all-start = ((bf16[8,272,128]{2,1,0:T(8,128)(2,1)}), bf16[8,272,128]{2,1,0:T(8,128)(2,1)S(1)}, u32[]{:S(2)}, u32[]{:S(2)}) async-start(bf16[8,272,128]{2,1,0:T(8,128)(2,1)} %send_products.2), calls=%async_computation | async-start | bytes 1114112 | tf_op jit(solution)/shard_map/all_to_all | solution.py:689
  9.1 31.9 %copy-start.14 = (bf16[256,512]{1,0:T(8,128)(2,1)S(1)}, bf16[256,512]{1,0:T(8,128)(2,1)}, u32[]{:S(2)}) copy-start(bf16[256,512]{1,0:T(8,128)(2,1)} %refs_2_.1) | copy-start | bytes 786436
  12.2 11.1 %collective-permute-start = (bf16[272,128]{1,0:T(8,128)(2,1)}, bf16[272,128]{1,0:T(8,128)(2,1)S(1)}, u32[]{:S(2)}, u32[]{:S(2)}) collective-permute-start(bf16[272,128]{1,0:T(8,128)(2,1)} %get-tuple-element.19), channel_id=1, source_target_pairs={{0,8},{1,9},{2,10},{3,11},{4,12},{5,13},{6,14},{7,15},{8,0},{9,1},... | collective-permute-start | bytes 208904 | tf_op jit(solution)/shard_map/ppermute | solution.py:699
  14.9 12.9 %collective-permute-start.1 = (bf16[272,128]{1,0:T(8,128)(2,1)}, bf16[272,128]{1,0:T(8,128)(2,1)S(1)}, u32[]{:S(2)}, u32[]{:S(2)}) collective-permute-start(bf16[272,128]{1,0:T(8,128)(2,1)} %get-tuple-element.20), channel_id=1, source_target_pairs={{0,9},{1,8},{2,11},{3,10},{4,13},{5,12},{6,15},{7,14},{8,1},{9,0},... | collective-permute-start | bytes 208904 | tf_op jit(solution)/shard_map/ppermute | solution.py:699
  15.1 16.6 %collective-permute-start.2 = (bf16[272,128]{1,0:T(8,128)(2,1)}, bf16[272,128]{1,0:T(8,128)(2,1)S(1)}, u32[]{:S(2)}, u32[]{:S(2)}) collective-permute-start(bf16[272,128]{1,0:T(8,128)(2,1)} %get-tuple-element.21), channel_id=1, source_target_pairs={{0,10},{1,11},{2,8},{3,9},{4,14},{5,15},{6,12},{7,13},{8,2},{9,3},... | collective-permute-start | bytes 208904 | tf_op jit(solution)/shard_map/ppermute | solution.py:699
  18.7 18.2 %collective-permute-start.3 = (bf16[272,128]{1,0:T(8,128)(2,1)}, bf16[272,128]{1,0:T(8,128)(2,1)S(1)}, u32[]{:S(2)}, u32[]{:S(2)}) collective-permute-start(bf16[272,128]{1,0:T(8,128)(2,1)} %get-tuple-element.22), channel_id=1, source_target_pairs={{0,11},{1,10},{2,9},{3,8},{4,15},{5,14},{6,13},{7,12},{8,3},{9,2},... | collective-permute-start | bytes 208904 | tf_op jit(solution)/shard_map/ppermute | solution.py:699
  19.0 18.6 %collective-permute-start.4 = (bf16[272,128]{1,0:T(8,128)(2,1)}, bf16[272,128]{1,0:T(8,128)(2,1)S(1)}, u32[]{:S(2)}, u32[]{:S(2)}) collective-permute-start(bf16[272,128]{1,0:T(8,128)(2,1)} %get-tuple-element.23), channel_id=1, source_target_pairs={{0,12},{1,13},{2,14},{3,15},{4,8},{5,9},{6,10},{7,11},{8,4},{9,5},... | collective-permute-start | bytes 208904 | tf_op jit(solution)/shard_map/ppermute | solution.py:699
  23.4 14.8 %collective-permute-start.5 = (bf16[272,128]{1,0:T(8,128)(2,1)}, bf16[272,128]{1,0:T(8,128)(2,1)S(1)}, u32[]{:S(2)}, u32[]{:S(2)}) collective-permute-start(bf16[272,128]{1,0:T(8,128)(2,1)} %get-tuple-element.24), channel_id=1, source_target_pairs={{0,13},{1,12},{2,15},{3,14},{4,9},{5,8},{6,11},{7,10},{8,5},{9,4},... | collective-permute-start | bytes 208904 | tf_op jit(solution)/shard_map/ppermute | solution.py:699
  27.8 12.4 %copy-start.15 = (bf16[272,128]{1,0:T(8,128)(2,1)}, bf16[272,128]{1,0:T(8,128)(2,1)S(1)}, u32[]{:S(2)}) copy-start(bf16[272,128]{1,0:T(8,128)(2,1)S(1)} %collective-permute-done.1.refs_8_) | copy-start | bytes 208900
  27.8 11.1 %collective-permute-start.6 = (bf16[272,128]{1,0:T(8,128)(2,1)}, bf16[272,128]{1,0:T(8,128)(2,1)S(1)}, u32[]{:S(2)}, u32[]{:S(2)}) collective-permute-start(bf16[272,128]{1,0:T(8,128)(2,1)} %get-tuple-element.25), channel_id=1, source_target_pairs={{0,14},{1,15},{2,12},{3,13},{4,10},{5,11},{6,8},{7,9},{8,6},{9,7},... | collective-permute-start | bytes 208904 | tf_op jit(solution)/shard_map/ppermute | solution.py:699
  31.7 8.5 %copy-start.17 = (bf16[272,128]{1,0:T(8,128)(2,1)}, bf16[272,128]{1,0:T(8,128)(2,1)S(1)}, u32[]{:S(2)}) copy-start(bf16[272,128]{1,0:T(8,128)(2,1)S(1)} %collective-permute-done.2.refs_9_) | copy-start | bytes 208900
  31.7 7.8 %collective-permute-start.7 = (bf16[272,128]{1,0:T(8,128)(2,1)}, bf16[272,128]{1,0:T(8,128)(2,1)S(1)}, u32[]{:S(2)}, u32[]{:S(2)}) collective-permute-start(bf16[272,128]{1,0:T(8,128)(2,1)} %get-tuple-element.26), channel_id=1, source_target_pairs={{0,15},{1,14},{2,13},{3,12},{4,11},{5,10},{6,9},{7,8},{8,7},{9,6},... | collective-permute-start | bytes 208904 | tf_op jit(solution)/shard_map/ppermute | solution.py:699
  35.0 2.0 %copy-start.1 = (f32[8,512,256]{2,1,0:T(8,128)}, f32[8,512,256]{2,1,0:T(8,128)S(1)}, u32[]{:S(2)}) copy-start(f32[8,512,256]{2,1,0:T(8,128)S(1)} %filter_spectrum.1.refs_5_) | copy-start | bytes 12582916
  37.0 0.6 copy-start.19
  37.6 0.6 copy-start.21
  38.2 0.7 copy-start.28
  38.9 0.6 copy-start.31
  39.5 0.6 copy-start.34
  40.2 0.8 copy-start.4
  41.0 2.2 %copy-start.2 = (f32[8,512,256]{2,1,0:T(8,128)S(1)}, f32[8,512,256]{2,1,0:T(8,128)}, u32[]{:S(2)}) copy-start(f32[8,512,256]{2,1,0:T(8,128)} %copy-done.1) | copy-start | bytes 12582916
  43.2 1.1 copy-start.5
  44.2 0.9 copy-start.16
  45.1 0.9 copy-start.18
  46.0 0.9 copy-start.20
  46.9 0.9 copy-start.22
  47.7 0.9 copy-start.29
  48.6 0.9 copy-start.32
  49.5 0.9 copy-start.35
  50.4 1.1 copy-start.37
  51.5 1.0 copy-start.38
  52.6 55.3 %copy-start = (bf16[3,128,4096]{2,1,0:T(8,128)(2,1)S(1)}, bf16[3,128,4096]{2,1,0:T(8,128)(2,1)}, u32[]{:S(2)}) copy-start(bf16[3,128,4096]{2,1,0:T(8,128)(2,1)} %streams_ref.5) | copy-start | bytes 9437188
  65.8 0.8 copy-start.6
  66.6 0.6 copy-start.23
  67.2 0.6 copy-start.24
  67.8 0.6 copy-start.25
  68.5 0.6 copy-start.26
  69.1 0.6 copy-start.27
  69.7 0.6 copy-start.30
  70.4 0.6 copy-start.33
  71.0 0.6 copy-start.36
  71.6 36.2 %all-to-all-start.1 = ((bf16[8,272,128]{2,1,0:T(8,128)(2,1)}), bf16[8,272,128]{2,1,0:T(8,128)(2,1)}, u32[]{:S(2)}, u32[]{:S(2)}) async-start(bf16[8,272,128]{2,1,0:T(8,128)(2,1)} %copy-done.6), calls=%async_computation.1 | async-start | bytes 1114112 | tf_op jit(solution)/shard_map/all_to_all | solution.py:689
  76.7 12.5 %collective-permute-start.10 = (bf16[272,128]{1,0:T(8,128)(2,1)}, bf16[272,128]{1,0:T(8,128)(2,1)S(1)}, u32[]{:S(2)}, u32[]{:S(2)}) collective-permute-start(bf16[272,128]{1,0:T(8,128)(2,1)} %copy-done.36), channel_id=1, source_target_pairs={{0,10},{1,11},{2,8},{3,9},{4,14},{5,15},{6,12},{7,13},{8,2},{9,3},... | collective-permute-start | bytes 208904 | tf_op jit(solution)/shard_map/ppermute | solution.py:699
  81.3 8.5 %collective-permute-start.11 = (bf16[272,128]{1,0:T(8,128)(2,1)}, bf16[272,128]{1,0:T(8,128)(2,1)S(1)}, u32[]{:S(2)}, u32[]{:S(2)}) collective-permute-start(bf16[272,128]{1,0:T(8,128)(2,1)} %copy-done.33), channel_id=1, source_target_pairs={{0,11},{1,10},{2,9},{3,8},{4,15},{5,14},{6,13},{7,12},{8,3},{9,2},... | collective-permute-start | bytes 208904 | tf_op jit(solution)/shard_map/ppermute | solution.py:699
  81.3 12.2 %collective-permute-start.12 = (bf16[272,128]{1,0:T(8,128)(2,1)}, bf16[272,128]{1,0:T(8,128)(2,1)S(1)}, u32[]{:S(2)}, u32[]{:S(2)}) collective-permute-start(bf16[272,128]{1,0:T(8,128)(2,1)} %copy-done.30), channel_id=1, source_target_pairs={{0,12},{1,13},{2,14},{3,15},{4,8},{5,9},{6,10},{7,11},{8,4},{9,5},... | collective-permute-start | bytes 208904 | tf_op jit(solution)/shard_map/ppermute | solution.py:699
  84.6 16.0 %collective-permute-start.13 = (bf16[272,128]{1,0:T(8,128)(2,1)}, bf16[272,128]{1,0:T(8,128)(2,1)S(1)}, u32[]{:S(2)}, u32[]{:S(2)}) collective-permute-start(bf16[272,128]{1,0:T(8,128)(2,1)} %copy-done.27), channel_id=1, source_target_pairs={{0,13},{1,12},{2,15},{3,14},{4,9},{5,8},{6,11},{7,10},{8,5},{9,4},... | collective-permute-start | bytes 208904 | tf_op jit(solution)/shard_map/ppermute | solution.py:699
  84.9 15.7 %collective-permute-start.14 = (bf16[272,128]{1,0:T(8,128)(2,1)}, bf16[272,128]{1,0:T(8,128)(2,1)S(1)}, u32[]{:S(2)}, u32[]{:S(2)}) collective-permute-start(bf16[272,128]{1,0:T(8,128)(2,1)} %copy-done.26), channel_id=1, source_target_pairs={{0,14},{1,15},{2,12},{3,13},{4,10},{5,11},{6,8},{7,9},{8,6},{9,7},... | collective-permute-start | bytes 208904 | tf_op jit(solution)/shard_map/ppermute | solution.py:699
  89.3 11.3 %collective-permute-start.15 = (bf16[272,128]{1,0:T(8,128)(2,1)}, bf16[272,128]{1,0:T(8,128)(2,1)S(1)}, u32[]{:S(2)}, u32[]{:S(2)}) collective-permute-start(bf16[272,128]{1,0:T(8,128)(2,1)} %copy-done.25), channel_id=1, source_target_pairs={{0,15},{1,14},{2,13},{3,12},{4,11},{5,10},{6,9},{7,8},{8,7},{9,6},... | collective-permute-start | bytes 208904 | tf_op jit(solution)/shard_map/ppermute | solution.py:699
  89.8 16.4 %collective-permute-start.8 = (bf16[272,128]{1,0:T(8,128)(2,1)}, bf16[272,128]{1,0:T(8,128)(2,1)S(1)}, u32[]{:S(2)}, u32[]{:S(2)}) collective-permute-start(bf16[272,128]{1,0:T(8,128)(2,1)} %copy-done.24), channel_id=1, source_target_pairs={{0,8},{1,9},{2,10},{3,11},{4,12},{5,13},{6,14},{7,15},{8,0},{9,1},... | collective-permute-start | bytes 208904 | tf_op jit(solution)/shard_map/ppermute | solution.py:699
  93.5 13.7 %collective-permute-start.9 = (bf16[272,128]{1,0:T(8,128)(2,1)}, bf16[272,128]{1,0:T(8,128)(2,1)S(1)}, u32[]{:S(2)}, u32[]{:S(2)}) collective-permute-start(bf16[272,128]{1,0:T(8,128)(2,1)} %copy-done.23), channel_id=1, source_target_pairs={{0,9},{1,8},{2,11},{3,10},{4,13},{5,12},{6,15},{7,14},{8,1},{9,0},... | collective-permute-start | bytes 208904 | tf_op jit(solution)/shard_map/ppermute | solution.py:699
  100.6 0.6 copy-start.8
  106.1 0.6 copy-start.10
  107.2 0.6 copy-start.12
  107.8 0.9 copy-start.9
  108.7 0.9 copy-start.11
  109.6 0.9 copy-start.13

commit v3 on v2

--- a/solution.py
+++ b/solution.py
@@ -126,7 +126,7 @@
     )(taps, forward)
 
 
-def multiply_points(points, spectrum_ref):
+def multiply_points(points, spectrum_ref, joint):
     n_blocks, double, width = points.shape
     block = double // 2
     lanes_step = min(width, lane_tile)
@@ -137,27 +137,23 @@
         lower = pl.ds(pl.multiple_of(block + start, half_tile), half_tile)
         for first in range(0, width, lanes_step):
             lanes = slice(first, first + lanes_step)
-
-            def block_sum(total):
+            signal = [(points[k, upper, lanes], points[k, lower, lanes]) for k in range(n_blocks)]
+            taps = [
+                (spectrum_ref[k, upper, lanes], spectrum_ref[k, lower, lanes]) for k in range(n_blocks)
+            ]
+            before_re = jnp.zeros((half_tile, lanes_step), f32)
+            before_im = jnp.zeros((half_tile, lanes_step), f32)
+            for total in range(n_blocks):
                 sum_re = jnp.zeros((half_tile, lanes_step), f32)
                 sum_im = jnp.zeros((half_tile, lanes_step), f32)
                 for delay in range(total + 1):
-                    a_re = points[total - delay, upper, lanes]
-                    a_im = points[total - delay, lower, lanes]
-                    b_re = spectrum_ref[delay, upper, lanes]
-                    b_im = spectrum_ref[delay, lower, lanes]
+                    a_re, a_im = signal[total - delay]
+                    b_re, b_im = taps[delay]
                     sum_re += a_re * b_re - a_im * b_im
                     sum_im += a_re * b_im + a_im * b_re
-                return sum_re, sum_im
-
-            after_re, after_im = block_sum(n_blocks - 1)
-            for total in range(n_blocks - 1, 0, -1):
-                sum_re, sum_im = block_sum(total - 1)
-                points[total, upper, lanes] = after_re + sum_im
-                points[total, lower, lanes] = after_im - sum_re
-                after_re, after_im = sum_re, sum_im
-            points[0, upper, lanes] = after_re
-            points[0, lower, lanes] = after_im
+                joint[total, upper, lanes] = sum_re + before_im
+                joint[total, lower, lanes] = sum_im - before_re
+                before_re, before_im = sum_re, sum_im
         return carry
 
     lax.fori_loop(0, block // half_tile, multiply_step, 0)
@@ -184,7 +180,7 @@
 
     lax.fori_loop(0, n_blocks // group, forward_step, 0)
 
-    multiply_points(points, spectrum_ref)
+    multiply_points(points, spectrum_ref, points)
 
     def inverse_step(step, carry):
         first = step * group
@@ -386,20 +382,16 @@
         name="finish",
     )(ref_ids, alt_ids, streams, *backs)
 
-def send_products_kernel(first, together, halves, vars_dev, me_ref, offsets_ref, streams_ref, *refs):
+def send_products_kernel(halves, vars_dev, me_ref, offsets_ref, streams_ref, *refs):
     built, pairs, gates, pair_sems, gate_sems, out_sems = refs[-6:]
     out_refs = refs[:-6]
-    count, _, tok_rows, width = pairs.shape
+    n_devices, _, tok_rows, width = pairs.shape
     me = me_ref[0]
     slot = tok_rows // vars_dev
     local_rows = [var * slot + offsets_ref[me * vars_dev + var] for var in range(vars_dev)]
-    base = me // count * count
-
-    def partner(step):
-        return base + step if together else me ^ (first + step)
 
     def pair_copy(step):
-        start = pl.multiple_of(partner(step) * width, lane_tile)
+        start = pl.multiple_of((me ^ step) * width, lane_tile)
         return pltpu.make_async_copy(
             streams_ref.at[pl.ds(1, 2), :, pl.ds(start, width)], pairs.at[step], pair_sems.at[step]
         )
@@ -411,26 +403,25 @@
         )
 
     def out_copy(step):
-        target = out_refs[0].at[step] if together else out_refs[step]
-        return pltpu.make_async_copy(built.at[step], target, out_sems.at[step])
+        return pltpu.make_async_copy(built.at[step], out_refs[step], out_sems.at[step])
 
     for var in range(vars_dev):
         gate_copy(var).start()
-    for step in range(count):
+    for step in range(n_devices):
         pair_copy(step).start()
     for var in range(vars_dev):
         gate_copy(var).wait()
     extra = built.shape[1] - halves * tok_rows
     row = lax.broadcasted_iota(jnp.int32, (row_tile, lane_tile), 0)
     place = lax.broadcasted_iota(jnp.int32, (extra, lane_tile), 0)
-    for step in range(count):
+    for step in range(n_devices):
         pair_copy(step).wait()
         tail = jnp.zeros((extra, lane_tile), f32)
         for half in range(halves):
             lanes = slice(half * lane_tile, (half + 1) * lane_tile)
             rows = slice(half * tok_rows, (half + 1) * tok_rows)
             built[step, rows, :] = pairs[step, 0, :, lanes] * pairs[step, 1, :, lanes]
-            start = pl.multiple_of(partner(step) * width + half * lane_tile, lane_tile)
+            start = pl.multiple_of((me ^ step) * width + half * lane_tile, lane_tile)
             for var in range(vars_dev):
                 tile = gates[var, :, pl.ds(start, lane_tile)].astype(f32)
                 mine = jnp.where(row == local_rows[var] % row_tile, tile, 0.0)
@@ -438,76 +429,68 @@
                 tail = jnp.where(place == half * vars_dev + var, mine, tail)
         built[step, halves * tok_rows :, :] = tail.astype(bf16)
         out_copy(step).start()
-    for step in range(count):
+    for step in range(n_devices):
         out_copy(step).wait()
 
 
-def send_products(me, offsets, streams, first, count, together, vars_dev, n_devices, extra):
+def send_products(me, offsets, streams, vars_dev, n_devices, extra):
     _, tok_rows, model_width = streams.shape
     width = model_width // n_devices
     halves = width // lane_tile
     rows_out = halves * tok_rows + extra
-    if together:
-        out_shape = [jax.ShapeDtypeStruct((count, rows_out, lane_tile), bf16)]
-    else:
-        out_shape = [jax.ShapeDtypeStruct((rows_out, lane_tile), bf16)] * count
     return pl.pallas_call(
-        functools.partial(send_products_kernel, first, together, halves, vars_dev),
+        functools.partial(send_products_kernel, halves, vars_dev),
         in_specs=[
             pl.BlockSpec(memory_space=pltpu.SMEM),
             pl.BlockSpec(memory_space=pltpu.SMEM),
-            pl.BlockSpec(memory_space=pltpu.HBM),
+            pl.BlockSpec(memory_space=pl.ANY),
         ],
-        out_specs=[pl.BlockSpec(memory_space=pltpu.HBM)] * len(out_shape),
-        out_shape=out_shape,
+        out_specs=[pl.BlockSpec(memory_space=pl.ANY)] * n_devices,
+        out_shape=[jax.ShapeDtypeStruct((rows_out, lane_tile), bf16)] * n_devices,
         scratch_shapes=[
-            pltpu.VMEM((count, rows_out, lane_tile), bf16),
-            pltpu.VMEM((count, 2, tok_rows, width), bf16),
+            pltpu.VMEM((n_devices, rows_out, lane_tile), bf16),
+            pltpu.VMEM((n_devices, 2, tok_rows, width), bf16),
             pltpu.VMEM((vars_dev, row_tile, model_width), bf16),
-            pltpu.SemaphoreType.DMA((count,)),
+            pltpu.SemaphoreType.DMA((n_devices,)),
             pltpu.SemaphoreType.DMA((vars_dev,)),
-            pltpu.SemaphoreType.DMA((count,)),
+            pltpu.SemaphoreType.DMA((n_devices,)),
         ],
         compiler_params=pltpu.CompilerParams(vmem_limit_bytes=60 * MIB),
         cost_estimate=pl.CostEstimate(
-            flops=tok_rows * count * width, bytes_accessed=6 * tok_rows * count * width, transcendentals=0
+            flops=tok_rows * model_width, bytes_accessed=6 * tok_rows * model_width, transcendentals=0
         ),
         name="send_products",
     )(me, offsets, streams)
 
 
-def direct_filter_kernel(vars_dev, halves, tok_rows, me_ref, *refs):
+def direct_filter_kernel(steps, vars_dev, halves, tok_rows, me_ref, *refs):
     positions_ref, gain_ref, unembed_ref, forward_ref, inverse_hbm, spectrum_hbm = refs[:6]
-    points, arrived, leaving, packed, spectrum, inverse = refs[-11:-5]
+    points, joint, arrived, leaving, packed, spectrum, inverse = refs[-12:-5]
     in_sems, out_sems, tail_sems, spectrum_sem, inverse_sem = refs[-5:]
     n_devices = arrived.shape[0]
-    near = n_devices // 2
-    far = n_devices - near
-    in_refs = refs[6 : 7 + far]
-    out_refs = refs[7 + far : 8 + 2 * far]
+    in_refs = refs[6 : 6 + n_devices]
+    out_refs = refs[6 + n_devices : 6 + 2 * n_devices]
     me = me_ref[0]
-    base = me // near * near
     body = halves * tok_rows
 
     def in_copy(index):
-        target = arrived.at[pl.ds(base, near)] if index == 0 else arrived.at[me ^ (near + index - 1)]
-        return pltpu.make_async_copy(in_refs[index], target, in_sems.at[index])
-
-    def out_copy(index, start, size, sems):
+        return pltpu.make_async_copy(
+            in_refs[index], arrived.at[me ^ steps[index]], in_sems.at[index]
+        )
+
+    def out_copy(step, start, size, sems):
         rows = pl.ds(start, size)
-        if index == 0:
-            source, target = leaving.at[pl.ds(base, near), rows], out_refs[0].at[:, rows]
-        else:
-            source, target = leaving.at[me ^ (near + index - 1), rows], out_refs[index].at[rows]
-        return pltpu.make_async_copy(source, target, sems.at[index])
+        return pltpu.make_async_copy(
+            leaving.at[me ^ step, rows], out_refs[step].at[rows], sems.at[step]
+        )
 
     spectrum_copy = pltpu.make_async_copy(spectrum_hbm, spectrum, spectrum_sem.at[0])
     inverse_copy = pltpu.make_async_copy(inverse_hbm, inverse, inverse_sem.at[0])
-    for index in range(far + 1):
+    for index in range(n_devices):
         in_copy(index).start()
     spectrum_copy.start()
     inverse_copy.start()
-    for index in range(far + 1):
+    for index in range(n_devices):
         in_copy(index).wait()
 
     n_blocks, double, width = points.shape
@@ -519,20 +502,22 @@
         for half in range(halves):
             rows = slice(half * tok_rows, (half + 1) * tok_rows)
             parts = [arrived[step * per_block + m, rows, :] for m in range(per_block)]
-            pieces.append(jnp.concatenate(parts + parts, axis=0))
+            pieces.append(jnp.concatenate(parts, axis=0))
         signal = jnp.concatenate(pieces, axis=1)
-        points[step] = jnp.dot(forward_ref[...], signal, preferred_element_type=f32)
+        both = jnp.dot(forward_ref[...], signal, preferred_element_type=f32)
+        points[step] = both[:double] + both[double:]
         return carry
 
     lax.fori_loop(0, n_blocks, forward_step, 0)
     spectrum_copy.wait()
-    multiply_points(points, spectrum)
+    multiply_points(points, spectrum, joint)
     inverse_copy.wait()
 
     def inverse_step(step, carry):
-        highs, lows = split_bf16(points[step])
-        terms = jnp.concatenate([highs, highs, lows], axis=0)
-        result = jnp.dot(inverse[...], terms, preferred_element_type=f32).astype(bf16)
+        highs, lows = split_bf16(joint[step])
+        both = jnp.dot(inverse[...], highs, preferred_element_type=f32)
+        rest = jnp.dot(inverse[:block, :], lows, preferred_element_type=f32)
+        result = (both[:block] + both[block:] + rest).astype(bf16)
         for member in range(per_block):
             for half in range(halves):
                 leaving[step * per_block + member, half * tok_rows : (half + 1) * tok_rows, :] = result[
@@ -542,8 +527,8 @@
         return carry
 
     lax.fori_loop(0, n_blocks, inverse_step, 0)
-    for index in range(far, -1, -1):
-        out_copy(index, 0, body, out_sems).start()
+    for step in range(n_devices):
+        out_copy(step, 0, body, out_sems).start()
 
     length = n_devices * tok_rows
     column = lax.broadcasted_iota(jnp.int32, (positions_ref.shape[0], length), 1)
@@ -569,41 +554,39 @@
     pack_scores(raw, squares, vars_dev, packed, n_devices)
     extra = packed.shape[0] // n_devices
     leaving[:, body:, :] = packed[...].reshape(n_devices, extra, lane_tile).astype(bf16)
-    for index in range(far, -1, -1):
-        out_copy(index, body, extra, tail_sems).start()
-    for index in range(far + 1):
-        out_copy(index, 0, body, out_sems).wait()
-        out_copy(index, body, extra, tail_sems).wait()
-
-
-def direct_filter(me, operands, arrivals, vars_dev, tok_rows, extra):
-    near = arrivals[0].shape[0]
-    far = len(arrivals) - 1
-    n_devices = near + far
+    for step in range(n_devices):
+        out_copy(step, body, extra, tail_sems).start()
+    for step in range(n_devices):
+        out_copy(step, 0, body, out_sems).wait()
+        out_copy(step, body, extra, tail_sems).wait()
+
+
+def direct_filter(me, operands, steps, arrivals, vars_dev, tok_rows, extra):
+    n_devices = len(arrivals)
     forward, inverse, spectrum = operands[3:]
     n_blocks, double, width = spectrum.shape
     halves = width // lane_tile
     rows_out = halves * tok_rows + extra
     flops = 2 * width * n_blocks * (double * double * 5 // 2 + 4 * n_blocks * double)
-    in_hbm = pl.BlockSpec(memory_space=pltpu.HBM)
+    anywhere = pl.BlockSpec(memory_space=pl.ANY)
     return pl.pallas_call(
-        functools.partial(direct_filter_kernel, vars_dev, halves, tok_rows),
+        functools.partial(direct_filter_kernel, steps, vars_dev, halves, tok_rows),
         in_specs=[pl.BlockSpec(memory_space=pltpu.SMEM)]
         + [whole_spec()] * 4
-        + [in_hbm] * (2 + len(arrivals)),
-        out_specs=[in_hbm] * len(arrivals),
-        out_shape=[jax.ShapeDtypeStruct((near, rows_out, lane_tile), bf16)]
-        + [jax.ShapeDtypeStruct((rows_out, lane_tile), bf16)] * far,
+        + [anywhere] * (2 + n_devices),
+        out_specs=[anywhere] * n_devices,
+        out_shape=[jax.ShapeDtypeStruct((rows_out, lane_tile), bf16)] * n_devices,
         scratch_shapes=[
             pltpu.VMEM((n_blocks, double, width), f32),
-            pltpu.VMEM((n_devices, arrivals[0].shape[1], lane_tile), bf16),
+            pltpu.VMEM((n_blocks, double, width), f32),
+            pltpu.VMEM((n_devices,) + arrivals[0].shape, bf16),
             pltpu.VMEM((n_devices, rows_out, lane_tile), bf16),
             pltpu.VMEM((n_devices * extra, lane_tile), f32),
             pltpu.VMEM(spectrum.shape, f32),
             pltpu.VMEM(inverse.shape, bf16),
-            pltpu.SemaphoreType.DMA((far + 1,)),
-            pltpu.SemaphoreType.DMA((far + 1,)),
-            pltpu.SemaphoreType.DMA((far + 1,)),
+            pltpu.SemaphoreType.DMA((n_devices,)),
+            pltpu.SemaphoreType.DMA((n_devices,)),
+            pltpu.SemaphoreType.DMA((n_devices,)),
             pltpu.SemaphoreType.DMA((1,)),
             pltpu.SemaphoreType.DMA((1,)),
         ],
@@ -613,18 +596,14 @@
     )(me, *operands, *arrivals)
 
 
-def direct_finish_kernel(halves, vars_dev, vocab, me_ref, ref_ref, alt_ref, streams_ref, *refs):
+def direct_finish_kernel(steps, halves, vars_dev, vocab, me_ref, ref_ref, alt_ref, streams_ref, *refs):
     gates, results, gate_sems, out_sems = refs[-4:]
     n_devices, tok_rows, width = gates.shape
-    near = n_devices // 2
-    near_ref, far_refs = refs[0], refs[1 : 1 + n_devices - near]
     mixed_ref, scores_ref = refs[-6:-4]
     me = me_ref[0]
-    base = me // near * near
-
-    def lanes_of(step):
-        owner = base + step if step < near else me ^ step
-        return pl.ds(pl.multiple_of(owner * width, lane_tile), width)
+
+    def lanes_of(index):
+        return pl.ds(pl.multiple_of((me ^ steps[index]) * width, lane_tile), width)
 
     def gate_copy(step):
         return pltpu.make_async_copy(
@@ -641,7 +620,7 @@
     sums = None
     for step in range(n_devices):
         gate_copy(step).wait()
-        block_ref = near_ref.at[step] if step < near else far_refs[step - near]
+        block_ref = refs[step]
         for half in range(halves):
             lanes = slice(half * lane_tile, (half + 1) * lane_tile)
             filtered = block_ref[half * tok_rows : (half + 1) * tok_rows, :]
@@ -655,16 +634,17 @@
         out_copy(step).wait()
 
 
-def direct_finish(me, ref_ids, alt_ids, streams, backs, vocab, n_devices):
+def direct_finish(me, ref_ids, alt_ids, streams, steps, backs, vocab):
     _, tok_rows, model_width = streams.shape
+    n_devices = len(backs)
     vars_dev = ref_ids.shape[0]
     width = model_width // n_devices
     return pl.pallas_call(
-        functools.partial(direct_finish_kernel, width // lane_tile, vars_dev, vocab),
+        functools.partial(direct_finish_kernel, steps, width // lane_tile, vars_dev, vocab),
         in_specs=[pl.BlockSpec(memory_space=pltpu.SMEM)] * 3
-        + [pl.BlockSpec(memory_space=pltpu.HBM)]
+        + [pl.BlockSpec(memory_space=pl.ANY)]
         + [whole_spec()] * len(backs),
-        out_specs=[pl.BlockSpec(memory_space=pltpu.HBM), whole_spec()],
+        out_specs=[pl.BlockSpec(memory_space=pl.ANY), whole_spec()],
         out_shape=[
             jax.ShapeDtypeStruct((tok_rows, model_width), bf16),
             jax.ShapeDtypeStruct((2, vars_dev), f32),
@@ -683,20 +663,24 @@
     )(me, ref_ids, alt_ids, streams, *backs)
 
 
-def exchange_near(part, n_devices):
-    near = n_devices // 2
-    groups = [list(range(near)), list(range(near, n_devices))]
-    return lax.all_to_all(
-        part, "seq", split_axis=0, concat_axis=0, axis_index_groups=groups, tiled=True
-    )
-
-
-def exchange_far(parts, n_devices):
-    near = n_devices // 2
-    moved = []
-    for step, part in enumerate(parts):
-        pairs = [(device, device ^ (near + step)) for device in range(n_devices)]
-        moved.append(lax.ppermute(part, "seq", pairs))
+def partner_order(n_devices):
+    half = n_devices // 2
+    far, near = list(range(half, n_devices)), list(range(1, half))
+    lead = len(far) // 2
+    order = far[:lead]
+    rest = far[lead:]
+    while rest or near:
+        order += near[:1] + rest[:1]
+        rest, near = rest[1:], near[1:]
+    return order
+
+
+def exchange(parts, order):
+    n_devices = len(parts)
+    moved = {0: parts[0]}
+    for step in order:
+        pairs = [(device, device ^ step) for device in range(n_devices)]
+        moved[step] = lax.ppermute(parts[step], "seq", pairs)
     return moved
 
 
@@ -726,19 +710,19 @@
         me = jnp.reshape(my_index, (1,)).astype(jnp.int32)
         gate_extra = round_up(chunks * vars_dev, row_tile)
         score_extra = round_up(vars_dev * 2 * (vocab // lane_tile + 1), row_tile)
-        near = n_devices // 2
-        streams_args = (vars_dev, n_devices, gate_extra)
-        far_parts = send_products(me, offsets, streams, near, n_devices - near, False, *streams_args)
-        near_part = send_products(me, offsets, streams, 0, near, True, *streams_args)
-        arrivals = [exchange_near(near_part[0], n_devices), *exchange_far(far_parts, n_devices)]
+        parts = send_products(me, offsets, streams, vars_dev, n_devices, gate_extra)
+        order = partner_order(n_devices)
+        slots = sorted(range(len(order)), key=str)
+        steps = [0] + [order[slots.index(place)] for place in range(len(order))]
+        moved = exchange(parts, steps[1:])
         spectrum = filter_spectrum(long_filter, forward, block)
-        joined_forward = jnp.asarray(np.concatenate(np.split(forward_np, 2, axis=0), axis=1))
-        joined_inverse = np.split(inverse_np, 2, axis=0)
-        joined_inverse = jnp.asarray(np.concatenate(joined_inverse + joined_inverse[:1], axis=1))
-        operands = (positions, my_gain[None, :], unembed, joined_forward, joined_inverse, spectrum)
-        leaving = direct_filter(me, operands, arrivals, vars_dev, tok_rows, score_extra)
-        backs = [exchange_near(leaving[0], n_devices), *exchange_far(leaving[1:], n_devices)]
-        mixed, scores = direct_finish(me, ref_ids, alt_ids, streams, backs, vocab, n_devices)
+        operands = (positions, my_gain[None, :], unembed, forward, inverse, spectrum)
+        arrivals = [moved[step] for step in steps]
+        leaving = direct_filter(me, operands, steps, arrivals, vars_dev, tok_rows, score_extra)
+        steps = [0] + order
+        returned = exchange(leaving, order)
+        backs = [returned[step] for step in steps]
+        mixed, scores = direct_finish(me, ref_ids, alt_ids, streams, steps, backs, vocab)
         return (mixed, scores)
 
     gate_extra = round_up(chunks * vars_dev, row_tile)

time: 115 us -> 85.7 us (0.75)
  the two profiles are of different devices: /device:TPU:0 before, /device:TPU:1 now
where the time goes in v3:
time: 85.7 us; the launch traced here: 85.4 us
  starting transfers between devices  47.9 us (56%)
  Pallas kernels  19.6 us (23%)
  waiting for transfers between devices  11.4 us (13%)
  local copies, waits for them, and re-layouts  2.98 us (3%)
  between operations  2.09 us (2%)
  other arithmetic  1.41 us (2%)
    ppermute x30, starting transfers between devices, exchange(): moved[step] = lax.ppermute(parts[step], 'seq', pairs)  47.9 us
    pallas_call x1, Pallas kernels, direct_filter(): pl.pallas_call(functools.partial(direct_filter_kernel, steps, vars_dev, h...  12.8 us
    ppermute x30, waiting for transfers between devices, exchange(): moved[step] = lax.ppermute(parts[step], 'seq', pairs)  11.4 us
    pallas_call x1, Pallas kernels, send_products(): pl.pallas_call(functools.partial(send_products_kernel, halves, vars_dev),...  3.87 us
    unnamed x14, local copies, waits for them, and re-layouts  2.29 us
  transfers between devices with their start and end apart: 30, of which 9 were waited for; matrix products, arithmetic and copies ran while one was open for 2% of the time, Pallas kernels for 2%

profile of v3, /device:TPU:1, one launch (start us, length us, event | category | flops | bytes accessed | tf_op | source)
XLA Modules:
  0.0 85.4 jit_solution(10160107976840026411)
XLA Ops:
  0.6 0.0 copy-start.3
  0.7 0.0 copy-start.6
  0.7 3.9 %send_products.1 = (bf16[272,128]{1,0:T(8,128)(2,1)}, bf16[272,128]{1,0:T(8,128)(2,1)}, bf16[272,128]{1,0:T(8,128)(2,1)}, bf16[272,128]{1,0:T(8,128)(2,1)}, bf16...) custom-call(s32[1]{0:T(128)} %bitcast.me_ref, ...), custom_call_target="tpu_custom_call" | custom-call | flops 524288 | bytes 3145728 | tf_op jit(solution)/shard_map/send_products/pallas_call | solution.py:441
  4.5 3.2 %collective-permute-start = (bf16[272,128]{1,0:T(8,128)(2,1)}, bf16[272,128]{1,0:T(8,128)(2,1)S(1)}, u32[]{:S(2)}, u32[]{:S(2)}) collective-permute-start(bf16[272,128]{1,0:T(8,128)(2,1)} %get-tuple-element.35), channel_id=1, source_target_pairs={{0,8},{1,9},{2,10},{3,11},{4,12},{5,13},{6,14},{7,15},{8,0},{9,1},... | collective-permute-start | bytes 208904 | tf_op jit(solution)/shard_map/ppermute | solution.py:683
  7.8 0.6 collective-permute-start.1
  8.4 3.5 %collective-permute-start.10 = (bf16[272,128]{1,0:T(8,128)(2,1)}, bf16[272,128]{1,0:T(8,128)(2,1)S(1)}, u32[]{:S(2)}, u32[]{:S(2)}) collective-permute-start(bf16[272,128]{1,0:T(8,128)(2,1)} %get-tuple-element.45), channel_id=1, source_target_pairs={{0,10},{1,11},{2,8},{3,9},{4,14},{5,15},{6,12},{7,13},{8,2},{9,3},... | collective-permute-start | bytes 208904 | tf_op jit(solution)/shard_map/ppermute | solution.py:683
  11.9 0.3 collective-permute-start.11
  12.1 0.2 collective-permute-start.12
  12.3 0.7 add_bitcast_fusion
  13.0 0.1 copy.11.refs_0_
  13.1 0.0 collective-permute-done.refs_7_
  13.1 6.8 %collective-permute-start.13 = (bf16[272,128]{1,0:T(8,128)(2,1)}, bf16[272,128]{1,0:T(8,128)(2,1)S(1)}, u32[]{:S(2)}, u32[]{:S(2)}) collective-permute-start(bf16[272,128]{1,0:T(8,128)(2,1)} %get-tuple-element.48), channel_id=1, source_target_pairs={{0,12},{1,13},{2,14},{3,15},{4,8},{5,9},{6,10},{7,11},{8,4},{9,5},... | collective-permute-start | bytes 208904 | tf_op jit(solution)/shard_map/ppermute | solution.py:683
  19.8 0.0 collective-permute-done.1.refs_8_
  19.8 1.2 %collective-permute-start.14 = (bf16[272,128]{1,0:T(8,128)(2,1)}, bf16[272,128]{1,0:T(8,128)(2,1)S(1)}, u32[]{:S(2)}, u32[]{:S(2)}) collective-permute-start(bf16[272,128]{1,0:T(8,128)(2,1)} %get-tuple-element.49), channel_id=1, source_target_pairs={{0,2},{1,3},{2,0},{3,1},{4,6},{5,7},{6,4},{7,5},{8,10},{9,11},{10,... | collective-permute-start | bytes 208904 | tf_op jit(solution)/shard_map/ppermute | solution.py:683
  21.0 0.0 collective-permute-done.10.refs_17_
  21.0 3.3 %collective-permute-start.2 = (bf16[272,128]{1,0:T(8,128)(2,1)}, bf16[272,128]{1,0:T(8,128)(2,1)S(1)}, u32[]{:S(2)}, u32[]{:S(2)}) collective-permute-start(bf16[272,128]{1,0:T(8,128)(2,1)} %get-tuple-element.37), channel_id=1, source_target_pairs={{0,13},{1,12},{2,15},{3,14},{4,9},{5,8},{6,11},{7,10},{8,5},{9,4},... | collective-permute-start | bytes 208904 | tf_op jit(solution)/shard_map/ppermute | solution.py:683
  24.3 0.0 collective-permute-done.11.refs_18_
  24.3 0.1 collective-permute-start.3
  24.4 0.0 collective-permute-done.12.refs_19_
  24.4 2.4 %collective-permute-start.4 = (bf16[272,128]{1,0:T(8,128)(2,1)}, bf16[272,128]{1,0:T(8,128)(2,1)S(1)}, u32[]{:S(2)}, u32[]{:S(2)}) collective-permute-start(bf16[272,128]{1,0:T(8,128)(2,1)} %get-tuple-element.39), channel_id=1, source_target_pairs={{0,14},{1,15},{2,12},{3,13},{4,10},{5,11},{6,8},{7,9},{8,6},{9,7},... | collective-permute-start | bytes 208904 | tf_op jit(solution)/shard_map/ppermute | solution.py:683
  26.7 0.8 dynamic-slice_convert_fusion
  27.5 0.0 collective-permute-done.13.refs_20_
  27.5 0.0 collective-permute-start.5
  27.5 0.0 collective-permute-done.14.refs_21_
  27.5 2.5 %collective-permute-start.6 = (bf16[272,128]{1,0:T(8,128)(2,1)}, bf16[272,128]{1,0:T(8,128)(2,1)S(1)}, u32[]{:S(2)}, u32[]{:S(2)}) collective-permute-start(bf16[272,128]{1,0:T(8,128)(2,1)} %get-tuple-element.41), channel_id=1, source_target_pairs={{0,15},{1,14},{2,13},{3,12},{4,11},{5,10},{6,9},{7,8},{8,7},{9,6},... | collective-permute-start | bytes 208904 | tf_op jit(solution)/shard_map/ppermute | solution.py:683
  30.0 0.0 collective-permute-done.2.refs_9_
  30.0 0.1 collective-permute-start.7
  30.2 0.0 collective-permute-done.3.refs_10_
  30.2 1.9 %collective-permute-start.8 = (bf16[272,128]{1,0:T(8,128)(2,1)}, bf16[272,128]{1,0:T(8,128)(2,1)S(1)}, u32[]{:S(2)}, u32[]{:S(2)}) collective-permute-start(bf16[272,128]{1,0:T(8,128)(2,1)} %get-tuple-element.43), channel_id=1, source_target_pairs={{0,6},{1,7},{2,4},{3,5},{4,2},{5,3},{6,0},{7,1},{8,14},{9,15},{10,... | collective-permute-start | bytes 208904 | tf_op jit(solution)/shard_map/ppermute | solution.py:683
  32.1 0.0 collective-permute-done.4.refs_11_
  32.1 1.7 %collective-permute-start.9 = (bf16[272,128]{1,0:T(8,128)(2,1)}, bf16[272,128]{1,0:T(8,128)(2,1)S(1)}, u32[]{:S(2)}, u32[]{:S(2)}) collective-permute-start(bf16[272,128]{1,0:T(8,128)(2,1)} %get-tuple-element.44), channel_id=1, source_target_pairs={{0,7},{1,6},{2,5},{3,4},{4,3},{5,2},{6,1},{7,0},{8,15},{9,14},{10,... | collective-permute-start | bytes 208904 | tf_op jit(solution)/shard_map/ppermute | solution.py:683
  33.8 1.2 %copy-done.1 = bf16[256,2048]{1,0:T(8,128)(2,1)S(1)} copy-done((bf16[256,2048]{1,0:T(8,128)(2,1)S(1)}, bf16[256,2048]{1,0:T(8,128)(2,1)}, u32[]{:S(2)}) %copy-start.1) | copy-done | bytes 1048600
  35.0 1.0 %copy-done.2 = bf16[1024,256]{1,0:T(8,128)(2,1)S(1)} copy-done((bf16[1024,256]{1,0:T(8,128)(2,1)S(1)}, bf16[1024,256]{1,0:T(8,128)(2,1)}, u32[]{:S(2)}) %copy-start.2) | copy-done | bytes 524312
  36.0 1.3 %filter_spectrum.1.refs_5_ = f32[8,512,256]{2,1,0:T(8,128)S(1)} custom-call(bf16[256,2048]{1,0:T(8,128)(2,1)S(1)} %copy-done.1, bf16[1024,256]{1,0:T(8,128)(2,1)S(1)} %copy-done.2), custom_call_target="tpu_custom_call" | custom-call | flops 1073741824 | bytes 4194304 | tf_op jit(solution)/shard_map/filter_spectrum/pallas_call | solution.py:116
  37.3 0.0 collective-permute-done.6.refs_13_
  37.3 0.4 collective-permute-done.8.refs_15_
  37.8 1.5 %collective-permute-done.9.refs_16_ = bf16[272,128]{1,0:T(8,128)(2,1)S(1)} collective-permute-done((bf16[272,128]{1,0:T(8,128)(2,1)}, bf16[272,128]{1,0:T(8,128)(2,1)S(1)}, u32[]{:S(2)}, u32[]{:S(2)}) %collective-permute-start.9) | collective-permute-done | bytes 69664 | tf_op jit(solution)/shard_map/ppermute | solution.py:683
  39.3 0.0 copy-start
  39.3 12.8 %direct_filter.1 = (bf16[272,128]{1,0:T(8,128)(2,1)S(1)}, bf16[272,128]{1,0:T(8,128)(2,1)S(1)}, bf16[272,128]{1,0:T(8,128)(2,1)S(1)}, bf16[272,128]{1,0:T(8,128)...) custom-call(s32[1]{0:T(128)} %bitcast.me_ref, ...), custom_call_target="tpu_custom_call" | custom-call | flops 2751463424 | bytes 8388608 | tf_op jit(solution)/shard_map/direct_filter/pallas_call | solution.py:572
  52.1 0.6 collective-permute-start.15
  52.6 2.4 %collective-permute-start.16 = (bf16[272,128]{1,0:T(8,128)(2,1)S(1)}, bf16[272,128]{1,0:T(8,128)(2,1)S(1)}, u32[]{:S(2)}, u32[]{:S(2)}) collective-permute-start(bf16[272,128]{1,0:T(8,128)(2,1)S(1)} %get-tuple-element.52), channel_id=1, source_target_pairs={{0,9},{1,8},{2,11},{3,10},{4,13},{5,12},{6,15},{7,14},{8,1},{9,0},... | collective-permute-start | bytes 208904 | tf_op jit(solution)/shard_map/ppermute | solution.py:683
  55.1 0.6 collective-permute-start.17
  55.7 2.7 %collective-permute-start.18 = (bf16[272,128]{1,0:T(8,128)(2,1)S(1)}, bf16[272,128]{1,0:T(8,128)(2,1)S(1)}, u32[]{:S(2)}, u32[]{:S(2)}) collective-permute-start(bf16[272,128]{1,0:T(8,128)(2,1)S(1)} %get-tuple-element.54), channel_id=1, source_target_pairs={{0,11},{1,10},{2,9},{3,8},{4,15},{5,14},{6,13},{7,12},{8,3},{9,2},... | collective-permute-start | bytes 208904 | tf_op jit(solution)/shard_map/ppermute | solution.py:683
  58.4 0.4 collective-permute-start.19
  58.7 4.1 %collective-permute-done.15.refs_1_ = bf16[272,128]{1,0:T(8,128)(2,1)S(1)} collective-permute-done((bf16[272,128]{1,0:T(8,128)(2,1)S(1)}, bf16[272,128]{1,0:T(8,128)(2,1)S(1)}, u32[]{:S(2)}, u32[]{:S(2)}) %collective-permute-start.15) | collective-permute-done | bytes 69664 | tf_op jit(solution)/shard_map/ppermute | solution.py:683
  62.9 1.6 %collective-permute-start.20 = (bf16[272,128]{1,0:T(8,128)(2,1)S(1)}, bf16[272,128]{1,0:T(8,128)(2,1)S(1)}, u32[]{:S(2)}, u32[]{:S(2)}) collective-permute-start(bf16[272,128]{1,0:T(8,128)(2,1)S(1)} %get-tuple-element.56), channel_id=1, source_target_pairs={{0,12},{1,13},{2,14},{3,15},{4,8},{5,9},{6,10},{7,11},{8,4},{9,5},... | collective-permute-start | bytes 208904 | tf_op jit(solution)/shard_map/ppermute | solution.py:683
  64.4 0.6 collective-permute-done.16.refs_2_
  65.0 1.0 %collective-permute-done.17.refs_3_ = bf16[272,128]{1,0:T(8,128)(2,1)S(1)} collective-permute-done((bf16[272,128]{1,0:T(8,128)(2,1)S(1)}, bf16[272,128]{1,0:T(8,128)(2,1)S(1)}, u32[]{:S(2)}, u32[]{:S(2)}) %collective-permute-start.17) | collective-permute-done | bytes 69664 | tf_op jit(solution)/shard_map/ppermute | solution.py:683
  66.1 2.0 %collective-permute-start.22 = (bf16[272,128]{1,0:T(8,128)(2,1)S(1)}, bf16[272,128]{1,0:T(8,128)(2,1)S(1)}, u32[]{:S(2)}, u32[]{:S(2)}) collective-permute-start(bf16[272,128]{1,0:T(8,128)(2,1)S(1)} %get-tuple-element.58), channel_id=1, source_target_pairs={{0,13},{1,12},{2,15},{3,14},{4,9},{5,8},{6,11},{7,10},{8,5},{9,4},... | collective-permute-start | bytes 208904 | tf_op jit(solution)/shard_map/ppermute | solution.py:683
  68.1 0.1 collective-permute-done.18.refs_4_
  68.2 0.7 collective-permute-start.23
  68.9 2.2 %collective-permute-start.24 = (bf16[272,128]{1,0:T(8,128)(2,1)S(1)}, bf16[272,128]{1,0:T(8,128)(2,1)S(1)}, u32[]{:S(2)}, u32[]{:S(2)}) collective-permute-start(bf16[272,128]{1,0:T(8,128)(2,1)S(1)} %get-tuple-element.60), channel_id=1, source_target_pairs={{0,14},{1,15},{2,12},{3,13},{4,10},{5,11},{6,8},{7,9},{8,6},{9,7},... | collective-permute-start | bytes 208904 | tf_op jit(solution)/shard_map/ppermute | solution.py:683
  71.1 0.0 collective-permute-start.25
  71.1 0.0 collective-permute-done.21.refs_7_
  71.1 3.4 %collective-permute-start.26 = (bf16[272,128]{1,0:T(8,128)(2,1)S(1)}, bf16[272,128]{1,0:T(8,128)(2,1)S(1)}, u32[]{:S(2)}, u32[]{:S(2)}) collective-permute-start(bf16[272,128]{1,0:T(8,128)(2,1)S(1)} %get-tuple-element.62), channel_id=1, source_target_pairs={{0,15},{1,14},{2,13},{3,12},{4,11},{5,10},{6,9},{7,8},{8,7},{9,6},... | collective-permute-start | bytes 208904 | tf_op jit(solution)/shard_map/ppermute | solution.py:683
  74.5 0.9 %collective-permute-start.28 = (bf16[272,128]{1,0:T(8,128)(2,1)S(1)}, bf16[272,128]{1,0:T(8,128)(2,1)S(1)}, u32[]{:S(2)}, u32[]{:S(2)}) collective-permute-start(bf16[272,128]{1,0:T(8,128)(2,1)S(1)} %get-tuple-element.64), channel_id=1, source_target_pairs={{0,6},{1,7},{2,4},{3,5},{4,2},{5,3},{6,0},{7,1},{8,14},{9,15},{10,... | collective-permute-start | bytes 208904 | tf_op jit(solution)/shard_map/ppermute | solution.py:683
  75.4 0.0 collective-permute-done.24.refs_10_
  75.4 2.8 %collective-permute-start.29 = (bf16[272,128]{1,0:T(8,128)(2,1)S(1)}, bf16[272,128]{1,0:T(8,128)(2,1)S(1)}, u32[]{:S(2)}, u32[]{:S(2)}) collective-permute-start(bf16[272,128]{1,0:T(8,128)(2,1)S(1)} %get-tuple-element.65), channel_id=1, source_target_pairs={{0,7},{1,6},{2,5},{3,4},{4,3},{5,2},{6,1},{7,0},{8,15},{9,14},{10,... | collective-permute-start | bytes 208904 | tf_op jit(solution)/shard_map/ppermute | solution.py:683
  79.5 0.0 collective-permute-done.26.refs_12_
  79.5 0.2 collective-permute-done.27.refs_13_
  79.7 1.5 %collective-permute-done.28.refs_14_ = bf16[272,128]{1,0:T(8,128)(2,1)S(1)} collective-permute-done((bf16[272,128]{1,0:T(8,128)(2,1)S(1)}, bf16[272,128]{1,0:T(8,128)(2,1)S(1)}, u32[]{:S(2)}, u32[]{:S(2)}) %collective-permute-start.28) | collective-permute-done | bytes 69664 | tf_op jit(solution)/shard_map/ppermute | solution.py:683
  81.2 1.9 %collective-permute-done.29.refs_15_ = bf16[272,128]{1,0:T(8,128)(2,1)S(1)} collective-permute-done((bf16[272,128]{1,0:T(8,128)(2,1)S(1)}, bf16[272,128]{1,0:T(8,128)(2,1)S(1)}, u32[]{:S(2)}, u32[]{:S(2)}) %collective-permute-start.29) | collective-permute-done | bytes 69664 | tf_op jit(solution)/shard_map/ppermute | solution.py:683
  83.1 1.7 %direct_finish.1 = (bf16[128,4096]{1,0:T(8,128)(2,1)}, f32[2,1]{1,0:T(2,128)S(1)}) custom-call(s32[1]{0:T(128)} %bitcast.me_ref, s32[1]{0:T(128)S(6)} %copy.13.ref_ref, s32[1]{0:T(128)S(6)} %copy.14.alt_ref, bf16[3,128,4096]{2,1,0:T(8,128)(2,1)S(1)} %copy-done, bf16[272,128]{1,0:T(8,128)(2,1)S(1)} %get-tuple-element.50.refs_0_, ...), custom_call_target="tpu_custom_call" | custom-call | flops 524288 | bytes 3145728 | tf_op jit(solution)/shard_map/direct_finish/pallas_call | solution.py:642
  84.8 0.6 copy.12
  (18 shorter events, 0.0 us)
Async XLA Ops:
  0.6 38.6 %copy-start.3 = (bf16[1024,256]{1,0:T(8,128)(2,1)S(1)}, bf16[1024,256]{1,0:T(8,128)(2,1)}, u32[]{:S(2)}) copy-start(bf16[1024,256]{1,0:T(8,128)(2,1)} %constant.16.clone.forward_ref.refs_3_) | copy-start | bytes 1572868
  0.6 38.6 %copy-start.4 = (bf16[256,512]{1,0:T(8,128)(2,1)S(1)}, bf16[256,512]{1,0:T(8,128)(2,1)}, u32[]{:S(2)}) copy-start(bf16[256,512]{1,0:T(8,128)(2,1)} %refs_2_.1) | copy-start | bytes 786436
  0.7 38.6 %copy-start.6 = (bf16[512,512]{1,0:T(8,128)(2,1)S(1)}, bf16[512,512]{1,0:T(8,128)(2,1)}, u32[]{:S(2)}) copy-start(bf16[512,512]{1,0:T(8,128)(2,1)} %constant.17.clone.refs_4_) | copy-start | bytes 1572868
  4.5 8.5 %collective-permute-start = (bf16[272,128]{1,0:T(8,128)(2,1)}, bf16[272,128]{1,0:T(8,128)(2,1)S(1)}, u32[]{:S(2)}, u32[]{:S(2)}) collective-permute-start(bf16[272,128]{1,0:T(8,128)(2,1)} %get-tuple-element.35), channel_id=1, source_target_pairs={{0,8},{1,9},{2,10},{3,11},{4,12},{5,13},{6,14},{7,15},{8,0},{9,1},... | collective-permute-start | bytes 208904 | tf_op jit(solution)/shard_map/ppermute | solution.py:683
  7.8 12.1 %collective-permute-start.1 = (bf16[272,128]{1,0:T(8,128)(2,1)}, bf16[272,128]{1,0:T(8,128)(2,1)S(1)}, u32[]{:S(2)}, u32[]{:S(2)}) collective-permute-start(bf16[272,128]{1,0:T(8,128)(2,1)} %get-tuple-element.36), channel_id=1, source_target_pairs={{0,9},{1,8},{2,11},{3,10},{4,13},{5,12},{6,15},{7,14},{8,1},{9,0},... | collective-permute-start | bytes 208904 | tf_op jit(solution)/shard_map/ppermute | solution.py:683
  8.4 12.6 %collective-permute-start.10 = (bf16[272,128]{1,0:T(8,128)(2,1)}, bf16[272,128]{1,0:T(8,128)(2,1)S(1)}, u32[]{:S(2)}, u32[]{:S(2)}) collective-permute-start(bf16[272,128]{1,0:T(8,128)(2,1)} %get-tuple-element.45), channel_id=1, source_target_pairs={{0,10},{1,11},{2,8},{3,9},{4,14},{5,15},{6,12},{7,13},{8,2},{9,3},... | collective-permute-start | bytes 208904 | tf_op jit(solution)/shard_map/ppermute | solution.py:683
  11.9 12.4 %collective-permute-start.11 = (bf16[272,128]{1,0:T(8,128)(2,1)}, bf16[272,128]{1,0:T(8,128)(2,1)S(1)}, u32[]{:S(2)}, u32[]{:S(2)}) collective-permute-start(bf16[272,128]{1,0:T(8,128)(2,1)} %get-tuple-element.46), channel_id=1, source_target_pairs={{0,11},{1,10},{2,9},{3,8},{4,15},{5,14},{6,13},{7,12},{8,3},{9,2},... | collective-permute-start | bytes 208904 | tf_op jit(solution)/shard_map/ppermute | solution.py:683
  12.1 12.2 %collective-permute-start.12 = (bf16[272,128]{1,0:T(8,128)(2,1)}, bf16[272,128]{1,0:T(8,128)(2,1)S(1)}, u32[]{:S(2)}, u32[]{:S(2)}) collective-permute-start(bf16[272,128]{1,0:T(8,128)(2,1)} %get-tuple-element.47), channel_id=1, source_target_pairs={{0,1},{1,0},{2,3},{3,2},{4,5},{5,4},{6,7},{7,6},{8,9},{9,8},{10,11... | collective-permute-start | bytes 208904 | tf_op jit(solution)/shard_map/ppermute | solution.py:683
  13.1 14.4 %collective-permute-start.13 = (bf16[272,128]{1,0:T(8,128)(2,1)}, bf16[272,128]{1,0:T(8,128)(2,1)S(1)}, u32[]{:S(2)}, u32[]{:S(2)}) collective-permute-start(bf16[272,128]{1,0:T(8,128)(2,1)} %get-tuple-element.48), channel_id=1, source_target_pairs={{0,12},{1,13},{2,14},{3,15},{4,8},{5,9},{6,10},{7,11},{8,4},{9,5},... | collective-permute-start | bytes 208904 | tf_op jit(solution)/shard_map/ppermute | solution.py:683
  19.8 7.7 %collective-permute-start.14 = (bf16[272,128]{1,0:T(8,128)(2,1)}, bf16[272,128]{1,0:T(8,128)(2,1)S(1)}, u32[]{:S(2)}, u32[]{:S(2)}) collective-permute-start(bf16[272,128]{1,0:T(8,128)(2,1)} %get-tuple-element.49), channel_id=1, source_target_pairs={{0,2},{1,3},{2,0},{3,1},{4,6},{5,7},{6,4},{7,5},{8,10},{9,11},{10,... | collective-permute-start | bytes 208904 | tf_op jit(solution)/shard_map/ppermute | solution.py:683
  21.0 9.0 %collective-permute-start.2 = (bf16[272,128]{1,0:T(8,128)(2,1)}, bf16[272,128]{1,0:T(8,128)(2,1)S(1)}, u32[]{:S(2)}, u32[]{:S(2)}) collective-permute-start(bf16[272,128]{1,0:T(8,128)(2,1)} %get-tuple-element.37), channel_id=1, source_target_pairs={{0,13},{1,12},{2,15},{3,14},{4,9},{5,8},{6,11},{7,10},{8,5},{9,4},... | collective-permute-start | bytes 208904 | tf_op jit(solution)/shard_map/ppermute | solution.py:683
  24.3 5.9 %collective-permute-start.3 = (bf16[272,128]{1,0:T(8,128)(2,1)}, bf16[272,128]{1,0:T(8,128)(2,1)S(1)}, u32[]{:S(2)}, u32[]{:S(2)}) collective-permute-start(bf16[272,128]{1,0:T(8,128)(2,1)} %get-tuple-element.38), channel_id=1, source_target_pairs={{0,3},{1,2},{2,1},{3,0},{4,7},{5,6},{6,5},{7,4},{8,11},{9,10},{10,... | collective-permute-start | bytes 208904 | tf_op jit(solution)/shard_map/ppermute | solution.py:683
  24.4 7.7 %collective-permute-start.4 = (bf16[272,128]{1,0:T(8,128)(2,1)}, bf16[272,128]{1,0:T(8,128)(2,1)S(1)}, u32[]{:S(2)}, u32[]{:S(2)}) collective-permute-start(bf16[272,128]{1,0:T(8,128)(2,1)} %get-tuple-element.39), channel_id=1, source_target_pairs={{0,14},{1,15},{2,12},{3,13},{4,10},{5,11},{6,8},{7,9},{8,6},{9,7},... | collective-permute-start | bytes 208904 | tf_op jit(solution)/shard_map/ppermute | solution.py:683
  27.5 9.8 %collective-permute-start.5 = (bf16[272,128]{1,0:T(8,128)(2,1)}, bf16[272,128]{1,0:T(8,128)(2,1)S(1)}, u32[]{:S(2)}, u32[]{:S(2)}) collective-permute-start(bf16[272,128]{1,0:T(8,128)(2,1)} %get-tuple-element.40), channel_id=1, source_target_pairs={{0,4},{1,5},{2,6},{3,7},{4,0},{5,1},{6,2},{7,3},{8,12},{9,13},{10,... | collective-permute-start | bytes 208904 | tf_op jit(solution)/shard_map/ppermute | solution.py:683
  27.5 9.8 %collective-permute-start.6 = (bf16[272,128]{1,0:T(8,128)(2,1)}, bf16[272,128]{1,0:T(8,128)(2,1)S(1)}, u32[]{:S(2)}, u32[]{:S(2)}) collective-permute-start(bf16[272,128]{1,0:T(8,128)(2,1)} %get-tuple-element.41), channel_id=1, source_target_pairs={{0,15},{1,14},{2,13},{3,12},{4,11},{5,10},{6,9},{7,8},{8,7},{9,6},... | collective-permute-start | bytes 208904 | tf_op jit(solution)/shard_map/ppermute | solution.py:683
  30.0 7.3 %collective-permute-start.7 = (bf16[272,128]{1,0:T(8,128)(2,1)}, bf16[272,128]{1,0:T(8,128)(2,1)S(1)}, u32[]{:S(2)}, u32[]{:S(2)}) collective-permute-start(bf16[272,128]{1,0:T(8,128)(2,1)} %get-tuple-element.42), channel_id=1, source_target_pairs={{0,5},{1,4},{2,7},{3,6},{4,1},{5,0},{6,3},{7,2},{8,13},{9,12},{10,... | collective-permute-start | bytes 208904 | tf_op jit(solution)/shard_map/ppermute | solution.py:683
  30.2 7.6 %collective-permute-start.8 = (bf16[272,128]{1,0:T(8,128)(2,1)}, bf16[272,128]{1,0:T(8,128)(2,1)S(1)}, u32[]{:S(2)}, u32[]{:S(2)}) collective-permute-start(bf16[272,128]{1,0:T(8,128)(2,1)} %get-tuple-element.43), channel_id=1, source_target_pairs={{0,6},{1,7},{2,4},{3,5},{4,2},{5,3},{6,0},{7,1},{8,14},{9,15},{10,... | collective-permute-start | bytes 208904 | tf_op jit(solution)/shard_map/ppermute | solution.py:683
  32.1 7.2 %collective-permute-start.9 = (bf16[272,128]{1,0:T(8,128)(2,1)}, bf16[272,128]{1,0:T(8,128)(2,1)S(1)}, u32[]{:S(2)}, u32[]{:S(2)}) collective-permute-start(bf16[272,128]{1,0:T(8,128)(2,1)} %get-tuple-element.44), channel_id=1, source_target_pairs={{0,7},{1,6},{2,5},{3,4},{4,3},{5,2},{6,1},{7,0},{8,15},{9,14},{10,... | collective-permute-start | bytes 208904 | tf_op jit(solution)/shard_map/ppermute | solution.py:683
  33.8 1.2 %copy-start.1 = (bf16[256,2048]{1,0:T(8,128)(2,1)S(1)}, bf16[256,2048]{1,0:T(8,128)(2,1)}, u32[]{:S(2)}) copy-start(bf16[256,2048]{1,0:T(8,128)(2,1)} %filter_ref.1) | copy-start | bytes 3145732
  35.0 1.0 %copy-start.2 = (bf16[1024,256]{1,0:T(8,128)(2,1)S(1)}, bf16[1024,256]{1,0:T(8,128)(2,1)}, u32[]{:S(2)}) copy-start(bf16[1024,256]{1,0:T(8,128)(2,1)} %constant.16.clone.forward_ref.refs_3_) | copy-start | bytes 1572868
  36.0 3.2 %copy-start.5 = (bf16[272,128]{1,0:T(8,128)(2,1)S(1)}, bf16[272,128]{1,0:T(8,128)(2,1)}, u32[]{:S(2)}) copy-start(bf16[272,128]{1,0:T(8,128)(2,1)} %get-tuple-element.34.refs_6_) | copy-start | bytes 208900
  39.3 43.8 %copy-start = (bf16[3,128,4096]{2,1,0:T(8,128)(2,1)S(1)}, bf16[3,128,4096]{2,1,0:T(8,128)(2,1)}, u32[]{:S(2)}) copy-start(bf16[3,128,4096]{2,1,0:T(8,128)(2,1)} %streams_ref.3) | copy-start | bytes 9437188
  52.1 10.8 %collective-permute-start.15 = (bf16[272,128]{1,0:T(8,128)(2,1)S(1)}, bf16[272,128]{1,0:T(8,128)(2,1)S(1)}, u32[]{:S(2)}, u32[]{:S(2)}) collective-permute-start(bf16[272,128]{1,0:T(8,128)(2,1)S(1)} %get-tuple-element.51), channel_id=1, source_target_pairs={{0,8},{1,9},{2,10},{3,11},{4,12},{5,13},{6,14},{7,15},{8,0},{9,1},... | collective-permute-start | bytes 208904 | tf_op jit(solution)/shard_map/ppermute | solution.py:683
  52.6 12.4 %collective-permute-start.16 = (bf16[272,128]{1,0:T(8,128)(2,1)S(1)}, bf16[272,128]{1,0:T(8,128)(2,1)S(1)}, u32[]{:S(2)}, u32[]{:S(2)}) collective-permute-start(bf16[272,128]{1,0:T(8,128)(2,1)S(1)} %get-tuple-element.52), channel_id=1, source_target_pairs={{0,9},{1,8},{2,11},{3,10},{4,13},{5,12},{6,15},{7,14},{8,1},{9,0},... | collective-permute-start | bytes 208904 | tf_op jit(solution)/shard_map/ppermute | solution.py:683
  55.1 11.0 %collective-permute-start.17 = (bf16[272,128]{1,0:T(8,128)(2,1)S(1)}, bf16[272,128]{1,0:T(8,128)(2,1)S(1)}, u32[]{:S(2)}, u32[]{:S(2)}) collective-permute-start(bf16[272,128]{1,0:T(8,128)(2,1)S(1)} %get-tuple-element.53), channel_id=1, source_target_pairs={{0,10},{1,11},{2,8},{3,9},{4,14},{5,15},{6,12},{7,13},{8,2},{9,3},... | collective-permute-start | bytes 208904 | tf_op jit(solution)/shard_map/ppermute | solution.py:683
  55.7 12.5 %collective-permute-start.18 = (bf16[272,128]{1,0:T(8,128)(2,1)S(1)}, bf16[272,128]{1,0:T(8,128)(2,1)S(1)}, u32[]{:S(2)}, u32[]{:S(2)}) collective-permute-start(bf16[272,128]{1,0:T(8,128)(2,1)S(1)} %get-tuple-element.54), channel_id=1, source_target_pairs={{0,11},{1,10},{2,9},{3,8},{4,15},{5,14},{6,13},{7,12},{8,3},{9,2},... | collective-permute-start | bytes 208904 | tf_op jit(solution)/shard_map/ppermute | solution.py:683
  58.4 10.5 %collective-permute-start.19 = (bf16[272,128]{1,0:T(8,128)(2,1)S(1)}, bf16[272,128]{1,0:T(8,128)(2,1)S(1)}, u32[]{:S(2)}, u32[]{:S(2)}) collective-permute-start(bf16[272,128]{1,0:T(8,128)(2,1)S(1)} %get-tuple-element.55), channel_id=1, source_target_pairs={{0,1},{1,0},{2,3},{3,2},{4,5},{5,4},{6,7},{7,6},{8,9},{9,8},{10,11... | collective-permute-start | bytes 208904 | tf_op jit(solution)/shard_map/ppermute | solution.py:683
  62.9 8.2 %collective-permute-start.20 = (bf16[272,128]{1,0:T(8,128)(2,1)S(1)}, bf16[272,128]{1,0:T(8,128)(2,1)S(1)}, u32[]{:S(2)}, u32[]{:S(2)}) collective-permute-start(bf16[272,128]{1,0:T(8,128)(2,1)S(1)} %get-tuple-element.56), channel_id=1, source_target_pairs={{0,12},{1,13},{2,14},{3,15},{4,8},{5,9},{6,10},{7,11},{8,4},{9,5},... | collective-permute-start | bytes 208904 | tf_op jit(solution)/shard_map/ppermute | solution.py:683
  65.0 6.0 %collective-permute-start.21 = (bf16[272,128]{1,0:T(8,128)(2,1)S(1)}, bf16[272,128]{1,0:T(8,128)(2,1)S(1)}, u32[]{:S(2)}, u32[]{:S(2)}) collective-permute-start(bf16[272,128]{1,0:T(8,128)(2,1)S(1)} %get-tuple-element.57), channel_id=1, source_target_pairs={{0,2},{1,3},{2,0},{3,1},{4,6},{5,7},{6,4},{7,5},{8,10},{9,11},{10,... | collective-permute-start | bytes 208904 | tf_op jit(solution)/shard_map/ppermute | solution.py:683
  66.1 8.4 %collective-permute-start.22 = (bf16[272,128]{1,0:T(8,128)(2,1)S(1)}, bf16[272,128]{1,0:T(8,128)(2,1)S(1)}, u32[]{:S(2)}, u32[]{:S(2)}) collective-permute-start(bf16[272,128]{1,0:T(8,128)(2,1)S(1)} %get-tuple-element.58), channel_id=1, source_target_pairs={{0,13},{1,12},{2,15},{3,14},{4,9},{5,8},{6,11},{7,10},{8,5},{9,4},... | collective-permute-start | bytes 208904 | tf_op jit(solution)/shard_map/ppermute | solution.py:683
  68.2 6.3 %collective-permute-start.23 = (bf16[272,128]{1,0:T(8,128)(2,1)S(1)}, bf16[272,128]{1,0:T(8,128)(2,1)S(1)}, u32[]{:S(2)}, u32[]{:S(2)}) collective-permute-start(bf16[272,128]{1,0:T(8,128)(2,1)S(1)} %get-tuple-element.59), channel_id=1, source_target_pairs={{0,3},{1,2},{2,1},{3,0},{4,7},{5,6},{6,5},{7,4},{8,11},{9,10},{10,... | collective-permute-start | bytes 208904 | tf_op jit(solution)/shard_map/ppermute | solution.py:683
  68.9 6.5 %collective-permute-start.24 = (bf16[272,128]{1,0:T(8,128)(2,1)S(1)}, bf16[272,128]{1,0:T(8,128)(2,1)S(1)}, u32[]{:S(2)}, u32[]{:S(2)}) collective-permute-start(bf16[272,128]{1,0:T(8,128)(2,1)S(1)} %get-tuple-element.60), channel_id=1, source_target_pairs={{0,14},{1,15},{2,12},{3,13},{4,10},{5,11},{6,8},{7,9},{8,6},{9,7},... | collective-permute-start | bytes 208904 | tf_op jit(solution)/shard_map/ppermute | solution.py:683
  71.1 8.4 %collective-permute-start.25 = (bf16[272,128]{1,0:T(8,128)(2,1)S(1)}, bf16[272,128]{1,0:T(8,128)(2,1)S(1)}, u32[]{:S(2)}, u32[]{:S(2)}) collective-permute-start(bf16[272,128]{1,0:T(8,128)(2,1)S(1)} %get-tuple-element.61), channel_id=1, source_target_pairs={{0,4},{1,5},{2,6},{3,7},{4,0},{5,1},{6,2},{7,3},{8,12},{9,13},{10,... | collective-permute-start | bytes 208904 | tf_op jit(solution)/shard_map/ppermute | solution.py:683
  71.1 8.4 %collective-permute-start.26 = (bf16[272,128]{1,0:T(8,128)(2,1)S(1)}, bf16[272,128]{1,0:T(8,128)(2,1)S(1)}, u32[]{:S(2)}, u32[]{:S(2)}) collective-permute-start(bf16[272,128]{1,0:T(8,128)(2,1)S(1)} %get-tuple-element.62), channel_id=1, source_target_pairs={{0,15},{1,14},{2,13},{3,12},{4,11},{5,10},{6,9},{7,8},{8,7},{9,6},... | collective-permute-start | bytes 208904 | tf_op jit(solution)/shard_map/ppermute | solution.py:683
  74.5 5.2 %collective-permute-start.27 = (bf16[272,128]{1,0:T(8,128)(2,1)S(1)}, bf16[272,128]{1,0:T(8,128)(2,1)S(1)}, u32[]{:S(2)}, u32[]{:S(2)}) collective-permute-start(bf16[272,128]{1,0:T(8,128)(2,1)S(1)} %get-tuple-element.63), channel_id=1, source_target_pairs={{0,5},{1,4},{2,7},{3,6},{4,1},{5,0},{6,3},{7,2},{8,13},{9,12},{10,... | collective-permute-start | bytes 208904 | tf_op jit(solution)/shard_map/ppermute | solution.py:683
  74.5 6.7 %collective-permute-start.28 = (bf16[272,128]{1,0:T(8,128)(2,1)S(1)}, bf16[272,128]{1,0:T(8,128)(2,1)S(1)}, u32[]{:S(2)}, u32[]{:S(2)}) collective-permute-start(bf16[272,128]{1,0:T(8,128)(2,1)S(1)} %get-tuple-element.64), channel_id=1, source_target_pairs={{0,6},{1,7},{2,4},{3,5},{4,2},{5,3},{6,0},{7,1},{8,14},{9,15},{10,... | collective-permute-start | bytes 208904 | tf_op jit(solution)/shard_map/ppermute | solution.py:683
  75.4 7.7 %collective-permute-start.29 = (bf16[272,128]{1,0:T(8,128)(2,1)S(1)}, bf16[272,128]{1,0:T(8,128)(2,1)S(1)}, u32[]{:S(2)}, u32[]{:S(2)}) collective-permute-start(bf16[272,128]{1,0:T(8,128)(2,1)S(1)} %get-tuple-element.65), channel_id=1, source_target_pairs={{0,7},{1,6},{2,5},{3,4},{4,3},{5,2},{6,1},{7,0},{8,15},{9,14},{10,... | collective-permute-start | bytes 208904 | tf_op jit(solution)/shard_map/ppermute | solution.py:683

commit v4 on v3

--- a/solution.py
+++ b/solution.py
@@ -100,7 +100,8 @@
     )(local_rows, streams)
 
 
-def spectrum_kernel(block, filter_ref, forward_ref, out_ref):
+def spectrum_kernel(block, filter_ref, forward_ref, *refs):
+    out_ref = refs[-1]
     n_blocks = out_ref.shape[0]
     for index in range(n_blocks):
         taps = filter_ref[:, index * block : (index + 1) * block]
@@ -110,12 +111,12 @@
         out_ref[index] = both[: 2 * block] + both[2 * block :]
 
 
-def filter_spectrum(taps, forward, block):
+def filter_spectrum(taps, forward, block, *earlier):
     width, length = taps.shape
     n_blocks = length // block
     return pl.pallas_call(
         functools.partial(spectrum_kernel, block),
-        in_specs=[whole_spec(), whole_spec()],
+        in_specs=[whole_spec(), whole_spec()] + [pl.BlockSpec(memory_space=pl.ANY)] * len(earlier),
         out_specs=whole_spec(),
         out_shape=jax.ShapeDtypeStruct((n_blocks, 2 * block, width), f32),
         compiler_params=pltpu.CompilerParams(vmem_limit_bytes=40 * MIB),
@@ -123,7 +124,7 @@
             flops=8 * block * length * width, bytes_accessed=4 * MIB, transcendentals=0
         ),
         name="filter_spectrum",
-    )(taps, forward)
+    )(taps, forward, *earlier)
 
 
 def multiply_points(points, spectrum_ref, joint):
@@ -382,18 +383,18 @@
         name="finish",
     )(ref_ids, alt_ids, streams, *backs)
 
-def send_products_kernel(halves, vars_dev, me_ref, offsets_ref, streams_ref, *refs):
-    built, pairs, gates, pair_sems, gate_sems, out_sems = refs[-6:]
-    out_refs = refs[:-6]
+def send_products_kernel(halves, vars_dev, me_ref, offsets_ref, streams_ref, out_ref, *scratch):
+    built, pairs, gates, gate_rows, pair_sems, gate_sems, out_sems = scratch
     n_devices, _, tok_rows, width = pairs.shape
     me = me_ref[0]
     slot = tok_rows // vars_dev
     local_rows = [var * slot + offsets_ref[me * vars_dev + var] for var in range(vars_dev)]
 
-    def pair_copy(step):
-        start = pl.multiple_of((me ^ step) * width, lane_tile)
+    def pair_copy(owner):
         return pltpu.make_async_copy(
-            streams_ref.at[pl.ds(1, 2), :, pl.ds(start, width)], pairs.at[step], pair_sems.at[step]
+            streams_ref.at[pl.ds(1, 2), :, pl.ds(owner * width, width)],
+            pairs.at[owner],
+            pair_sems.at[owner],
         )
 
     def gate_copy(var):
@@ -402,35 +403,35 @@
             streams_ref.at[0, pl.ds(start, row_tile), :], gates.at[var], gate_sems.at[var]
         )
 
-    def out_copy(step):
-        return pltpu.make_async_copy(built.at[step], out_refs[step], out_sems.at[step])
+    def out_copy(owner):
+        return pltpu.make_async_copy(built.at[owner], out_ref.at[owner], out_sems.at[owner])
 
     for var in range(vars_dev):
         gate_copy(var).start()
-    for step in range(n_devices):
-        pair_copy(step).start()
+    for owner in range(n_devices):
+        pair_copy(owner).start()
+    row = lax.broadcasted_iota(jnp.int32, gates.shape[1:], 0)
     for var in range(vars_dev):
         gate_copy(var).wait()
+        mine = jnp.where(row == local_rows[var] % row_tile, gates[var].astype(f32), 0.0)
+        gate_rows[var : var + 1, :] = jnp.sum(mine, axis=0, keepdims=True)
     extra = built.shape[1] - halves * tok_rows
-    row = lax.broadcasted_iota(jnp.int32, (row_tile, lane_tile), 0)
     place = lax.broadcasted_iota(jnp.int32, (extra, lane_tile), 0)
-    for step in range(n_devices):
-        pair_copy(step).wait()
+    for owner in range(n_devices):
+        pair_copy(owner).wait()
         tail = jnp.zeros((extra, lane_tile), f32)
         for half in range(halves):
             lanes = slice(half * lane_tile, (half + 1) * lane_tile)
             rows = slice(half * tok_rows, (half + 1) * tok_rows)
-            built[step, rows, :] = pairs[step, 0, :, lanes] * pairs[step, 1, :, lanes]
-            start = pl.multiple_of((me ^ step) * width + half * lane_tile, lane_tile)
+            built[owner, rows, :] = pairs[owner, 0, :, lanes] * pairs[owner, 1, :, lanes]
+            start = owner * width + half * lane_tile
             for var in range(vars_dev):
-                tile = gates[var, :, pl.ds(start, lane_tile)].astype(f32)
-                mine = jnp.where(row == local_rows[var] % row_tile, tile, 0.0)
-                mine = jnp.sum(mine, axis=0, keepdims=True)
+                mine = gate_rows[var : var + 1, start : start + lane_tile]
                 tail = jnp.where(place == half * vars_dev + var, mine, tail)
-        built[step, halves * tok_rows :, :] = tail.astype(bf16)
-        out_copy(step).start()
-    for step in range(n_devices):
-        out_copy(step).wait()
+        built[owner, halves * tok_rows :, :] = tail.astype(bf16)
+        out_copy(owner).start()
+    for owner in range(n_devices):
+        out_copy(owner).wait()
 
 
 def send_products(me, offsets, streams, vars_dev, n_devices, extra):
@@ -445,12 +446,13 @@
             pl.BlockSpec(memory_space=pltpu.SMEM),
             pl.BlockSpec(memory_space=pl.ANY),
         ],
-        out_specs=[pl.BlockSpec(memory_space=pl.ANY)] * n_devices,
-        out_shape=[jax.ShapeDtypeStruct((rows_out, lane_tile), bf16)] * n_devices,
+        out_specs=pl.BlockSpec(memory_space=pl.ANY),
+        out_shape=jax.ShapeDtypeStruct((n_devices, rows_out, lane_tile), bf16),
         scratch_shapes=[
             pltpu.VMEM((n_devices, rows_out, lane_tile), bf16),
             pltpu.VMEM((n_devices, 2, tok_rows, width), bf16),
             pltpu.VMEM((vars_dev, row_tile, model_width), bf16),
+            pltpu.VMEM((round_up(vars_dev, half_tile), model_width), f32),
             pltpu.SemaphoreType.DMA((n_devices,)),
             pltpu.SemaphoreType.DMA((vars_dev,)),
             pltpu.SemaphoreType.DMA((n_devices,)),
@@ -463,36 +465,11 @@
     )(me, offsets, streams)
 
 
-def direct_filter_kernel(steps, vars_dev, halves, tok_rows, me_ref, *refs):
-    positions_ref, gain_ref, unembed_ref, forward_ref, inverse_hbm, spectrum_hbm = refs[:6]
-    points, joint, arrived, leaving, packed, spectrum, inverse = refs[-12:-5]
-    in_sems, out_sems, tail_sems, spectrum_sem, inverse_sem = refs[-5:]
+def stacked_filter_kernel(vars_dev, halves, tok_rows, *refs):
+    positions_ref, gain_ref, unembed_ref, forward_ref, inverse_ref, spectrum_ref = refs[:6]
+    arrived, leaving, points, joint, packed = refs[6:]
     n_devices = arrived.shape[0]
-    in_refs = refs[6 : 6 + n_devices]
-    out_refs = refs[6 + n_devices : 6 + 2 * n_devices]
-    me = me_ref[0]
     body = halves * tok_rows
-
-    def in_copy(index):
-        return pltpu.make_async_copy(
-            in_refs[index], arrived.at[me ^ steps[index]], in_sems.at[index]
-        )
-
-    def out_copy(step, start, size, sems):
-        rows = pl.ds(start, size)
-        return pltpu.make_async_copy(
-            leaving.at[me ^ step, rows], out_refs[step].at[rows], sems.at[step]
-        )
-
-    spectrum_copy = pltpu.make_async_copy(spectrum_hbm, spectrum, spectrum_sem.at[0])
-    inverse_copy = pltpu.make_async_copy(inverse_hbm, inverse, inverse_sem.at[0])
-    for index in range(n_devices):
-        in_copy(index).start()
-    spectrum_copy.start()
-    inverse_copy.start()
-    for index in range(n_devices):
-        in_copy(index).wait()
-
     n_blocks, double, width = points.shape
     block = double // 2
     per_block = block // tok_rows
@@ -509,14 +486,12 @@
         return carry
 
     lax.fori_loop(0, n_blocks, forward_step, 0)
-    spectrum_copy.wait()
-    multiply_points(points, spectrum, joint)
-    inverse_copy.wait()
+    multiply_points(points, spectrum_ref, joint)
 
     def inverse_step(step, carry):
         highs, lows = split_bf16(joint[step])
-        both = jnp.dot(inverse[...], highs, preferred_element_type=f32)
-        rest = jnp.dot(inverse[:block, :], lows, preferred_element_type=f32)
+        both = jnp.dot(inverse_ref[...], highs, preferred_element_type=f32)
+        rest = jnp.dot(inverse_ref[:block, :], lows, preferred_element_type=f32)
         result = (both[:block] + both[block:] + rest).astype(bf16)
         for member in range(per_block):
             for half in range(halves):
@@ -527,8 +502,6 @@
         return carry
 
     lax.fori_loop(0, n_blocks, inverse_step, 0)
-    for step in range(n_devices):
-        out_copy(step, 0, body, out_sems).start()
 
     length = n_devices * tok_rows
     column = lax.broadcasted_iota(jnp.int32, (positions_ref.shape[0], length), 1)
@@ -554,96 +527,71 @@
     pack_scores(raw, squares, vars_dev, packed, n_devices)
     extra = packed.shape[0] // n_devices
     leaving[:, body:, :] = packed[...].reshape(n_devices, extra, lane_tile).astype(bf16)
-    for step in range(n_devices):
-        out_copy(step, body, extra, tail_sems).start()
-    for step in range(n_devices):
-        out_copy(step, 0, body, out_sems).wait()
-        out_copy(step, body, extra, tail_sems).wait()
-
-
-def direct_filter(me, operands, steps, arrivals, vars_dev, tok_rows, extra):
-    n_devices = len(arrivals)
-    forward, inverse, spectrum = operands[3:]
-    n_blocks, double, width = spectrum.shape
+
+
+def stacked_filter(operands, arrived, vars_dev, tok_rows, extra):
+    n_devices = arrived.shape[0]
+    n_blocks, double, width = operands[-1].shape
     halves = width // lane_tile
     rows_out = halves * tok_rows + extra
     flops = 2 * width * n_blocks * (double * double * 5 // 2 + 4 * n_blocks * double)
-    anywhere = pl.BlockSpec(memory_space=pl.ANY)
     return pl.pallas_call(
-        functools.partial(direct_filter_kernel, steps, vars_dev, halves, tok_rows),
-        in_specs=[pl.BlockSpec(memory_space=pltpu.SMEM)]
-        + [whole_spec()] * 4
-        + [anywhere] * (2 + n_devices),
-        out_specs=[anywhere] * n_devices,
-        out_shape=[jax.ShapeDtypeStruct((rows_out, lane_tile), bf16)] * n_devices,
+        functools.partial(stacked_filter_kernel, vars_dev, halves, tok_rows),
+        in_specs=[whole_spec()] * (len(operands) + 1),
+        out_specs=whole_spec(),
+        out_shape=jax.ShapeDtypeStruct((n_devices, rows_out, lane_tile), bf16),
         scratch_shapes=[
             pltpu.VMEM((n_blocks, double, width), f32),
             pltpu.VMEM((n_blocks, double, width), f32),
-            pltpu.VMEM((n_devices,) + arrivals[0].shape, bf16),
-            pltpu.VMEM((n_devices, rows_out, lane_tile), bf16),
             pltpu.VMEM((n_devices * extra, lane_tile), f32),
-            pltpu.VMEM(spectrum.shape, f32),
-            pltpu.VMEM(inverse.shape, bf16),
-            pltpu.SemaphoreType.DMA((n_devices,)),
-            pltpu.SemaphoreType.DMA((n_devices,)),
-            pltpu.SemaphoreType.DMA((n_devices,)),
-            pltpu.SemaphoreType.DMA((1,)),
-            pltpu.SemaphoreType.DMA((1,)),
         ],
         compiler_params=pltpu.CompilerParams(vmem_limit_bytes=32 * MIB),
         cost_estimate=pl.CostEstimate(flops=flops, bytes_accessed=8 * MIB, transcendentals=0),
-        name="direct_filter",
-    )(me, *operands, *arrivals)
-
-
-def direct_finish_kernel(steps, halves, vars_dev, vocab, me_ref, ref_ref, alt_ref, streams_ref, *refs):
-    gates, results, gate_sems, out_sems = refs[-4:]
+        name="stacked_filter",
+    )(*operands, arrived)
+
+
+def stacked_finish_kernel(halves, vars_dev, vocab, ref_ref, alt_ref, streams_ref, back_ref, *refs):
+    mixed_ref, scores_ref, gates, results, gate_sems, out_sems = refs
     n_devices, tok_rows, width = gates.shape
-    mixed_ref, scores_ref = refs[-6:-4]
-    me = me_ref[0]
-
-    def lanes_of(index):
-        return pl.ds(pl.multiple_of((me ^ steps[index]) * width, lane_tile), width)
-
-    def gate_copy(step):
+
+    def gate_copy(owner):
         return pltpu.make_async_copy(
-            streams_ref.at[0, :, lanes_of(step)], gates.at[step], gate_sems.at[step]
+            streams_ref.at[0, :, pl.ds(owner * width, width)], gates.at[owner], gate_sems.at[owner]
         )
 
-    def out_copy(step):
+    def out_copy(owner):
         return pltpu.make_async_copy(
-            results.at[step], mixed_ref.at[:, lanes_of(step)], out_sems.at[step]
+            results.at[owner], mixed_ref.at[:, pl.ds(owner * width, width)], out_sems.at[owner]
         )
 
-    for step in range(n_devices):
-        gate_copy(step).start()
+    for owner in range(n_devices):
+        gate_copy(owner).start()
     sums = None
-    for step in range(n_devices):
-        gate_copy(step).wait()
-        block_ref = refs[step]
+    for owner in range(n_devices):
+        gate_copy(owner).wait()
         for half in range(halves):
             lanes = slice(half * lane_tile, (half + 1) * lane_tile)
-            filtered = block_ref[half * tok_rows : (half + 1) * tok_rows, :]
-            results[step, :, lanes] = gates[step, :, lanes] * filtered
-        out_copy(step).start()
-        tail = block_ref[halves * tok_rows :, :].astype(f32)
+            filtered = back_ref[owner, half * tok_rows : (half + 1) * tok_rows, :]
+            results[owner, :, lanes] = gates[owner, :, lanes] * filtered
+        out_copy(owner).start()
+        tail = back_ref[owner, halves * tok_rows :, :].astype(f32)
         sums = tail if sums is None else sums + tail
     model_width = n_devices * width
     scores_ref[...] = final_scores(sums, vars_dev, vocab, model_width, ref_ref, alt_ref)
-    for step in range(n_devices):
-        out_copy(step).wait()
-
-
-def direct_finish(me, ref_ids, alt_ids, streams, steps, backs, vocab):
+    for owner in range(n_devices):
+        out_copy(owner).wait()
+
+
+def stacked_finish(ref_ids, alt_ids, streams, back, vocab):
     _, tok_rows, model_width = streams.shape
-    n_devices = len(backs)
+    n_devices = back.shape[0]
     vars_dev = ref_ids.shape[0]
     width = model_width // n_devices
     return pl.pallas_call(
-        functools.partial(direct_finish_kernel, steps, width // lane_tile, vars_dev, vocab),
-        in_specs=[pl.BlockSpec(memory_space=pltpu.SMEM)] * 3
-        + [pl.BlockSpec(memory_space=pl.ANY)]
-        + [whole_spec()] * len(backs),
+        functools.partial(stacked_finish_kernel, width // lane_tile, vars_dev, vocab),
+        in_specs=[pl.BlockSpec(memory_space=pltpu.SMEM)] * 2
+        + [pl.BlockSpec(memory_space=pl.ANY), whole_spec()],
         out_specs=[pl.BlockSpec(memory_space=pl.ANY), whole_spec()],
         out_shape=[
             jax.ShapeDtypeStruct((tok_rows, model_width), bf16),
@@ -659,29 +607,12 @@
         cost_estimate=pl.CostEstimate(
             flops=tok_rows * model_width, bytes_accessed=6 * tok_rows * model_width, transcendentals=0
         ),
-        name="direct_finish",
-    )(me, ref_ids, alt_ids, streams, *backs)
-
-
-def partner_order(n_devices):
-    half = n_devices // 2
-    far, near = list(range(half, n_devices)), list(range(1, half))
-    lead = len(far) // 2
-    order = far[:lead]
-    rest = far[lead:]
-    while rest or near:
-        order += near[:1] + rest[:1]
-        rest, near = rest[1:], near[1:]
-    return order
-
-
-def exchange(parts, order):
-    n_devices = len(parts)
-    moved = {0: parts[0]}
-    for step in order:
-        pairs = [(device, device ^ step) for device in range(n_devices)]
-        moved[step] = lax.ppermute(parts[step], "seq", pairs)
-    return moved
+        name="stacked_finish",
+    )(ref_ids, alt_ids, streams, back)
+
+
+def transposed(blocks):
+    return lax.all_to_all(blocks, "seq", split_axis=0, concat_axis=0, tiled=True)
 
 
 def shards(streams, long_filter, gain, unembed, offsets, ref_ids, alt_ids):
@@ -706,23 +637,16 @@
     positions = positions.T.reshape(n_devices * vars_dev, 1)
     my_gain = lax.dynamic_slice_in_dim(gain, my_index * group_width, group_width).astype(f32)
 
-    if chunks * lane_tile == group_width and n_devices & (n_devices - 1) == 0:
+    if chunks * lane_tile == group_width:
         me = jnp.reshape(my_index, (1,)).astype(jnp.int32)
         gate_extra = round_up(chunks * vars_dev, row_tile)
         score_extra = round_up(vars_dev * 2 * (vocab // lane_tile + 1), row_tile)
-        parts = send_products(me, offsets, streams, vars_dev, n_devices, gate_extra)
-        order = partner_order(n_devices)
-        slots = sorted(range(len(order)), key=str)
-        steps = [0] + [order[slots.index(place)] for place in range(len(order))]
-        moved = exchange(parts, steps[1:])
-        spectrum = filter_spectrum(long_filter, forward, block)
+        blocks = send_products(me, offsets, streams, vars_dev, n_devices, gate_extra)
+        arrived = transposed(blocks)
+        spectrum = filter_spectrum(long_filter, forward, block, blocks)
         operands = (positions, my_gain[None, :], unembed, forward, inverse, spectrum)
-        arrivals = [moved[step] for step in steps]
-        leaving = direct_filter(me, operands, steps, arrivals, vars_dev, tok_rows, score_extra)
-        steps = [0] + order
-        returned = exchange(leaving, order)
-        backs = [returned[step] for step in steps]
-        mixed, scores = direct_finish(me, ref_ids, alt_ids, streams, steps, backs, vocab)
+        leaving = stacked_filter(operands, arrived, vars_dev, tok_rows, score_extra)
+        mixed, scores = stacked_finish(ref_ids, alt_ids, streams, transposed(leaving), vocab)
         return (mixed, scores)
 
     gate_extra = round_up(chunks * vars_dev, row_tile)

time: 85.7 us -> 89 us (1.039)
  the two profiles are of different devices: /device:TPU:1 before, /device:TPU:13 now
where the time goes in v4:
time: 89 us; the launch traced here: 88.3 us
  waiting for transfers between devices  46.1 us (52%)
  Pallas kernels  16.5 us (19%)
  starting transfers between devices  11.7 us (13%)
  local copies, waits for them, and re-layouts  11.2 us (13%)
  between operations  2.02 us (2%)
    all_to_all x2, waiting for transfers between devices, transposed(): lax.all_to_all(blocks, 'seq', split_axis=0, concat_axis=0, tiled=True)  46.1 us
    all_to_all x2, starting transfers between devices, transposed(): lax.all_to_all(blocks, 'seq', split_axis=0, concat_axis=0, tiled=True)  11.7 us
    unnamed x26, local copies, waits for them, and re-layouts  10.5 us
    pallas_call x1, Pallas kernels, stacked_filter(): pl.pallas_call(functools.partial(stacked_filter_kernel, vars_dev, halves,...  8.71 us
    pallas_call x1, Pallas kernels, send_products(): pl.pallas_call(functools.partial(send_products_kernel, halves, vars_dev),...  3.7 us
    pallas_call x1, Pallas kernels, stacked_finish(): pl.pallas_call(functools.partial(stacked_finish_kernel, width // lane_til...  2.81 us
  transfers between devices with their start and end apart: 2, of which 2 were waited for; matrix products, arithmetic and copies ran while one was open for 1% of the time, Pallas kernels for 1%

profile of v4, /device:TPU:13, one launch (start us, length us, event | category | flops | bytes accessed | tf_op | source)
XLA Modules:
  0.0 88.3 jit_solution(121383221491303532)
XLA Ops:
  0.6 3.7 %send_products.1.refs_0_ = bf16[16,272,128]{2,1,0:T(8,128)(2,1)} custom-call(s32[1]{0:T(128)} %bitcast.2.me_ref, s32[16]{0:T(128)} %offsets_ref.1, bf16[3,128,4096]{2,1,0:T(8,128)(2,1)} %streams_ref.3), custom_call_target="tpu_custom_call" | custom-call | flops 524288 | bytes 3145728 | tf_op jit(solution)/shard_map/send_products/pallas_call | solution.py:442
  4.3 0.0 copy-start.12
  4.4 0.0 copy-start.1
  4.4 0.0 copy-start.7
  4.4 6.7 %all-to-all-start = ((bf16[16,272,128]{2,1,0:T(8,128)(2,1)}), bf16[16,272,128]{2,1,0:T(8,128)(2,1)S(1)}, u32[]{:S(2)}, u32[]{:S(2)}) async-start(bf16[16,272,128]{2,1,0:T(8,128)(2,1)} %send_products.1.refs_0_), calls=%async_computation | async-start | bytes 2228224 | tf_op jit(solution)/shard_map/all_to_all | solution.py:615
  11.1 0.0 copy-done.12
  11.1 0.1 copy.11.refs_0_
  11.2 0.0 copy-done.1
  11.2 0.0 copy-done.7
  11.2 0.0 copy-start.8
  11.2 1.0 %copy-done.8 = bf16[1024,256]{1,0:T(8,128)(2,1)S(1)} copy-done((bf16[1024,256]{1,0:T(8,128)(2,1)S(1)}, bf16[1024,256]{1,0:T(8,128)(2,1)}, u32[]{:S(2)}) %copy-start.8) | copy-done | bytes 524312
  12.3 0.0 copy-start.10
  12.3 1.3 %filter_spectrum.1.refs_5_ = f32[8,512,256]{2,1,0:T(8,128)S(1)} custom-call(bf16[256,2048]{1,0:T(8,128)(2,1)S(1)} %copy-done.7, bf16[1024,256]{1,0:T(8,128)(2,1)S(1)} %copy-done.8, bf16[16,272,128]{2,1,0:T(8,128)(2,1)S(1)} %copy-done.1), custom_call_target="tpu_custom_call" | custom-call | flops 1073741824 | bytes 4194304 | tf_op jit(solution)/shard_map/filter_spectrum/pallas_call | solution.py:117
  13.5 0.0 copy-start.2
  13.6 2.0 %copy-done.2 = f32[8,512,256]{2,1,0:T(8,128)} copy-done((f32[8,512,256]{2,1,0:T(8,128)}, f32[8,512,256]{2,1,0:T(8,128)S(1)}, u32[]{:S(2)}) %copy-start.2) | copy-done | bytes 4194328
  15.5 0.8 dynamic-slice_convert_fusion
  16.3 21.1 %all-to-all-done.refs_6_ = bf16[16,272,128]{2,1,0:T(8,128)(2,1)S(1)} async-done(((bf16[16,272,128]{2,1,0:T(8,128)(2,1)}), bf16[16,272,128]{2,1,0:T(8,128)(2,1)S(1)}, u32[]{:S(2)}, u32[]{:S(2)}) %all-to-all-start) | async-done | bytes 1114144 | tf_op jit(solution)/shard_map/all_to_all | solution.py:615
  37.3 0.0 copy-start.4
  37.3 1.0 %copy-done.4 = bf16[16,272,128]{2,1,0:T(8,128)(2,1)} copy-done((bf16[16,272,128]{2,1,0:T(8,128)(2,1)}, bf16[16,272,128]{2,1,0:T(8,128)(2,1)S(1)}, u32[]{:S(2)}) %copy-start.4) | copy-done | bytes 1114136
  38.3 0.0 copy-done.10
  38.3 0.0 copy-start.3
  38.3 2.2 %copy-done.3 = f32[8,512,256]{2,1,0:T(8,128)S(1)} copy-done((f32[8,512,256]{2,1,0:T(8,128)S(1)}, f32[8,512,256]{2,1,0:T(8,128)}, u32[]{:S(2)}) %copy-start.3) | copy-done | bytes 4194328
  40.5 0.0 copy-start.5
  40.5 1.2 %copy-done.5 = bf16[16,272,128]{2,1,0:T(8,128)(2,1)S(1)} copy-done((bf16[16,272,128]{2,1,0:T(8,128)(2,1)S(1)}, bf16[16,272,128]{2,1,0:T(8,128)(2,1)}, u32[]{:S(2)}) %copy-start.5) | copy-done | bytes 1114136
  41.8 0.0 copy-start.9
  41.8 1.0 %copy-done.9 = bf16[1024,256]{1,0:T(8,128)(2,1)S(1)} copy-done((bf16[1024,256]{1,0:T(8,128)(2,1)S(1)}, bf16[1024,256]{1,0:T(8,128)(2,1)}, u32[]{:S(2)}) %copy-start.9) | copy-done | bytes 524312
  42.8 0.0 copy-start.11
  42.8 1.0 %copy-done.11 = bf16[512,512]{1,0:T(8,128)(2,1)S(1)} copy-done((bf16[512,512]{1,0:T(8,128)(2,1)S(1)}, bf16[512,512]{1,0:T(8,128)(2,1)}, u32[]{:S(2)}) %copy-start.11) | copy-done | bytes 524312
  43.9 0.0 copy-start
  43.9 8.7 %stacked_filter.1 = bf16[16,272,128]{2,1,0:T(8,128)(2,1)S(1)} custom-call(s32[16,1]{1,0:T(8,128)S(1)} %copy.11.refs_0_, f32[1,256]{1,0:T(1,128)S(1)} %bitcast.4, bf16[256,512]{1,0:T(8,128)(2,1)S(1)} %copy-done.10, bf16[1024,256]{1,0:T(8,128)(2,1)S(1)} %copy-done.9, bf16[512,512]{1,0:T(8,128)(2,1)S(1)} %copy-done.11, f32[8,512,256]{2,1,0:T(8,128)S(1)} %copy-done.3, ...), custom_call_target="tpu_custom_call" | custom-call | flops 2751463424 | bytes 8388608 | tf_op jit(solution)/shard_map/stacked_filter/pallas_call | solution.py:538
  52.6 0.0 copy-start.6
  52.6 1.0 %copy-done.6 = bf16[16,272,128]{2,1,0:T(8,128)(2,1)} copy-done((bf16[16,272,128]{2,1,0:T(8,128)(2,1)}, bf16[16,272,128]{2,1,0:T(8,128)(2,1)S(1)}, u32[]{:S(2)}) %copy-start.6) | copy-done | bytes 1114136
  53.6 5.0 %all-to-all-start.1 = ((bf16[16,272,128]{2,1,0:T(8,128)(2,1)}), bf16[16,272,128]{2,1,0:T(8,128)(2,1)}, u32[]{:S(2)}, u32[]{:S(2)}) async-start(bf16[16,272,128]{2,1,0:T(8,128)(2,1)} %copy-done.6), calls=%async_computation.1 | async-start | bytes 2228224 | tf_op jit(solution)/shard_map/all_to_all | solution.py:615
  59.9 25.0 %all-to-all-done.1.back_ref = bf16[16,272,128]{2,1,0:T(8,128)(2,1)} async-done(((bf16[16,272,128]{2,1,0:T(8,128)(2,1)}), bf16[16,272,128]{2,1,0:T(8,128)(2,1)}, u32[]{:S(2)}, u32[]{:S(2)}) %all-to-all-start.1) | async-done | bytes 1114144 | tf_op jit(solution)/shard_map/all_to_all | solution.py:615
  84.9 0.0 copy-done
  84.9 2.8 %stacked_finish.1 = (bf16[128,4096]{1,0:T(8,128)(2,1)}, f32[2,1]{1,0:T(2,128)S(1)}) custom-call(s32[1]{0:T(128)S(6)} %copy.13.ref_ref, s32[1]{0:T(128)S(6)} %copy.14.alt_ref, bf16[3,128,4096]{2,1,0:T(8,128)(2,1)S(1)} %copy-done, bf16[16,272,128]{2,1,0:T(8,128)(2,1)} %all-to-all-done.1.back_ref), custom_call_target="tpu_custom_call" | custom-call | flops 524288 | bytes 3145728 | tf_op jit(solution)/shard_map/stacked_finish/pallas_call | solution.py:591
  87.7 0.6 copy.12
  (1 shorter events, 0.0 us)
Async XLA Ops:
  4.3 6.8 %copy-start.12 = (s32[16]{0:T(128)S(1)}, s32[16]{0:T(128)}, u32[]{:S(2)}) copy-start(s32[16]{0:T(128)} %offsets_ref.1) | copy-start | bytes 196
  4.4 6.9 %copy-start.1 = (bf16[16,272,128]{2,1,0:T(8,128)(2,1)S(1)}, bf16[16,272,128]{2,1,0:T(8,128)(2,1)}, u32[]{:S(2)}) copy-start(bf16[16,272,128]{2,1,0:T(8,128)(2,1)} %send_products.1.refs_0_) | copy-start | bytes 3342340
  4.4 6.8 %copy-start.7 = (bf16[256,2048]{1,0:T(8,128)(2,1)S(1)}, bf16[256,2048]{1,0:T(8,128)(2,1)}, u32[]{:S(2)}) copy-start(bf16[256,2048]{1,0:T(8,128)(2,1)} %filter_ref.1) | copy-start | bytes 3145732
  4.4 33.0 %all-to-all-start = ((bf16[16,272,128]{2,1,0:T(8,128)(2,1)}), bf16[16,272,128]{2,1,0:T(8,128)(2,1)S(1)}, u32[]{:S(2)}, u32[]{:S(2)}) async-start(bf16[16,272,128]{2,1,0:T(8,128)(2,1)} %send_products.1.refs_0_), calls=%async_computation | async-start | bytes 2228224 | tf_op jit(solution)/shard_map/all_to_all | solution.py:615
  11.2 1.0 %copy-start.8 = (bf16[1024,256]{1,0:T(8,128)(2,1)S(1)}, bf16[1024,256]{1,0:T(8,128)(2,1)}, u32[]{:S(2)}) copy-start(bf16[1024,256]{1,0:T(8,128)(2,1)} %constant.16.clone.forward_ref.refs_3_) | copy-start | bytes 1572868
  12.3 26.1 %copy-start.10 = (bf16[256,512]{1,0:T(8,128)(2,1)S(1)}, bf16[256,512]{1,0:T(8,128)(2,1)}, u32[]{:S(2)}) copy-start(bf16[256,512]{1,0:T(8,128)(2,1)} %refs_2_.1) | copy-start | bytes 786436
  13.5 2.0 %copy-start.2 = (f32[8,512,256]{2,1,0:T(8,128)}, f32[8,512,256]{2,1,0:T(8,128)S(1)}, u32[]{:S(2)}) copy-start(f32[8,512,256]{2,1,0:T(8,128)S(1)} %filter_spectrum.1.refs_5_) | copy-start | bytes 12582916
  37.3 1.0 %copy-start.4 = (bf16[16,272,128]{2,1,0:T(8,128)(2,1)}, bf16[16,272,128]{2,1,0:T(8,128)(2,1)S(1)}, u32[]{:S(2)}) copy-start(bf16[16,272,128]{2,1,0:T(8,128)(2,1)S(1)} %all-to-all-done.refs_6_) | copy-start | bytes 3342340
  38.3 2.2 %copy-start.3 = (f32[8,512,256]{2,1,0:T(8,128)S(1)}, f32[8,512,256]{2,1,0:T(8,128)}, u32[]{:S(2)}) copy-start(f32[8,512,256]{2,1,0:T(8,128)} %copy-done.2) | copy-start | bytes 12582916
  40.5 1.2 %copy-start.5 = (bf16[16,272,128]{2,1,0:T(8,128)(2,1)S(1)}, bf16[16,272,128]{2,1,0:T(8,128)(2,1)}, u32[]{:S(2)}) copy-start(bf16[16,272,128]{2,1,0:T(8,128)(2,1)} %copy-done.4) | copy-start | bytes 3342340
  41.8 1.0 %copy-start.9 = (bf16[1024,256]{1,0:T(8,128)(2,1)S(1)}, bf16[1024,256]{1,0:T(8,128)(2,1)}, u32[]{:S(2)}) copy-start(bf16[1024,256]{1,0:T(8,128)(2,1)} %constant.16.clone.forward_ref.refs_3_) | copy-start | bytes 1572868
  42.8 1.0 %copy-start.11 = (bf16[512,512]{1,0:T(8,128)(2,1)S(1)}, bf16[512,512]{1,0:T(8,128)(2,1)}, u32[]{:S(2)}) copy-start(bf16[512,512]{1,0:T(8,128)(2,1)} %constant.17.clone.refs_4_) | copy-start | bytes 1572868
  43.9 41.0 %copy-start = (bf16[3,128,4096]{2,1,0:T(8,128)(2,1)S(1)}, bf16[3,128,4096]{2,1,0:T(8,128)(2,1)}, u32[]{:S(2)}) copy-start(bf16[3,128,4096]{2,1,0:T(8,128)(2,1)} %streams_ref.3) | copy-start | bytes 9437188
  52.6 1.0 %copy-start.6 = (bf16[16,272,128]{2,1,0:T(8,128)(2,1)}, bf16[16,272,128]{2,1,0:T(8,128)(2,1)S(1)}, u32[]{:S(2)}) copy-start(bf16[16,272,128]{2,1,0:T(8,128)(2,1)S(1)} %stacked_filter.1) | copy-start | bytes 3342340
  53.6 31.3 %all-to-all-start.1 = ((bf16[16,272,128]{2,1,0:T(8,128)(2,1)}), bf16[16,272,128]{2,1,0:T(8,128)(2,1)}, u32[]{:S(2)}, u32[]{:S(2)}) async-start(bf16[16,272,128]{2,1,0:T(8,128)(2,1)} %copy-done.6), calls=%async_computation.1 | async-start | bytes 2228224 | tf_op jit(solution)/shard_map/all_to_all | solution.py:615

commit v5 on v4

--- a/solution.py
+++ b/solution.py
@@ -50,6 +50,10 @@
 
 def whole_spec():
     return pl.BlockSpec(memory_space=pltpu.VMEM)
+
+
+anywhere = pl.BlockSpec(memory_space=pl.ANY)
+in_hbm = pl.BlockSpec(memory_space=pltpu.HBM)
 
 
 def product_kernel(chunks, width, vars_dev, rows_ref, streams_ref, *out_refs):
@@ -100,8 +104,7 @@
     )(local_rows, streams)
 
 
-def spectrum_kernel(block, filter_ref, forward_ref, *refs):
-    out_ref = refs[-1]
+def spectrum_kernel(block, filter_ref, forward_ref, out_ref):
     n_blocks = out_ref.shape[0]
     for index in range(n_blocks):
         taps = filter_ref[:, index * block : (index + 1) * block]
@@ -111,12 +114,12 @@
         out_ref[index] = both[: 2 * block] + both[2 * block :]
 
 
-def filter_spectrum(taps, forward, block, *earlier):
+def filter_spectrum(taps, forward, block):
     width, length = taps.shape
     n_blocks = length // block
     return pl.pallas_call(
         functools.partial(spectrum_kernel, block),
-        in_specs=[whole_spec(), whole_spec()] + [pl.BlockSpec(memory_space=pl.ANY)] * len(earlier),
+        in_specs=[whole_spec()] * 2,
         out_specs=whole_spec(),
         out_shape=jax.ShapeDtypeStruct((n_blocks, 2 * block, width), f32),
         compiler_params=pltpu.CompilerParams(vmem_limit_bytes=40 * MIB),
@@ -124,7 +127,7 @@
             flops=8 * block * length * width, bytes_accessed=4 * MIB, transcendentals=0
         ),
         name="filter_spectrum",
-    )(taps, forward, *earlier)
+    )(taps, forward)
 
 
 def multiply_points(points, spectrum_ref, joint):
@@ -383,18 +386,24 @@
         name="finish",
     )(ref_ids, alt_ids, streams, *backs)
 
-def send_products_kernel(halves, vars_dev, me_ref, offsets_ref, streams_ref, out_ref, *scratch):
-    built, pairs, gates, gate_rows, pair_sems, gate_sems, out_sems = scratch
-    n_devices, _, tok_rows, width = pairs.shape
+def send_products_kernel(first, together, halves, vars_dev, me_ref, offsets_ref, streams_ref, *refs):
+    built, pairs, gates, gate_rows, pair_sems, gate_sems, out_sems = refs[-7:]
+    count, _, tok_rows, width = pairs.shape
+    out_refs = refs[-8:-7] if together else refs[-7 - count : -7]
     me = me_ref[0]
     slot = tok_rows // vars_dev
     local_rows = [var * slot + offsets_ref[me * vars_dev + var] for var in range(vars_dev)]
-
-    def pair_copy(owner):
+    base = me // count * count
+
+    def lanes_from(step, offset):
+        owner = base + step if together else me ^ (first + step)
+        return pl.multiple_of(owner * width + offset, lane_tile)
+
+    def pair_copy(step):
         return pltpu.make_async_copy(
-            streams_ref.at[pl.ds(1, 2), :, pl.ds(owner * width, width)],
-            pairs.at[owner],
-            pair_sems.at[owner],
+            streams_ref.at[pl.ds(1, 2), :, pl.ds(lanes_from(step, 0), width)],
+            pairs.at[step],
+            pair_sems.at[step],
         )
 
     def gate_copy(var):
@@ -403,13 +412,14 @@
             streams_ref.at[0, pl.ds(start, row_tile), :], gates.at[var], gate_sems.at[var]
         )
 
-    def out_copy(owner):
-        return pltpu.make_async_copy(built.at[owner], out_ref.at[owner], out_sems.at[owner])
+    def out_copy(step):
+        target = out_refs[0].at[step] if together else out_refs[step]
+        return pltpu.make_async_copy(built.at[step], target, out_sems.at[step])
 
     for var in range(vars_dev):
         gate_copy(var).start()
-    for owner in range(n_devices):
-        pair_copy(owner).start()
+    for step in range(count):
+        pair_copy(step).start()
     row = lax.broadcasted_iota(jnp.int32, gates.shape[1:], 0)
     for var in range(vars_dev):
         gate_copy(var).wait()
@@ -417,91 +427,107 @@
         gate_rows[var : var + 1, :] = jnp.sum(mine, axis=0, keepdims=True)
     extra = built.shape[1] - halves * tok_rows
     place = lax.broadcasted_iota(jnp.int32, (extra, lane_tile), 0)
-    for owner in range(n_devices):
-        pair_copy(owner).wait()
+    for step in range(count):
+        pair_copy(step).wait()
         tail = jnp.zeros((extra, lane_tile), f32)
         for half in range(halves):
             lanes = slice(half * lane_tile, (half + 1) * lane_tile)
             rows = slice(half * tok_rows, (half + 1) * tok_rows)
-            built[owner, rows, :] = pairs[owner, 0, :, lanes] * pairs[owner, 1, :, lanes]
-            start = owner * width + half * lane_tile
+            built[step, rows, :] = pairs[step, 0, :, lanes] * pairs[step, 1, :, lanes]
             for var in range(vars_dev):
-                mine = gate_rows[var : var + 1, start : start + lane_tile]
+                mine = gate_rows[var : var + 1, pl.ds(lanes_from(step, half * lane_tile), lane_tile)]
                 tail = jnp.where(place == half * vars_dev + var, mine, tail)
-        built[owner, halves * tok_rows :, :] = tail.astype(bf16)
-        out_copy(owner).start()
-    for owner in range(n_devices):
-        out_copy(owner).wait()
-
-
-def send_products(me, offsets, streams, vars_dev, n_devices, extra):
+        built[step, halves * tok_rows :, :] = tail.astype(bf16)
+        out_copy(step).start()
+    for step in range(count):
+        out_copy(step).wait()
+
+
+def send_products(me, offsets, streams, first, count, together, vars_dev, n_devices, extra, *earlier):
     _, tok_rows, model_width = streams.shape
     width = model_width // n_devices
     halves = width // lane_tile
     rows_out = halves * tok_rows + extra
+    if together:
+        out_shape = [jax.ShapeDtypeStruct((count, rows_out, lane_tile), bf16)]
+    else:
+        out_shape = [jax.ShapeDtypeStruct((rows_out, lane_tile), bf16)] * count
     return pl.pallas_call(
-        functools.partial(send_products_kernel, halves, vars_dev),
-        in_specs=[
-            pl.BlockSpec(memory_space=pltpu.SMEM),
-            pl.BlockSpec(memory_space=pltpu.SMEM),
-            pl.BlockSpec(memory_space=pl.ANY),
-        ],
-        out_specs=pl.BlockSpec(memory_space=pl.ANY),
-        out_shape=jax.ShapeDtypeStruct((n_devices, rows_out, lane_tile), bf16),
+        functools.partial(send_products_kernel, first, together, halves, vars_dev),
+        in_specs=[pl.BlockSpec(memory_space=pltpu.SMEM)] * 2 + [in_hbm] + [anywhere] * len(earlier),
+        out_specs=[anywhere] * len(out_shape),
+        out_shape=out_shape,
         scratch_shapes=[
-            pltpu.VMEM((n_devices, rows_out, lane_tile), bf16),
-            pltpu.VMEM((n_devices, 2, tok_rows, width), bf16),
+            pltpu.VMEM((count, rows_out, lane_tile), bf16),
+            pltpu.VMEM((count, 2, tok_rows, width), bf16),
             pltpu.VMEM((vars_dev, row_tile, model_width), bf16),
             pltpu.VMEM((round_up(vars_dev, half_tile), model_width), f32),
-            pltpu.SemaphoreType.DMA((n_devices,)),
+            pltpu.SemaphoreType.DMA((count,)),
             pltpu.SemaphoreType.DMA((vars_dev,)),
-            pltpu.SemaphoreType.DMA((n_devices,)),
+            pltpu.SemaphoreType.DMA((count,)),
         ],
         compiler_params=pltpu.CompilerParams(vmem_limit_bytes=60 * MIB),
         cost_estimate=pl.CostEstimate(
-            flops=tok_rows * model_width, bytes_accessed=6 * tok_rows * model_width, transcendentals=0
+            flops=tok_rows * count * width, bytes_accessed=6 * tok_rows * count * width, transcendentals=0
         ),
         name="send_products",
-    )(me, offsets, streams)
-
-
-def stacked_filter_kernel(vars_dev, halves, tok_rows, *refs):
-    positions_ref, gain_ref, unembed_ref, forward_ref, inverse_ref, spectrum_ref = refs[:6]
-    arrived, leaving, points, joint, packed = refs[6:]
+    )(me, offsets, streams, *earlier)
+
+
+def split_filter_kernel(steps, vars_dev, halves, tok_rows, me_ref, positions_ref, gain_ref, *refs):
+    forward, inverse, unembed, taps = refs[:4]
+    points, joint, spectrum, packed, arrived, leaving = refs[-6:]
     n_devices = arrived.shape[0]
+    near = n_devices // 2
+    count = 1 + len(steps)
+    in_refs, out_refs = refs[4 : 4 + count], refs[4 + count : 4 + 2 * count]
+    me = me_ref[0]
+    base = me // near * near
     body = halves * tok_rows
     n_blocks, double, width = points.shape
     block = double // 2
     per_block = block // tok_rows
-
-    def forward_step(step, carry):
+    group = 2 if n_blocks % 2 == 0 else 1
+
+    for index in range(near):
+        arrived[base + index] = in_refs[0][index]
+    for index, step in enumerate(steps):
+        arrived[me ^ step] = in_refs[1 + index][...]
+    for index in range(n_blocks):
+        both = lax.dot_general(
+            forward[...],
+            taps[:, index * block : (index + 1) * block],
+            (((1,), (1,)), ((), ())),
+            preferred_element_type=f32,
+        )
+        spectrum[index] = both[:double] + both[double:]
+
+    for step in range(0, n_blocks, group):
         pieces = []
-        for half in range(halves):
-            rows = slice(half * tok_rows, (half + 1) * tok_rows)
-            parts = [arrived[step * per_block + m, rows, :] for m in range(per_block)]
-            pieces.append(jnp.concatenate(parts, axis=0))
+        for index in range(step, step + group):
+            for half in range(halves):
+                rows = slice(half * tok_rows, (half + 1) * tok_rows)
+                parts = [arrived[index * per_block + m, rows, :] for m in range(per_block)]
+                pieces.append(jnp.concatenate(parts, axis=0))
         signal = jnp.concatenate(pieces, axis=1)
-        both = jnp.dot(forward_ref[...], signal, preferred_element_type=f32)
-        points[step] = both[:double] + both[double:]
-        return carry
-
-    lax.fori_loop(0, n_blocks, forward_step, 0)
-    multiply_points(points, spectrum_ref, joint)
-
-    def inverse_step(step, carry):
-        highs, lows = split_bf16(joint[step])
-        both = jnp.dot(inverse_ref[...], highs, preferred_element_type=f32)
-        rest = jnp.dot(inverse_ref[:block, :], lows, preferred_element_type=f32)
+        both = jnp.dot(forward[...], signal, preferred_element_type=f32)
+        total = both[:double] + both[double:]
+        for member in range(group):
+            points[step + member] = total[:, member * width : (member + 1) * width]
+    multiply_points(points, spectrum, joint)
+
+    for step in range(0, n_blocks, group):
+        highs, lows = split_bf16(jnp.concatenate([joint[step + m] for m in range(group)], axis=1))
+        both = jnp.dot(inverse[...], highs, preferred_element_type=f32)
+        rest = jnp.dot(inverse[:block, :], lows, preferred_element_type=f32)
         result = (both[:block] + both[block:] + rest).astype(bf16)
-        for member in range(per_block):
-            for half in range(halves):
-                leaving[step * per_block + member, half * tok_rows : (half + 1) * tok_rows, :] = result[
-                    member * tok_rows : (member + 1) * tok_rows,
-                    half * lane_tile : (half + 1) * lane_tile,
-                ]
-        return carry
-
-    lax.fori_loop(0, n_blocks, inverse_step, 0)
+        for index in range(group):
+            for member in range(per_block):
+                for half in range(halves):
+                    start = index * width + half * lane_tile
+                    leaving[
+                        (step + index) * per_block + member, half * tok_rows : (half + 1) * tok_rows, :
+                    ] = result[member * tok_rows : (member + 1) * tok_rows, start : start + lane_tile]
 
     length = n_devices * tok_rows
     column = lax.broadcasted_iota(jnp.int32, (positions_ref.shape[0], length), 1)
@@ -521,98 +547,136 @@
         filtered = jnp.dot(picker, filtered, preferred_element_type=f32)
         rows = (gate_rows * filtered).astype(bf16).astype(f32)
         weighted = (rows * gain_ref[:, lanes]).astype(bf16)
-        part = jnp.dot(weighted, unembed_ref[lanes, :], preferred_element_type=f32)
+        part = jnp.dot(weighted, unembed[lanes, :], preferred_element_type=f32)
         raw = part if raw is None else raw + part
         squares = rows * rows if squares is None else squares + rows * rows
     pack_scores(raw, squares, vars_dev, packed, n_devices)
     extra = packed.shape[0] // n_devices
     leaving[:, body:, :] = packed[...].reshape(n_devices, extra, lane_tile).astype(bf16)
-
-
-def stacked_filter(operands, arrived, vars_dev, tok_rows, extra):
-    n_devices = arrived.shape[0]
-    n_blocks, double, width = operands[-1].shape
+    for index, step in enumerate(steps):
+        out_refs[1 + index][...] = leaving[me ^ step]
+    for index in range(near):
+        out_refs[0][index] = leaving[base + index]
+
+
+def split_filter(me, positions, gain_row, tables, steps, arrivals, vars_dev, tok_rows, extra):
+    width, length = tables[3].shape
+    near = arrivals[0].shape[0]
+    n_devices = 2 * near
+    double = tables[0].shape[0] // 2
+    n_blocks = 2 * length // double
     halves = width // lane_tile
     rows_out = halves * tok_rows + extra
+    count = len(arrivals)
     flops = 2 * width * n_blocks * (double * double * 5 // 2 + 4 * n_blocks * double)
     return pl.pallas_call(
-        functools.partial(stacked_filter_kernel, vars_dev, halves, tok_rows),
-        in_specs=[whole_spec()] * (len(operands) + 1),
-        out_specs=whole_spec(),
-        out_shape=jax.ShapeDtypeStruct((n_devices, rows_out, lane_tile), bf16),
+        functools.partial(split_filter_kernel, steps, vars_dev, halves, tok_rows),
+        in_specs=[pl.BlockSpec(memory_space=pltpu.SMEM)] + [whole_spec()] * (6 + count),
+        out_specs=[whole_spec()] * count,
+        out_shape=[jax.ShapeDtypeStruct((near, rows_out, lane_tile), bf16)]
+        + [jax.ShapeDtypeStruct((rows_out, lane_tile), bf16)] * (count - 1),
         scratch_shapes=[
             pltpu.VMEM((n_blocks, double, width), f32),
             pltpu.VMEM((n_blocks, double, width), f32),
+            pltpu.VMEM((n_blocks, double, width), f32),
             pltpu.VMEM((n_devices * extra, lane_tile), f32),
+            pltpu.VMEM((n_devices,) + arrivals[1].shape, bf16),
+            pltpu.VMEM((n_devices, rows_out, lane_tile), bf16),
         ],
-        compiler_params=pltpu.CompilerParams(vmem_limit_bytes=32 * MIB),
+        compiler_params=pltpu.CompilerParams(vmem_limit_bytes=24 * MIB),
         cost_estimate=pl.CostEstimate(flops=flops, bytes_accessed=8 * MIB, transcendentals=0),
-        name="stacked_filter",
-    )(*operands, arrived)
-
-
-def stacked_finish_kernel(halves, vars_dev, vocab, ref_ref, alt_ref, streams_ref, back_ref, *refs):
-    mixed_ref, scores_ref, gates, results, gate_sems, out_sems = refs
-    n_devices, tok_rows, width = gates.shape
-
-    def gate_copy(owner):
+        name="split_filter",
+    )(me, positions, gain_row, *tables, *arrivals)
+
+
+def split_finish_kernel(steps, halves, vars_dev, vocab, me_ref, ref_ref, alt_ref, gates_ref, *refs):
+    mixed_ref, scores_ref, results, out_sems = refs[-4:]
+    n_devices, tok_rows, width = results.shape
+    near = n_devices // 2
+    me = me_ref[0]
+    base = me // near * near
+
+    def lanes_of(index, offset=0, size=width):
+        owner = base + index if index < near else me ^ steps[index - near]
+        return pl.ds(pl.multiple_of(owner * width + offset, lane_tile), size)
+
+    def out_copy(index):
         return pltpu.make_async_copy(
-            streams_ref.at[0, :, pl.ds(owner * width, width)], gates.at[owner], gate_sems.at[owner]
+            results.at[index], mixed_ref.at[:, lanes_of(index)], out_sems.at[index]
         )
 
-    def out_copy(owner):
-        return pltpu.make_async_copy(
-            results.at[owner], mixed_ref.at[:, pl.ds(owner * width, width)], out_sems.at[owner]
-        )
-
-    for owner in range(n_devices):
-        gate_copy(owner).start()
     sums = None
-    for owner in range(n_devices):
-        gate_copy(owner).wait()
+    for index in range(n_devices):
+        back_ref = refs[0].at[index] if index < near else refs[1 + index - near]
         for half in range(halves):
             lanes = slice(half * lane_tile, (half + 1) * lane_tile)
-            filtered = back_ref[owner, half * tok_rows : (half + 1) * tok_rows, :]
-            results[owner, :, lanes] = gates[owner, :, lanes] * filtered
-        out_copy(owner).start()
-        tail = back_ref[owner, halves * tok_rows :, :].astype(f32)
+            filtered = back_ref[half * tok_rows : (half + 1) * tok_rows, :]
+            gate = gates_ref[:, lanes_of(index, half * lane_tile, lane_tile)]
+            results[index, :, lanes] = gate * filtered
+        out_copy(index).start()
+        tail = back_ref[halves * tok_rows :, :].astype(f32)
         sums = tail if sums is None else sums + tail
     model_width = n_devices * width
     scores_ref[...] = final_scores(sums, vars_dev, vocab, model_width, ref_ref, alt_ref)
-    for owner in range(n_devices):
-        out_copy(owner).wait()
-
-
-def stacked_finish(ref_ids, alt_ids, streams, back, vocab):
-    _, tok_rows, model_width = streams.shape
-    n_devices = back.shape[0]
+    for index in range(n_devices):
+        out_copy(index).wait()
+
+
+def split_finish(me, ref_ids, alt_ids, gates, steps, backs, vocab):
+    tok_rows, model_width = gates.shape
+    n_devices = 2 * backs[0].shape[0]
     vars_dev = ref_ids.shape[0]
     width = model_width // n_devices
     return pl.pallas_call(
-        functools.partial(stacked_finish_kernel, width // lane_tile, vars_dev, vocab),
-        in_specs=[pl.BlockSpec(memory_space=pltpu.SMEM)] * 2
-        + [pl.BlockSpec(memory_space=pl.ANY), whole_spec()],
-        out_specs=[pl.BlockSpec(memory_space=pl.ANY), whole_spec()],
+        functools.partial(split_finish_kernel, steps, width // lane_tile, vars_dev, vocab),
+        in_specs=[pl.BlockSpec(memory_space=pltpu.SMEM)] * 3 + [whole_spec()] * (1 + len(backs)),
+        out_specs=[anywhere, whole_spec()],
         out_shape=[
             jax.ShapeDtypeStruct((tok_rows, model_width), bf16),
             jax.ShapeDtypeStruct((2, vars_dev), f32),
         ],
         scratch_shapes=[
             pltpu.VMEM((n_devices, tok_rows, width), bf16),
-            pltpu.VMEM((n_devices, tok_rows, width), bf16),
-            pltpu.SemaphoreType.DMA((n_devices,)),
             pltpu.SemaphoreType.DMA((n_devices,)),
         ],
-        compiler_params=pltpu.CompilerParams(vmem_limit_bytes=12 * MIB),
+        compiler_params=pltpu.CompilerParams(vmem_limit_bytes=16 * MIB),
         cost_estimate=pl.CostEstimate(
             flops=tok_rows * model_width, bytes_accessed=6 * tok_rows * model_width, transcendentals=0
         ),
-        name="stacked_finish",
-    )(ref_ids, alt_ids, streams, back)
-
-
-def transposed(blocks):
-    return lax.all_to_all(blocks, "seq", split_axis=0, concat_axis=0, tiled=True)
+        name="split_finish",
+    )(me, ref_ids, alt_ids, gates, *backs)
+
+
+def hold_kernel(part_ref, earlier_ref, out_ref):
+    pass
+
+
+def held_until(part, earlier):
+    return pl.pallas_call(
+        hold_kernel,
+        in_specs=[anywhere, anywhere],
+        out_specs=anywhere,
+        out_shape=jax.ShapeDtypeStruct(part.shape, part.dtype),
+        input_output_aliases={0: 0},
+        compiler_params=pltpu.CompilerParams(vmem_limit_bytes=16 * MIB),
+        name="hold",
+    )(part, earlier)
+
+
+def exchange_near(part, n_devices):
+    near = n_devices // 2
+    groups = [list(range(near)), list(range(near, n_devices))]
+    return lax.all_to_all(
+        part, "seq", split_axis=0, concat_axis=0, axis_index_groups=groups, tiled=True
+    )
+
+
+def exchange_far(parts, steps, n_devices):
+    moved = []
+    for step, part in zip(steps, parts):
+        pairs = [(device, device ^ step) for device in range(n_devices)]
+        moved.append(lax.ppermute(part, "seq", pairs))
+    return moved
 
 
 def shards(streams, long_filter, gain, unembed, offsets, ref_ids, alt_ids):
@@ -637,16 +701,25 @@
     positions = positions.T.reshape(n_devices * vars_dev, 1)
     my_gain = lax.dynamic_slice_in_dim(gain, my_index * group_width, group_width).astype(f32)
 
-    if chunks * lane_tile == group_width:
+    if chunks * lane_tile == group_width and n_devices & (n_devices - 1) == 0:
         me = jnp.reshape(my_index, (1,)).astype(jnp.int32)
         gate_extra = round_up(chunks * vars_dev, row_tile)
         score_extra = round_up(vars_dev * 2 * (vocab // lane_tile + 1), row_tile)
-        blocks = send_products(me, offsets, streams, vars_dev, n_devices, gate_extra)
-        arrived = transposed(blocks)
-        spectrum = filter_spectrum(long_filter, forward, block, blocks)
-        operands = (positions, my_gain[None, :], unembed, forward, inverse, spectrum)
-        leaving = stacked_filter(operands, arrived, vars_dev, tok_rows, score_extra)
-        mixed, scores = stacked_finish(ref_ids, alt_ids, streams, transposed(leaving), vocab)
+        near = n_devices // 2
+        steps = list(range(near, n_devices))
+        sizes = (vars_dev, n_devices, gate_extra)
+        far_parts = send_products(me, offsets, streams, near, near, False, *sizes)
+        far_moved = exchange_far(far_parts, steps, n_devices)
+        near_part = send_products(me, offsets, streams, 0, near, True, *sizes, far_moved[0])[0]
+        arrivals = [exchange_near(near_part, n_devices)] + far_moved
+        tables = (forward, inverse, unembed, long_filter)
+        leaving = split_filter(
+            me, positions, my_gain[None, :], tables, steps, arrivals, vars_dev, tok_rows, score_extra
+        )
+        returned = exchange_far(leaving[1:], steps, n_devices)
+        near_back = exchange_near(held_until(leaving[0], returned[0]), n_devices)
+        backs = [near_back] + returned
+        mixed, scores = split_finish(me, ref_ids, alt_ids, streams[0], steps, backs, vocab)
         return (mixed, scores)
 
     gate_extra = round_up(chunks * vars_dev, row_tile)

time: 89 us -> 89.5 us (level)
  starting transfers between devices: 11.7 us -> 35.2 us
  waiting for transfers between devices: 46.1 us -> 30.4 us
  local copies, waits for them, and re-layouts: 11.2 us -> 4.57 us
  Pallas kernels: 16.5 us -> 15.6 us
    all_to_all x2, waiting for transfers between devices: 46.1 us -> 0.01 us  [exchange_near(): lax.all_to_all(part, 'seq', split_axis=0, concat_axis=0, axis_index_group...]
    ppermute x0 -> x16, waiting for transfers between devices: none -> 30.4 us  [exchange_far(): moved.append(lax.ppermute(part, 'seq', pairs))]
    ppermute x0 -> x16, starting transfers between devices: none -> 19.7 us  [exchange_far(): moved.append(lax.ppermute(part, 'seq', pairs))]
    unnamed x26 -> x28, local copies, waits for them, and re-layouts: 10.5 us -> 2.6 us
    all_to_all x2, starting transfers between devices: 11.7 us -> 15.5 us  [exchange_near(): lax.all_to_all(part, 'seq', split_axis=0, concat_axis=0, axis_index_group...]
    squeeze x0 -> x1, local copies, waits for them, and re-layouts: none -> 1.29 us  [shards(): streams[0]]
    pallas_call x4 -> x5, Pallas kernels: 16.5 us -> 15.6 us  [the longest x1 8.22 us: split_filter(): pl.pallas_call(functools.partial(split_filter_kernel, steps, vars_dev, ha...]
  transfers between devices with their start and end apart: 2 -> 18, of which waited for: 2 -> 13; matrix products, arithmetic and copies ran while one was open for 1% -> 2% of each run, Pallas kernels for 1% -> 0%
where the time goes in v5:
time: 89.5 us; the launch traced here: 88.6 us
  starting transfers between devices  35.2 us (39%)
  waiting for transfers between devices  30.4 us (34%)
  Pallas kernels  15.6 us (17%)
  local copies, waits for them, and re-layouts  4.57 us (5%)
  between operations  2.09 us (2%)
    ppermute x16, waiting for transfers between devices, exchange_far(): moved.append(lax.ppermute(part, 'seq', pairs))  30.4 us
    ppermute x16, starting transfers between devices, exchange_far(): moved.append(lax.ppermute(part, 'seq', pairs))  19.7 us
    all_to_all x2, starting transfers between devices, exchange_near(): lax.all_to_all(part, 'seq', split_axis=0, concat_axis=0, axis_index_group...  15.5 us
    pallas_call x1, Pallas kernels, split_filter(): pl.pallas_call(functools.partial(split_filter_kernel, steps, vars_dev, ha...  8.22 us
    pallas_call x2, Pallas kernels, send_products(): pl.pallas_call(functools.partial(send_products_kernel, first, together, h...  6.04 us
    unnamed x28, local copies, waits for them, and re-layouts  2.6 us
  transfers between devices with their start and end apart: 18, of which 13 were waited for; matrix products, arithmetic and copies ran while one was open for 2% of the time, Pallas kernels for 0%

profile of v5, /device:TPU:13, one launch (start us, length us, event | category | flops | bytes accessed | tf_op | source)
XLA Modules:
  0.0 88.6 jit_solution(17880951226905752058)
XLA Ops:
  0.6 3.0 %send_products.2 = (bf16[272,128]{1,0:T(8,128)(2,1)}, bf16[272,128]{1,0:T(8,128)(2,1)}, bf16[272,128]{1,0:T(8,128)(2,1)}, bf16[272,128]{1,0:T(8,128)(2,1)}, bf16...) custom-call(s32[1]{0:T(128)} %bitcast.me_ref, ...), custom_call_target="tpu_custom_call" | custom-call | flops 262144 | bytes 1572864 | tf_op jit(solution)/shard_map/send_products/pallas_call | solution.py:455
  3.7 0.0 copy-start.13
  3.7 0.0 copy-start.12
  3.7 0.0 copy-start.11
  3.7 0.0 copy-start.10
  3.7 0.0 copy-start.9
  3.7 0.0 copy-start.6
  3.7 0.0 copy-start.8
  3.7 0.0 copy-start.7
  3.7 0.0 copy-start.2
  3.7 0.0 copy-start.3
  3.8 0.0 copy-start.4
  3.8 2.4 %collective-permute-start = (bf16[272,128]{1,0:T(8,128)(2,1)}, bf16[272,128]{1,0:T(8,128)(2,1)S(1)}, u32[]{:S(2)}, u32[]{:S(2)}) collective-permute-start(bf16[272,128]{1,0:T(8,128)(2,1)} %get-tuple-element.19), channel_id=1, source_target_pairs={{0,8},{1,9},{2,10},{3,11},{4,12},{5,13},{6,14},{7,15},{8,0},{9,1},... | collective-permute-start | bytes 208904 | tf_op jit(solution)/shard_map/ppermute | solution.py:678
  6.1 3.1 %collective-permute-done.refs_0_.refs_5_ = bf16[272,128]{1,0:T(8,128)(2,1)S(1)} collective-permute-done((bf16[272,128]{1,0:T(8,128)(2,1)}, bf16[272,128]{1,0:T(8,128)(2,1)S(1)}, u32[]{:S(2)}, u32[]{:S(2)}) %collective-permute-start) | collective-permute-done | bytes 69664 | tf_op jit(solution)/shard_map/ppermute | solution.py:678
  9.3 0.6 copy-done
  9.9 3.0 %send_products.3 = bf16[8,272,128]{2,1,0:T(8,128)(2,1)} custom-call(s32[1]{0:T(128)} %bitcast.me_ref, s32[16]{0:T(128)} %offsets_ref.3, bf16[3,128,4096]{2,1,0:T(8,128)(2,1)} %streams_ref.3, bf16[272,128]{1,0:T(8,128)(2,1)} %copy-done), custom_call_target="tpu_custom_call" | custom-call | flops 262144 | bytes 1572864 | tf_op jit(solution)/shard_map/send_products/pallas_call | solution.py:455
  13.0 5.6 %all-to-all-start = ((bf16[8,272,128]{2,1,0:T(8,128)(2,1)}), bf16[8,272,128]{2,1,0:T(8,128)(2,1)S(1)}, u32[]{:S(2)}, u32[]{:S(2)}) async-start(bf16[8,272,128]{2,1,0:T(8,128)(2,1)} %send_products.3), calls=%async_computation | async-start | bytes 1114112 | tf_op jit(solution)/shard_map/all_to_all | solution.py:669
  18.5 0.0 copy-done.13
  18.5 2.5 %collective-permute-start.1 = (bf16[272,128]{1,0:T(8,128)(2,1)S(1)}, bf16[272,128]{1,0:T(8,128)(2,1)S(1)}, u32[]{:S(2)}, u32[]{:S(2)}) collective-permute-start(bf16[272,128]{1,0:T(8,128)(2,1)S(1)} %copy-done.13), channel_id=1, source_target_pairs={{0,9},{1,8},{2,11},{3,10},{4,13},{5,12},{6,15},{7,14},{8,1},{9,0},... | collective-permute-start | bytes 208904 | tf_op jit(solution)/shard_map/ppermute | solution.py:678
  21.0 0.0 copy-done.12
  21.0 1.0 %collective-permute-start.2 = (bf16[272,128]{1,0:T(8,128)(2,1)S(1)}, bf16[272,128]{1,0:T(8,128)(2,1)S(1)}, u32[]{:S(2)}, u32[]{:S(2)}) collective-permute-start(bf16[272,128]{1,0:T(8,128)(2,1)S(1)} %copy-done.12), channel_id=1, source_target_pairs={{0,10},{1,11},{2,8},{3,9},{4,14},{5,15},{6,12},{7,13},{8,2},{9,3},... | collective-permute-start | bytes 208904 | tf_op jit(solution)/shard_map/ppermute | solution.py:678
  22.1 0.0 copy-done.11
  22.1 2.6 %collective-permute-start.3 = (bf16[272,128]{1,0:T(8,128)(2,1)S(1)}, bf16[272,128]{1,0:T(8,128)(2,1)S(1)}, u32[]{:S(2)}, u32[]{:S(2)}) collective-permute-start(bf16[272,128]{1,0:T(8,128)(2,1)S(1)} %copy-done.11), channel_id=1, source_target_pairs={{0,11},{1,10},{2,9},{3,8},{4,15},{5,14},{6,13},{7,12},{8,3},{9,2},... | collective-permute-start | bytes 208904 | tf_op jit(solution)/shard_map/ppermute | solution.py:678
  24.6 0.0 copy-done.10
  24.6 0.0 collective-permute-start.4
  24.6 0.0 copy-done.9
  24.6 1.7 %collective-permute-start.5 = (bf16[272,128]{1,0:T(8,128)(2,1)S(1)}, bf16[272,128]{1,0:T(8,128)(2,1)S(1)}, u32[]{:S(2)}, u32[]{:S(2)}) collective-permute-start(bf16[272,128]{1,0:T(8,128)(2,1)S(1)} %copy-done.9), channel_id=1, source_target_pairs={{0,13},{1,12},{2,15},{3,14},{4,9},{5,8},{6,11},{7,10},{8,5},{9,4},... | collective-permute-start | bytes 208904 | tf_op jit(solution)/shard_map/ppermute | solution.py:678
  26.3 0.1 copy.12.positions_ref
  26.4 3.5 %collective-permute-done.1.refs_6_ = bf16[272,128]{1,0:T(8,128)(2,1)S(1)} collective-permute-done((bf16[272,128]{1,0:T(8,128)(2,1)S(1)}, bf16[272,128]{1,0:T(8,128)(2,1)S(1)}, u32[]{:S(2)}, u32[]{:S(2)}) %collective-permute-start.1) | collective-permute-done | bytes 69664 | tf_op jit(solution)/shard_map/ppermute | solution.py:678
  30.0 0.3 collective-permute-start.6
  30.3 1.3 %collective-permute-done.2.refs_7_ = bf16[272,128]{1,0:T(8,128)(2,1)S(1)} collective-permute-done((bf16[272,128]{1,0:T(8,128)(2,1)S(1)}, bf16[272,128]{1,0:T(8,128)(2,1)S(1)}, u32[]{:S(2)}, u32[]{:S(2)}) %collective-permute-start.2) | collective-permute-done | bytes 69664 | tf_op jit(solution)/shard_map/ppermute | solution.py:678
  31.6 0.6 collective-permute-start.7
  32.2 0.8 dynamic-slice_convert_fusion
  33.0 3.7 %collective-permute-done.3.refs_8_ = bf16[272,128]{1,0:T(8,128)(2,1)S(1)} collective-permute-done((bf16[272,128]{1,0:T(8,128)(2,1)S(1)}, bf16[272,128]{1,0:T(8,128)(2,1)S(1)}, u32[]{:S(2)}, u32[]{:S(2)}) %collective-permute-start.3) | collective-permute-done | bytes 69664 | tf_op jit(solution)/shard_map/ppermute | solution.py:678
  36.7 2.6 %collective-permute-done.4.refs_9_ = bf16[272,128]{1,0:T(8,128)(2,1)S(1)} collective-permute-done((bf16[272,128]{1,0:T(8,128)(2,1)S(1)}, bf16[272,128]{1,0:T(8,128)(2,1)S(1)}, u32[]{:S(2)}, u32[]{:S(2)}) %collective-permute-start.4) | collective-permute-done | bytes 69664 | tf_op jit(solution)/shard_map/ppermute | solution.py:678
  39.3 1.7 %collective-permute-done.5.refs_10_ = bf16[272,128]{1,0:T(8,128)(2,1)S(1)} collective-permute-done((bf16[272,128]{1,0:T(8,128)(2,1)S(1)}, bf16[272,128]{1,0:T(8,128)(2,1)S(1)}, u32[]{:S(2)}, u32[]{:S(2)}) %collective-permute-start.5) | collective-permute-done | bytes 69664 | tf_op jit(solution)/shard_map/ppermute | solution.py:678
  41.1 1.7 %collective-permute-done.6.refs_11_ = bf16[272,128]{1,0:T(8,128)(2,1)S(1)} collective-permute-done((bf16[272,128]{1,0:T(8,128)(2,1)S(1)}, bf16[272,128]{1,0:T(8,128)(2,1)S(1)}, u32[]{:S(2)}, u32[]{:S(2)}) %collective-permute-start.6) | collective-permute-done | bytes 69664 | tf_op jit(solution)/shard_map/ppermute | solution.py:678
  42.8 1.6 %collective-permute-done.7.refs_12_ = bf16[272,128]{1,0:T(8,128)(2,1)S(1)} collective-permute-done((bf16[272,128]{1,0:T(8,128)(2,1)S(1)}, bf16[272,128]{1,0:T(8,128)(2,1)S(1)}, u32[]{:S(2)}, u32[]{:S(2)}) %collective-permute-start.7) | collective-permute-done | bytes 69664 | tf_op jit(solution)/shard_map/ppermute | solution.py:678
  44.3 0.0 all-to-all-done.refs_4_
  44.4 0.0 copy-done.3
  44.4 0.9 copy-done.1
  45.3 1.0 %copy-done.5 = bf16[1024,256]{1,0:T(8,128)(2,1)S(1)} copy-done((bf16[1024,256]{1,0:T(8,128)(2,1)S(1)}, bf16[1024,256]{1,0:T(8,128)(2,1)}, u32[]{:S(2)}) %copy-start.5) | copy-done | bytes 524312
  46.3 8.2 %split_filter.1 = (bf16[8,272,128]{2,1,0:T(8,128)(2,1)}, bf16[272,128]{1,0:T(8,128)(2,1)S(1)}, bf16[272,128]{1,0:T(8,128)(2,1)S(1)}, bf16[272,128]{1,0:T(8,128)(...) custom-call(s32[1]{0:T(128)} %bitcast.me_ref, ...), custom_call_target="tpu_custom_call" | custom-call | flops 2751463424 | bytes 8388608 | tf_op jit(solution)/shard_map/split_filter/pallas_call | solution.py:572
  54.5 0.0 collective-permute-start.8
  54.5 2.8 %collective-permute-start.9 = (bf16[272,128]{1,0:T(8,128)(2,1)S(1)}, bf16[272,128]{1,0:T(8,128)(2,1)S(1)}, u32[]{:S(2)}, u32[]{:S(2)}) collective-permute-start(bf16[272,128]{1,0:T(8,128)(2,1)S(1)} %get-tuple-element.29), channel_id=1, source_target_pairs={{0,9},{1,8},{2,11},{3,10},{4,13},{5,12},{6,15},{7,14},{8,1},{9,0},... | collective-permute-start | bytes 208904 | tf_op jit(solution)/shard_map/ppermute | solution.py:678
  57.3 0.2 collective-permute-start.10
  57.6 1.1 %collective-permute-done.8.earlier_ref.refs_1_ = bf16[272,128]{1,0:T(8,128)(2,1)S(1)} collective-permute-done((bf16[272,128]{1,0:T(8,128)(2,1)S(1)}, bf16[272,128]{1,0:T(8,128)(2,1)S(1)}, u32[]{:S(2)}, u32[]{:S(2)}) %collective-permute-start.8) | collective-permute-done | bytes 69664 | tf_op jit(solution)/shard_map/ppermute | solution.py:678
  58.7 9.9 %all-to-all-start.1 = ((bf16[8,272,128]{2,1,0:T(8,128)(2,1)}), bf16[8,272,128]{2,1,0:T(8,128)(2,1)S(1)}, u32[]{:S(2)}, u32[]{:S(2)}) async-start(bf16[8,272,128]{2,1,0:T(8,128)(2,1)} %hold.1), calls=%async_computation.1 | async-start | bytes 1114112 | tf_op jit(solution)/shard_map/all_to_all | solution.py:669
  68.6 0.3 collective-permute-start.11
  68.9 2.3 %collective-permute-start.12 = (bf16[272,128]{1,0:T(8,128)(2,1)S(1)}, bf16[272,128]{1,0:T(8,128)(2,1)S(1)}, u32[]{:S(2)}, u32[]{:S(2)}) collective-permute-start(bf16[272,128]{1,0:T(8,128)(2,1)S(1)} %get-tuple-element.32), channel_id=1, source_target_pairs={{0,12},{1,13},{2,14},{3,15},{4,8},{5,9},{6,10},{7,11},{8,4},{9,5},... | collective-permute-start | bytes 208904 | tf_op jit(solution)/shard_map/ppermute | solution.py:678
  71.2 0.1 collective-permute-start.13
  71.3 0.0 collective-permute-done.9.refs_2_
  71.3 1.5 %collective-permute-start.14 = (bf16[272,128]{1,0:T(8,128)(2,1)S(1)}, bf16[272,128]{1,0:T(8,128)(2,1)S(1)}, u32[]{:S(2)}, u32[]{:S(2)}) collective-permute-start(bf16[272,128]{1,0:T(8,128)(2,1)S(1)} %get-tuple-element.34), channel_id=1, source_target_pairs={{0,14},{1,15},{2,12},{3,13},{4,10},{5,11},{6,8},{7,9},{8,6},{9,7},... | collective-permute-start | bytes 208904 | tf_op jit(solution)/shard_map/ppermute | solution.py:678
  72.8 0.0 collective-permute-done.10.refs_3_
  72.8 1.4 %collective-permute-start.15 = (bf16[272,128]{1,0:T(8,128)(2,1)S(1)}, bf16[272,128]{1,0:T(8,128)(2,1)S(1)}, u32[]{:S(2)}, u32[]{:S(2)}) collective-permute-start(bf16[272,128]{1,0:T(8,128)(2,1)S(1)} %get-tuple-element.35), channel_id=1, source_target_pairs={{0,15},{1,14},{2,13},{3,12},{4,11},{5,10},{6,9},{7,8},{8,7},{9,6},... | collective-permute-start | bytes 208904 | tf_op jit(solution)/shard_map/ppermute | solution.py:678
  74.2 1.3 %slice_bitcast_fusion.gates_ref = bf16[128,4096]{1,0:T(8,128)(2,1)S(1)} fusion(bf16[3,128,4096]{2,1,0:T(8,128)(2,1)} %streams_ref.3), kind=kLoop, calls=%fused_computation | loop fusion | bytes 2097152 | tf_op jit(solution)/shard_map/squeeze | solution.py:722
  76.8 1.0 %collective-permute-done.11.refs_4_ = bf16[272,128]{1,0:T(8,128)(2,1)S(1)} collective-permute-done((bf16[272,128]{1,0:T(8,128)(2,1)S(1)}, bf16[272,128]{1,0:T(8,128)(2,1)S(1)}, u32[]{:S(2)}, u32[]{:S(2)}) %collective-permute-start.11) | collective-permute-done | bytes 69664 | tf_op jit(solution)/shard_map/ppermute | solution.py:678
  77.9 0.0 collective-permute-done.12.refs_5_
  77.9 6.9 %collective-permute-done.13.refs_6_ = bf16[272,128]{1,0:T(8,128)(2,1)S(1)} collective-permute-done((bf16[272,128]{1,0:T(8,128)(2,1)S(1)}, bf16[272,128]{1,0:T(8,128)(2,1)S(1)}, u32[]{:S(2)}, u32[]{:S(2)}) %collective-permute-start.13) | collective-permute-done | bytes 69664 | tf_op jit(solution)/shard_map/ppermute | solution.py:678
  84.8 0.3 collective-permute-done.14.refs_7_
  85.1 1.6 %collective-permute-done.15.refs_8_ = bf16[272,128]{1,0:T(8,128)(2,1)S(1)} collective-permute-done((bf16[272,128]{1,0:T(8,128)(2,1)S(1)}, bf16[272,128]{1,0:T(8,128)(2,1)S(1)}, u32[]{:S(2)}, u32[]{:S(2)}) %collective-permute-start.15) | collective-permute-done | bytes 69664 | tf_op jit(solution)/shard_map/ppermute | solution.py:678
  86.7 0.0 all-to-all-done.1.refs_0_
  86.7 1.3 %split_finish.1 = (bf16[128,4096]{1,0:T(8,128)(2,1)}, f32[2,1]{1,0:T(2,128)S(1)}) custom-call(s32[1]{0:T(128)} %bitcast.me_ref, s32[1]{0:T(128)S(6)} %copy.15.ref_ref, s32[1]{0:T(128)S(6)} %copy.16.alt_ref, bf16[128,4096]{1,0:T(8,128)(2,1)S(1)} %slice_bitcast_fusion.gates_ref, bf16[8,272,128]{2,1,0:T(8,128)(2,1)S(1)} %all-to-all-done.1.refs_0_, ...), custom_call_target="tpu_custom_call" | custom-call | flops 524288 | bytes 3145728 | tf_op jit(solution)/shard_map/split_finish/pallas_call | solution.py:630
  88.0 0.6 copy.13
  (10 shorter events, 0.0 us)
Async XLA Ops:
  3.7 14.9 %copy-start.13 = (bf16[272,128]{1,0:T(8,128)(2,1)S(1)}, bf16[272,128]{1,0:T(8,128)(2,1)}, u32[]{:S(2)}) copy-start(bf16[272,128]{1,0:T(8,128)(2,1)} %get-tuple-element.20) | copy-start | bytes 208900
  3.7 17.4 %copy-start.12 = (bf16[272,128]{1,0:T(8,128)(2,1)S(1)}, bf16[272,128]{1,0:T(8,128)(2,1)}, u32[]{:S(2)}) copy-start(bf16[272,128]{1,0:T(8,128)(2,1)} %get-tuple-element.21) | copy-start | bytes 208900
  3.7 18.4 %copy-start.11 = (bf16[272,128]{1,0:T(8,128)(2,1)S(1)}, bf16[272,128]{1,0:T(8,128)(2,1)}, u32[]{:S(2)}) copy-start(bf16[272,128]{1,0:T(8,128)(2,1)} %get-tuple-element.22) | copy-start | bytes 208900
  3.7 20.9 %copy-start.10 = (bf16[272,128]{1,0:T(8,128)(2,1)S(1)}, bf16[272,128]{1,0:T(8,128)(2,1)}, u32[]{:S(2)}) copy-start(bf16[272,128]{1,0:T(8,128)(2,1)} %get-tuple-element.23) | copy-start | bytes 208900
  3.7 20.9 %copy-start.9 = (bf16[272,128]{1,0:T(8,128)(2,1)S(1)}, bf16[272,128]{1,0:T(8,128)(2,1)}, u32[]{:S(2)}) copy-start(bf16[272,128]{1,0:T(8,128)(2,1)} %get-tuple-element.24) | copy-start | bytes 208900
  3.7 22.6 %copy-start.6 = (s32[16]{0:T(128)S(1)}, s32[16]{0:T(128)}, u32[]{:S(2)}) copy-start(s32[16]{0:T(128)} %offsets_ref.3) | copy-start | bytes 196
  3.7 26.2 %copy-start.8 = (bf16[272,128]{1,0:T(8,128)(2,1)S(1)}, bf16[272,128]{1,0:T(8,128)(2,1)}, u32[]{:S(2)}) copy-start(bf16[272,128]{1,0:T(8,128)(2,1)} %get-tuple-element.25) | copy-start | bytes 208900
  3.7 27.9 %copy-start.7 = (bf16[272,128]{1,0:T(8,128)(2,1)S(1)}, bf16[272,128]{1,0:T(8,128)(2,1)}, u32[]{:S(2)}) copy-start(bf16[272,128]{1,0:T(8,128)(2,1)} %get-tuple-element.26) | copy-start | bytes 208900
  3.7 40.6 %copy-start.2 = (bf16[256,2048]{1,0:T(8,128)(2,1)S(1)}, bf16[256,2048]{1,0:T(8,128)(2,1)}, u32[]{:S(2)}) copy-start(bf16[256,2048]{1,0:T(8,128)(2,1)} %refs_3_.1) | copy-start | bytes 3145732
  3.7 40.6 %copy-start.3 = (bf16[256,512]{1,0:T(8,128)(2,1)S(1)}, bf16[256,512]{1,0:T(8,128)(2,1)}, u32[]{:S(2)}) copy-start(bf16[256,512]{1,0:T(8,128)(2,1)} %refs_2_.1) | copy-start | bytes 786436
  3.8 40.6 %copy-start.4 = (bf16[512,512]{1,0:T(8,128)(2,1)S(1)}, bf16[512,512]{1,0:T(8,128)(2,1)}, u32[]{:S(2)}) copy-start(bf16[512,512]{1,0:T(8,128)(2,1)} %constant.17.clone.refs_1_) | copy-start | bytes 1572868
  3.8 5.5 %collective-permute-start = (bf16[272,128]{1,0:T(8,128)(2,1)}, bf16[272,128]{1,0:T(8,128)(2,1)S(1)}, u32[]{:S(2)}, u32[]{:S(2)}) collective-permute-start(bf16[272,128]{1,0:T(8,128)(2,1)} %get-tuple-element.19), channel_id=1, source_target_pairs={{0,8},{1,9},{2,10},{3,11},{4,12},{5,13},{6,14},{7,15},{8,0},{9,1},... | collective-permute-start | bytes 208904 | tf_op jit(solution)/shard_map/ppermute | solution.py:678
  9.3 0.6 copy-start
  13.0 31.4 %all-to-all-start = ((bf16[8,272,128]{2,1,0:T(8,128)(2,1)}), bf16[8,272,128]{2,1,0:T(8,128)(2,1)S(1)}, u32[]{:S(2)}, u32[]{:S(2)}) async-start(bf16[8,272,128]{2,1,0:T(8,128)(2,1)} %send_products.3), calls=%async_computation | async-start | bytes 1114112 | tf_op jit(solution)/shard_map/all_to_all | solution.py:669
  18.5 11.4 %collective-permute-start.1 = (bf16[272,128]{1,0:T(8,128)(2,1)S(1)}, bf16[272,128]{1,0:T(8,128)(2,1)S(1)}, u32[]{:S(2)}, u32[]{:S(2)}) collective-permute-start(bf16[272,128]{1,0:T(8,128)(2,1)S(1)} %copy-done.13), channel_id=1, source_target_pairs={{0,9},{1,8},{2,11},{3,10},{4,13},{5,12},{6,15},{7,14},{8,1},{9,0},... | collective-permute-start | bytes 208904 | tf_op jit(solution)/shard_map/ppermute | solution.py:678
  21.0 10.6 %collective-permute-start.2 = (bf16[272,128]{1,0:T(8,128)(2,1)S(1)}, bf16[272,128]{1,0:T(8,128)(2,1)S(1)}, u32[]{:S(2)}, u32[]{:S(2)}) collective-permute-start(bf16[272,128]{1,0:T(8,128)(2,1)S(1)} %copy-done.12), channel_id=1, source_target_pairs={{0,10},{1,11},{2,8},{3,9},{4,14},{5,15},{6,12},{7,13},{8,2},{9,3},... | collective-permute-start | bytes 208904 | tf_op jit(solution)/shard_map/ppermute | solution.py:678
  22.1 14.7 %collective-permute-start.3 = (bf16[272,128]{1,0:T(8,128)(2,1)S(1)}, bf16[272,128]{1,0:T(8,128)(2,1)S(1)}, u32[]{:S(2)}, u32[]{:S(2)}) collective-permute-start(bf16[272,128]{1,0:T(8,128)(2,1)S(1)} %copy-done.11), channel_id=1, source_target_pairs={{0,11},{1,10},{2,9},{3,8},{4,15},{5,14},{6,13},{7,12},{8,3},{9,2},... | collective-permute-start | bytes 208904 | tf_op jit(solution)/shard_map/ppermute | solution.py:678
  24.6 14.7 %collective-permute-start.4 = (bf16[272,128]{1,0:T(8,128)(2,1)S(1)}, bf16[272,128]{1,0:T(8,128)(2,1)S(1)}, u32[]{:S(2)}, u32[]{:S(2)}) collective-permute-start(bf16[272,128]{1,0:T(8,128)(2,1)S(1)} %copy-done.10), channel_id=1, source_target_pairs={{0,12},{1,13},{2,14},{3,15},{4,8},{5,9},{6,10},{7,11},{8,4},{9,5},... | collective-permute-start | bytes 208904 | tf_op jit(solution)/shard_map/ppermute | solution.py:678
  24.6 16.4 %collective-permute-start.5 = (bf16[272,128]{1,0:T(8,128)(2,1)S(1)}, bf16[272,128]{1,0:T(8,128)(2,1)S(1)}, u32[]{:S(2)}, u32[]{:S(2)}) collective-permute-start(bf16[272,128]{1,0:T(8,128)(2,1)S(1)} %copy-done.9), channel_id=1, source_target_pairs={{0,13},{1,12},{2,15},{3,14},{4,9},{5,8},{6,11},{7,10},{8,5},{9,4},... | collective-permute-start | bytes 208904 | tf_op jit(solution)/shard_map/ppermute | solution.py:678
  30.0 12.8 %collective-permute-start.6 = (bf16[272,128]{1,0:T(8,128)(2,1)S(1)}, bf16[272,128]{1,0:T(8,128)(2,1)S(1)}, u32[]{:S(2)}, u32[]{:S(2)}) collective-permute-start(bf16[272,128]{1,0:T(8,128)(2,1)S(1)} %copy-done.8), channel_id=1, source_target_pairs={{0,14},{1,15},{2,12},{3,13},{4,10},{5,11},{6,8},{7,9},{8,6},{9,7},... | collective-permute-start | bytes 208904 | tf_op jit(solution)/shard_map/ppermute | solution.py:678
  31.6 12.7 %collective-permute-start.7 = (bf16[272,128]{1,0:T(8,128)(2,1)S(1)}, bf16[272,128]{1,0:T(8,128)(2,1)S(1)}, u32[]{:S(2)}, u32[]{:S(2)}) collective-permute-start(bf16[272,128]{1,0:T(8,128)(2,1)S(1)} %copy-done.7), channel_id=1, source_target_pairs={{0,15},{1,14},{2,13},{3,12},{4,11},{5,10},{6,9},{7,8},{8,7},{9,6},... | collective-permute-start | bytes 208904 | tf_op jit(solution)/shard_map/ppermute | solution.py:678
  44.4 0.9 copy-start.1
  45.3 1.0 %copy-start.5 = (bf16[1024,256]{1,0:T(8,128)(2,1)S(1)}, bf16[1024,256]{1,0:T(8,128)(2,1)}, u32[]{:S(2)}) copy-start(bf16[1024,256]{1,0:T(8,128)(2,1)} %constant.16.clone.refs_0_) | copy-start | bytes 1572868
  54.5 4.2 %collective-permute-start.8 = (bf16[272,128]{1,0:T(8,128)(2,1)S(1)}, bf16[272,128]{1,0:T(8,128)(2,1)S(1)}, u32[]{:S(2)}, u32[]{:S(2)}) collective-permute-start(bf16[272,128]{1,0:T(8,128)(2,1)S(1)} %get-tuple-element.28), channel_id=1, source_target_pairs={{0,8},{1,9},{2,10},{3,11},{4,12},{5,13},{6,14},{7,15},{8,0},{9,1},... | collective-permute-start | bytes 208904 | tf_op jit(solution)/shard_map/ppermute | solution.py:678
  54.5 16.8 %collective-permute-start.9 = (bf16[272,128]{1,0:T(8,128)(2,1)S(1)}, bf16[272,128]{1,0:T(8,128)(2,1)S(1)}, u32[]{:S(2)}, u32[]{:S(2)}) collective-permute-start(bf16[272,128]{1,0:T(8,128)(2,1)S(1)} %get-tuple-element.29), channel_id=1, source_target_pairs={{0,9},{1,8},{2,11},{3,10},{4,13},{5,12},{6,15},{7,14},{8,1},{9,0},... | collective-permute-start | bytes 208904 | tf_op jit(solution)/shard_map/ppermute | solution.py:678
  57.3 15.5 %collective-permute-start.10 = (bf16[272,128]{1,0:T(8,128)(2,1)S(1)}, bf16[272,128]{1,0:T(8,128)(2,1)S(1)}, u32[]{:S(2)}, u32[]{:S(2)}) collective-permute-start(bf16[272,128]{1,0:T(8,128)(2,1)S(1)} %get-tuple-element.30), channel_id=1, source_target_pairs={{0,10},{1,11},{2,8},{3,9},{4,14},{5,15},{6,12},{7,13},{8,2},{9,3},... | collective-permute-start | bytes 208904 | tf_op jit(solution)/shard_map/ppermute | solution.py:678
  58.7 28.1 %all-to-all-start.1 = ((bf16[8,272,128]{2,1,0:T(8,128)(2,1)}), bf16[8,272,128]{2,1,0:T(8,128)(2,1)S(1)}, u32[]{:S(2)}, u32[]{:S(2)}) async-start(bf16[8,272,128]{2,1,0:T(8,128)(2,1)} %hold.1), calls=%async_computation.1 | async-start | bytes 1114112 | tf_op jit(solution)/shard_map/all_to_all | solution.py:669
  68.6 9.2 %collective-permute-start.11 = (bf16[272,128]{1,0:T(8,128)(2,1)S(1)}, bf16[272,128]{1,0:T(8,128)(2,1)S(1)}, u32[]{:S(2)}, u32[]{:S(2)}) collective-permute-start(bf16[272,128]{1,0:T(8,128)(2,1)S(1)} %get-tuple-element.31), channel_id=1, source_target_pairs={{0,11},{1,10},{2,9},{3,8},{4,15},{5,14},{6,13},{7,12},{8,3},{9,2},... | collective-permute-start | bytes 208904 | tf_op jit(solution)/shard_map/ppermute | solution.py:678
  68.9 8.9 %collective-permute-start.12 = (bf16[272,128]{1,0:T(8,128)(2,1)S(1)}, bf16[272,128]{1,0:T(8,128)(2,1)S(1)}, u32[]{:S(2)}, u32[]{:S(2)}) collective-permute-start(bf16[272,128]{1,0:T(8,128)(2,1)S(1)} %get-tuple-element.32), channel_id=1, source_target_pairs={{0,12},{1,13},{2,14},{3,15},{4,8},{5,9},{6,10},{7,11},{8,4},{9,5},... | collective-permute-start | bytes 208904 | tf_op jit(solution)/shard_map/ppermute | solution.py:678
  71.2 13.5 %collective-permute-start.13 = (bf16[272,128]{1,0:T(8,128)(2,1)S(1)}, bf16[272,128]{1,0:T(8,128)(2,1)S(1)}, u32[]{:S(2)}, u32[]{:S(2)}) collective-permute-start(bf16[272,128]{1,0:T(8,128)(2,1)S(1)} %get-tuple-element.33), channel_id=1, source_target_pairs={{0,13},{1,12},{2,15},{3,14},{4,9},{5,8},{6,11},{7,10},{8,5},{9,4},... | collective-permute-start | bytes 208904 | tf_op jit(solution)/shard_map/ppermute | solution.py:678
  71.3 13.8 %collective-permute-start.14 = (bf16[272,128]{1,0:T(8,128)(2,1)S(1)}, bf16[272,128]{1,0:T(8,128)(2,1)S(1)}, u32[]{:S(2)}, u32[]{:S(2)}) collective-permute-start(bf16[272,128]{1,0:T(8,128)(2,1)S(1)} %get-tuple-element.34), channel_id=1, source_target_pairs={{0,14},{1,15},{2,12},{3,13},{4,10},{5,11},{6,8},{7,9},{8,6},{9,7},... | collective-permute-start | bytes 208904 | tf_op jit(solution)/shard_map/ppermute | solution.py:678
  72.8 13.9 %collective-permute-start.15 = (bf16[272,128]{1,0:T(8,128)(2,1)S(1)}, bf16[272,128]{1,0:T(8,128)(2,1)S(1)}, u32[]{:S(2)}, u32[]{:S(2)}) collective-permute-start(bf16[272,128]{1,0:T(8,128)(2,1)S(1)} %get-tuple-element.35), channel_id=1, source_target_pairs={{0,15},{1,14},{2,13},{3,12},{4,11},{5,10},{6,9},{7,8},{8,7},{9,6},... | collective-permute-start | bytes 208904 | tf_op jit(solution)/shard_map/ppermute | solution.py:678

commit v6 on v4

--- a/solution.py
+++ b/solution.py
@@ -100,8 +100,7 @@
     )(local_rows, streams)
 
 
-def spectrum_kernel(block, filter_ref, forward_ref, *refs):
-    out_ref = refs[-1]
+def spectrum_kernel(block, filter_ref, forward_ref, out_ref):
     n_blocks = out_ref.shape[0]
     for index in range(n_blocks):
         taps = filter_ref[:, index * block : (index + 1) * block]
@@ -111,12 +110,12 @@
         out_ref[index] = both[: 2 * block] + both[2 * block :]
 
 
-def filter_spectrum(taps, forward, block, *earlier):
+def filter_spectrum(taps, forward, block):
     width, length = taps.shape
     n_blocks = length // block
     return pl.pallas_call(
         functools.partial(spectrum_kernel, block),
-        in_specs=[whole_spec(), whole_spec()] + [pl.BlockSpec(memory_space=pl.ANY)] * len(earlier),
+        in_specs=[whole_spec()] * 2,
         out_specs=whole_spec(),
         out_shape=jax.ShapeDtypeStruct((n_blocks, 2 * block, width), f32),
         compiler_params=pltpu.CompilerParams(vmem_limit_bytes=40 * MIB),
@@ -124,7 +123,7 @@
             flops=8 * block * length * width, bytes_accessed=4 * MIB, transcendentals=0
         ),
         name="filter_spectrum",
-    )(taps, forward, *earlier)
+    )(taps, forward)
 
 
 def multiply_points(points, spectrum_ref, joint):
@@ -220,19 +219,21 @@
     return jnp.dot(weighted, unembed, preferred_element_type=f32), rows * rows
 
 
-def pack_scores(raw, squares, vars_dev, packed, n_devices):
+def pack_scores(raw, squares, raw_parts, vars_dev, packed, n_devices):
     total, width = packed.shape
     extra = total // n_devices
     per_row = raw.shape[1] // width
+    count = raw_parts * per_row + 2
     packed[...] = jnp.zeros_like(packed)
     for var in range(vars_dev):
         mine = slice(var * n_devices, (var + 1) * n_devices)
-        pieces = [raw[mine, r * width : (r + 1) * width] for r in range(per_row)] + [squares[mine]]
-        for row, piece in enumerate(pieces):
-            rounded = piece.astype(bf16).astype(f32)
-            base = var * 2 * (per_row + 1) + row
-            packed[pl.ds(base, n_devices, stride=extra), :] = rounded
-            packed[pl.ds(base + per_row + 1, n_devices, stride=extra), :] = piece - rounded
+        pieces = [raw[mine, r * width : (r + 1) * width] for r in range(per_row)]
+        rounded = [piece.astype(bf16).astype(f32) for piece in pieces]
+        rows = rounded + [piece - high for piece, high in zip(pieces, rounded)][: (raw_parts - 1) * per_row]
+        high = squares[mine].astype(bf16).astype(f32)
+        rows += [high, squares[mine] - high]
+        for row, piece in enumerate(rows):
+            packed[pl.ds(var * count + row, n_devices, stride=extra), :] = piece
 
 
 def chunk_kernel(index, chunks, vars_dev, tok_rows, *refs):
@@ -264,7 +265,7 @@
     packed = refs[1]
     n_devices, _, width = out_ref.shape
     extra = out_ref.shape[1] - tok_rows
-    pack_scores(raw, squares, vars_dev, packed, n_devices)
+    pack_scores(raw, squares, 2, vars_dev, packed, n_devices)
     out_ref[:, tok_rows:, :] = packed[...].reshape(n_devices, extra, width).astype(bf16)
 
 
@@ -298,30 +299,32 @@
     )(*operands, *carried)
 
 
-def final_scores(sums, vars_dev, vocab, model_width, ref_ref, alt_ref):
+def final_scores(sums, raw_parts, vars_dev, vocab, model_width, ref_ref, alt_ref):
     width = sums.shape[1]
     per_row = vocab // width
+    count = raw_parts * per_row + 2
     ids = lax.broadcasted_iota(jnp.int32, (per_row, width), 0) * width
     ids += lax.broadcasted_iota(jnp.int32, (per_row, width), 1)
-    row = lax.broadcasted_iota(jnp.int32, (2, vars_dev), 0)
-    column = lax.broadcasted_iota(jnp.int32, (2, vars_dev), 1)
-    scores = jnp.zeros((2, vars_dev), f32)
+    row = lax.broadcasted_iota(jnp.int32, (vars_dev, 2), 0)
+    column = lax.broadcasted_iota(jnp.int32, (vars_dev, 2), 1)
+    scores = jnp.zeros((vars_dev, 2), f32)
 
     def whole_sum(values):
         return jnp.sum(jnp.sum(values, axis=1, keepdims=True), axis=0, keepdims=True)
 
     for var in range(vars_dev):
-        base = var * 2 * (per_row + 1)
-        both = sums[base : base + per_row + 1, :]
-        both = both + sums[base + per_row + 1 : base + 2 * (per_row + 1), :]
-        square = jnp.sum(both[per_row:, :], axis=1, keepdims=True)
-        logits = both[:per_row, :] * lax.rsqrt(square / model_width + norm_eps)
+        base = var * count
+        raw = sums[base : base + per_row, :]
+        if raw_parts == 2:
+            raw = raw + sums[base + per_row : base + 2 * per_row, :]
+        square = whole_sum(sums[base + count - 2 : base + count, :])
+        logits = raw * lax.rsqrt(square / model_width + norm_eps)
         largest = jnp.max(jnp.max(logits, axis=1, keepdims=True), axis=0, keepdims=True)
         log_total = largest + jnp.log(whole_sum(jnp.exp(logits - largest)))
         ref_logit = whole_sum(jnp.where(ids == ref_ref[var], logits, 0.0))
         alt_logit = whole_sum(jnp.where(ids == alt_ref[var], logits, 0.0))
-        pair = jnp.where(row == 0, ref_logit - log_total, alt_logit - ref_logit)
-        scores = jnp.where(column == var, pair, scores)
+        pair = jnp.where(column == 0, ref_logit - log_total, alt_logit - ref_logit)
+        scores = jnp.where(row == var, pair, scores)
     return scores
 
 
@@ -349,7 +352,7 @@
     @pl.when(step == pl.num_programs(0) - 1)
     def _():
         model_width = pl.num_programs(0) * owners * chunks * width
-        scores_ref[...] = final_scores(sums[...], vars_dev, vocab, model_width, ref_ref, alt_ref)
+        scores_ref[...] = final_scores(sums[...], 2, vars_dev, vocab, model_width, ref_ref, alt_ref)
 
 
 def finish(streams, backs, ref_ids, alt_ids, vocab):
@@ -372,136 +375,106 @@
         + [pl.BlockSpec((owners, back.shape[1], width), lambda i: (i, 0, 0)) for back in backs],
         out_specs=[
             pl.BlockSpec((tok_rows, owners * chunks * width), lambda i: (0, i)),
-            pl.BlockSpec((2, vars_dev), lambda i: (0, 0)),
+            pl.BlockSpec((vars_dev, 2), lambda i: (0, 0)),
         ],
         out_shape=[
             jax.ShapeDtypeStruct((tok_rows, model_width), bf16),
-            jax.ShapeDtypeStruct((2, vars_dev), f32),
+            jax.ShapeDtypeStruct((vars_dev, 2), f32),
         ],
         scratch_shapes=[pltpu.VMEM((extra, width), f32)],
         compiler_params=pltpu.CompilerParams(vmem_limit_bytes=24 * MIB),
         name="finish",
     )(ref_ids, alt_ids, streams, *backs)
 
-def send_products_kernel(halves, vars_dev, me_ref, offsets_ref, streams_ref, out_ref, *scratch):
-    built, pairs, gates, gate_rows, pair_sems, gate_sems, out_sems = scratch
-    n_devices, _, tok_rows, width = pairs.shape
+def stacked_products_kernel(halves, vars_dev, me_ref, offsets_ref, streams_ref, out_ref):
+    _, tok_rows, model_width = streams_ref.shape
+    n_devices = out_ref.shape[0]
+    extra = out_ref.shape[1] - halves * tok_rows
     me = me_ref[0]
     slot = tok_rows // vars_dev
-    local_rows = [var * slot + offsets_ref[me * vars_dev + var] for var in range(vars_dev)]
-
-    def pair_copy(owner):
-        return pltpu.make_async_copy(
-            streams_ref.at[pl.ds(1, 2), :, pl.ds(owner * width, width)],
-            pairs.at[owner],
-            pair_sems.at[owner],
-        )
-
-    def gate_copy(var):
-        start = pl.multiple_of(local_rows[var] // row_tile * row_tile, row_tile)
-        return pltpu.make_async_copy(
-            streams_ref.at[0, pl.ds(start, row_tile), :], gates.at[var], gate_sems.at[var]
-        )
-
-    def out_copy(owner):
-        return pltpu.make_async_copy(built.at[owner], out_ref.at[owner], out_sems.at[owner])
-
+    row = lax.broadcasted_iota(jnp.int32, (row_tile, model_width), 0)
+    place = lax.broadcasted_iota(jnp.int32, (extra, lane_tile), 0)
+    gate_rows = []
     for var in range(vars_dev):
-        gate_copy(var).start()
+        local = var * slot + offsets_ref[me * vars_dev + var]
+        start = pl.multiple_of(local // row_tile * row_tile, row_tile)
+        tile = streams_ref[0, pl.ds(start, row_tile), :].astype(f32)
+        mine = jnp.where(row == local % row_tile, tile, 0.0)
+        gate_rows.append(jnp.sum(mine, axis=0, keepdims=True))
     for owner in range(n_devices):
-        pair_copy(owner).start()
-    row = lax.broadcasted_iota(jnp.int32, gates.shape[1:], 0)
-    for var in range(vars_dev):
-        gate_copy(var).wait()
-        mine = jnp.where(row == local_rows[var] % row_tile, gates[var].astype(f32), 0.0)
-        gate_rows[var : var + 1, :] = jnp.sum(mine, axis=0, keepdims=True)
-    extra = built.shape[1] - halves * tok_rows
-    place = lax.broadcasted_iota(jnp.int32, (extra, lane_tile), 0)
-    for owner in range(n_devices):
-        pair_copy(owner).wait()
         tail = jnp.zeros((extra, lane_tile), f32)
         for half in range(halves):
-            lanes = slice(half * lane_tile, (half + 1) * lane_tile)
+            start = (owner * halves + half) * lane_tile
+            lanes = slice(start, start + lane_tile)
             rows = slice(half * tok_rows, (half + 1) * tok_rows)
-            built[owner, rows, :] = pairs[owner, 0, :, lanes] * pairs[owner, 1, :, lanes]
-            start = owner * width + half * lane_tile
+            out_ref[owner, rows, :] = streams_ref[1, :, lanes] * streams_ref[2, :, lanes]
             for var in range(vars_dev):
-                mine = gate_rows[var : var + 1, start : start + lane_tile]
-                tail = jnp.where(place == half * vars_dev + var, mine, tail)
-        built[owner, halves * tok_rows :, :] = tail.astype(bf16)
-        out_copy(owner).start()
-    for owner in range(n_devices):
-        out_copy(owner).wait()
-
-
-def send_products(me, offsets, streams, vars_dev, n_devices, extra):
+                tail = jnp.where(place == half * vars_dev + var, gate_rows[var][:, lanes], tail)
+        out_ref[owner, halves * tok_rows :, :] = tail.astype(bf16)
+
+
+def stacked_products(me, offsets, streams, vars_dev, n_devices, extra):
     _, tok_rows, model_width = streams.shape
-    width = model_width // n_devices
-    halves = width // lane_tile
+    halves = model_width // n_devices // lane_tile
     rows_out = halves * tok_rows + extra
     return pl.pallas_call(
-        functools.partial(send_products_kernel, halves, vars_dev),
-        in_specs=[
-            pl.BlockSpec(memory_space=pltpu.SMEM),
-            pl.BlockSpec(memory_space=pltpu.SMEM),
-            pl.BlockSpec(memory_space=pl.ANY),
-        ],
-        out_specs=pl.BlockSpec(memory_space=pl.ANY),
+        functools.partial(stacked_products_kernel, halves, vars_dev),
+        in_specs=[pl.BlockSpec(memory_space=pltpu.SMEM)] * 2 + [whole_spec()],
+        out_specs=whole_spec(),
         out_shape=jax.ShapeDtypeStruct((n_devices, rows_out, lane_tile), bf16),
-        scratch_shapes=[
-            pltpu.VMEM((n_devices, rows_out, lane_tile), bf16),
-            pltpu.VMEM((n_devices, 2, tok_rows, width), bf16),
-            pltpu.VMEM((vars_dev, row_tile, model_width), bf16),
-            pltpu.VMEM((round_up(vars_dev, half_tile), model_width), f32),
-            pltpu.SemaphoreType.DMA((n_devices,)),
-            pltpu.SemaphoreType.DMA((vars_dev,)),
-            pltpu.SemaphoreType.DMA((n_devices,)),
-        ],
-        compiler_params=pltpu.CompilerParams(vmem_limit_bytes=60 * MIB),
+        compiler_params=pltpu.CompilerParams(vmem_limit_bytes=16 * MIB),
         cost_estimate=pl.CostEstimate(
             flops=tok_rows * model_width, bytes_accessed=6 * tok_rows * model_width, transcendentals=0
         ),
-        name="send_products",
+        name="stacked_products",
     )(me, offsets, streams)
 
 
 def stacked_filter_kernel(vars_dev, halves, tok_rows, *refs):
-    positions_ref, gain_ref, unembed_ref, forward_ref, inverse_ref, spectrum_ref = refs[:6]
-    arrived, leaving, points, joint, packed = refs[6:]
+    positions_ref, gain_ref, forward, inverse, unembed, taps, arrived = refs[:7]
+    leaving, points, joint, spectrum, packed = refs[7:]
     n_devices = arrived.shape[0]
     body = halves * tok_rows
     n_blocks, double, width = points.shape
     block = double // 2
     per_block = block // tok_rows
-
-    def forward_step(step, carry):
+    group = 2 if n_blocks % 2 == 0 else 1
+
+    for index in range(n_blocks):
+        both = lax.dot_general(
+            forward[...],
+            taps[:, index * block : (index + 1) * block],
+            (((1,), (1,)), ((), ())),
+            preferred_element_type=f32,
+        )
+        spectrum[index] = both[:double] + both[double:]
+
+    for step in range(0, n_blocks, group):
         pieces = []
-        for half in range(halves):
-            rows = slice(half * tok_rows, (half + 1) * tok_rows)
-            parts = [arrived[step * per_block + m, rows, :] for m in range(per_block)]
-            pieces.append(jnp.concatenate(parts, axis=0))
+        for index in range(step, step + group):
+            for half in range(halves):
+                rows = slice(half * tok_rows, (half + 1) * tok_rows)
+                parts = [arrived[index * per_block + m, rows, :] for m in range(per_block)]
+                pieces.append(jnp.concatenate(parts, axis=0))
         signal = jnp.concatenate(pieces, axis=1)
-        both = jnp.dot(forward_ref[...], signal, preferred_element_type=f32)
-        points[step] = both[:double] + both[double:]
-        return carry
-
-    lax.fori_loop(0, n_blocks, forward_step, 0)
-    multiply_points(points, spectrum_ref, joint)
-
-    def inverse_step(step, carry):
-        highs, lows = split_bf16(joint[step])
-        both = jnp.dot(inverse_ref[...], highs, preferred_element_type=f32)
-        rest = jnp.dot(inverse_ref[:block, :], lows, preferred_element_type=f32)
+        both = jnp.dot(forward[...], signal, preferred_element_type=f32)
+        total = both[:double] + both[double:]
+        for member in range(group):
+            points[step + member] = total[:, member * width : (member + 1) * width]
+    multiply_points(points, spectrum, joint)
+
+    for step in range(0, n_blocks, group):
+        highs, lows = split_bf16(jnp.concatenate([joint[step + m] for m in range(group)], axis=1))
+        both = jnp.dot(inverse[...], highs, preferred_element_type=f32)
+        rest = jnp.dot(inverse[:block, :], lows, preferred_element_type=f32)
         result = (both[:block] + both[block:] + rest).astype(bf16)
-        for member in range(per_block):
-            for half in range(halves):
-                leaving[step * per_block + member, half * tok_rows : (half + 1) * tok_rows, :] = result[
-                    member * tok_rows : (member + 1) * tok_rows,
-                    half * lane_tile : (half + 1) * lane_tile,
-                ]
-        return carry
-
-    lax.fori_loop(0, n_blocks, inverse_step, 0)
+        for index in range(group):
+            for member in range(per_block):
+                for half in range(halves):
+                    start = index * width + half * lane_tile
+                    leaving[
+                        (step + index) * per_block + member, half * tok_rows : (half + 1) * tok_rows, :
+                    ] = result[member * tok_rows : (member + 1) * tok_rows, start : start + lane_tile]
 
     length = n_devices * tok_rows
     column = lax.broadcasted_iota(jnp.int32, (positions_ref.shape[0], length), 1)
@@ -521,94 +494,83 @@
         filtered = jnp.dot(picker, filtered, preferred_element_type=f32)
         rows = (gate_rows * filtered).astype(bf16).astype(f32)
         weighted = (rows * gain_ref[:, lanes]).astype(bf16)
-        part = jnp.dot(weighted, unembed_ref[lanes, :], preferred_element_type=f32)
+        part = jnp.dot(weighted, unembed[lanes, :], preferred_element_type=f32)
         raw = part if raw is None else raw + part
         squares = rows * rows if squares is None else squares + rows * rows
-    pack_scores(raw, squares, vars_dev, packed, n_devices)
+    pack_scores(raw, squares, 1, vars_dev, packed, n_devices)
     extra = packed.shape[0] // n_devices
     leaving[:, body:, :] = packed[...].reshape(n_devices, extra, lane_tile).astype(bf16)
 
 
-def stacked_filter(operands, arrived, vars_dev, tok_rows, extra):
+def stacked_filter(positions, gain_row, tables, arrived, vars_dev, tok_rows, extra):
+    width, length = tables[3].shape
     n_devices = arrived.shape[0]
-    n_blocks, double, width = operands[-1].shape
+    double = tables[0].shape[0] // 2
+    n_blocks = 2 * length // double
     halves = width // lane_tile
     rows_out = halves * tok_rows + extra
     flops = 2 * width * n_blocks * (double * double * 5 // 2 + 4 * n_blocks * double)
     return pl.pallas_call(
         functools.partial(stacked_filter_kernel, vars_dev, halves, tok_rows),
-        in_specs=[whole_spec()] * (len(operands) + 1),
+        in_specs=[whole_spec()] * 7,
         out_specs=whole_spec(),
         out_shape=jax.ShapeDtypeStruct((n_devices, rows_out, lane_tile), bf16),
-        scratch_shapes=[
-            pltpu.VMEM((n_blocks, double, width), f32),
-            pltpu.VMEM((n_blocks, double, width), f32),
-            pltpu.VMEM((n_devices * extra, lane_tile), f32),
-        ],
-        compiler_params=pltpu.CompilerParams(vmem_limit_bytes=32 * MIB),
+        scratch_shapes=[pltpu.VMEM((n_blocks, double, width), f32)] * 3
+        + [pltpu.VMEM((n_devices * extra, lane_tile), f32)],
+        compiler_params=pltpu.CompilerParams(vmem_limit_bytes=24 * MIB),
         cost_estimate=pl.CostEstimate(flops=flops, bytes_accessed=8 * MIB, transcendentals=0),
         name="stacked_filter",
-    )(*operands, arrived)
-
-
-def stacked_finish_kernel(halves, vars_dev, vocab, ref_ref, alt_ref, streams_ref, back_ref, *refs):
-    mixed_ref, scores_ref, gates, results, gate_sems, out_sems = refs
-    n_devices, tok_rows, width = gates.shape
-
-    def gate_copy(owner):
-        return pltpu.make_async_copy(
-            streams_ref.at[0, :, pl.ds(owner * width, width)], gates.at[owner], gate_sems.at[owner]
-        )
+    )(positions, gain_row, *tables, arrived)
+
+
+def stacked_finish_kernel(halves, vars_dev, vocab, ref_ref, alt_ref, gates_ref, back_ref, *refs):
+    mixed_ref, scores_ref, results, out_sems = refs
+    n_devices, tok_rows, width = results.shape
 
     def out_copy(owner):
         return pltpu.make_async_copy(
             results.at[owner], mixed_ref.at[:, pl.ds(owner * width, width)], out_sems.at[owner]
         )
 
-    for owner in range(n_devices):
-        gate_copy(owner).start()
     sums = None
     for owner in range(n_devices):
-        gate_copy(owner).wait()
         for half in range(halves):
             lanes = slice(half * lane_tile, (half + 1) * lane_tile)
+            start = owner * width + half * lane_tile
             filtered = back_ref[owner, half * tok_rows : (half + 1) * tok_rows, :]
-            results[owner, :, lanes] = gates[owner, :, lanes] * filtered
+            results[owner, :, lanes] = gates_ref[:, start : start + lane_tile] * filtered
         out_copy(owner).start()
         tail = back_ref[owner, halves * tok_rows :, :].astype(f32)
         sums = tail if sums is None else sums + tail
     model_width = n_devices * width
-    scores_ref[...] = final_scores(sums, vars_dev, vocab, model_width, ref_ref, alt_ref)
+    scores_ref[...] = final_scores(sums, 1, vars_dev, vocab, model_width, ref_ref, alt_ref)
     for owner in range(n_devices):
         out_copy(owner).wait()
 
 
-def stacked_finish(ref_ids, alt_ids, streams, back, vocab):
-    _, tok_rows, model_width = streams.shape
+def stacked_finish(ref_ids, alt_ids, gates, back, vocab):
+    tok_rows, model_width = gates.shape
     n_devices = back.shape[0]
     vars_dev = ref_ids.shape[0]
     width = model_width // n_devices
     return pl.pallas_call(
         functools.partial(stacked_finish_kernel, width // lane_tile, vars_dev, vocab),
-        in_specs=[pl.BlockSpec(memory_space=pltpu.SMEM)] * 2
-        + [pl.BlockSpec(memory_space=pl.ANY), whole_spec()],
+        in_specs=[pl.BlockSpec(memory_space=pltpu.SMEM)] * 2 + [whole_spec()] * 2,
         out_specs=[pl.BlockSpec(memory_space=pl.ANY), whole_spec()],
         out_shape=[
             jax.ShapeDtypeStruct((tok_rows, model_width), bf16),
-            jax.ShapeDtypeStruct((2, vars_dev), f32),
+            jax.ShapeDtypeStruct((vars_dev, 2), f32),
         ],
         scratch_shapes=[
             pltpu.VMEM((n_devices, tok_rows, width), bf16),
-            pltpu.VMEM((n_devices, tok_rows, width), bf16),
-            pltpu.SemaphoreType.DMA((n_devices,)),
             pltpu.SemaphoreType.DMA((n_devices,)),
         ],
-        compiler_params=pltpu.CompilerParams(vmem_limit_bytes=12 * MIB),
+        compiler_params=pltpu.CompilerParams(vmem_limit_bytes=16 * MIB),
         cost_estimate=pl.CostEstimate(
             flops=tok_rows * model_width, bytes_accessed=6 * tok_rows * model_width, transcendentals=0
         ),
         name="stacked_finish",
-    )(ref_ids, alt_ids, streams, back)
+    )(ref_ids, alt_ids, gates, back)
 
 
 def transposed(blocks):
@@ -639,15 +601,15 @@
 
     if chunks * lane_tile == group_width:
         me = jnp.reshape(my_index, (1,)).astype(jnp.int32)
-        gate_extra = round_up(chunks * vars_dev, row_tile)
-        score_extra = round_up(vars_dev * 2 * (vocab // lane_tile + 1), row_tile)
-        blocks = send_products(me, offsets, streams, vars_dev, n_devices, gate_extra)
-        arrived = transposed(blocks)
-        spectrum = filter_spectrum(long_filter, forward, block, blocks)
-        operands = (positions, my_gain[None, :], unembed, forward, inverse, spectrum)
-        leaving = stacked_filter(operands, arrived, vars_dev, tok_rows, score_extra)
-        mixed, scores = stacked_finish(ref_ids, alt_ids, streams, transposed(leaving), vocab)
-        return (mixed, scores)
+        gate_extra = round_up(chunks * vars_dev, half_tile)
+        score_extra = round_up(vars_dev * (vocab // lane_tile + 2), half_tile)
+        arrived = transposed(stacked_products(me, offsets, streams, vars_dev, n_devices, gate_extra))
+        tables = (forward, inverse, unembed, long_filter)
+        gain_row = my_gain[None, :]
+        leaving = stacked_filter(positions, gain_row, tables, arrived, vars_dev, tok_rows, score_extra)
+        back = transposed(leaving)
+        mixed, scores = stacked_finish(ref_ids, alt_ids, streams[0], back, vocab)
+        return (mixed, scores.T)
 
     gate_extra = round_up(chunks * vars_dev, row_tile)
     score_extra = round_up(vars_dev * 2 * (vocab // width + 1), row_tile)
@@ -670,7 +632,7 @@
             gates = results[3]
         backs.append(lax.all_to_all(results[0], "seq", split_axis=0, concat_axis=0, tiled=True))
     mixed, scores = finish(streams, backs, ref_ids, alt_ids, vocab)
-    return (mixed, scores)
+    return (mixed, scores.T)
 
 
 def solution(mesh):

time: 89 us -> 78.5 us (0.88)
  local copies, waits for them, and re-layouts: 11.2 us -> 3.94 us
  Pallas kernels: 16.5 us -> 12 us
  waiting for transfers between devices: 46.1 us -> 47.7 us
    unnamed x26 -> x14, local copies, waits for them, and re-layouts: 10.5 us -> 2.56 us
    pallas_call x2 -> x1, Pallas kernels: 4.99 us -> 1.77 us  [stacked_products(): pl.pallas_call(functools.partial(stacked_products_kernel, halves, vars_de...]
    all_to_all x2, waiting for transfers between devices: 46.1 us -> 47.7 us  [transposed(): lax.all_to_all(blocks, 'seq', split_axis=0, concat_axis=0, tiled=True)]
    squeeze x0 -> x1, local copies, waits for them, and re-layouts: none -> 1.3 us  [shards(): mixed, scores = stacked_finish(ref_ids, alt_ids, streams[0], back, vocab)]
    pallas_call x1, Pallas kernels: 2.81 us -> 1.8 us  [stacked_finish(): pl.pallas_call(functools.partial(stacked_finish_kernel, width // lane_til...]
  transfers between devices with their start and end apart: 2 -> 2, of which waited for: 2 -> 2; matrix products, arithmetic and copies ran while one was open for 1% -> 3% of each run, Pallas kernels for 1% -> 0%
where the time goes in v6:
time: 78.5 us; the launch traced here: 78 us
  waiting for transfers between devices  47.7 us (61%)
  Pallas kernels  12 us (15%)
  starting transfers between devices  11.7 us (15%)
  local copies, waits for them, and re-layouts  3.94 us (5%)
  between operations  1.98 us (3%)
    all_to_all x2, waiting for transfers between devices, transposed(): lax.all_to_all(blocks, 'seq', split_axis=0, concat_axis=0, tiled=True)  47.7 us
    all_to_all x2, starting transfers between devices, transposed(): lax.all_to_all(blocks, 'seq', split_axis=0, concat_axis=0, tiled=True)  11.7 us
    pallas_call x1, Pallas kernels, stacked_filter(): pl.pallas_call(functools.partial(stacked_filter_kernel, vars_dev, halves,...  8.42 us
    unnamed x14, local copies, waits for them, and re-layouts  2.56 us
    pallas_call x1, Pallas kernels, stacked_finish(): pl.pallas_call(functools.partial(stacked_finish_kernel, width // lane_til...  1.8 us
    pallas_call x1, Pallas kernels, stacked_products(): pl.pallas_call(functools.partial(stacked_products_kernel, halves, vars_de...  1.77 us
  transfers between devices with their start and end apart: 2, of which 2 were waited for; matrix products, arithmetic and copies ran while one was open for 3% of the time, Pallas kernels for 0%

profile of v6, /device:TPU:13, one launch (start us, length us, event | category | flops | bytes accessed | tf_op | source)
XLA Modules:
  0.0 78.0 jit_solution(5058201334559600852)
XLA Ops:
  0.6 0.0 copy-start
  0.6 1.9 %copy-done = bf16[3,128,4096]{2,1,0:T(8,128)(2,1)S(1)} copy-done((bf16[3,128,4096]{2,1,0:T(8,128)(2,1)S(1)}, bf16[3,128,4096]{2,1,0:T(8,128)(2,1)}, u32[]{:S(2)}) %copy-start) | copy-done | bytes 3145752
  2.5 0.0 copy-start.1
  2.5 0.7 copy-done.1
  3.2 0.0 copy-start.6
  3.2 1.8 %stacked_products.1 = bf16[16,264,128]{2,1,0:T(8,128)(2,1)} custom-call(s32[1]{0:T(128)} %bitcast.3.me_ref, s32[16]{0:T(128)S(1)} %copy-done.1, bf16[3,128,4096]{2,1,0:T(8,128)(2,1)S(1)} %copy-done), custom_call_target="tpu_custom_call" | custom-call | flops 524288 | bytes 3145728 | tf_op jit(solution)/shard_map/stacked_products/pallas_call | solution.py:420
  5.0 0.0 copy-start.2
  5.0 0.0 copy-start.3
  5.0 0.0 copy-start.4
  5.0 0.0 copy-start.5
  5.0 6.7 %all-to-all-start = ((bf16[16,264,128]{2,1,0:T(8,128)(2,1)}), bf16[16,264,128]{2,1,0:T(8,128)(2,1)S(1)}, u32[]{:S(2)}, u32[]{:S(2)}) async-start(bf16[16,264,128]{2,1,0:T(8,128)(2,1)} %stacked_products.1), calls=%async_computation | async-start | bytes 2162688 | tf_op jit(solution)/shard_map/all_to_all | solution.py:577
  11.7 0.0 copy-done.2
  11.7 0.1 copy.11.refs_0_
  11.8 0.8 dynamic-slice_convert_fusion
  12.6 24.7 %all-to-all-done.refs_6_ = bf16[16,264,128]{2,1,0:T(8,128)(2,1)S(1)} async-done(((bf16[16,264,128]{2,1,0:T(8,128)(2,1)}), bf16[16,264,128]{2,1,0:T(8,128)(2,1)S(1)}, u32[]{:S(2)}, u32[]{:S(2)}) %all-to-all-start) | async-done | bytes 1081376 | tf_op jit(solution)/shard_map/all_to_all | solution.py:577
  37.3 0.0 copy-done.6
  37.3 0.0 copy-done.3
  37.3 0.0 copy-done.4
  37.3 0.0 copy-done.5
  37.3 8.4 %stacked_filter.1 = bf16[16,264,128]{2,1,0:T(8,128)(2,1)} custom-call(s32[16,1]{1,0:T(8,128)S(1)} %copy.11.refs_0_, f32[1,256]{1,0:T(1,128)S(1)} %bitcast.7, bf16[1024,256]{1,0:T(8,128)(2,1)S(1)} %copy-done.5, bf16[512,512]{1,0:T(8,128)(2,1)S(1)} %copy-done.6, bf16[256,512]{1,0:T(8,128)(2,1)S(1)} %copy-done.4, bf16[256,2048]{1,0:T(8,128)(2,1)S(1)} %copy-done.3, ...), custom_call_target="tpu_custom_call" | custom-call | flops 2751463424 | bytes 8388608 | tf_op jit(solution)/shard_map/stacked_filter/pallas_call | solution.py:513
  45.7 4.9 %all-to-all-start.1 = ((bf16[16,264,128]{2,1,0:T(8,128)(2,1)}), bf16[16,264,128]{2,1,0:T(8,128)(2,1)S(1)}, u32[]{:S(2)}, u32[]{:S(2)}) async-start(bf16[16,264,128]{2,1,0:T(8,128)(2,1)} %stacked_filter.1), calls=%async_computation.1 | async-start | bytes 2162688 | tf_op jit(solution)/shard_map/all_to_all | solution.py:577
  51.9 1.3 %slice_bitcast_fusion.gates_ref = bf16[128,4096]{1,0:T(8,128)(2,1)S(1)} fusion(bf16[3,128,4096]{2,1,0:T(8,128)(2,1)} %streams_ref.1), kind=kLoop, calls=%fused_computation | loop fusion | bytes 2097152 | tf_op jit(solution)/shard_map/squeeze | solution.py:611
  53.2 23.0 %all-to-all-done.1.back_ref = bf16[16,264,128]{2,1,0:T(8,128)(2,1)S(1)} async-done(((bf16[16,264,128]{2,1,0:T(8,128)(2,1)}), bf16[16,264,128]{2,1,0:T(8,128)(2,1)S(1)}, u32[]{:S(2)}, u32[]{:S(2)}) %all-to-all-start.1) | async-done | bytes 1081376 | tf_op jit(solution)/shard_map/all_to_all | solution.py:577
  76.2 1.8 %stacked_finish.1 = (bf16[128,4096]{1,0:T(8,128)(2,1)}, f32[1,2]{1,0:T(1,128)}) custom-call(s32[1]{0:T(128)S(6)} %copy.12.ref_ref, s32[1]{0:T(128)S(6)} %copy.13.alt_ref, bf16[128,4096]{1,0:T(8,128)(2,1)S(1)} %slice_bitcast_fusion.gates_ref, bf16[16,264,128]{2,1,0:T(8,128)(2,1)S(1)} %all-to-all-done.1.back_ref), custom_call_target="tpu_custom_call" | custom-call | flops 524288 | bytes 3145728 | tf_op jit(solution)/shard_map/stacked_finish/pallas_call | solution.py:556
  (1 shorter events, 0.0 us)
Async XLA Ops:
  0.6 1.9 %copy-start = (bf16[3,128,4096]{2,1,0:T(8,128)(2,1)S(1)}, bf16[3,128,4096]{2,1,0:T(8,128)(2,1)}, u32[]{:S(2)}) copy-start(bf16[3,128,4096]{2,1,0:T(8,128)(2,1)} %streams_ref.1) | copy-start | bytes 9437188
  2.5 0.7 copy-start.1
  3.2 34.1 %copy-start.6 = (bf16[512,512]{1,0:T(8,128)(2,1)S(1)}, bf16[512,512]{1,0:T(8,128)(2,1)}, u32[]{:S(2)}) copy-start(bf16[512,512]{1,0:T(8,128)(2,1)} %constant.17.clone.refs_3_) | copy-start | bytes 1572868
  5.0 6.7 %copy-start.2 = (s32[16]{0:T(128)S(1)}, s32[16]{0:T(128)}, u32[]{:S(2)}) copy-start(s32[16]{0:T(128)} %offsets_ref.1) | copy-start | bytes 196
  5.0 32.3 %copy-start.3 = (bf16[256,2048]{1,0:T(8,128)(2,1)S(1)}, bf16[256,2048]{1,0:T(8,128)(2,1)}, u32[]{:S(2)}) copy-start(bf16[256,2048]{1,0:T(8,128)(2,1)} %refs_5_.1) | copy-start | bytes 3145732
  5.0 32.3 %copy-start.4 = (bf16[256,512]{1,0:T(8,128)(2,1)S(1)}, bf16[256,512]{1,0:T(8,128)(2,1)}, u32[]{:S(2)}) copy-start(bf16[256,512]{1,0:T(8,128)(2,1)} %refs_4_.1) | copy-start | bytes 786436
  5.0 32.3 %copy-start.5 = (bf16[1024,256]{1,0:T(8,128)(2,1)S(1)}, bf16[1024,256]{1,0:T(8,128)(2,1)}, u32[]{:S(2)}) copy-start(bf16[1024,256]{1,0:T(8,128)(2,1)} %constant.16.clone.refs_2_) | copy-start | bytes 1572868
  5.0 32.3 %all-to-all-start = ((bf16[16,264,128]{2,1,0:T(8,128)(2,1)}), bf16[16,264,128]{2,1,0:T(8,128)(2,1)S(1)}, u32[]{:S(2)}, u32[]{:S(2)}) async-start(bf16[16,264,128]{2,1,0:T(8,128)(2,1)} %stacked_products.1), calls=%async_computation | async-start | bytes 2162688 | tf_op jit(solution)/shard_map/all_to_all | solution.py:577
  45.7 30.5 %all-to-all-start.1 = ((bf16[16,264,128]{2,1,0:T(8,128)(2,1)}), bf16[16,264,128]{2,1,0:T(8,128)(2,1)S(1)}, u32[]{:S(2)}, u32[]{:S(2)}) async-start(bf16[16,264,128]{2,1,0:T(8,128)(2,1)} %stacked_filter.1), calls=%async_computation.1 | async-start | bytes 2162688 | tf_op jit(solution)/shard_map/all_to_all | solution.py:577

commit v7 on v6

--- a/solution.py
+++ b/solution.py
@@ -386,43 +386,86 @@
         name="finish",
     )(ref_ids, alt_ids, streams, *backs)
 
-def stacked_products_kernel(halves, vars_dev, me_ref, offsets_ref, streams_ref, out_ref):
-    _, tok_rows, model_width = streams_ref.shape
-    n_devices = out_ref.shape[0]
-    extra = out_ref.shape[1] - halves * tok_rows
+def half_order(n_devices):
+    half = n_devices // 2
+    return [device for pair in zip(range(half), range(half, n_devices)) for device in pair]
+
+
+def stacked_products_kernel(halves, vars_dev, order, me_ref, offsets_ref, streams_ref, out_ref, *scratch):
+    gates, pairs, built, gate_sem, pair_sems, out_sems = scratch
+    n_devices = len(order)
+    pieces, _, tok_rows, lanes_each = pairs.shape
+    body = halves * tok_rows
+    width = halves * lane_tile
+    owners = lanes_each // width
     me = me_ref[0]
     slot = tok_rows // vars_dev
-    row = lax.broadcasted_iota(jnp.int32, (row_tile, model_width), 0)
+    rank_of = {device: rank for rank, device in enumerate(order)}
+
+    def pair_copy(piece):
+        lanes = pl.ds(piece * lanes_each, lanes_each)
+        return pltpu.make_async_copy(
+            streams_ref.at[pl.ds(1, 2), :, lanes], pairs.at[piece], pair_sems.at[piece]
+        )
+
+    def out_copy(rank):
+        return pltpu.make_async_copy(built.at[rank], out_ref.at[rank], out_sems.at[rank])
+
+    gate_copy = pltpu.make_async_copy(streams_ref.at[0], gates, gate_sem.at[0])
+    gate_copy.start()
+    for piece in range(pieces):
+        pair_copy(piece).start()
+    extra = built.shape[1] - body
+    row = lax.broadcasted_iota(jnp.int32, (row_tile, gates.shape[1]), 0)
     place = lax.broadcasted_iota(jnp.int32, (extra, lane_tile), 0)
+    gate_copy.wait()
     gate_rows = []
     for var in range(vars_dev):
         local = var * slot + offsets_ref[me * vars_dev + var]
         start = pl.multiple_of(local // row_tile * row_tile, row_tile)
-        tile = streams_ref[0, pl.ds(start, row_tile), :].astype(f32)
+        tile = gates[pl.ds(start, row_tile), :].astype(f32)
         mine = jnp.where(row == local % row_tile, tile, 0.0)
         gate_rows.append(jnp.sum(mine, axis=0, keepdims=True))
-    for owner in range(n_devices):
-        tail = jnp.zeros((extra, lane_tile), f32)
-        for half in range(halves):
-            start = (owner * halves + half) * lane_tile
-            lanes = slice(start, start + lane_tile)
-            rows = slice(half * tok_rows, (half + 1) * tok_rows)
-            out_ref[owner, rows, :] = streams_ref[1, :, lanes] * streams_ref[2, :, lanes]
-            for var in range(vars_dev):
-                tail = jnp.where(place == half * vars_dev + var, gate_rows[var][:, lanes], tail)
-        out_ref[owner, halves * tok_rows :, :] = tail.astype(bf16)
-
-
-def stacked_products(me, offsets, streams, vars_dev, n_devices, extra):
+    for piece in range(pieces):
+        pair_copy(piece).wait()
+        for member in range(owners):
+            owner = piece * owners + member
+            rank = rank_of[owner]
+            tail = jnp.zeros((extra, lane_tile), f32)
+            for half in range(halves):
+                lanes = slice(member * width + half * lane_tile, member * width + (half + 1) * lane_tile)
+                rows = slice(half * tok_rows, (half + 1) * tok_rows)
+                built[rank, rows, :] = pairs[piece, 0, :, lanes] * pairs[piece, 1, :, lanes]
+                start = owner * width + half * lane_tile
+                for var in range(vars_dev):
+                    mine = gate_rows[var][:, start : start + lane_tile]
+                    tail = jnp.where(place == half * vars_dev + var, mine, tail)
+            built[rank, body:, :] = tail.astype(bf16)
+            out_copy(rank).start()
+    for rank in range(n_devices):
+        out_copy(rank).wait()
+
+
+def stacked_products(me, offsets, streams, vars_dev, order, extra):
     _, tok_rows, model_width = streams.shape
+    n_devices = len(order)
     halves = model_width // n_devices // lane_tile
     rows_out = halves * tok_rows + extra
+    pieces = math.gcd(n_devices, 4)
     return pl.pallas_call(
-        functools.partial(stacked_products_kernel, halves, vars_dev),
-        in_specs=[pl.BlockSpec(memory_space=pltpu.SMEM)] * 2 + [whole_spec()],
-        out_specs=whole_spec(),
+        functools.partial(stacked_products_kernel, halves, vars_dev, order),
+        in_specs=[pl.BlockSpec(memory_space=pltpu.SMEM)] * 2 + [pl.BlockSpec(memory_space=pl.ANY)],
+        out_specs=pl.BlockSpec(memory_space=pl.ANY),
         out_shape=jax.ShapeDtypeStruct((n_devices, rows_out, lane_tile), bf16),
-        compiler_params=pltpu.CompilerParams(vmem_limit_bytes=16 * MIB),
+        scratch_shapes=[
+            pltpu.VMEM((tok_rows, model_width), bf16),
+            pltpu.VMEM((pieces, 2, tok_rows, model_width // pieces), bf16),
+            pltpu.VMEM((n_devices, rows_out, lane_tile), bf16),
+            pltpu.SemaphoreType.DMA((1,)),
+            pltpu.SemaphoreType.DMA((pieces,)),
+            pltpu.SemaphoreType.DMA((n_devices,)),
+        ],
+        compiler_params=pltpu.CompilerParams(vmem_limit_bytes=60 * MIB),
         cost_estimate=pl.CostEstimate(
             flops=tok_rows * model_width, bytes_accessed=6 * tok_rows * model_width, transcendentals=0
         ),
@@ -430,10 +473,11 @@
     )(me, offsets, streams)
 
 
-def stacked_filter_kernel(vars_dev, halves, tok_rows, *refs):
+def stacked_filter_kernel(vars_dev, halves, tok_rows, order, *refs):
     positions_ref, gain_ref, forward, inverse, unembed, taps, arrived = refs[:7]
     leaving, points, joint, spectrum, packed = refs[7:]
     n_devices = arrived.shape[0]
+    rank_of = {device: rank for rank, device in enumerate(order)}
     body = halves * tok_rows
     n_blocks, double, width = points.shape
     block = double // 2
@@ -441,40 +485,39 @@
     group = 2 if n_blocks % 2 == 0 else 1
 
     for index in range(n_blocks):
-        both = lax.dot_general(
+        part = taps[:, index * block : (index + 1) * block]
+        spectrum[index] = lax.dot_general(
             forward[...],
-            taps[:, index * block : (index + 1) * block],
+            jnp.concatenate([part, part], axis=1),
             (((1,), (1,)), ((), ())),
             preferred_element_type=f32,
         )
-        spectrum[index] = both[:double] + both[double:]
 
     for step in range(0, n_blocks, group):
         pieces = []
         for index in range(step, step + group):
             for half in range(halves):
                 rows = slice(half * tok_rows, (half + 1) * tok_rows)
-                parts = [arrived[index * per_block + m, rows, :] for m in range(per_block)]
-                pieces.append(jnp.concatenate(parts, axis=0))
+                parts = [arrived[rank_of[index * per_block + m], rows, :] for m in range(per_block)]
+                pieces.append(jnp.concatenate(parts + parts, axis=0))
         signal = jnp.concatenate(pieces, axis=1)
-        both = jnp.dot(forward[...], signal, preferred_element_type=f32)
-        total = both[:double] + both[double:]
+        total = jnp.dot(forward[...], signal, preferred_element_type=f32)
         for member in range(group):
             points[step + member] = total[:, member * width : (member + 1) * width]
     multiply_points(points, spectrum, joint)
 
     for step in range(0, n_blocks, group):
         highs, lows = split_bf16(jnp.concatenate([joint[step + m] for m in range(group)], axis=1))
-        both = jnp.dot(inverse[...], highs, preferred_element_type=f32)
-        rest = jnp.dot(inverse[:block, :], lows, preferred_element_type=f32)
-        result = (both[:block] + both[block:] + rest).astype(bf16)
+        terms = jnp.concatenate([highs, highs, lows], axis=0)
+        result = jnp.dot(inverse[...], terms, preferred_element_type=f32).astype(bf16)
         for index in range(group):
             for member in range(per_block):
+                rank = rank_of[(step + index) * per_block + member]
                 for half in range(halves):
                     start = index * width + half * lane_tile
-                    leaving[
-                        (step + index) * per_block + member, half * tok_rows : (half + 1) * tok_rows, :
-                    ] = result[member * tok_rows : (member + 1) * tok_rows, start : start + lane_tile]
+                    leaving[rank, half * tok_rows : (half + 1) * tok_rows, :] = result[
+                        member * tok_rows : (member + 1) * tok_rows, start : start + lane_tile
+                    ]
 
     length = n_devices * tok_rows
     column = lax.broadcasted_iota(jnp.int32, (positions_ref.shape[0], length), 1)
@@ -502,16 +545,16 @@
     leaving[:, body:, :] = packed[...].reshape(n_devices, extra, lane_tile).astype(bf16)
 
 
-def stacked_filter(positions, gain_row, tables, arrived, vars_dev, tok_rows, extra):
+def stacked_filter(positions, gain_row, tables, arrived, vars_dev, tok_rows, order, extra):
     width, length = tables[3].shape
     n_devices = arrived.shape[0]
-    double = tables[0].shape[0] // 2
+    double = tables[0].shape[0]
     n_blocks = 2 * length // double
     halves = width // lane_tile
     rows_out = halves * tok_rows + extra
     flops = 2 * width * n_blocks * (double * double * 5 // 2 + 4 * n_blocks * double)
     return pl.pallas_call(
-        functools.partial(stacked_filter_kernel, vars_dev, halves, tok_rows),
+        functools.partial(stacked_filter_kernel, vars_dev, halves, tok_rows, order),
         in_specs=[whole_spec()] * 7,
         out_specs=whole_spec(),
         out_shape=jax.ShapeDtypeStruct((n_devices, rows_out, lane_tile), bf16),
@@ -523,7 +566,7 @@
     )(positions, gain_row, *tables, arrived)
 
 
-def stacked_finish_kernel(halves, vars_dev, vocab, ref_ref, alt_ref, gates_ref, back_ref, *refs):
+def stacked_finish_kernel(halves, vars_dev, vocab, order, ref_ref, alt_ref, gates_ref, back_ref, *refs):
     mixed_ref, scores_ref, results, out_sems = refs
     n_devices, tok_rows, width = results.shape
 
@@ -533,14 +576,14 @@
         )
 
     sums = None
-    for owner in range(n_devices):
+    for rank, owner in enumerate(order):
         for half in range(halves):
             lanes = slice(half * lane_tile, (half + 1) * lane_tile)
             start = owner * width + half * lane_tile
-            filtered = back_ref[owner, half * tok_rows : (half + 1) * tok_rows, :]
+            filtered = back_ref[rank, half * tok_rows : (half + 1) * tok_rows, :]
             results[owner, :, lanes] = gates_ref[:, start : start + lane_tile] * filtered
         out_copy(owner).start()
-        tail = back_ref[owner, halves * tok_rows :, :].astype(f32)
+        tail = back_ref[rank, halves * tok_rows :, :].astype(f32)
         sums = tail if sums is None else sums + tail
     model_width = n_devices * width
     scores_ref[...] = final_scores(sums, 1, vars_dev, vocab, model_width, ref_ref, alt_ref)
@@ -548,13 +591,13 @@
         out_copy(owner).wait()
 
 
-def stacked_finish(ref_ids, alt_ids, gates, back, vocab):
+def stacked_finish(ref_ids, alt_ids, gates, back, vocab, order):
     tok_rows, model_width = gates.shape
     n_devices = back.shape[0]
     vars_dev = ref_ids.shape[0]
     width = model_width // n_devices
     return pl.pallas_call(
-        functools.partial(stacked_finish_kernel, width // lane_tile, vars_dev, vocab),
+        functools.partial(stacked_finish_kernel, width // lane_tile, vars_dev, vocab, order),
         in_specs=[pl.BlockSpec(memory_space=pltpu.SMEM)] * 2 + [whole_spec()] * 2,
         out_specs=[pl.BlockSpec(memory_space=pl.ANY), whole_spec()],
         out_shape=[
@@ -573,8 +616,10 @@
     )(ref_ids, alt_ids, gates, back)
 
 
-def transposed(blocks):
-    return lax.all_to_all(blocks, "seq", split_axis=0, concat_axis=0, tiled=True)
+def transposed(blocks, order):
+    return lax.all_to_all(
+        blocks, "seq", split_axis=0, concat_axis=0, axis_index_groups=[order], tiled=True
+    )
 
 
 def shards(streams, long_filter, gain, unembed, offsets, ref_ids, alt_ids):
@@ -599,16 +644,25 @@
     positions = positions.T.reshape(n_devices * vars_dev, 1)
     my_gain = lax.dynamic_slice_in_dim(gain, my_index * group_width, group_width).astype(f32)
 
-    if chunks * lane_tile == group_width:
+    if chunks * lane_tile == group_width and n_devices % 2 == 0:
         me = jnp.reshape(my_index, (1,)).astype(jnp.int32)
         gate_extra = round_up(chunks * vars_dev, half_tile)
         score_extra = round_up(vars_dev * (vocab // lane_tile + 2), half_tile)
-        arrived = transposed(stacked_products(me, offsets, streams, vars_dev, n_devices, gate_extra))
-        tables = (forward, inverse, unembed, long_filter)
-        gain_row = my_gain[None, :]
-        leaving = stacked_filter(positions, gain_row, tables, arrived, vars_dev, tok_rows, score_extra)
-        back = transposed(leaving)
-        mixed, scores = stacked_finish(ref_ids, alt_ids, streams[0], back, vocab)
+        order = half_order(n_devices)
+        arrived = transposed(stacked_products(me, offsets, streams, vars_dev, order, gate_extra), order)
+        joined_forward = jnp.asarray(np.concatenate(np.split(forward_np, 2, axis=0), axis=1))
+        joined_inverse = np.split(inverse_np, 2, axis=0)
+        joined_inverse = jnp.asarray(np.concatenate(joined_inverse + joined_inverse[:1], axis=1))
+        tables = (joined_forward, joined_inverse, unembed, long_filter)
+        places = by_device.reshape(2, n_devices // 2, vars_dev).transpose(1, 0, 2)
+        places = places.reshape(n_devices, vars_dev) + starts[None, :]
+        places += jnp.arange(n_devices, dtype=jnp.int32)[:, None] * tok_rows
+        places = places.T.reshape(n_devices * vars_dev, 1)
+        leaving = stacked_filter(
+            places, my_gain[None, :], tables, arrived, vars_dev, tok_rows, order, score_extra
+        )
+        back = transposed(leaving, order)
+        mixed, scores = stacked_finish(ref_ids, alt_ids, streams[0], back, vocab, order)
         return (mixed, scores.T)
 
     gate_extra = round_up(chunks * vars_dev, row_tile)

time: 78.5 us -> 81.5 us (1.038)
  the two profiles are of different devices: /device:TPU:13 before, /device:TPU:0 now
where the time goes in v7:
time: 81.5 us; the launch traced here: 81.1 us
  waiting for transfers between devices  50.8 us (62%)
  Pallas kernels  13.8 us (17%)
  starting transfers between devices  11.2 us (14%)
  local copies, waits for them, and re-layouts  2.6 us (3%)
  between operations  2.01 us (2%)
    all_to_all x2, waiting for transfers between devices, transposed(): lax.all_to_all(blocks, 'seq', split_axis=0, concat_axis=0, axis_index_gro...  50.8 us
    all_to_all x2, starting transfers between devices, transposed(): lax.all_to_all(blocks, 'seq', split_axis=0, concat_axis=0, axis_index_gro...  11.2 us
    pallas_call x1, Pallas kernels, stacked_filter(): pl.pallas_call(functools.partial(stacked_filter_kernel, vars_dev, halves,...  8.32 us
    pallas_call x1, Pallas kernels, stacked_products(): pl.pallas_call(functools.partial(stacked_products_kernel, halves, vars_de...  3.64 us
    pallas_call x1, Pallas kernels, stacked_finish(): pl.pallas_call(functools.partial(stacked_finish_kernel, width // lane_til...  1.8 us
  transfers between devices with their start and end apart: 2, of which 2 were waited for; matrix products, arithmetic and copies ran while one was open for 3% of the time, Pallas kernels for 0%

profile of v7, /device:TPU:0, one launch (start us, length us, event | category | flops | bytes accessed | tf_op | source)
XLA Modules:
  0.0 81.1 jit_solution(5348923780770380241)
XLA Ops:
  0.6 3.6 %stacked_products.1 = bf16[16,264,128]{2,1,0:T(8,128)(2,1)} custom-call(s32[1]{0:T(128)} %bitcast.3.me_ref, s32[16]{0:T(128)} %offsets_ref.1, bf16[3,128,4096]{2,1,0:T(8,128)(2,1)} %streams_ref.1), custom_call_target="tpu_custom_call" | custom-call | flops 524288 | bytes 3145728 | tf_op jit(solution)/shard_map/stacked_products/pallas_call | solution.py:455
  4.3 0.0 copy-start.4
  4.3 0.0 copy-start
  4.3 0.0 copy-start.1
  4.3 0.0 copy-start.2
  4.3 7.5 %all-to-all-start = ((bf16[16,264,128]{2,1,0:T(8,128)(2,1)}), bf16[16,264,128]{2,1,0:T(8,128)(2,1)S(1)}, u32[]{:S(2)}, u32[]{:S(2)}) async-start(bf16[16,264,128]{2,1,0:T(8,128)(2,1)} %stacked_products.1), calls=%async_computation | async-start | bytes 2162688 | tf_op jit(solution)/shard_map/all_to_all | solution.py:620
  11.8 0.0 copy-done.4
  11.8 0.1 reshape_reshape.3
  11.9 0.1 copy.13
  12.0 0.1 reshape.33
  12.1 0.8 dynamic-slice_convert_fusion
  12.9 26.2 %all-to-all-done.refs_6_ = bf16[16,264,128]{2,1,0:T(8,128)(2,1)S(1)} async-done(((bf16[16,264,128]{2,1,0:T(8,128)(2,1)}), bf16[16,264,128]{2,1,0:T(8,128)(2,1)S(1)}, u32[]{:S(2)}, u32[]{:S(2)}) %all-to-all-start) | async-done | bytes 1081376 | tf_op jit(solution)/shard_map/all_to_all | solution.py:620
  39.1 0.0 copy-done
  39.1 0.0 copy-done.1
  39.1 0.0 copy-done.2
  39.1 0.0 copy-start.3
  39.1 1.0 %copy-done.3 = bf16[512,512]{1,0:T(8,128)(2,1)S(1)} copy-done((bf16[512,512]{1,0:T(8,128)(2,1)S(1)}, bf16[512,512]{1,0:T(8,128)(2,1)}, u32[]{:S(2)}) %copy-start.3) | copy-done | bytes 524312
  40.1 8.3 %stacked_filter.1 = bf16[16,264,128]{2,1,0:T(8,128)(2,1)} custom-call(s32[16,1]{1,0:T(8,128)S(1)} %multiply_add_fusion.refs_0_, f32[1,256]{1,0:T(1,128)S(1)} %bitcast.8, bf16[512,512]{1,0:T(8,128)(2,1)S(1)} %copy-done.3, bf16[256,1536]{1,0:T(8,128)(2,1)S(1)} %copy-done.2, bf16[256,512]{1,0:T(8,128)(2,1)S(1)} %copy-done.1, bf16[256,2048]{1,0:T(8,128)(2,1)S(1)} %copy-done, ...), custom_call_target="tpu_custom_call" | custom-call | flops 2751463424 | bytes 8388608 | tf_op jit(solution)/shard_map/stacked_filter/pallas_call | solution.py:556
  48.5 3.7 %all-to-all-start.1 = ((bf16[16,264,128]{2,1,0:T(8,128)(2,1)}), bf16[16,264,128]{2,1,0:T(8,128)(2,1)S(1)}, u32[]{:S(2)}, u32[]{:S(2)}) async-start(bf16[16,264,128]{2,1,0:T(8,128)(2,1)} %stacked_filter.1), calls=%async_computation.1 | async-start | bytes 2162688 | tf_op jit(solution)/shard_map/all_to_all | solution.py:620
  53.5 1.3 %slice_bitcast_fusion.gates_ref = bf16[128,4096]{1,0:T(8,128)(2,1)S(1)} fusion(bf16[3,128,4096]{2,1,0:T(8,128)(2,1)} %streams_ref.1), kind=kLoop, calls=%fused_computation | loop fusion | bytes 2097152 | tf_op jit(solution)/shard_map/squeeze | solution.py:665
  54.8 24.5 %all-to-all-done.1.back_ref = bf16[16,264,128]{2,1,0:T(8,128)(2,1)S(1)} async-done(((bf16[16,264,128]{2,1,0:T(8,128)(2,1)}), bf16[16,264,128]{2,1,0:T(8,128)(2,1)S(1)}, u32[]{:S(2)}, u32[]{:S(2)}) %all-to-all-start.1) | async-done | bytes 1081376 | tf_op jit(solution)/shard_map/all_to_all | solution.py:620
  79.3 1.8 %stacked_finish.1 = (bf16[128,4096]{1,0:T(8,128)(2,1)}, f32[1,2]{1,0:T(1,128)}) custom-call(s32[1]{0:T(128)S(6)} %copy.15.ref_ref, s32[1]{0:T(128)S(6)} %copy.16.alt_ref, bf16[128,4096]{1,0:T(8,128)(2,1)S(1)} %slice_bitcast_fusion.gates_ref, bf16[16,264,128]{2,1,0:T(8,128)(2,1)S(1)} %all-to-all-done.1.back_ref), custom_call_target="tpu_custom_call" | custom-call | flops 524288 | bytes 3145728 | tf_op jit(solution)/shard_map/stacked_finish/pallas_call | solution.py:599
  (1 shorter events, 0.0 us)
Async XLA Ops:
  4.3 7.6 %copy-start.4 = (s32[16]{0:T(128)S(1)}, s32[16]{0:T(128)}, u32[]{:S(2)}) copy-start(s32[16]{0:T(128)} %offsets_ref.1) | copy-start | bytes 196
  4.3 34.8 %copy-start = (bf16[256,2048]{1,0:T(8,128)(2,1)S(1)}, bf16[256,2048]{1,0:T(8,128)(2,1)}, u32[]{:S(2)}) copy-start(bf16[256,2048]{1,0:T(8,128)(2,1)} %refs_5_.1) | copy-start | bytes 3145732
  4.3 34.8 %copy-start.1 = (bf16[256,512]{1,0:T(8,128)(2,1)S(1)}, bf16[256,512]{1,0:T(8,128)(2,1)}, u32[]{:S(2)}) copy-start(bf16[256,512]{1,0:T(8,128)(2,1)} %refs_4_.1) | copy-start | bytes 786436
  4.3 34.8 %copy-start.2 = (bf16[256,1536]{1,0:T(8,128)(2,1)S(1)}, bf16[256,1536]{1,0:T(8,128)(2,1)}, u32[]{:S(2)}) copy-start(bf16[256,1536]{1,0:T(8,128)(2,1)} %constant.17.clone.refs_3_) | copy-start | bytes 2359300
  4.3 34.8 %all-to-all-start = ((bf16[16,264,128]{2,1,0:T(8,128)(2,1)}), bf16[16,264,128]{2,1,0:T(8,128)(2,1)S(1)}, u32[]{:S(2)}, u32[]{:S(2)}) async-start(bf16[16,264,128]{2,1,0:T(8,128)(2,1)} %stacked_products.1), calls=%async_computation | async-start | bytes 2162688 | tf_op jit(solution)/shard_map/all_to_all | solution.py:620
  39.1 1.0 %copy-start.3 = (bf16[512,512]{1,0:T(8,128)(2,1)S(1)}, bf16[512,512]{1,0:T(8,128)(2,1)}, u32[]{:S(2)}) copy-start(bf16[512,512]{1,0:T(8,128)(2,1)} %constant.16.clone.refs_2_) | copy-start | bytes 1572868
  48.5 30.8 %all-to-all-start.1 = ((bf16[16,264,128]{2,1,0:T(8,128)(2,1)}), bf16[16,264,128]{2,1,0:T(8,128)(2,1)S(1)}, u32[]{:S(2)}, u32[]{:S(2)}) async-start(bf16[16,264,128]{2,1,0:T(8,128)(2,1)} %stacked_filter.1), calls=%async_computation.1 | async-start | bytes 2162688 | tf_op jit(solution)/shard_map/all_to_all | solution.py:620

commit v8 on v6

--- a/solution.py
+++ b/solution.py
@@ -386,43 +386,87 @@
         name="finish",
     )(ref_ids, alt_ids, streams, *backs)
 
-def stacked_products_kernel(halves, vars_dev, me_ref, offsets_ref, streams_ref, out_ref):
-    _, tok_rows, model_width = streams_ref.shape
-    n_devices = out_ref.shape[0]
-    extra = out_ref.shape[1] - halves * tok_rows
+def stacked_products_kernel(halves, vars_dev, me_ref, offsets_ref, streams_ref, out_ref, *scratch):
+    gates, pairs, built, gate_sem, pair_sems, body_sems, tail_sem = scratch
+    n_devices = built.shape[0]
+    pieces, _, tok_rows, lanes_each = pairs.shape
+    body = halves * tok_rows
+    width = halves * lane_tile
+    owners = lanes_each // width
     me = me_ref[0]
     slot = tok_rows // vars_dev
-    row = lax.broadcasted_iota(jnp.int32, (row_tile, model_width), 0)
+
+    def pair_copy(piece):
+        lanes = pl.ds(piece * lanes_each, lanes_each)
+        return pltpu.make_async_copy(
+            streams_ref.at[pl.ds(1, 2), :, lanes], pairs.at[piece], pair_sems.at[piece]
+        )
+
+    def body_copy(rank):
+        rows = pl.ds(0, body)
+        return pltpu.make_async_copy(built.at[rank, rows], out_ref.at[rank, rows], body_sems.at[rank])
+
+    gate_copy = pltpu.make_async_copy(streams_ref.at[0], gates, gate_sem.at[0])
+    for piece in range(pieces):
+        pair_copy(piece).start()
+    gate_copy.start()
+    for piece in range(pieces):
+        pair_copy(piece).wait()
+        for member in range(owners):
+            owner = piece * owners + member
+            for half in range(halves):
+                lanes = slice(member * width + half * lane_tile, member * width + (half + 1) * lane_tile)
+                rows = slice(half * tok_rows, (half + 1) * tok_rows)
+                built[owner, rows, :] = pairs[piece, 0, :, lanes] * pairs[piece, 1, :, lanes]
+            body_copy(owner).start()
+
+    extra = built.shape[1] - body
+    row = lax.broadcasted_iota(jnp.int32, (row_tile, gates.shape[1]), 0)
     place = lax.broadcasted_iota(jnp.int32, (extra, lane_tile), 0)
+    gate_copy.wait()
     gate_rows = []
     for var in range(vars_dev):
         local = var * slot + offsets_ref[me * vars_dev + var]
         start = pl.multiple_of(local // row_tile * row_tile, row_tile)
-        tile = streams_ref[0, pl.ds(start, row_tile), :].astype(f32)
+        tile = gates[pl.ds(start, row_tile), :].astype(f32)
         mine = jnp.where(row == local % row_tile, tile, 0.0)
         gate_rows.append(jnp.sum(mine, axis=0, keepdims=True))
     for owner in range(n_devices):
         tail = jnp.zeros((extra, lane_tile), f32)
         for half in range(halves):
-            start = (owner * halves + half) * lane_tile
-            lanes = slice(start, start + lane_tile)
-            rows = slice(half * tok_rows, (half + 1) * tok_rows)
-            out_ref[owner, rows, :] = streams_ref[1, :, lanes] * streams_ref[2, :, lanes]
+            start = owner * width + half * lane_tile
             for var in range(vars_dev):
-                tail = jnp.where(place == half * vars_dev + var, gate_rows[var][:, lanes], tail)
-        out_ref[owner, halves * tok_rows :, :] = tail.astype(bf16)
+                mine = gate_rows[var][:, start : start + lane_tile]
+                tail = jnp.where(place == half * vars_dev + var, mine, tail)
+        built[owner, body:, :] = tail.astype(bf16)
+    rows = pl.ds(body, extra)
+    tail_copy = pltpu.make_async_copy(built.at[:, rows], out_ref.at[:, rows], tail_sem.at[0])
+    tail_copy.start()
+    for rank in range(n_devices):
+        body_copy(rank).wait()
+    tail_copy.wait()
 
 
 def stacked_products(me, offsets, streams, vars_dev, n_devices, extra):
     _, tok_rows, model_width = streams.shape
     halves = model_width // n_devices // lane_tile
     rows_out = halves * tok_rows + extra
+    pieces = math.gcd(n_devices, 4)
     return pl.pallas_call(
         functools.partial(stacked_products_kernel, halves, vars_dev),
-        in_specs=[pl.BlockSpec(memory_space=pltpu.SMEM)] * 2 + [whole_spec()],
-        out_specs=whole_spec(),
+        in_specs=[pl.BlockSpec(memory_space=pltpu.SMEM)] * 2 + [pl.BlockSpec(memory_space=pl.ANY)],
+        out_specs=pl.BlockSpec(memory_space=pl.ANY),
         out_shape=jax.ShapeDtypeStruct((n_devices, rows_out, lane_tile), bf16),
-        compiler_params=pltpu.CompilerParams(vmem_limit_bytes=16 * MIB),
+        scratch_shapes=[
+            pltpu.VMEM((tok_rows, model_width), bf16),
+            pltpu.VMEM((pieces, 2, tok_rows, model_width // pieces), bf16),
+            pltpu.VMEM((n_devices, rows_out, lane_tile), bf16),
+            pltpu.SemaphoreType.DMA((1,)),
+            pltpu.SemaphoreType.DMA((pieces,)),
+            pltpu.SemaphoreType.DMA((n_devices,)),
+            pltpu.SemaphoreType.DMA((1,)),
+        ],
+        compiler_params=pltpu.CompilerParams(vmem_limit_bytes=60 * MIB),
         cost_estimate=pl.CostEstimate(
             flops=tok_rows * model_width, bytes_accessed=6 * tok_rows * model_width, transcendentals=0
         ),
@@ -432,13 +476,17 @@
 
 def stacked_filter_kernel(vars_dev, halves, tok_rows, *refs):
     positions_ref, gain_ref, forward, inverse, unembed, taps, arrived = refs[:7]
-    leaving, points, joint, spectrum, packed = refs[7:]
+    out_ref, points, joint, spectrum, packed, leaving, body_sems, tail_sem = refs[7:]
     n_devices = arrived.shape[0]
     body = halves * tok_rows
     n_blocks, double, width = points.shape
     block = double // 2
     per_block = block // tok_rows
     group = 2 if n_blocks % 2 == 0 else 1
+
+    def body_copy(rank):
+        rows = pl.ds(0, body)
+        return pltpu.make_async_copy(leaving.at[rank, rows], out_ref.at[rank, rows], body_sems.at[rank])
 
     for index in range(n_blocks):
         both = lax.dot_general(
@@ -470,11 +518,13 @@
         result = (both[:block] + both[block:] + rest).astype(bf16)
         for index in range(group):
             for member in range(per_block):
+                rank = (step + index) * per_block + member
                 for half in range(halves):
                     start = index * width + half * lane_tile
-                    leaving[
-                        (step + index) * per_block + member, half * tok_rows : (half + 1) * tok_rows, :
-                    ] = result[member * tok_rows : (member + 1) * tok_rows, start : start + lane_tile]
+                    leaving[rank, half * tok_rows : (half + 1) * tok_rows, :] = result[
+                        member * tok_rows : (member + 1) * tok_rows, start : start + lane_tile
+                    ]
+                body_copy(rank).start()
 
     length = n_devices * tok_rows
     column = lax.broadcasted_iota(jnp.int32, (positions_ref.shape[0], length), 1)
@@ -497,9 +547,15 @@
         part = jnp.dot(weighted, unembed[lanes, :], preferred_element_type=f32)
         raw = part if raw is None else raw + part
         squares = rows * rows if squares is None else squares + rows * rows
-    pack_scores(raw, squares, 1, vars_dev, packed, n_devices)
+    pack_scores(raw, squares, 2, vars_dev, packed, n_devices)
     extra = packed.shape[0] // n_devices
     leaving[:, body:, :] = packed[...].reshape(n_devices, extra, lane_tile).astype(bf16)
+    rows = pl.ds(body, extra)
+    tail_copy = pltpu.make_async_copy(leaving.at[:, rows], out_ref.at[:, rows], tail_sem.at[0])
+    tail_copy.start()
+    for rank in range(n_devices):
+        body_copy(rank).wait()
+    tail_copy.wait()
 
 
 def stacked_filter(positions, gain_row, tables, arrived, vars_dev, tok_rows, extra):
@@ -513,10 +569,15 @@
     return pl.pallas_call(
         functools.partial(stacked_filter_kernel, vars_dev, halves, tok_rows),
         in_specs=[whole_spec()] * 7,
-        out_specs=whole_spec(),
+        out_specs=pl.BlockSpec(memory_space=pl.ANY),
         out_shape=jax.ShapeDtypeStruct((n_devices, rows_out, lane_tile), bf16),
         scratch_shapes=[pltpu.VMEM((n_blocks, double, width), f32)] * 3
-        + [pltpu.VMEM((n_devices * extra, lane_tile), f32)],
+        + [
+            pltpu.VMEM((n_devices * extra, lane_tile), f32),
+            pltpu.VMEM((n_devices, rows_out, lane_tile), bf16),
+            pltpu.SemaphoreType.DMA((n_devices,)),
+            pltpu.SemaphoreType.DMA((1,)),
+        ],
         compiler_params=pltpu.CompilerParams(vmem_limit_bytes=24 * MIB),
         cost_estimate=pl.CostEstimate(flops=flops, bytes_accessed=8 * MIB, transcendentals=0),
         name="stacked_filter",
@@ -543,7 +604,7 @@
         tail = back_ref[owner, halves * tok_rows :, :].astype(f32)
         sums = tail if sums is None else sums + tail
     model_width = n_devices * width
-    scores_ref[...] = final_scores(sums, 1, vars_dev, vocab, model_width, ref_ref, alt_ref)
+    scores_ref[...] = final_scores(sums, 2, vars_dev, vocab, model_width, ref_ref, alt_ref)
     for owner in range(n_devices):
         out_copy(owner).wait()
 
@@ -601,8 +662,8 @@
 
     if chunks * lane_tile == group_width:
         me = jnp.reshape(my_index, (1,)).astype(jnp.int32)
-        gate_extra = round_up(chunks * vars_dev, half_tile)
-        score_extra = round_up(vars_dev * (vocab // lane_tile + 2), half_tile)
+        gate_extra = round_up(chunks * vars_dev, row_tile)
+        score_extra = round_up(2 * vars_dev * (vocab // lane_tile + 1), row_tile)
         arrived = transposed(stacked_products(me, offsets, streams, vars_dev, n_devices, gate_extra))
         tables = (forward, inverse, unembed, long_filter)
         gain_row = my_gain[None, :]

time: 78.5 us -> 78.9 us (level)
  local copies, waits for them, and re-layouts: 3.94 us -> 1.41 us
  Pallas kernels: 12 us -> 13.5 us
  waiting for transfers between devices: 47.7 us -> 49 us
    unnamed x14 -> x10, local copies, waits for them, and re-layouts: 2.56 us -> 0.03 us
    pallas_call x1, Pallas kernels: 1.77 us -> 3.56 us  [stacked_products(): pl.pallas_call(functools.partial(stacked_products_kernel, halves, vars_de...]
    all_to_all x2, waiting for transfers between devices: 47.7 us -> 49 us  [transposed(): lax.all_to_all(blocks, 'seq', split_axis=0, concat_axis=0, tiled=True)]
where the time goes in v8:
time: 78.9 us; the launch traced here: 78.4 us
  waiting for transfers between devices  49 us (62%)
  Pallas kernels  13.5 us (17%)
  starting transfers between devices  11.7 us (15%)
  between operations  2.02 us (3%)
  local copies, waits for them, and re-layouts  1.41 us (2%)
    all_to_all x2, waiting for transfers between devices, transposed(): lax.all_to_all(blocks, 'seq', split_axis=0, concat_axis=0, tiled=True)  49 us
    all_to_all x2, starting transfers between devices, transposed(): lax.all_to_all(blocks, 'seq', split_axis=0, concat_axis=0, tiled=True)  11.7 us
    pallas_call x1, Pallas kernels, stacked_filter(): pl.pallas_call(functools.partial(stacked_filter_kernel, vars_dev, halves,...  8.14 us
    pallas_call x1, Pallas kernels, stacked_products(): pl.pallas_call(functools.partial(stacked_products_kernel, halves, vars_de...  3.56 us
    pallas_call x1, Pallas kernels, stacked_finish(): pl.pallas_call(functools.partial(stacked_finish_kernel, width // lane_til...  1.8 us
  transfers between devices with their start and end apart: 2, of which 2 were waited for; matrix products, arithmetic and copies ran while one was open for 3% of the time, Pallas kernels for 0%

profile of v8, /device:TPU:13, one launch (start us, length us, event | category | flops | bytes accessed | tf_op | source)
XLA Modules:
  0.0 78.4 jit_solution(6906116411695064791)
XLA Ops:
  0.6 0.0 copy-start.3
  0.6 3.6 %stacked_products.1 = bf16[16,272,128]{2,1,0:T(8,128)(2,1)} custom-call(s32[1]{0:T(128)} %bitcast.3.me_ref, s32[16]{0:T(128)} %offsets_ref.1, bf16[3,128,4096]{2,1,0:T(8,128)(2,1)} %streams_ref.1), custom_call_target="tpu_custom_call" | custom-call | flops 524288 | bytes 3145728 | tf_op jit(solution)/shard_map/stacked_products/pallas_call | solution.py:455
  4.2 0.0 copy-start.4
  4.2 0.0 copy-start
  4.2 0.0 copy-start.1
  4.3 0.0 copy-start.2
  4.3 6.7 %all-to-all-start = ((bf16[16,272,128]{2,1,0:T(8,128)(2,1)}), bf16[16,272,128]{2,1,0:T(8,128)(2,1)S(1)}, u32[]{:S(2)}, u32[]{:S(2)}) async-start(bf16[16,272,128]{2,1,0:T(8,128)(2,1)} %stacked_products.1), calls=%async_computation | async-start | bytes 2228224 | tf_op jit(solution)/shard_map/all_to_all | solution.py:638
  11.0 0.0 copy-done.4
  11.0 0.1 copy.11.refs_0_
  11.1 0.8 dynamic-slice_convert_fusion
  11.8 25.4 %all-to-all-done.refs_6_ = bf16[16,272,128]{2,1,0:T(8,128)(2,1)S(1)} async-done(((bf16[16,272,128]{2,1,0:T(8,128)(2,1)}), bf16[16,272,128]{2,1,0:T(8,128)(2,1)S(1)}, u32[]{:S(2)}, u32[]{:S(2)}) %all-to-all-start) | async-done | bytes 1114144 | tf_op jit(solution)/shard_map/all_to_all | solution.py:638
  37.2 0.0 copy-done.3
  37.2 0.0 copy-done
  37.2 0.0 copy-done.1
  37.2 0.0 copy-done.2
  37.2 8.1 %stacked_filter.1 = bf16[16,272,128]{2,1,0:T(8,128)(2,1)} custom-call(s32[16,1]{1,0:T(8,128)S(1)} %copy.11.refs_0_, f32[1,256]{1,0:T(1,128)S(1)} %bitcast.7, bf16[1024,256]{1,0:T(8,128)(2,1)S(1)} %copy-done.2, bf16[512,512]{1,0:T(8,128)(2,1)S(1)} %copy-done.3, bf16[256,512]{1,0:T(8,128)(2,1)S(1)} %copy-done.1, bf16[256,2048]{1,0:T(8,128)(2,1)S(1)} %copy-done, ...), custom_call_target="tpu_custom_call" | custom-call | flops 2751463424 | bytes 8388608 | tf_op jit(solution)/shard_map/stacked_filter/pallas_call | solution.py:569
  45.4 5.0 %all-to-all-start.1 = ((bf16[16,272,128]{2,1,0:T(8,128)(2,1)}), bf16[16,272,128]{2,1,0:T(8,128)(2,1)S(1)}, u32[]{:S(2)}, u32[]{:S(2)}) async-start(bf16[16,272,128]{2,1,0:T(8,128)(2,1)} %stacked_filter.1), calls=%async_computation.1 | async-start | bytes 2228224 | tf_op jit(solution)/shard_map/all_to_all | solution.py:638
  51.7 1.3 %slice_bitcast_fusion.gates_ref = bf16[128,4096]{1,0:T(8,128)(2,1)S(1)} fusion(bf16[3,128,4096]{2,1,0:T(8,128)(2,1)} %streams_ref.1), kind=kLoop, calls=%fused_computation | loop fusion | bytes 2097152 | tf_op jit(solution)/shard_map/squeeze | solution.py:672
  53.0 23.6 %all-to-all-done.1.back_ref = bf16[16,272,128]{2,1,0:T(8,128)(2,1)S(1)} async-done(((bf16[16,272,128]{2,1,0:T(8,128)(2,1)}), bf16[16,272,128]{2,1,0:T(8,128)(2,1)S(1)}, u32[]{:S(2)}, u32[]{:S(2)}) %all-to-all-start.1) | async-done | bytes 1114144 | tf_op jit(solution)/shard_map/all_to_all | solution.py:638
  76.6 1.8 %stacked_finish.1 = (bf16[128,4096]{1,0:T(8,128)(2,1)}, f32[1,2]{1,0:T(1,128)}) custom-call(s32[1]{0:T(128)S(6)} %copy.12.ref_ref, s32[1]{0:T(128)S(6)} %copy.13.alt_ref, bf16[128,4096]{1,0:T(8,128)(2,1)S(1)} %slice_bitcast_fusion.gates_ref, bf16[16,272,128]{2,1,0:T(8,128)(2,1)S(1)} %all-to-all-done.1.back_ref), custom_call_target="tpu_custom_call" | custom-call | flops 524288 | bytes 3145728 | tf_op jit(solution)/shard_map/stacked_finish/pallas_call | solution.py:617
  (1 shorter events, 0.0 us)
Async XLA Ops:
  0.6 36.6 %copy-start.3 = (bf16[512,512]{1,0:T(8,128)(2,1)S(1)}, bf16[512,512]{1,0:T(8,128)(2,1)}, u32[]{:S(2)}) copy-start(bf16[512,512]{1,0:T(8,128)(2,1)} %constant.17.clone.refs_3_) | copy-start | bytes 1572868
  4.2 6.8 %copy-start.4 = (s32[16]{0:T(128)S(1)}, s32[16]{0:T(128)}, u32[]{:S(2)}) copy-start(s32[16]{0:T(128)} %offsets_ref.1) | copy-start | bytes 196
  4.2 33.0 %copy-start = (bf16[256,2048]{1,0:T(8,128)(2,1)S(1)}, bf16[256,2048]{1,0:T(8,128)(2,1)}, u32[]{:S(2)}) copy-start(bf16[256,2048]{1,0:T(8,128)(2,1)} %refs_5_.1) | copy-start | bytes 3145732
  4.2 33.0 %copy-start.1 = (bf16[256,512]{1,0:T(8,128)(2,1)S(1)}, bf16[256,512]{1,0:T(8,128)(2,1)}, u32[]{:S(2)}) copy-start(bf16[256,512]{1,0:T(8,128)(2,1)} %refs_4_.1) | copy-start | bytes 786436
  4.3 33.0 %copy-start.2 = (bf16[1024,256]{1,0:T(8,128)(2,1)S(1)}, bf16[1024,256]{1,0:T(8,128)(2,1)}, u32[]{:S(2)}) copy-start(bf16[1024,256]{1,0:T(8,128)(2,1)} %constant.16.clone.refs_2_) | copy-start | bytes 1572868
  4.3 33.0 %all-to-all-start = ((bf16[16,272,128]{2,1,0:T(8,128)(2,1)}), bf16[16,272,128]{2,1,0:T(8,128)(2,1)S(1)}, u32[]{:S(2)}, u32[]{:S(2)}) async-start(bf16[16,272,128]{2,1,0:T(8,128)(2,1)} %stacked_products.1), calls=%async_computation | async-start | bytes 2228224 | tf_op jit(solution)/shard_map/all_to_all | solution.py:638
  45.4 31.2 %all-to-all-start.1 = ((bf16[16,272,128]{2,1,0:T(8,128)(2,1)}), bf16[16,272,128]{2,1,0:T(8,128)(2,1)S(1)}, u32[]{:S(2)}, u32[]{:S(2)}) async-start(bf16[16,272,128]{2,1,0:T(8,128)(2,1)} %stacked_filter.1), calls=%async_computation.1 | async-start | bytes 2228224 | tf_op jit(solution)/shard_map/all_to_all | solution.py:638

commit v9 on v8

--- a/solution.py
+++ b/solution.py
@@ -126,37 +126,38 @@
     )(taps, forward)
 
 
+def multiply_tile(points, spectrum_ref, joint, start, lanes):
+    n_blocks, double, _ = points.shape
+    upper = pl.ds(start, half_tile)
+    lower = pl.ds(pl.multiple_of(double // 2 + start, half_tile), half_tile)
+    signal = [(points[k, upper, lanes], points[k, lower, lanes]) for k in range(n_blocks)]
+    taps = [(spectrum_ref[k, upper, lanes], spectrum_ref[k, lower, lanes]) for k in range(n_blocks)]
+    before_re = jnp.zeros_like(signal[0][0])
+    before_im = before_re
+    for total in range(n_blocks):
+        sum_re = jnp.zeros_like(before_re)
+        sum_im = sum_re
+        for delay in range(total + 1):
+            a_re, a_im = signal[total - delay]
+            b_re, b_im = taps[delay]
+            sum_re += a_re * b_re - a_im * b_im
+            sum_im += a_re * b_im + a_im * b_re
+        joint[total, upper, lanes] = sum_re + before_im
+        joint[total, lower, lanes] = sum_im - before_re
+        before_re, before_im = sum_re, sum_im
+
+
 def multiply_points(points, spectrum_ref, joint):
     n_blocks, double, width = points.shape
-    block = double // 2
     lanes_step = min(width, lane_tile)
 
     def multiply_step(step, carry):
         start = pl.multiple_of(step * half_tile, half_tile)
-        upper = pl.ds(start, half_tile)
-        lower = pl.ds(pl.multiple_of(block + start, half_tile), half_tile)
         for first in range(0, width, lanes_step):
-            lanes = slice(first, first + lanes_step)
-            signal = [(points[k, upper, lanes], points[k, lower, lanes]) for k in range(n_blocks)]
-            taps = [
-                (spectrum_ref[k, upper, lanes], spectrum_ref[k, lower, lanes]) for k in range(n_blocks)
-            ]
-            before_re = jnp.zeros((half_tile, lanes_step), f32)
-            before_im = jnp.zeros((half_tile, lanes_step), f32)
-            for total in range(n_blocks):
-                sum_re = jnp.zeros((half_tile, lanes_step), f32)
-                sum_im = jnp.zeros((half_tile, lanes_step), f32)
-                for delay in range(total + 1):
-                    a_re, a_im = signal[total - delay]
-                    b_re, b_im = taps[delay]
-                    sum_re += a_re * b_re - a_im * b_im
-                    sum_im += a_re * b_im + a_im * b_re
-                joint[total, upper, lanes] = sum_re + before_im
-                joint[total, lower, lanes] = sum_im - before_re
-                before_re, before_im = sum_re, sum_im
+            multiply_tile(points, spectrum_ref, joint, start, slice(first, first + lanes_step))
         return carry
 
-    lax.fori_loop(0, block // half_tile, multiply_step, 0)
+    lax.fori_loop(0, double // 2 // half_tile, multiply_step, 0)
 
 
 def convolve(chunk_ref, spectrum_ref, forward_ref, inverse_ref, out_ref, points, tok_rows):
@@ -387,7 +388,7 @@
     )(ref_ids, alt_ids, streams, *backs)
 
 def stacked_products_kernel(halves, vars_dev, me_ref, offsets_ref, streams_ref, out_ref, *scratch):
-    gates, pairs, built, gate_sem, pair_sems, body_sems, tail_sem = scratch
+    gates, pairs, built, gate_sems, pair_sems, out_sems = scratch
     n_devices = built.shape[0]
     pieces, _, tok_rows, lanes_each = pairs.shape
     body = halves * tok_rows
@@ -402,69 +403,65 @@
             streams_ref.at[pl.ds(1, 2), :, lanes], pairs.at[piece], pair_sems.at[piece]
         )
 
-    def body_copy(rank):
-        rows = pl.ds(0, body)
-        return pltpu.make_async_copy(built.at[rank, rows], out_ref.at[rank, rows], body_sems.at[rank])
-
-    gate_copy = pltpu.make_async_copy(streams_ref.at[0], gates, gate_sem.at[0])
+    local_rows = [var * slot + offsets_ref[me * vars_dev + var] for var in range(vars_dev)]
+
+    def out_copy(owner):
+        return pltpu.make_async_copy(built.at[owner], out_ref.at[owner], out_sems.at[owner])
+
+    def gate_copy(var):
+        start = pl.multiple_of(local_rows[var] // row_tile * row_tile, row_tile)
+        return pltpu.make_async_copy(
+            streams_ref.at[0, pl.ds(start, row_tile), :], gates.at[var], gate_sems.at[var]
+        )
+
+    for var in range(vars_dev):
+        gate_copy(var).start()
     for piece in range(pieces):
         pair_copy(piece).start()
-    gate_copy.start()
+    extra = built.shape[1] - body
+    row = lax.broadcasted_iota(jnp.int32, gates.shape[1:], 0)
+    place = lax.broadcasted_iota(jnp.int32, (extra, lane_tile), 0)
+    gate_rows = []
+    for var in range(vars_dev):
+        gate_copy(var).wait()
+        mine = jnp.where(row == local_rows[var] % row_tile, gates[var].astype(f32), 0.0)
+        gate_rows.append(jnp.sum(mine, axis=0, keepdims=True))
     for piece in range(pieces):
         pair_copy(piece).wait()
         for member in range(owners):
             owner = piece * owners + member
+            tail = jnp.zeros((extra, lane_tile), f32)
             for half in range(halves):
                 lanes = slice(member * width + half * lane_tile, member * width + (half + 1) * lane_tile)
                 rows = slice(half * tok_rows, (half + 1) * tok_rows)
                 built[owner, rows, :] = pairs[piece, 0, :, lanes] * pairs[piece, 1, :, lanes]
-            body_copy(owner).start()
-
-    extra = built.shape[1] - body
-    row = lax.broadcasted_iota(jnp.int32, (row_tile, gates.shape[1]), 0)
-    place = lax.broadcasted_iota(jnp.int32, (extra, lane_tile), 0)
-    gate_copy.wait()
-    gate_rows = []
-    for var in range(vars_dev):
-        local = var * slot + offsets_ref[me * vars_dev + var]
-        start = pl.multiple_of(local // row_tile * row_tile, row_tile)
-        tile = gates[pl.ds(start, row_tile), :].astype(f32)
-        mine = jnp.where(row == local % row_tile, tile, 0.0)
-        gate_rows.append(jnp.sum(mine, axis=0, keepdims=True))
+                start = owner * width + half * lane_tile
+                for var in range(vars_dev):
+                    mine = gate_rows[var][:, start : start + lane_tile]
+                    tail = jnp.where(place == half * vars_dev + var, mine, tail)
+            built[owner, body:, :] = tail.astype(bf16)
+            out_copy(owner).start()
     for owner in range(n_devices):
-        tail = jnp.zeros((extra, lane_tile), f32)
-        for half in range(halves):
-            start = owner * width + half * lane_tile
-            for var in range(vars_dev):
-                mine = gate_rows[var][:, start : start + lane_tile]
-                tail = jnp.where(place == half * vars_dev + var, mine, tail)
-        built[owner, body:, :] = tail.astype(bf16)
-    rows = pl.ds(body, extra)
-    tail_copy = pltpu.make_async_copy(built.at[:, rows], out_ref.at[:, rows], tail_sem.at[0])
-    tail_copy.start()
-    for rank in range(n_devices):
-        body_copy(rank).wait()
-    tail_copy.wait()
+        out_copy(owner).wait()
 
 
 def stacked_products(me, offsets, streams, vars_dev, n_devices, extra):
     _, tok_rows, model_width = streams.shape
     halves = model_width // n_devices // lane_tile
     rows_out = halves * tok_rows + extra
-    pieces = math.gcd(n_devices, 4)
+    pieces = math.gcd(n_devices, 8)
     return pl.pallas_call(
         functools.partial(stacked_products_kernel, halves, vars_dev),
         in_specs=[pl.BlockSpec(memory_space=pltpu.SMEM)] * 2 + [pl.BlockSpec(memory_space=pl.ANY)],
         out_specs=pl.BlockSpec(memory_space=pl.ANY),
         out_shape=jax.ShapeDtypeStruct((n_devices, rows_out, lane_tile), bf16),
         scratch_shapes=[
-            pltpu.VMEM((tok_rows, model_width), bf16),
+            pltpu.VMEM((vars_dev, row_tile, model_width), bf16),
             pltpu.VMEM((pieces, 2, tok_rows, model_width // pieces), bf16),
             pltpu.VMEM((n_devices, rows_out, lane_tile), bf16),
-            pltpu.SemaphoreType.DMA((1,)),
+            pltpu.SemaphoreType.DMA((vars_dev,)),
             pltpu.SemaphoreType.DMA((pieces,)),
             pltpu.SemaphoreType.DMA((n_devices,)),
-            pltpu.SemaphoreType.DMA((1,)),
         ],
         compiler_params=pltpu.CompilerParams(vmem_limit_bytes=60 * MIB),
         cost_estimate=pl.CostEstimate(
@@ -476,55 +473,81 @@
 
 def stacked_filter_kernel(vars_dev, halves, tok_rows, *refs):
     positions_ref, gain_ref, forward, inverse, unembed, taps, arrived = refs[:7]
-    out_ref, points, joint, spectrum, packed, leaving, body_sems, tail_sem = refs[7:]
+    out_ref, packed, leaving, body_sems, tail_sem = refs[7:12]
+    points, spectrum, joint = (refs[12 + k * halves : 12 + (k + 1) * halves] for k in range(3))
     n_devices = arrived.shape[0]
     body = halves * tok_rows
-    n_blocks, double, width = points.shape
+    n_blocks, double, _ = points[0].shape
     block = double // 2
     per_block = block // tok_rows
     group = 2 if n_blocks % 2 == 0 else 1
-
-    def body_copy(rank):
+    n_groups = n_blocks // group
+    tiles = block // half_tile
+    n_steps = math.gcd(n_groups, tiles)
+    groups_each, tiles_each = n_groups // n_steps, tiles // n_steps
+
+    def body_copy(device):
         rows = pl.ds(0, body)
-        return pltpu.make_async_copy(leaving.at[rank, rows], out_ref.at[rank, rows], body_sems.at[rank])
-
-    for index in range(n_blocks):
+        return pltpu.make_async_copy(
+            leaving.at[device, rows], out_ref.at[device, rows], body_sems.at[device]
+        )
+
+    def transform(half, first):
+        channels = slice(half * lane_tile, (half + 1) * lane_tile)
+        rows = slice(half * tok_rows, (half + 1) * tok_rows)
+        filters = [
+            taps[channels, pl.ds(pl.multiple_of((first + m) * block, lane_tile), block)]
+            for m in range(group)
+        ]
         both = lax.dot_general(
             forward[...],
-            taps[:, index * block : (index + 1) * block],
+            jnp.concatenate(filters, axis=0),
             (((1,), (1,)), ((), ())),
             preferred_element_type=f32,
         )
-        spectrum[index] = both[:double] + both[double:]
-
-    for step in range(0, n_blocks, group):
-        pieces = []
-        for index in range(step, step + group):
-            for half in range(halves):
-                rows = slice(half * tok_rows, (half + 1) * tok_rows)
-                parts = [arrived[index * per_block + m, rows, :] for m in range(per_block)]
-                pieces.append(jnp.concatenate(parts, axis=0))
-        signal = jnp.concatenate(pieces, axis=1)
-        both = jnp.dot(forward[...], signal, preferred_element_type=f32)
         total = both[:double] + both[double:]
-        for member in range(group):
-            points[step + member] = total[:, member * width : (member + 1) * width]
-    multiply_points(points, spectrum, joint)
-
-    for step in range(0, n_blocks, group):
-        highs, lows = split_bf16(jnp.concatenate([joint[step + m] for m in range(group)], axis=1))
+        for m in range(group):
+            spectrum[half][first + m] = total[:, m * lane_tile : (m + 1) * lane_tile]
+        signal = [
+            jnp.concatenate([arrived[(first + m) * per_block + k, rows, :] for k in range(per_block)], axis=0)
+            for m in range(group)
+        ]
+        both = jnp.dot(forward[...], jnp.concatenate(signal, axis=1), preferred_element_type=f32)
+        total = both[:double] + both[double:]
+        for m in range(group):
+            points[half][first + m] = total[:, m * lane_tile : (m + 1) * lane_tile]
+
+    def invert(half, first):
+        rows = slice(half * tok_rows, (half + 1) * tok_rows)
+        highs, lows = split_bf16(jnp.concatenate([joint[half][first + m] for m in range(group)], axis=1))
         both = jnp.dot(inverse[...], highs, preferred_element_type=f32)
         rest = jnp.dot(inverse[:block, :], lows, preferred_element_type=f32)
         result = (both[:block] + both[block:] + rest).astype(bf16)
-        for index in range(group):
-            for member in range(per_block):
-                rank = (step + index) * per_block + member
-                for half in range(halves):
-                    start = index * width + half * lane_tile
-                    leaving[rank, half * tok_rows : (half + 1) * tok_rows, :] = result[
-                        member * tok_rows : (member + 1) * tok_rows, start : start + lane_tile
-                    ]
-                body_copy(rank).start()
+        for m in range(group):
+            for k in range(per_block):
+                leaving[(first + m) * per_block + k, rows, :] = result[
+                    k * tok_rows : (k + 1) * tok_rows, m * lane_tile : (m + 1) * lane_tile
+                ]
+                if half == halves - 1:
+                    body_copy((first + m) * per_block + k).start()
+
+    for stage in range(halves + 2):
+
+        def run_step(step, carry, stage=stage):
+            if 0 <= stage - 2:
+                for index in range(groups_each):
+                    invert(stage - 2, (step * groups_each + index) * group)
+            if 0 <= stage - 1 < halves:
+                for index in range(tiles_each):
+                    start = pl.multiple_of((step * tiles_each + index) * half_tile, half_tile)
+                    half = stage - 1
+                    multiply_tile(points[half], spectrum[half], joint[half], start, slice(None))
+            if stage < halves:
+                for index in range(groups_each):
+                    transform(stage, (step * groups_each + index) * group)
+            return carry
+
+        lax.fori_loop(0, n_steps, run_step, 0)
 
     length = n_devices * tok_rows
     column = lax.broadcasted_iota(jnp.int32, (positions_ref.shape[0], length), 1)
@@ -553,8 +576,8 @@
     rows = pl.ds(body, extra)
     tail_copy = pltpu.make_async_copy(leaving.at[:, rows], out_ref.at[:, rows], tail_sem.at[0])
     tail_copy.start()
-    for rank in range(n_devices):
-        body_copy(rank).wait()
+    for device in range(n_devices):
+        body_copy(device).wait()
     tail_copy.wait()
 
 
@@ -571,13 +594,13 @@
         in_specs=[whole_spec()] * 7,
         out_specs=pl.BlockSpec(memory_space=pl.ANY),
         out_shape=jax.ShapeDtypeStruct((n_devices, rows_out, lane_tile), bf16),
-        scratch_shapes=[pltpu.VMEM((n_blocks, double, width), f32)] * 3
-        + [
+        scratch_shapes=[
             pltpu.VMEM((n_devices * extra, lane_tile), f32),
             pltpu.VMEM((n_devices, rows_out, lane_tile), bf16),
             pltpu.SemaphoreType.DMA((n_devices,)),
             pltpu.SemaphoreType.DMA((1,)),
-        ],
+        ]
+        + [pltpu.VMEM((n_blocks, double, lane_tile), f32)] * (3 * halves),
         compiler_params=pltpu.CompilerParams(vmem_limit_bytes=24 * MIB),
         cost_estimate=pl.CostEstimate(flops=flops, bytes_accessed=8 * MIB, transcendentals=0),
         name="stacked_filter",
@@ -585,7 +608,7 @@
 
 
 def stacked_finish_kernel(halves, vars_dev, vocab, ref_ref, alt_ref, gates_ref, back_ref, *refs):
-    mixed_ref, scores_ref, results, out_sems = refs
+    mixed_ref, scores_ref, results, scores, out_sems, score_sem = refs
     n_devices, tok_rows, width = results.shape
 
     def out_copy(owner):
@@ -595,18 +618,21 @@
 
     sums = None
     for owner in range(n_devices):
+        tail = back_ref[owner, halves * tok_rows :, :].astype(f32)
+        sums = tail if sums is None else sums + tail
         for half in range(halves):
             lanes = slice(half * lane_tile, (half + 1) * lane_tile)
             start = owner * width + half * lane_tile
             filtered = back_ref[owner, half * tok_rows : (half + 1) * tok_rows, :]
             results[owner, :, lanes] = gates_ref[:, start : start + lane_tile] * filtered
         out_copy(owner).start()
-        tail = back_ref[owner, halves * tok_rows :, :].astype(f32)
-        sums = tail if sums is None else sums + tail
     model_width = n_devices * width
-    scores_ref[...] = final_scores(sums, 2, vars_dev, vocab, model_width, ref_ref, alt_ref)
+    scores[...] = final_scores(sums, 2, vars_dev, vocab, model_width, ref_ref, alt_ref)
+    score_copy = pltpu.make_async_copy(scores, scores_ref, score_sem.at[0])
+    score_copy.start()
     for owner in range(n_devices):
         out_copy(owner).wait()
+    score_copy.wait()
 
 
 def stacked_finish(ref_ids, alt_ids, gates, back, vocab):
@@ -617,14 +643,16 @@
     return pl.pallas_call(
         functools.partial(stacked_finish_kernel, width // lane_tile, vars_dev, vocab),
         in_specs=[pl.BlockSpec(memory_space=pltpu.SMEM)] * 2 + [whole_spec()] * 2,
-        out_specs=[pl.BlockSpec(memory_space=pl.ANY), whole_spec()],
+        out_specs=[pl.BlockSpec(memory_space=pl.ANY)] * 2,
         out_shape=[
             jax.ShapeDtypeStruct((tok_rows, model_width), bf16),
             jax.ShapeDtypeStruct((vars_dev, 2), f32),
         ],
         scratch_shapes=[
             pltpu.VMEM((n_devices, tok_rows, width), bf16),
+            pltpu.VMEM((vars_dev, 2), f32),
             pltpu.SemaphoreType.DMA((n_devices,)),
+            pltpu.SemaphoreType.DMA((1,)),
         ],
         compiler_params=pltpu.CompilerParams(vmem_limit_bytes=16 * MIB),
         cost_estimate=pl.CostEstimate(

time: 78.9 us -> 80.8 us (1.024)
  Pallas kernels: 13.5 us -> 15.4 us
    pallas_call x1, Pallas kernels: 8.14 us -> 10.4 us  [stacked_filter(): pl.pallas_call(functools.partial(stacked_filter_kernel, vars_dev, halves,...]
where the time goes in v9:
time: 80.8 us; the launch traced here: 80.3 us
  waiting for transfers between devices  49 us (61%)
  Pallas kernels  15.4 us (19%)
  starting transfers between devices  11.7 us (14%)
  between operations  2.02 us (2%)
  local copies, waits for them, and re-layouts  1.41 us (2%)
    all_to_all x2, waiting for transfers between devices, transposed(): lax.all_to_all(blocks, 'seq', split_axis=0, concat_axis=0, tiled=True)  49 us
    all_to_all x2, starting transfers between devices, transposed(): lax.all_to_all(blocks, 'seq', split_axis=0, concat_axis=0, tiled=True)  11.7 us
    pallas_call x1, Pallas kernels, stacked_filter(): pl.pallas_call(functools.partial(stacked_filter_kernel, vars_dev, halves,...  10.4 us
    pallas_call x1, Pallas kernels, stacked_products(): pl.pallas_call(functools.partial(stacked_products_kernel, halves, vars_de...  3.63 us
  transfers between devices with their start and end apart: 2, of which 2 were waited for; matrix products, arithmetic and copies ran while one was open for 3% of the time, Pallas kernels for 0%

profile of v9, /device:TPU:13, one launch (start us, length us, event | category | flops | bytes accessed | tf_op | source)
XLA Modules:
  0.0 80.3 jit_solution(7551330106178179224)
XLA Ops:
  0.6 0.0 copy-start.3
  0.6 3.6 %stacked_products.1 = bf16[16,272,128]{2,1,0:T(8,128)(2,1)} custom-call(s32[1]{0:T(128)} %bitcast.3.me_ref, s32[16]{0:T(128)} %offsets_ref.1, bf16[3,128,4096]{2,1,0:T(8,128)(2,1)} %streams_ref.1), custom_call_target="tpu_custom_call" | custom-call | flops 524288 | bytes 3145728 | tf_op jit(solution)/shard_map/stacked_products/pallas_call | solution.py:453
  4.3 0.0 copy-start.4
  4.3 0.0 copy-start
  4.3 0.0 copy-start.1
  4.3 0.0 copy-start.2
  4.3 6.7 %all-to-all-start = ((bf16[16,272,128]{2,1,0:T(8,128)(2,1)}), bf16[16,272,128]{2,1,0:T(8,128)(2,1)S(1)}, u32[]{:S(2)}, u32[]{:S(2)}) async-start(bf16[16,272,128]{2,1,0:T(8,128)(2,1)} %stacked_products.1), calls=%async_computation | async-start | bytes 2228224 | tf_op jit(solution)/shard_map/all_to_all | solution.py:666
  11.1 0.0 copy-done.4
  11.1 0.1 copy.11.refs_0_
  11.2 0.8 dynamic-slice_convert_fusion
  11.9 25.4 %all-to-all-done.refs_6_ = bf16[16,272,128]{2,1,0:T(8,128)(2,1)S(1)} async-done(((bf16[16,272,128]{2,1,0:T(8,128)(2,1)}), bf16[16,272,128]{2,1,0:T(8,128)(2,1)S(1)}, u32[]{:S(2)}, u32[]{:S(2)}) %all-to-all-start) | async-done | bytes 1114144 | tf_op jit(solution)/shard_map/all_to_all | solution.py:666
  37.3 0.0 copy-done.3
  37.3 0.0 copy-done
  37.3 0.0 copy-done.1
  37.3 0.0 copy-done.2
  37.3 10.4 %stacked_filter.1 = bf16[16,272,128]{2,1,0:T(8,128)(2,1)} custom-call(s32[16,1]{1,0:T(8,128)S(1)} %copy.11.refs_0_, f32[1,256]{1,0:T(1,128)S(1)} %bitcast.7, bf16[1024,256]{1,0:T(8,128)(2,1)S(1)} %copy-done.2, bf16[512,512]{1,0:T(8,128)(2,1)S(1)} %copy-done.3, bf16[256,512]{1,0:T(8,128)(2,1)S(1)} %copy-done.1, bf16[256,2048]{1,0:T(8,128)(2,1)S(1)} %copy-done, ...), custom_call_target="tpu_custom_call" | custom-call | flops 2751463424 | bytes 8388608 | tf_op jit(solution)/shard_map/stacked_filter/pallas_call | solution.py:592
  47.8 5.0 %all-to-all-start.1 = ((bf16[16,272,128]{2,1,0:T(8,128)(2,1)}), bf16[16,272,128]{2,1,0:T(8,128)(2,1)S(1)}, u32[]{:S(2)}, u32[]{:S(2)}) async-start(bf16[16,272,128]{2,1,0:T(8,128)(2,1)} %stacked_filter.1), calls=%async_computation.1 | async-start | bytes 2228224 | tf_op jit(solution)/shard_map/all_to_all | solution.py:666
  54.1 1.3 %slice_bitcast_fusion.gates_ref = bf16[128,4096]{1,0:T(8,128)(2,1)S(1)} fusion(bf16[3,128,4096]{2,1,0:T(8,128)(2,1)} %streams_ref.1), kind=kLoop, calls=%fused_computation | loop fusion | bytes 2097152 | tf_op jit(solution)/shard_map/squeeze | solution.py:700
  55.4 23.6 %all-to-all-done.1.back_ref = bf16[16,272,128]{2,1,0:T(8,128)(2,1)S(1)} async-done(((bf16[16,272,128]{2,1,0:T(8,128)(2,1)}), bf16[16,272,128]{2,1,0:T(8,128)(2,1)S(1)}, u32[]{:S(2)}, u32[]{:S(2)}) %all-to-all-start.1) | async-done | bytes 1114144 | tf_op jit(solution)/shard_map/all_to_all | solution.py:666
  79.0 1.3 %stacked_finish.1 = (bf16[128,4096]{1,0:T(8,128)(2,1)}, f32[1,2]{1,0:T(1,128)}) custom-call(s32[1]{0:T(128)S(6)} %copy.12.ref_ref, s32[1]{0:T(128)S(6)} %copy.13.alt_ref, bf16[128,4096]{1,0:T(8,128)(2,1)S(1)} %slice_bitcast_fusion.gates_ref, bf16[16,272,128]{2,1,0:T(8,128)(2,1)S(1)} %all-to-all-done.1.back_ref), custom_call_target="tpu_custom_call" | custom-call | flops 524288 | bytes 3145728 | tf_op jit(solution)/shard_map/stacked_finish/pallas_call | solution.py:643
  (1 shorter events, 0.0 us)
Async XLA Ops:
  0.6 36.7 %copy-start.3 = (bf16[512,512]{1,0:T(8,128)(2,1)S(1)}, bf16[512,512]{1,0:T(8,128)(2,1)}, u32[]{:S(2)}) copy-start(bf16[512,512]{1,0:T(8,128)(2,1)} %constant.17.clone.refs_3_) | copy-start | bytes 1572868
  4.3 6.8 %copy-start.4 = (s32[16]{0:T(128)S(1)}, s32[16]{0:T(128)}, u32[]{:S(2)}) copy-start(s32[16]{0:T(128)} %offsets_ref.1) | copy-start | bytes 196
  4.3 33.0 %copy-start = (bf16[256,2048]{1,0:T(8,128)(2,1)S(1)}, bf16[256,2048]{1,0:T(8,128)(2,1)}, u32[]{:S(2)}) copy-start(bf16[256,2048]{1,0:T(8,128)(2,1)} %refs_5_.1) | copy-start | bytes 3145732
  4.3 33.0 %copy-start.1 = (bf16[256,512]{1,0:T(8,128)(2,1)S(1)}, bf16[256,512]{1,0:T(8,128)(2,1)}, u32[]{:S(2)}) copy-start(bf16[256,512]{1,0:T(8,128)(2,1)} %refs_4_.1) | copy-start | bytes 786436
  4.3 33.0 %copy-start.2 = (bf16[1024,256]{1,0:T(8,128)(2,1)S(1)}, bf16[1024,256]{1,0:T(8,128)(2,1)}, u32[]{:S(2)}) copy-start(bf16[1024,256]{1,0:T(8,128)(2,1)} %constant.16.clone.refs_2_) | copy-start | bytes 1572868
  4.3 33.0 %all-to-all-start = ((bf16[16,272,128]{2,1,0:T(8,128)(2,1)}), bf16[16,272,128]{2,1,0:T(8,128)(2,1)S(1)}, u32[]{:S(2)}, u32[]{:S(2)}) async-start(bf16[16,272,128]{2,1,0:T(8,128)(2,1)} %stacked_products.1), calls=%async_computation | async-start | bytes 2228224 | tf_op jit(solution)/shard_map/all_to_all | solution.py:666
  47.8 31.2 %all-to-all-start.1 = ((bf16[16,272,128]{2,1,0:T(8,128)(2,1)}), bf16[16,272,128]{2,1,0:T(8,128)(2,1)S(1)}, u32[]{:S(2)}, u32[]{:S(2)}) async-start(bf16[16,272,128]{2,1,0:T(8,128)(2,1)} %stacked_filter.1), calls=%async_computation.1 | async-start | bytes 2228224 | tf_op jit(solution)/shard_map/all_to_all | solution.py:666

commit v10 on v9

--- a/solution.py
+++ b/solution.py
@@ -387,14 +387,14 @@
         name="finish",
     )(ref_ids, alt_ids, streams, *backs)
 
-def stacked_products_kernel(halves, vars_dev, me_ref, offsets_ref, streams_ref, out_ref, *scratch):
-    gates, pairs, built, gate_sems, pair_sems, out_sems = scratch
+def stacked_products_kernel(halves, vars_dev, offsets_ref, streams_ref, out_ref, *scratch):
+    gates, pairs, built, offsets, gate_sems, pair_sems, out_sems, offset_sem = scratch
     n_devices = built.shape[0]
     pieces, _, tok_rows, lanes_each = pairs.shape
     body = halves * tok_rows
     width = halves * lane_tile
     owners = lanes_each // width
-    me = me_ref[0]
+    me = lax.axis_index("seq")
     slot = tok_rows // vars_dev
 
     def pair_copy(piece):
@@ -403,7 +403,6 @@
             streams_ref.at[pl.ds(1, 2), :, lanes], pairs.at[piece], pair_sems.at[piece]
         )
 
-    local_rows = [var * slot + offsets_ref[me * vars_dev + var] for var in range(vars_dev)]
 
     def out_copy(owner):
         return pltpu.make_async_copy(built.at[owner], out_ref.at[owner], out_sems.at[owner])
@@ -414,10 +413,14 @@
             streams_ref.at[0, pl.ds(start, row_tile), :], gates.at[var], gate_sems.at[var]
         )
 
+    offset_copy = pltpu.make_async_copy(offsets_ref, offsets, offset_sem.at[0])
+    offset_copy.start()
+    for piece in range(pieces):
+        pair_copy(piece).start()
+    offset_copy.wait()
+    local_rows = [var * slot + offsets[me * vars_dev + var] for var in range(vars_dev)]
     for var in range(vars_dev):
         gate_copy(var).start()
-    for piece in range(pieces):
-        pair_copy(piece).start()
     extra = built.shape[1] - body
     row = lax.broadcasted_iota(jnp.int32, gates.shape[1:], 0)
     place = lax.broadcasted_iota(jnp.int32, (extra, lane_tile), 0)
@@ -445,60 +448,50 @@
         out_copy(owner).wait()
 
 
-def stacked_products(me, offsets, streams, vars_dev, n_devices, extra):
+def stacked_products(offsets, streams, vars_dev, n_devices, extra):
     _, tok_rows, model_width = streams.shape
     halves = model_width // n_devices // lane_tile
     rows_out = halves * tok_rows + extra
     pieces = math.gcd(n_devices, 8)
     return pl.pallas_call(
         functools.partial(stacked_products_kernel, halves, vars_dev),
-        in_specs=[pl.BlockSpec(memory_space=pltpu.SMEM)] * 2 + [pl.BlockSpec(memory_space=pl.ANY)],
+        in_specs=[pl.BlockSpec(memory_space=pl.ANY)] * 2,
         out_specs=pl.BlockSpec(memory_space=pl.ANY),
         out_shape=jax.ShapeDtypeStruct((n_devices, rows_out, lane_tile), bf16),
         scratch_shapes=[
             pltpu.VMEM((vars_dev, row_tile, model_width), bf16),
             pltpu.VMEM((pieces, 2, tok_rows, model_width // pieces), bf16),
             pltpu.VMEM((n_devices, rows_out, lane_tile), bf16),
+            pltpu.SMEM(offsets.shape, jnp.int32),
             pltpu.SemaphoreType.DMA((vars_dev,)),
             pltpu.SemaphoreType.DMA((pieces,)),
             pltpu.SemaphoreType.DMA((n_devices,)),
+            pltpu.SemaphoreType.DMA((1,)),
         ],
         compiler_params=pltpu.CompilerParams(vmem_limit_bytes=60 * MIB),
         cost_estimate=pl.CostEstimate(
             flops=tok_rows * model_width, bytes_accessed=6 * tok_rows * model_width, transcendentals=0
         ),
         name="stacked_products",
-    )(me, offsets, streams)
+    )(offsets, streams)
 
 
 def stacked_filter_kernel(vars_dev, halves, tok_rows, *refs):
     positions_ref, gain_ref, forward, inverse, unembed, taps, arrived = refs[:7]
-    out_ref, packed, leaving, body_sems, tail_sem = refs[7:12]
-    points, spectrum, joint = (refs[12 + k * halves : 12 + (k + 1) * halves] for k in range(3))
+    out_ref, points, joint, spectrum, packed, leaving, body_sems, tail_sem = refs[7:]
     n_devices = arrived.shape[0]
     body = halves * tok_rows
-    n_blocks, double, _ = points[0].shape
+    n_blocks, double, width = points.shape
     block = double // 2
     per_block = block // tok_rows
-    group = 2 if n_blocks % 2 == 0 else 1
-    n_groups = n_blocks // group
-    tiles = block // half_tile
-    n_steps = math.gcd(n_groups, tiles)
-    groups_each, tiles_each = n_groups // n_steps, tiles // n_steps
-
-    def body_copy(device):
+    group = math.gcd(n_blocks, 4)
+
+    def body_copy(rank):
         rows = pl.ds(0, body)
-        return pltpu.make_async_copy(
-            leaving.at[device, rows], out_ref.at[device, rows], body_sems.at[device]
-        )
-
-    def transform(half, first):
-        channels = slice(half * lane_tile, (half + 1) * lane_tile)
-        rows = slice(half * tok_rows, (half + 1) * tok_rows)
-        filters = [
-            taps[channels, pl.ds(pl.multiple_of((first + m) * block, lane_tile), block)]
-            for m in range(group)
-        ]
+        return pltpu.make_async_copy(leaving.at[rank, rows], out_ref.at[rank, rows], body_sems.at[rank])
+
+    for step in range(0, n_blocks, group):
+        filters = [taps[:, index * block : (index + 1) * block] for index in range(step, step + group)]
         both = lax.dot_general(
             forward[...],
             jnp.concatenate(filters, axis=0),
@@ -506,48 +499,37 @@
             preferred_element_type=f32,
         )
         total = both[:double] + both[double:]
-        for m in range(group):
-            spectrum[half][first + m] = total[:, m * lane_tile : (m + 1) * lane_tile]
-        signal = [
-            jnp.concatenate([arrived[(first + m) * per_block + k, rows, :] for k in range(per_block)], axis=0)
-            for m in range(group)
-        ]
-        both = jnp.dot(forward[...], jnp.concatenate(signal, axis=1), preferred_element_type=f32)
+        for member in range(group):
+            spectrum[step + member] = total[:, member * width : (member + 1) * width]
+
+    for step in range(0, n_blocks, group):
+        pieces = []
+        for index in range(step, step + group):
+            for half in range(halves):
+                rows = slice(half * tok_rows, (half + 1) * tok_rows)
+                parts = [arrived[index * per_block + m, rows, :] for m in range(per_block)]
+                pieces.append(jnp.concatenate(parts, axis=0))
+        signal = jnp.concatenate(pieces, axis=1)
+        both = jnp.dot(forward[...], signal, preferred_element_type=f32)
         total = both[:double] + both[double:]
-        for m in range(group):
-            points[half][first + m] = total[:, m * lane_tile : (m + 1) * lane_tile]
-
-    def invert(half, first):
-        rows = slice(half * tok_rows, (half + 1) * tok_rows)
-        highs, lows = split_bf16(jnp.concatenate([joint[half][first + m] for m in range(group)], axis=1))
+        for member in range(group):
+            points[step + member] = total[:, member * width : (member + 1) * width]
+    multiply_points(points, spectrum, joint)
+
+    for step in range(0, n_blocks, group):
+        highs, lows = split_bf16(jnp.concatenate([joint[step + m] for m in range(group)], axis=1))
         both = jnp.dot(inverse[...], highs, preferred_element_type=f32)
         rest = jnp.dot(inverse[:block, :], lows, preferred_element_type=f32)
         result = (both[:block] + both[block:] + rest).astype(bf16)
-        for m in range(group):
-            for k in range(per_block):
-                leaving[(first + m) * per_block + k, rows, :] = result[
-                    k * tok_rows : (k + 1) * tok_rows, m * lane_tile : (m + 1) * lane_tile
-                ]
-                if half == halves - 1:
-                    body_copy((first + m) * per_block + k).start()
-
-    for stage in range(halves + 2):
-
-        def run_step(step, carry, stage=stage):
-            if 0 <= stage - 2:
-                for index in range(groups_each):
-                    invert(stage - 2, (step * groups_each + index) * group)
-            if 0 <= stage - 1 < halves:
-                for index in range(tiles_each):
-                    start = pl.multiple_of((step * tiles_each + index) * half_tile, half_tile)
-                    half = stage - 1
-                    multiply_tile(points[half], spectrum[half], joint[half], start, slice(None))
-            if stage < halves:
-                for index in range(groups_each):
-                    transform(stage, (step * groups_each + index) * group)
-            return carry
-
-        lax.fori_loop(0, n_steps, run_step, 0)
+        for index in range(group):
+            for member in range(per_block):
+                rank = (step + index) * per_block + member
+                for half in range(halves):
+                    start = index * width + half * lane_tile
+                    leaving[rank, half * tok_rows : (half + 1) * tok_rows, :] = result[
+                        member * tok_rows : (member + 1) * tok_rows, start : start + lane_tile
+                    ]
+                body_copy(rank).start()
 
     length = n_devices * tok_rows
     column = lax.broadcasted_iota(jnp.int32, (positions_ref.shape[0], length), 1)
@@ -576,8 +558,8 @@
     rows = pl.ds(body, extra)
     tail_copy = pltpu.make_async_copy(leaving.at[:, rows], out_ref.at[:, rows], tail_sem.at[0])
     tail_copy.start()
-    for device in range(n_devices):
-        body_copy(device).wait()
+    for rank in range(n_devices):
+        body_copy(rank).wait()
     tail_copy.wait()
 
 
@@ -594,13 +576,13 @@
         in_specs=[whole_spec()] * 7,
         out_specs=pl.BlockSpec(memory_space=pl.ANY),
         out_shape=jax.ShapeDtypeStruct((n_devices, rows_out, lane_tile), bf16),
-        scratch_shapes=[
+        scratch_shapes=[pltpu.VMEM((n_blocks, double, width), f32)] * 3
+        + [
             pltpu.VMEM((n_devices * extra, lane_tile), f32),
             pltpu.VMEM((n_devices, rows_out, lane_tile), bf16),
             pltpu.SemaphoreType.DMA((n_devices,)),
             pltpu.SemaphoreType.DMA((1,)),
-        ]
-        + [pltpu.VMEM((n_blocks, double, lane_tile), f32)] * (3 * halves),
+        ],
         compiler_params=pltpu.CompilerParams(vmem_limit_bytes=24 * MIB),
         cost_estimate=pl.CostEstimate(flops=flops, bytes_accessed=8 * MIB, transcendentals=0),
         name="stacked_filter",
@@ -689,10 +671,9 @@
     my_gain = lax.dynamic_slice_in_dim(gain, my_index * group_width, group_width).astype(f32)
 
     if chunks * lane_tile == group_width:
-        me = jnp.reshape(my_index, (1,)).astype(jnp.int32)
         gate_extra = round_up(chunks * vars_dev, row_tile)
         score_extra = round_up(2 * vars_dev * (vocab // lane_tile + 1), row_tile)
-        arrived = transposed(stacked_products(me, offsets, streams, vars_dev, n_devices, gate_extra))
+        arrived = transposed(stacked_products(offsets, streams, vars_dev, n_devices, gate_extra))
         tables = (forward, inverse, unembed, long_filter)
         gain_row = my_gain[None, :]
         leaving = stacked_filter(positions, gain_row, tables, arrived, vars_dev, tok_rows, score_extra)

time: 80.8 us -> 78 us (0.965)
  Pallas kernels: 15.4 us -> 12.6 us
    pallas_call x1, Pallas kernels: 10.4 us -> 8.14 us  [stacked_filter(): pl.pallas_call(functools.partial(stacked_filter_kernel, vars_dev, halves,...]
where the time goes in v10:
time: 78 us; the launch traced here: 77.5 us
  waiting for transfers between devices  49 us (63%)
  Pallas kernels  12.6 us (16%)
  starting transfers between devices  11.7 us (15%)
  between operations  2.01 us (3%)
  local copies, waits for them, and re-layouts  1.41 us (2%)
    all_to_all x2, waiting for transfers between devices, transposed(): lax.all_to_all(blocks, 'seq', split_axis=0, concat_axis=0, tiled=True)  49 us
    all_to_all x2, starting transfers between devices, transposed(): lax.all_to_all(blocks, 'seq', split_axis=0, concat_axis=0, tiled=True)  11.7 us
    pallas_call x1, Pallas kernels, stacked_filter(): pl.pallas_call(functools.partial(stacked_filter_kernel, vars_dev, halves,...  8.14 us
    pallas_call x1, Pallas kernels, stacked_products(): pl.pallas_call(functools.partial(stacked_products_kernel, halves, vars_de...  3.17 us
  transfers between devices with their start and end apart: 2, of which 2 were waited for; matrix products, arithmetic and copies ran while one was open for 3% of the time, Pallas kernels for 0%

profile of v10, /device:TPU:13, one launch (start us, length us, event | category | flops | bytes accessed | tf_op | source)
XLA Modules:
  0.0 77.5 jit_solution(2019427245367916054)
XLA Ops:
  0.6 0.0 copy-start.3
  0.6 3.2 %stacked_products.1 = bf16[16,272,128]{2,1,0:T(8,128)(2,1)} custom-call(s32[16]{0:T(128)} %offsets_ref.1, bf16[3,128,4096]{2,1,0:T(8,128)(2,1)} %streams_ref.1), custom_call_target="tpu_custom_call" | custom-call | flops 524288 | bytes 3145728 | tf_op jit(solution)/shard_map/stacked_products/pallas_call | solution.py:456
  3.8 0.0 copy-start.4
  3.8 0.0 copy-start
  3.8 0.0 copy-start.1
  3.9 0.0 copy-start.2
  3.9 6.7 %all-to-all-start = ((bf16[16,272,128]{2,1,0:T(8,128)(2,1)}), bf16[16,272,128]{2,1,0:T(8,128)(2,1)S(1)}, u32[]{:S(2)}, u32[]{:S(2)}) async-start(bf16[16,272,128]{2,1,0:T(8,128)(2,1)} %stacked_products.1), calls=%async_computation | async-start | bytes 2228224 | tf_op jit(solution)/shard_map/all_to_all | solution.py:648
  10.6 0.0 copy-done.4
  10.6 0.1 copy.11.refs_0_
  10.7 0.8 dynamic-slice_convert_fusion
  11.4 25.4 %all-to-all-done.refs_6_ = bf16[16,272,128]{2,1,0:T(8,128)(2,1)S(1)} async-done(((bf16[16,272,128]{2,1,0:T(8,128)(2,1)}), bf16[16,272,128]{2,1,0:T(8,128)(2,1)S(1)}, u32[]{:S(2)}, u32[]{:S(2)}) %all-to-all-start) | async-done | bytes 1114144 | tf_op jit(solution)/shard_map/all_to_all | solution.py:648
  36.8 0.0 copy-done.3
  36.8 0.0 copy-done
  36.8 0.0 copy-done.1
  36.8 0.0 copy-done.2
  36.8 8.1 %stacked_filter.1 = bf16[16,272,128]{2,1,0:T(8,128)(2,1)} custom-call(s32[16,1]{1,0:T(8,128)S(1)} %copy.11.refs_0_, f32[1,256]{1,0:T(1,128)S(1)} %bitcast.6, bf16[1024,256]{1,0:T(8,128)(2,1)S(1)} %copy-done.2, bf16[512,512]{1,0:T(8,128)(2,1)S(1)} %copy-done.3, bf16[256,512]{1,0:T(8,128)(2,1)S(1)} %copy-done.1, bf16[256,2048]{1,0:T(8,128)(2,1)S(1)} %copy-done, ...), custom_call_target="tpu_custom_call" | custom-call | flops 2751463424 | bytes 8388608 | tf_op jit(solution)/shard_map/stacked_filter/pallas_call | solution.py:574
  45.0 5.0 %all-to-all-start.1 = ((bf16[16,272,128]{2,1,0:T(8,128)(2,1)}), bf16[16,272,128]{2,1,0:T(8,128)(2,1)S(1)}, u32[]{:S(2)}, u32[]{:S(2)}) async-start(bf16[16,272,128]{2,1,0:T(8,128)(2,1)} %stacked_filter.1), calls=%async_computation.1 | async-start | bytes 2228224 | tf_op jit(solution)/shard_map/all_to_all | solution.py:648
  51.3 1.3 %slice_bitcast_fusion.gates_ref = bf16[128,4096]{1,0:T(8,128)(2,1)S(1)} fusion(bf16[3,128,4096]{2,1,0:T(8,128)(2,1)} %streams_ref.1), kind=kLoop, calls=%fused_computation | loop fusion | bytes 2097152 | tf_op jit(solution)/shard_map/squeeze | solution.py:681
  52.6 23.6 %all-to-all-done.1.back_ref = bf16[16,272,128]{2,1,0:T(8,128)(2,1)S(1)} async-done(((bf16[16,272,128]{2,1,0:T(8,128)(2,1)}), bf16[16,272,128]{2,1,0:T(8,128)(2,1)S(1)}, u32[]{:S(2)}, u32[]{:S(2)}) %all-to-all-start.1) | async-done | bytes 1114144 | tf_op jit(solution)/shard_map/all_to_all | solution.py:648
  76.2 1.3 %stacked_finish.1 = (bf16[128,4096]{1,0:T(8,128)(2,1)}, f32[1,2]{1,0:T(1,128)}) custom-call(s32[1]{0:T(128)S(6)} %copy.12.ref_ref, s32[1]{0:T(128)S(6)} %copy.13.alt_ref, bf16[128,4096]{1,0:T(8,128)(2,1)S(1)} %slice_bitcast_fusion.gates_ref, bf16[16,272,128]{2,1,0:T(8,128)(2,1)S(1)} %all-to-all-done.1.back_ref), custom_call_target="tpu_custom_call" | custom-call | flops 524288 | bytes 3145728 | tf_op jit(solution)/shard_map/stacked_finish/pallas_call | solution.py:625
  (1 shorter events, 0.0 us)
Async XLA Ops:
  0.6 36.2 %copy-start.3 = (bf16[512,512]{1,0:T(8,128)(2,1)S(1)}, bf16[512,512]{1,0:T(8,128)(2,1)}, u32[]{:S(2)}) copy-start(bf16[512,512]{1,0:T(8,128)(2,1)} %constant.17.clone.refs_3_) | copy-start | bytes 1572868
  3.8 6.8 %copy-start.4 = (s32[16]{0:T(128)S(1)}, s32[16]{0:T(128)}, u32[]{:S(2)}) copy-start(s32[16]{0:T(128)} %offsets_ref.1) | copy-start | bytes 196
  3.8 33.0 %copy-start = (bf16[256,2048]{1,0:T(8,128)(2,1)S(1)}, bf16[256,2048]{1,0:T(8,128)(2,1)}, u32[]{:S(2)}) copy-start(bf16[256,2048]{1,0:T(8,128)(2,1)} %refs_5_.1) | copy-start | bytes 3145732
  3.8 33.0 %copy-start.1 = (bf16[256,512]{1,0:T(8,128)(2,1)S(1)}, bf16[256,512]{1,0:T(8,128)(2,1)}, u32[]{:S(2)}) copy-start(bf16[256,512]{1,0:T(8,128)(2,1)} %refs_4_.1) | copy-start | bytes 786436
  3.9 33.0 %copy-start.2 = (bf16[1024,256]{1,0:T(8,128)(2,1)S(1)}, bf16[1024,256]{1,0:T(8,128)(2,1)}, u32[]{:S(2)}) copy-start(bf16[1024,256]{1,0:T(8,128)(2,1)} %constant.16.clone.refs_2_) | copy-start | bytes 1572868
  3.9 33.0 %all-to-all-start = ((bf16[16,272,128]{2,1,0:T(8,128)(2,1)}), bf16[16,272,128]{2,1,0:T(8,128)(2,1)S(1)}, u32[]{:S(2)}, u32[]{:S(2)}) async-start(bf16[16,272,128]{2,1,0:T(8,128)(2,1)} %stacked_products.1), calls=%async_computation | async-start | bytes 2228224 | tf_op jit(solution)/shard_map/all_to_all | solution.py:648
  45.0 31.2 %all-to-all-start.1 = ((bf16[16,272,128]{2,1,0:T(8,128)(2,1)}), bf16[16,272,128]{2,1,0:T(8,128)(2,1)S(1)}, u32[]{:S(2)}, u32[]{:S(2)}) async-start(bf16[16,272,128]{2,1,0:T(8,128)(2,1)} %stacked_filter.1), calls=%async_computation.1 | async-start | bytes 2228224 | tf_op jit(solution)/shard_map/all_to_all | solution.py:648

commit v11 on v10

--- a/solution.py
+++ b/solution.py
@@ -131,17 +131,21 @@
     upper = pl.ds(start, half_tile)
     lower = pl.ds(pl.multiple_of(double // 2 + start, half_tile), half_tile)
     signal = [(points[k, upper, lanes], points[k, lower, lanes]) for k in range(n_blocks)]
+    signal = [(a_re, a_im, a_re + a_im) for a_re, a_im in signal]
     taps = [(spectrum_ref[k, upper, lanes], spectrum_ref[k, lower, lanes]) for k in range(n_blocks)]
+    taps = [(b_re, b_im - b_re, b_re + b_im) for b_re, b_im in taps]
     before_re = jnp.zeros_like(signal[0][0])
     before_im = before_re
     for total in range(n_blocks):
-        sum_re = jnp.zeros_like(before_re)
-        sum_im = sum_re
+        first = second = third = None
         for delay in range(total + 1):
-            a_re, a_im = signal[total - delay]
-            b_re, b_im = taps[delay]
-            sum_re += a_re * b_re - a_im * b_im
-            sum_im += a_re * b_im + a_im * b_re
+            a_re, a_im, a_sum = signal[total - delay]
+            b_re, b_less, b_sum = taps[delay]
+            one, two, three = b_re * a_sum, a_re * b_less, a_im * b_sum
+            first = one if first is None else first + one
+            second = two if second is None else second + two
+            third = three if third is None else third + three
+        sum_re, sum_im = first - third, first + second
         joint[total, upper, lanes] = sum_re + before_im
         joint[total, lower, lanes] = sum_im - before_re
         before_re, before_im = sum_re, sum_im
@@ -516,6 +520,9 @@
             points[step + member] = total[:, member * width : (member + 1) * width]
     multiply_points(points, spectrum, joint)
 
+    row = lax.broadcasted_iota(jnp.int32, (tok_rows, width), 0)
+    rows_of = [[None] * n_devices for _ in range(vars_dev)]
+    group = math.gcd(n_blocks, 2)
     for step in range(0, n_blocks, group):
         highs, lows = split_bf16(jnp.concatenate([joint[step + m] for m in range(group)], axis=1))
         both = jnp.dot(inverse[...], highs, preferred_element_type=f32)
@@ -523,17 +530,22 @@
         result = (both[:block] + both[block:] + rest).astype(bf16)
         for index in range(group):
             for member in range(per_block):
-                rank = (step + index) * per_block + member
+                device = (step + index) * per_block + member
+                piece = result[
+                    member * tok_rows : (member + 1) * tok_rows, index * width : (index + 1) * width
+                ]
                 for half in range(halves):
-                    start = index * width + half * lane_tile
-                    leaving[rank, half * tok_rows : (half + 1) * tok_rows, :] = result[
-                        member * tok_rows : (member + 1) * tok_rows, start : start + lane_tile
+                    leaving[device, half * tok_rows : (half + 1) * tok_rows, :] = piece[
+                        :, half * lane_tile : (half + 1) * lane_tile
                     ]
-                body_copy(rank).start()
-
-    length = n_devices * tok_rows
-    column = lax.broadcasted_iota(jnp.int32, (positions_ref.shape[0], length), 1)
-    picker = (column == positions_ref[...]).astype(f32).astype(bf16)
+                body_copy(device).start()
+                for var in range(vars_dev):
+                    spot = var * n_devices + device
+                    local = positions_ref[spot : spot + 1, :] - device * tok_rows
+                    mine = jnp.where(row == local, piece.astype(f32), 0.0)
+                    rows_of[var][device] = jnp.sum(mine, axis=0, keepdims=True)
+
+    picked_rows = jnp.concatenate([mine for rows in rows_of for mine in rows], axis=0)
     tails = arrived[:, body:, :].astype(f32)
     place = lax.broadcasted_iota(jnp.int32, tails.shape, 1)
     raw = None
@@ -545,9 +557,7 @@
             for var in range(vars_dev)
         ]
         gate_rows = picked[0] if vars_dev == 1 else jnp.concatenate(picked, axis=0)
-        filtered = leaving[:, half * tok_rows : (half + 1) * tok_rows, :].reshape(length, lane_tile)
-        filtered = jnp.dot(picker, filtered, preferred_element_type=f32)
-        rows = (gate_rows * filtered).astype(bf16).astype(f32)
+        rows = (gate_rows * picked_rows[:, lanes]).astype(bf16).astype(f32)
         weighted = (rows * gain_ref[:, lanes]).astype(bf16)
         part = jnp.dot(weighted, unembed[lanes, :], preferred_element_type=f32)
         raw = part if raw is None else raw + part

time: 78 us -> 77.9 us (level)
  no operation moved by 1% of the time
where the time goes in v11:
time: 77.9 us; the launch traced here: 77.4 us
  waiting for transfers between devices  49 us (63%)
  Pallas kernels  12.5 us (16%)
  starting transfers between devices  11.7 us (15%)
  between operations  2.01 us (3%)
  local copies, waits for them, and re-layouts  1.41 us (2%)
    all_to_all x2, waiting for transfers between devices, transposed(): lax.all_to_all(blocks, 'seq', split_axis=0, concat_axis=0, tiled=True)  49 us
    all_to_all x2, starting transfers between devices, transposed(): lax.all_to_all(blocks, 'seq', split_axis=0, concat_axis=0, tiled=True)  11.7 us
    pallas_call x1, Pallas kernels, stacked_filter(): pl.pallas_call(functools.partial(stacked_filter_kernel, vars_dev, halves,...  7.99 us
    pallas_call x1, Pallas kernels, stacked_products(): pl.pallas_call(functools.partial(stacked_products_kernel, halves, vars_de...  3.17 us
  transfers between devices with their start and end apart: 2, of which 2 were waited for; matrix products, arithmetic and copies ran while one was open for 3% of the time, Pallas kernels for 0%

profile of v11, /device:TPU:13, one launch (start us, length us, event | category | flops | bytes accessed | tf_op | source)
XLA Modules:
  0.0 77.4 jit_solution(16614903259778903017)
XLA Ops:
  0.6 0.0 copy-start.3
  0.6 3.2 %stacked_products.1 = bf16[16,272,128]{2,1,0:T(8,128)(2,1)} custom-call(s32[16]{0:T(128)} %offsets_ref.1, bf16[3,128,4096]{2,1,0:T(8,128)(2,1)} %streams_ref.1), custom_call_target="tpu_custom_call" | custom-call | flops 524288 | bytes 3145728 | tf_op jit(solution)/shard_map/stacked_products/pallas_call | solution.py:460
  3.8 0.0 copy-start.4
  3.8 0.0 copy-start
  3.8 0.0 copy-start.1
  3.9 0.0 copy-start.2
  3.9 6.7 %all-to-all-start = ((bf16[16,272,128]{2,1,0:T(8,128)(2,1)}), bf16[16,272,128]{2,1,0:T(8,128)(2,1)S(1)}, u32[]{:S(2)}, u32[]{:S(2)}) async-start(bf16[16,272,128]{2,1,0:T(8,128)(2,1)} %stacked_products.1), calls=%async_computation | async-start | bytes 2228224 | tf_op jit(solution)/shard_map/all_to_all | solution.py:658
  10.6 0.0 copy-done.4
  10.6 0.1 copy.11.refs_0_
  10.7 0.8 dynamic-slice_convert_fusion
  11.4 25.4 %all-to-all-done.refs_6_ = bf16[16,272,128]{2,1,0:T(8,128)(2,1)S(1)} async-done(((bf16[16,272,128]{2,1,0:T(8,128)(2,1)}), bf16[16,272,128]{2,1,0:T(8,128)(2,1)S(1)}, u32[]{:S(2)}, u32[]{:S(2)}) %all-to-all-start) | async-done | bytes 1114144 | tf_op jit(solution)/shard_map/all_to_all | solution.py:658
  36.8 0.0 copy-done.3
  36.8 0.0 copy-done
  36.8 0.0 copy-done.1
  36.8 0.0 copy-done.2
  36.8 8.0 %stacked_filter.1 = bf16[16,272,128]{2,1,0:T(8,128)(2,1)} custom-call(s32[16,1]{1,0:T(8,128)S(1)} %copy.11.refs_0_, f32[1,256]{1,0:T(1,128)S(1)} %bitcast.6, bf16[1024,256]{1,0:T(8,128)(2,1)S(1)} %copy-done.2, bf16[512,512]{1,0:T(8,128)(2,1)S(1)} %copy-done.3, bf16[256,512]{1,0:T(8,128)(2,1)S(1)} %copy-done.1, bf16[256,2048]{1,0:T(8,128)(2,1)S(1)} %copy-done, ...), custom_call_target="tpu_custom_call" | custom-call | flops 2751463424 | bytes 8388608 | tf_op jit(solution)/shard_map/stacked_filter/pallas_call | solution.py:584
  44.8 5.0 %all-to-all-start.1 = ((bf16[16,272,128]{2,1,0:T(8,128)(2,1)}), bf16[16,272,128]{2,1,0:T(8,128)(2,1)S(1)}, u32[]{:S(2)}, u32[]{:S(2)}) async-start(bf16[16,272,128]{2,1,0:T(8,128)(2,1)} %stacked_filter.1), calls=%async_computation.1 | async-start | bytes 2228224 | tf_op jit(solution)/shard_map/all_to_all | solution.py:658
  51.1 1.3 %slice_bitcast_fusion.gates_ref = bf16[128,4096]{1,0:T(8,128)(2,1)S(1)} fusion(bf16[3,128,4096]{2,1,0:T(8,128)(2,1)} %streams_ref.1), kind=kLoop, calls=%fused_computation | loop fusion | bytes 2097152 | tf_op jit(solution)/shard_map/squeeze | solution.py:691
  52.4 23.6 %all-to-all-done.1.back_ref = bf16[16,272,128]{2,1,0:T(8,128)(2,1)S(1)} async-done(((bf16[16,272,128]{2,1,0:T(8,128)(2,1)}), bf16[16,272,128]{2,1,0:T(8,128)(2,1)S(1)}, u32[]{:S(2)}, u32[]{:S(2)}) %all-to-all-start.1) | async-done | bytes 1114144 | tf_op jit(solution)/shard_map/all_to_all | solution.py:658
  76.1 1.3 %stacked_finish.1 = (bf16[128,4096]{1,0:T(8,128)(2,1)}, f32[1,2]{1,0:T(1,128)}) custom-call(s32[1]{0:T(128)S(6)} %copy.12.ref_ref, s32[1]{0:T(128)S(6)} %copy.13.alt_ref, bf16[128,4096]{1,0:T(8,128)(2,1)S(1)} %slice_bitcast_fusion.gates_ref, bf16[16,272,128]{2,1,0:T(8,128)(2,1)S(1)} %all-to-all-done.1.back_ref), custom_call_target="tpu_custom_call" | custom-call | flops 524288 | bytes 3145728 | tf_op jit(solution)/shard_map/stacked_finish/pallas_call | solution.py:635
  (1 shorter events, 0.0 us)
Async XLA Ops:
  0.6 36.2 %copy-start.3 = (bf16[512,512]{1,0:T(8,128)(2,1)S(1)}, bf16[512,512]{1,0:T(8,128)(2,1)}, u32[]{:S(2)}) copy-start(bf16[512,512]{1,0:T(8,128)(2,1)} %constant.17.clone.refs_3_) | copy-start | bytes 1572868
  3.8 6.8 %copy-start.4 = (s32[16]{0:T(128)S(1)}, s32[16]{0:T(128)}, u32[]{:S(2)}) copy-start(s32[16]{0:T(128)} %offsets_ref.1) | copy-start | bytes 196
  3.8 33.0 %copy-start = (bf16[256,2048]{1,0:T(8,128)(2,1)S(1)}, bf16[256,2048]{1,0:T(8,128)(2,1)}, u32[]{:S(2)}) copy-start(bf16[256,2048]{1,0:T(8,128)(2,1)} %refs_5_.1) | copy-start | bytes 3145732
  3.8 33.0 %copy-start.1 = (bf16[256,512]{1,0:T(8,128)(2,1)S(1)}, bf16[256,512]{1,0:T(8,128)(2,1)}, u32[]{:S(2)}) copy-start(bf16[256,512]{1,0:T(8,128)(2,1)} %refs_4_.1) | copy-start | bytes 786436
  3.9 33.0 %copy-start.2 = (bf16[1024,256]{1,0:T(8,128)(2,1)S(1)}, bf16[1024,256]{1,0:T(8,128)(2,1)}, u32[]{:S(2)}) copy-start(bf16[1024,256]{1,0:T(8,128)(2,1)} %constant.16.clone.refs_2_) | copy-start | bytes 1572868
  3.9 33.0 %all-to-all-start = ((bf16[16,272,128]{2,1,0:T(8,128)(2,1)}), bf16[16,272,128]{2,1,0:T(8,128)(2,1)S(1)}, u32[]{:S(2)}, u32[]{:S(2)}) async-start(bf16[16,272,128]{2,1,0:T(8,128)(2,1)} %stacked_products.1), calls=%async_computation | async-start | bytes 2228224 | tf_op jit(solution)/shard_map/all_to_all | solution.py:658
  44.8 31.2 %all-to-all-start.1 = ((bf16[16,272,128]{2,1,0:T(8,128)(2,1)}), bf16[16,272,128]{2,1,0:T(8,128)(2,1)S(1)}, u32[]{:S(2)}, u32[]{:S(2)}) async-start(bf16[16,272,128]{2,1,0:T(8,128)(2,1)} %stacked_filter.1), calls=%async_computation.1 | async-start | bytes 2228224 | tf_op jit(solution)/shard_map/all_to_all | solution.py:658

commit v12 on v11

--- a/solution.py
+++ b/solution.py
@@ -391,9 +391,20 @@
         name="finish",
     )(ref_ids, alt_ids, streams, *backs)
 
+def group_order(n_devices):
+    quarters = math.gcd(n_devices, 4)
+    size = n_devices // quarters
+    return [quarter * size + index for index in range(size) for quarter in range(quarters)]
+
+
+def ranks(n_devices):
+    return {device: rank for rank, device in enumerate(group_order(n_devices))}
+
+
 def stacked_products_kernel(halves, vars_dev, offsets_ref, streams_ref, out_ref, *scratch):
     gates, pairs, built, offsets, gate_sems, pair_sems, out_sems, offset_sem = scratch
     n_devices = built.shape[0]
+    rank_of = ranks(n_devices)
     pieces, _, tok_rows, lanes_each = pairs.shape
     body = halves * tok_rows
     width = halves * lane_tile
@@ -437,17 +448,18 @@
         pair_copy(piece).wait()
         for member in range(owners):
             owner = piece * owners + member
+            rank = rank_of[owner]
             tail = jnp.zeros((extra, lane_tile), f32)
             for half in range(halves):
                 lanes = slice(member * width + half * lane_tile, member * width + (half + 1) * lane_tile)
                 rows = slice(half * tok_rows, (half + 1) * tok_rows)
-                built[owner, rows, :] = pairs[piece, 0, :, lanes] * pairs[piece, 1, :, lanes]
+                built[rank, rows, :] = pairs[piece, 0, :, lanes] * pairs[piece, 1, :, lanes]
                 start = owner * width + half * lane_tile
                 for var in range(vars_dev):
                     mine = gate_rows[var][:, start : start + lane_tile]
                     tail = jnp.where(place == half * vars_dev + var, mine, tail)
-            built[owner, body:, :] = tail.astype(bf16)
-            out_copy(owner).start()
+            built[rank, body:, :] = tail.astype(bf16)
+            out_copy(rank).start()
     for owner in range(n_devices):
         out_copy(owner).wait()
 
@@ -484,6 +496,7 @@
     positions_ref, gain_ref, forward, inverse, unembed, taps, arrived = refs[:7]
     out_ref, points, joint, spectrum, packed, leaving, body_sems, tail_sem = refs[7:]
     n_devices = arrived.shape[0]
+    rank_of = ranks(n_devices)
     body = halves * tok_rows
     n_blocks, double, width = points.shape
     block = double // 2
@@ -511,7 +524,7 @@
         for index in range(step, step + group):
             for half in range(halves):
                 rows = slice(half * tok_rows, (half + 1) * tok_rows)
-                parts = [arrived[index * per_block + m, rows, :] for m in range(per_block)]
+                parts = [arrived[rank_of[index * per_block + m], rows, :] for m in range(per_block)]
                 pieces.append(jnp.concatenate(parts, axis=0))
         signal = jnp.concatenate(pieces, axis=1)
         both = jnp.dot(forward[...], signal, preferred_element_type=f32)
@@ -531,19 +544,20 @@
         for index in range(group):
             for member in range(per_block):
                 device = (step + index) * per_block + member
+                rank = rank_of[device]
                 piece = result[
                     member * tok_rows : (member + 1) * tok_rows, index * width : (index + 1) * width
                 ]
                 for half in range(halves):
-                    leaving[device, half * tok_rows : (half + 1) * tok_rows, :] = piece[
+                    leaving[rank, half * tok_rows : (half + 1) * tok_rows, :] = piece[
                         :, half * lane_tile : (half + 1) * lane_tile
                     ]
-                body_copy(device).start()
+                body_copy(rank).start()
                 for var in range(vars_dev):
                     spot = var * n_devices + device
                     local = positions_ref[spot : spot + 1, :] - device * tok_rows
                     mine = jnp.where(row == local, piece.astype(f32), 0.0)
-                    rows_of[var][device] = jnp.sum(mine, axis=0, keepdims=True)
+                    rows_of[var][rank] = jnp.sum(mine, axis=0, keepdims=True)
 
     picked_rows = jnp.concatenate([mine for rows in rows_of for mine in rows], axis=0)
     tails = arrived[:, body:, :].astype(f32)
@@ -602,6 +616,7 @@
 def stacked_finish_kernel(halves, vars_dev, vocab, ref_ref, alt_ref, gates_ref, back_ref, *refs):
     mixed_ref, scores_ref, results, scores, out_sems, score_sem = refs
     n_devices, tok_rows, width = results.shape
+    rank_of = ranks(n_devices)
 
     def out_copy(owner):
         return pltpu.make_async_copy(
@@ -610,12 +625,12 @@
 
     sums = None
     for owner in range(n_devices):
-        tail = back_ref[owner, halves * tok_rows :, :].astype(f32)
+        tail = back_ref[rank_of[owner], halves * tok_rows :, :].astype(f32)
         sums = tail if sums is None else sums + tail
         for half in range(halves):
             lanes = slice(half * lane_tile, (half + 1) * lane_tile)
             start = owner * width + half * lane_tile
-            filtered = back_ref[owner, half * tok_rows : (half + 1) * tok_rows, :]
+            filtered = back_ref[rank_of[owner], half * tok_rows : (half + 1) * tok_rows, :]
             results[owner, :, lanes] = gates_ref[:, start : start + lane_tile] * filtered
         out_copy(owner).start()
     model_width = n_devices * width
@@ -655,7 +670,10 @@
 
 
 def transposed(blocks):
-    return lax.all_to_all(blocks, "seq", split_axis=0, concat_axis=0, tiled=True)
+    groups = [group_order(blocks.shape[0])]
+    return lax.all_to_all(
+        blocks, "seq", split_axis=0, concat_axis=0, axis_index_groups=groups, tiled=True
+    )
 
 
 def shards(streams, long_filter, gain, unembed, offsets, ref_ids, alt_ids):

time: 77.9 us -> 81.6 us (1.047)
  the two profiles are of different devices: /device:TPU:13 before, /device:TPU:0 now
where the time goes in v12:
time: 81.6 us; the launch traced here: 81.1 us
  waiting for transfers between devices  53.2 us (65%)
  Pallas kernels  12.5 us (15%)
  starting transfers between devices  11.2 us (14%)
  between operations  2.03 us (2%)
  local copies, waits for them, and re-layouts  1.41 us (2%)
    all_to_all x2, waiting for transfers between devices, transposed(): lax.all_to_all(blocks, 'seq', split_axis=0, concat_axis=0, axis_index_gro...  53.2 us
    all_to_all x2, starting transfers between devices, transposed(): lax.all_to_all(blocks, 'seq', split_axis=0, concat_axis=0, axis_index_gro...  11.2 us
    pallas_call x1, Pallas kernels, stacked_filter(): pl.pallas_call(functools.partial(stacked_filter_kernel, vars_dev, halves,...  8 us
    pallas_call x1, Pallas kernels, stacked_products(): pl.pallas_call(functools.partial(stacked_products_kernel, halves, vars_de...  3.19 us
  transfers between devices with their start and end apart: 2, of which 2 were waited for; matrix products, arithmetic and copies ran while one was open for 3% of the time, Pallas kernels for 0%

profile of v12, /device:TPU:0, one launch (start us, length us, event | category | flops | bytes accessed | tf_op | source)
XLA Modules:
  0.0 81.1 jit_solution(5492953046401926253)
XLA Ops:
  0.6 0.0 copy-start.3
  0.6 3.2 %stacked_products.1 = bf16[16,272,128]{2,1,0:T(8,128)(2,1)} custom-call(s32[16]{0:T(128)} %offsets_ref.1, bf16[3,128,4096]{2,1,0:T(8,128)(2,1)} %streams_ref.1), custom_call_target="tpu_custom_call" | custom-call | flops 524288 | bytes 3145728 | tf_op jit(solution)/shard_map/stacked_products/pallas_call | solution.py:472
  3.8 0.0 copy-start.4
  3.9 0.0 copy-start
  3.9 0.0 copy-start.1
  3.9 0.0 copy-start.2
  3.9 7.5 %all-to-all-start = ((bf16[16,272,128]{2,1,0:T(8,128)(2,1)}), bf16[16,272,128]{2,1,0:T(8,128)(2,1)S(1)}, u32[]{:S(2)}, u32[]{:S(2)}) async-start(bf16[16,272,128]{2,1,0:T(8,128)(2,1)} %stacked_products.1), calls=%async_computation | async-start | bytes 2228224 | tf_op jit(solution)/shard_map/all_to_all | solution.py:674
  11.4 0.0 copy-done.4
  11.4 0.1 copy.11.refs_0_
  11.5 0.8 dynamic-slice_convert_fusion
  12.3 27.5 %all-to-all-done.refs_6_ = bf16[16,272,128]{2,1,0:T(8,128)(2,1)S(1)} async-done(((bf16[16,272,128]{2,1,0:T(8,128)(2,1)}), bf16[16,272,128]{2,1,0:T(8,128)(2,1)S(1)}, u32[]{:S(2)}, u32[]{:S(2)}) %all-to-all-start) | async-done | bytes 1114144 | tf_op jit(solution)/shard_map/all_to_all | solution.py:674
  39.8 0.0 copy-done.3
  39.8 0.0 copy-done
  39.8 0.0 copy-done.1
  39.8 0.0 copy-done.2
  39.8 8.0 %stacked_filter.1 = bf16[16,272,128]{2,1,0:T(8,128)(2,1)} custom-call(s32[16,1]{1,0:T(8,128)S(1)} %copy.11.refs_0_, f32[1,256]{1,0:T(1,128)S(1)} %bitcast.6, bf16[1024,256]{1,0:T(8,128)(2,1)S(1)} %copy-done.2, bf16[512,512]{1,0:T(8,128)(2,1)S(1)} %copy-done.3, bf16[256,512]{1,0:T(8,128)(2,1)S(1)} %copy-done.1, bf16[256,2048]{1,0:T(8,128)(2,1)S(1)} %copy-done, ...), custom_call_target="tpu_custom_call" | custom-call | flops 2751463424 | bytes 8388608 | tf_op jit(solution)/shard_map/stacked_filter/pallas_call | solution.py:598
  47.8 3.7 %all-to-all-start.1 = ((bf16[16,272,128]{2,1,0:T(8,128)(2,1)}), bf16[16,272,128]{2,1,0:T(8,128)(2,1)S(1)}, u32[]{:S(2)}, u32[]{:S(2)}) async-start(bf16[16,272,128]{2,1,0:T(8,128)(2,1)} %stacked_filter.1), calls=%async_computation.1 | async-start | bytes 2228224 | tf_op jit(solution)/shard_map/all_to_all | solution.py:674
  52.8 1.3 %slice_bitcast_fusion.gates_ref = bf16[128,4096]{1,0:T(8,128)(2,1)S(1)} fusion(bf16[3,128,4096]{2,1,0:T(8,128)(2,1)} %streams_ref.1), kind=kLoop, calls=%fused_computation | loop fusion | bytes 2097152 | tf_op jit(solution)/shard_map/squeeze | solution.py:709
  54.1 25.7 %all-to-all-done.1.back_ref = bf16[16,272,128]{2,1,0:T(8,128)(2,1)S(1)} async-done(((bf16[16,272,128]{2,1,0:T(8,128)(2,1)}), bf16[16,272,128]{2,1,0:T(8,128)(2,1)S(1)}, u32[]{:S(2)}, u32[]{:S(2)}) %all-to-all-start.1) | async-done | bytes 1114144 | tf_op jit(solution)/shard_map/all_to_all | solution.py:674
  79.8 1.3 %stacked_finish.1 = (bf16[128,4096]{1,0:T(8,128)(2,1)}, f32[1,2]{1,0:T(1,128)}) custom-call(s32[1]{0:T(128)S(6)} %copy.12.ref_ref, s32[1]{0:T(128)S(6)} %copy.13.alt_ref, bf16[128,4096]{1,0:T(8,128)(2,1)S(1)} %slice_bitcast_fusion.gates_ref, bf16[16,272,128]{2,1,0:T(8,128)(2,1)S(1)} %all-to-all-done.1.back_ref), custom_call_target="tpu_custom_call" | custom-call | flops 524288 | bytes 3145728 | tf_op jit(solution)/shard_map/stacked_finish/pallas_call | solution.py:650
  (1 shorter events, 0.0 us)
Async XLA Ops:
  0.6 39.1 %copy-start.3 = (bf16[512,512]{1,0:T(8,128)(2,1)S(1)}, bf16[512,512]{1,0:T(8,128)(2,1)}, u32[]{:S(2)}) copy-start(bf16[512,512]{1,0:T(8,128)(2,1)} %constant.17.clone.refs_3_) | copy-start | bytes 1572868
  3.8 7.6 %copy-start.4 = (s32[16]{0:T(128)S(1)}, s32[16]{0:T(128)}, u32[]{:S(2)}) copy-start(s32[16]{0:T(128)} %offsets_ref.1) | copy-start | bytes 196
  3.9 35.9 %copy-start = (bf16[256,2048]{1,0:T(8,128)(2,1)S(1)}, bf16[256,2048]{1,0:T(8,128)(2,1)}, u32[]{:S(2)}) copy-start(bf16[256,2048]{1,0:T(8,128)(2,1)} %refs_5_.1) | copy-start | bytes 3145732
  3.9 35.9 %copy-start.1 = (bf16[256,512]{1,0:T(8,128)(2,1)S(1)}, bf16[256,512]{1,0:T(8,128)(2,1)}, u32[]{:S(2)}) copy-start(bf16[256,512]{1,0:T(8,128)(2,1)} %refs_4_.1) | copy-start | bytes 786436
  3.9 35.9 %copy-start.2 = (bf16[1024,256]{1,0:T(8,128)(2,1)S(1)}, bf16[1024,256]{1,0:T(8,128)(2,1)}, u32[]{:S(2)}) copy-start(bf16[1024,256]{1,0:T(8,128)(2,1)} %constant.16.clone.refs_2_) | copy-start | bytes 1572868
  3.9 35.9 %all-to-all-start = ((bf16[16,272,128]{2,1,0:T(8,128)(2,1)}), bf16[16,272,128]{2,1,0:T(8,128)(2,1)S(1)}, u32[]{:S(2)}, u32[]{:S(2)}) async-start(bf16[16,272,128]{2,1,0:T(8,128)(2,1)} %stacked_products.1), calls=%async_computation | async-start | bytes 2228224 | tf_op jit(solution)/shard_map/all_to_all | solution.py:674
  47.8 32.0 %all-to-all-start.1 = ((bf16[16,272,128]{2,1,0:T(8,128)(2,1)}), bf16[16,272,128]{2,1,0:T(8,128)(2,1)S(1)}, u32[]{:S(2)}, u32[]{:S(2)}) async-start(bf16[16,272,128]{2,1,0:T(8,128)(2,1)} %stacked_filter.1), calls=%async_computation.1 | async-start | bytes 2228224 | tf_op jit(solution)/shard_map/all_to_all | solution.py:674

commit v13 on v11

--- a/solution.py
+++ b/solution.py
@@ -392,7 +392,7 @@
     )(ref_ids, alt_ids, streams, *backs)
 
 def stacked_products_kernel(halves, vars_dev, offsets_ref, streams_ref, out_ref, *scratch):
-    gates, pairs, built, offsets, gate_sems, pair_sems, out_sems, offset_sem = scratch
+    gates, pairs, built, offsets, gate_sems, pair_sems, out_sems, offset_sem, tail_sem = scratch
     n_devices = built.shape[0]
     pieces, _, tok_rows, lanes_each = pairs.shape
     body = halves * tok_rows
@@ -408,8 +408,9 @@
         )
 
 
-    def out_copy(owner):
-        return pltpu.make_async_copy(built.at[owner], out_ref.at[owner], out_sems.at[owner])
+    def body_copy(owner):
+        rows = pl.ds(0, body)
+        return pltpu.make_async_copy(built.at[owner, rows], out_ref.at[owner, rows], out_sems.at[owner])
 
     def gate_copy(var):
         start = pl.multiple_of(local_rows[var] // row_tile * row_tile, row_tile)
@@ -425,6 +426,16 @@
     local_rows = [var * slot + offsets[me * vars_dev + var] for var in range(vars_dev)]
     for var in range(vars_dev):
         gate_copy(var).start()
+    for piece in range(pieces):
+        pair_copy(piece).wait()
+        for member in range(owners):
+            owner = piece * owners + member
+            for half in range(halves):
+                lanes = slice(member * width + half * lane_tile, member * width + (half + 1) * lane_tile)
+                rows = slice(half * tok_rows, (half + 1) * tok_rows)
+                built[owner, rows, :] = pairs[piece, 0, :, lanes] * pairs[piece, 1, :, lanes]
+            body_copy(owner).start()
+
     extra = built.shape[1] - body
     row = lax.broadcasted_iota(jnp.int32, gates.shape[1:], 0)
     place = lax.broadcasted_iota(jnp.int32, (extra, lane_tile), 0)
@@ -433,23 +444,20 @@
         gate_copy(var).wait()
         mine = jnp.where(row == local_rows[var] % row_tile, gates[var].astype(f32), 0.0)
         gate_rows.append(jnp.sum(mine, axis=0, keepdims=True))
-    for piece in range(pieces):
-        pair_copy(piece).wait()
-        for member in range(owners):
-            owner = piece * owners + member
-            tail = jnp.zeros((extra, lane_tile), f32)
-            for half in range(halves):
-                lanes = slice(member * width + half * lane_tile, member * width + (half + 1) * lane_tile)
-                rows = slice(half * tok_rows, (half + 1) * tok_rows)
-                built[owner, rows, :] = pairs[piece, 0, :, lanes] * pairs[piece, 1, :, lanes]
-                start = owner * width + half * lane_tile
-                for var in range(vars_dev):
-                    mine = gate_rows[var][:, start : start + lane_tile]
-                    tail = jnp.where(place == half * vars_dev + var, mine, tail)
-            built[owner, body:, :] = tail.astype(bf16)
-            out_copy(owner).start()
     for owner in range(n_devices):
-        out_copy(owner).wait()
+        tail = jnp.zeros((extra, lane_tile), f32)
+        for half in range(halves):
+            start = owner * width + half * lane_tile
+            for var in range(vars_dev):
+                mine = gate_rows[var][:, start : start + lane_tile]
+                tail = jnp.where(place == half * vars_dev + var, mine, tail)
+        built[owner, body:, :] = tail.astype(bf16)
+    rows = pl.ds(body, extra)
+    tail_copy = pltpu.make_async_copy(built.at[:, rows], out_ref.at[:, rows], tail_sem.at[0])
+    tail_copy.start()
+    for owner in range(n_devices):
+        body_copy(owner).wait()
+    tail_copy.wait()
 
 
 def stacked_products(offsets, streams, vars_dev, n_devices, extra):
@@ -470,6 +478,7 @@
             pltpu.SemaphoreType.DMA((vars_dev,)),
             pltpu.SemaphoreType.DMA((pieces,)),
             pltpu.SemaphoreType.DMA((n_devices,)),
+            pltpu.SemaphoreType.DMA((1,)),
             pltpu.SemaphoreType.DMA((1,)),
         ],
         compiler_params=pltpu.CompilerParams(vmem_limit_bytes=60 * MIB),

time: 77.9 us -> 77.5 us (level)
  no operation moved by 1% of the time
where the time goes in v13:
time: 77.5 us; the launch traced here: 77 us
  waiting for transfers between devices  49 us (63%)
  Pallas kernels  12.1 us (16%)
  starting transfers between devices  11.7 us (15%)
  between operations  2.01 us (3%)
  local copies, waits for them, and re-layouts  1.41 us (2%)
    all_to_all x2, waiting for transfers between devices, transposed(): lax.all_to_all(blocks, 'seq', split_axis=0, concat_axis=0, tiled=True)  49 us
    all_to_all x2, starting transfers between devices, transposed(): lax.all_to_all(blocks, 'seq', split_axis=0, concat_axis=0, tiled=True)  11.7 us
    pallas_call x1, Pallas kernels, stacked_filter(): pl.pallas_call(functools.partial(stacked_filter_kernel, vars_dev, halves,...  8 us
    pallas_call x1, Pallas kernels, stacked_products(): pl.pallas_call(functools.partial(stacked_products_kernel, halves, vars_de...  2.81 us
  transfers between devices with their start and end apart: 2, of which 2 were waited for; matrix products, arithmetic and copies ran while one was open for 3% of the time, Pallas kernels for 0%

profile of v13, /device:TPU:13, one launch (start us, length us, event | category | flops | bytes accessed | tf_op | source)
XLA Modules:
  0.0 77.0 jit_solution(385491445534435808)
XLA Ops:
  0.6 0.0 copy-start.3
  0.6 2.8 %stacked_products.1 = bf16[16,272,128]{2,1,0:T(8,128)(2,1)} custom-call(s32[16]{0:T(128)} %offsets_ref.1, bf16[3,128,4096]{2,1,0:T(8,128)(2,1)} %streams_ref.1), custom_call_target="tpu_custom_call" | custom-call | flops 524288 | bytes 3145728 | tf_op jit(solution)/shard_map/stacked_products/pallas_call | solution.py:468
  3.5 0.0 copy-start.4
  3.5 0.0 copy-start
  3.5 0.0 copy-start.1
  3.5 0.0 copy-start.2
  3.5 6.7 %all-to-all-start = ((bf16[16,272,128]{2,1,0:T(8,128)(2,1)}), bf16[16,272,128]{2,1,0:T(8,128)(2,1)S(1)}, u32[]{:S(2)}, u32[]{:S(2)}) async-start(bf16[16,272,128]{2,1,0:T(8,128)(2,1)} %stacked_products.1), calls=%async_computation | async-start | bytes 2228224 | tf_op jit(solution)/shard_map/all_to_all | solution.py:667
  10.2 0.0 copy-done.4
  10.3 0.1 copy.11.refs_0_
  10.3 0.8 dynamic-slice_convert_fusion
  11.1 25.4 %all-to-all-done.refs_6_ = bf16[16,272,128]{2,1,0:T(8,128)(2,1)S(1)} async-done(((bf16[16,272,128]{2,1,0:T(8,128)(2,1)}), bf16[16,272,128]{2,1,0:T(8,128)(2,1)S(1)}, u32[]{:S(2)}, u32[]{:S(2)}) %all-to-all-start) | async-done | bytes 1114144 | tf_op jit(solution)/shard_map/all_to_all | solution.py:667
  36.5 0.0 copy-done.3
  36.5 0.0 copy-done
  36.5 0.0 copy-done.1
  36.5 0.0 copy-done.2
  36.5 8.0 %stacked_filter.1 = bf16[16,272,128]{2,1,0:T(8,128)(2,1)} custom-call(s32[16,1]{1,0:T(8,128)S(1)} %copy.11.refs_0_, f32[1,256]{1,0:T(1,128)S(1)} %bitcast.6, bf16[1024,256]{1,0:T(8,128)(2,1)S(1)} %copy-done.2, bf16[512,512]{1,0:T(8,128)(2,1)S(1)} %copy-done.3, bf16[256,512]{1,0:T(8,128)(2,1)S(1)} %copy-done.1, bf16[256,2048]{1,0:T(8,128)(2,1)S(1)} %copy-done, ...), custom_call_target="tpu_custom_call" | custom-call | flops 2751463424 | bytes 8388608 | tf_op jit(solution)/shard_map/stacked_filter/pallas_call | solution.py:593
  44.5 5.0 %all-to-all-start.1 = ((bf16[16,272,128]{2,1,0:T(8,128)(2,1)}), bf16[16,272,128]{2,1,0:T(8,128)(2,1)S(1)}, u32[]{:S(2)}, u32[]{:S(2)}) async-start(bf16[16,272,128]{2,1,0:T(8,128)(2,1)} %stacked_filter.1), calls=%async_computation.1 | async-start | bytes 2228224 | tf_op jit(solution)/shard_map/all_to_all | solution.py:667
  50.8 1.3 %slice_bitcast_fusion.gates_ref = bf16[128,4096]{1,0:T(8,128)(2,1)S(1)} fusion(bf16[3,128,4096]{2,1,0:T(8,128)(2,1)} %streams_ref.1), kind=kLoop, calls=%fused_computation | loop fusion | bytes 2097152 | tf_op jit(solution)/shard_map/squeeze | solution.py:700
  52.1 23.6 %all-to-all-done.1.back_ref = bf16[16,272,128]{2,1,0:T(8,128)(2,1)S(1)} async-done(((bf16[16,272,128]{2,1,0:T(8,128)(2,1)}), bf16[16,272,128]{2,1,0:T(8,128)(2,1)S(1)}, u32[]{:S(2)}, u32[]{:S(2)}) %all-to-all-start.1) | async-done | bytes 1114144 | tf_op jit(solution)/shard_map/all_to_all | solution.py:667
  75.7 1.3 %stacked_finish.1 = (bf16[128,4096]{1,0:T(8,128)(2,1)}, f32[1,2]{1,0:T(1,128)}) custom-call(s32[1]{0:T(128)S(6)} %copy.12.ref_ref, s32[1]{0:T(128)S(6)} %copy.13.alt_ref, bf16[128,4096]{1,0:T(8,128)(2,1)S(1)} %slice_bitcast_fusion.gates_ref, bf16[16,272,128]{2,1,0:T(8,128)(2,1)S(1)} %all-to-all-done.1.back_ref), custom_call_target="tpu_custom_call" | custom-call | flops 524288 | bytes 3145728 | tf_op jit(solution)/shard_map/stacked_finish/pallas_call | solution.py:644
  (1 shorter events, 0.0 us)
Async XLA Ops:
  0.6 35.8 %copy-start.3 = (bf16[512,512]{1,0:T(8,128)(2,1)S(1)}, bf16[512,512]{1,0:T(8,128)(2,1)}, u32[]{:S(2)}) copy-start(bf16[512,512]{1,0:T(8,128)(2,1)} %constant.17.clone.refs_3_) | copy-start | bytes 1572868
  3.5 6.8 %copy-start.4 = (s32[16]{0:T(128)S(1)}, s32[16]{0:T(128)}, u32[]{:S(2)}) copy-start(s32[16]{0:T(128)} %offsets_ref.1) | copy-start | bytes 196
  3.5 33.0 %copy-start = (bf16[256,2048]{1,0:T(8,128)(2,1)S(1)}, bf16[256,2048]{1,0:T(8,128)(2,1)}, u32[]{:S(2)}) copy-start(bf16[256,2048]{1,0:T(8,128)(2,1)} %refs_5_.1) | copy-start | bytes 3145732
  3.5 33.0 %copy-start.1 = (bf16[256,512]{1,0:T(8,128)(2,1)S(1)}, bf16[256,512]{1,0:T(8,128)(2,1)}, u32[]{:S(2)}) copy-start(bf16[256,512]{1,0:T(8,128)(2,1)} %refs_4_.1) | copy-start | bytes 786436
  3.5 33.0 %copy-start.2 = (bf16[1024,256]{1,0:T(8,128)(2,1)S(1)}, bf16[1024,256]{1,0:T(8,128)(2,1)}, u32[]{:S(2)}) copy-start(bf16[1024,256]{1,0:T(8,128)(2,1)} %constant.16.clone.refs_2_) | copy-start | bytes 1572868
  3.5 33.0 %all-to-all-start = ((bf16[16,272,128]{2,1,0:T(8,128)(2,1)}), bf16[16,272,128]{2,1,0:T(8,128)(2,1)S(1)}, u32[]{:S(2)}, u32[]{:S(2)}) async-start(bf16[16,272,128]{2,1,0:T(8,128)(2,1)} %stacked_products.1), calls=%async_computation | async-start | bytes 2228224 | tf_op jit(solution)/shard_map/all_to_all | solution.py:667
  44.5 31.2 %all-to-all-start.1 = ((bf16[16,272,128]{2,1,0:T(8,128)(2,1)}), bf16[16,272,128]{2,1,0:T(8,128)(2,1)S(1)}, u32[]{:S(2)}, u32[]{:S(2)}) async-start(bf16[16,272,128]{2,1,0:T(8,128)(2,1)} %stacked_filter.1), calls=%async_computation.1 | async-start | bytes 2228224 | tf_op jit(solution)/shard_map/all_to_all | solution.py:667
